TPU v7x, 32 devices: a whole 2x2x4 slice. The times are simulated.
32 devices in a mesh: gx: 8 (over z, y), gy: 4 (over x, core).
Axes of the slice: x: 2, y: 2, z: 4, core: 2. Of those that a mesh axis runs over, the one named last changes fastest.
Arguments:
- phi_init: float32 [64, 32768], P(('gx', 'gy')), may hold values from -12 to 12
- source: float32 [64, 32768], P(('gx', 'gy')), may hold values from -6 to 6
- tile_mat: int32 [64, 32768], P(('gx', 'gy')), may hold values from 0 to 3
- tile_pos: int32 [64, 3], replicated, may hold values from 0 to 7, as said below
- neighbours: int32 [64, 6], P(('gx', 'gy')), may hold values from -1 to 63, as said below
- sigma_table: float32 [4], replicated, may hold values from 0.5 to 4
- temp_init: float32 [256, 16384], P('gx', 'gy'), may hold values from -6 to 6
- slab_mat: int32 [256, 16384], P('gx', 'gy'), may hold values from 0 to 3
- k0_table: float32 [4], replicated, may hold values from 0.5 to 1
- beta_table: float32 [4], replicated, may hold values from 0.1 to 1
Outputs:
- potential: float32 [64, 32768], P(('gx', 'gy'))
- temperature: float32 [256, 16384], P('gx', 'gy')
- tile_temps: float32 [64, 32768], P(('gx', 'gy'))
Inputs may be any that keep to these rules, and one draw needn't show every extreme that they name: `tile_pos`: tiles are listed in dealt order, 2 to a device, devices in mesh order (gx slowest). Positions are distinct; every tile dealt to gx index i has first coordinate in [i, (i+1)); third coordinate is 0 or 1. Of the tiles of one gx row, at most 4 lie within one slab of 1 x 2 x 2 tile positions, and some slab holds exactly 4 in every row. neighbours[t, d] is the list index of the tile at tile_pos[t] moved one step in direction d, or -1 where there is none.
All inputs are finite; a program needn't handle non-finite values.
Results may differ from a plain program's by a relative error of at most 0.00012.
Values sent between devices are 32-bit elements; how exact they have to be, the bound alone decides.
No kernel may reach another device: no remote copies, remote signals or barrier semaphores. Data moves between devices by JAX's collectives and lax.ppermute only.
A program may use at most 64 MiB of HBM per device.

v0:
```python
import functools
import math

import jax
import jax.numpy as jnp
from jax import lax
from jax.experimental import pallas as pl
from jax.experimental.pallas import tpu as pltpu
from jax.sharding import PartitionSpec as P

TE = 32
SWEEPS = 4
CSWEEPS = 3
NZ = 64
EPS = 2.0
DT = 0.15
LANES = 128
SUB = 8
TILES = 2
ROW = SUB * TILES

LOW = (SWEEPS + 2, SWEEPS + 1, 2)
HIGH = (SWEEPS + 3, SWEEPS + 2, 2)
LOW_ROWS = sum(LOW) * ROW
HIGH_ROWS = sum(HIGH) * ROW
SLABX = TE + SUB
HALO = CSWEEPS
PAD = 256


def cheb_weight(step, count):
    return 1.0 / (1.0 + 0.75 * math.cos(math.pi * (2 * step + 1) / (2 * count)))


def lookup(table, ids):
    out = jnp.full(ids.shape, table[3], jnp.float32)
    for which in (2, 1, 0):
        out = jnp.where(ids == which, table[which], out)
    return out


def prep_kernel(table, phi, src, mat, body, up, down):
    rows = TE * ROW
    sigma = lookup(table, mat[...])
    s = src[...] / sigma
    body[0:rows] = phi[...]
    body[rows : 2 * rows] = s
    body[2 * rows : 3 * rows] = sigma
    at_up, at_down = 0, 0
    for which in range(3):
        size = LOW[which] * ROW
        up[at_up : at_up + size] = body[(which + 1) * rows - size : (which + 1) * rows]
        at_up += size
        size = HIGH[which] * ROW
        down[at_down : at_down + size] = body[which * rows : which * rows + size]
        at_down += size


def slab_kernel(k0_table, beta_table, temp, mat, ylow, yhigh, xlow, xhigh, t_ext, k0_ext, b_ext):
    width = temp.shape[1]
    inner = slice(HALO, HALO + TE)
    high = slice(HALO + TE, 2 * HALO + TE)

    def fill(ref, which, own):
        wide = width + 2 * PAD
        ref[0:HALO, 0:wide] = xlow[which * HALO : (which + 1) * HALO, :]
        ref[inner, 0:PAD] = ylow[which]
        ref[inner, PAD : PAD + width] = own
        ref[inner, PAD + width : wide] = yhigh[which]
        ref[high, 0:wide] = xhigh[which * HALO : (which + 1) * HALO, :]
        ref[2 * HALO + TE :, 0:wide] = jnp.zeros((SLABX - TE - 2 * HALO, wide), jnp.float32)
        ref[:, wide:] = jnp.zeros((SLABX, ref.shape[1] - wide), jnp.float32)

    fill(t_ext, 0, temp[...])
    fill(b_ext, 1, mat[...].astype(jnp.float32))

    def block(at, carry):
        lanes = pl.ds(pl.multiple_of(at * LANES, LANES), LANES)
        ids = b_ext[:, lanes]
        k0_ext[:, lanes] = lookup(k0_table, ids)
        b_ext[:, lanes] = lookup(beta_table, ids)
        return carry

    lax.fori_loop(0, t_ext.shape[1] // LANES, block, 0)


def roll(value, by, axis):
    return pltpu.roll(value, by % value.shape[axis], axis)


def step_kernel(chips, pos, *refs):
    width_gy = 2 * chips
    tiles = width_gy * TILES
    none = tiles
    bodies = refs[:width_gy]
    halos = refs[width_gy : 2 * width_gy]
    t_in, k0_ext, b_ext = refs[2 * width_gy : 2 * width_gy + 3]
    outs = refs[2 * width_gy + 3 :]
    pot, temp_out = outs[:2]
    sends = outs[2 : 2 + width_gy]
    cell_at, cell_of, pa, pb, la, lb, ua, ub, s_c, s_l, s_u, g_c, g_l, g_u, heat, q_ext, t_ext, blocks = outs[
        2 + width_gy :
    ]
    i = lax.axis_index("gx")
    j = lax.axis_index("gy")
    rows_gx = lax.axis_size("gx")

    def clear_map(at, carry):
        for which in range(3):
            cell_at[which, at] = none
        return carry

    lax.fori_loop(0, 2 * (2 * width_gy + 2), clear_map, 0)
    mate = j + 1 - 2 * lax.rem(j, 2)
    for which, by in enumerate((0, -1, 1)):
        row = i + by
        valid = (row >= 0) & (row < rows_gx)
        first = jnp.clip(row, 0, rows_gx - 1) * tiles
        for part in range(width_gy):
            base = j if part < chips else mate
            dev = lax.rem(base - 2 * (part % chips) + width_gy, width_gy)
            for t in range(TILES):
                tile = first + dev * TILES + t
                cell = (pos[tile, 1] + 1) * 2 + pos[tile, 2]
                slot = part * TILES + t
                cell_of[which, slot] = cell
                cell_at[which, cell] = jnp.where(valid, slot, none)

    zero = jnp.zeros((SUB, LANES), jnp.float32)

    def unpack(source, start, t, target, first, count):
        def plane(p, carry):
            at = pl.multiple_of(p * ROW, ROW)
            target[first + p] = source[pl.ds(start + at + t, SUB, stride=TILES), :]
            return carry

        lax.fori_loop(0, count, plane, 0, unroll=min(count, 8))

    for part in range(width_gy):
        for t in range(TILES):
            slot = part * TILES + t
            for which, target in enumerate((pa, s_c, g_c)):
                unpack(bodies[part], which * TE * ROW, t, target, slot * TE, TE)
            at = 0
            for which, target in enumerate((la, s_l, g_l)):
                unpack(halos[part], at, t, target, slot * LOW[which], LOW[which])
                at += LOW[which] * ROW
            for which, target in enumerate((ua, s_u, g_u)):
                unpack(halos[part], at, t, target, slot * HIGH[which], HIGH[which])
                at += HIGH[which] * ROW
    for ref, count in ((pa, TE), (pb, TE), (la, LOW[0]), (lb, LOW[0]), (ua, HIGH[0]), (ub, HIGH[0])):
        for p in range(count):
            ref[none * count + p] = zero

    lane = lax.broadcasted_iota(jnp.int32, (SUB, LANES), 1)
    sub = lax.broadcasted_iota(jnp.int32, (SUB, LANES), 0)
    depth = lane % TE
    first_y, last_y = lane < TE, lane >= LANES - TE
    first_sub, last_sub = sub == 0, sub == SUB - 1
    first_z, last_z = depth == 0, depth == TE - 1

    def y_plus(own, ghost):
        turned = roll(jnp.where(first_sub, ghost, own), -1, 0)
        return roll(jnp.where(first_y, turned, own), -TE, 1)

    def y_minus(own, ghost):
        turned = roll(jnp.where(last_sub, ghost, own), 1, 0)
        return roll(jnp.where(last_y, turned, own), TE, 1)

    def z_plus(own, ghost):
        return jnp.where(last_z, roll(ghost, TE - 1, 1), roll(own, -1, 1))

    def z_minus(own, ghost):
        return jnp.where(first_z, roll(ghost, 1 - TE, 1), roll(own, 1, 1))

    def around(which, slot):
        cell = cell_of[which, slot]
        upper = cell % 2
        y_m = cell_at[which, cell - 2]
        y_p = cell_at[which, cell + 2]
        z_m = jnp.where(upper == 1, cell_at[which, cell - upper], none)
        z_p = jnp.where(upper == 0, cell_at[which, cell + 1 - upper], none)
        return cell, y_m, y_p, z_m, z_p

    bufs = ((pa, la, ua), (pb, lb, ub))
    for k in range(SWEEPS):
        weight = cheb_weight(k, SWEEPS)
        keep, gain = 1.0 - weight, weight / (6.0 + EPS)
        (c_src, l_src, u_src), (c_dst, l_dst, u_dst) = bufs[k % 2], bufs[(k + 1) % 2]

        def relax(field, size, slots, p, x_m, x_p, s):
            slot, y_m, y_p, z_m, z_p = slots
            own = field[slot * size + p]
            total = (x_m + x_p) + s
            total = total + y_minus(own, field[y_m * size + p])
            total = total + y_plus(own, field[y_p * size + p])
            total = total + z_minus(own, field[z_m * size + p])
            total = total + z_plus(own, field[z_p * size + p])
            return keep * own + gain * total

        def sweep_tile(slot, carry):
            cell, *near = around(0, slot)
            slots = (slot, *near)
            below, above = cell_at[1, cell], cell_at[2, cell]
            for p in range(TE):
                x_m = c_src[slot * TE + p - 1] if p > 0 else l_src[below * LOW[0] + LOW[0] - 1]
                x_p = c_src[slot * TE + p + 1] if p < TE - 1 else u_src[above * HIGH[0]]
                c_dst[slot * TE + p] = relax(c_src, TE, slots, p, x_m, x_p, s_c[slot * TE + p])
            cell, *near = around(1, slot)
            slots = (slot, *near)
            centre = cell_at[0, cell]
            for p in range(k + 1, LOW[0]):
                x_m = l_src[slot * LOW[0] + p - 1]
                x_p = l_src[slot * LOW[0] + p + 1] if p < LOW[0] - 1 else c_src[centre * TE]
                s = s_l[slot * LOW[1] + p - (LOW[0] - LOW[1])]
                l_dst[slot * LOW[0] + p] = relax(l_src, LOW[0], slots, p, x_m, x_p, s)
            cell, *near = around(2, slot)
            slots = (slot, *near)
            centre = cell_at[0, cell]
            for p in range(HIGH[0] - 1 - k):
                x_m = u_src[slot * HIGH[0] + p - 1] if p > 0 else c_src[centre * TE + TE - 1]
                x_p = u_src[slot * HIGH[0] + p + 1]
                u_dst[slot * HIGH[0] + p] = relax(u_src, HIGH[0], slots, p, x_m, x_p, s_u[slot * HIGH[1] + p])
            return carry

        lax.fori_loop(0, tiles, sweep_tile, 0)

    field, f_l, f_u = bufs[SWEEPS % 2]
    for t in range(TILES):
        for p in range(TE):
            pot[pl.ds(p * ROW + t, SUB, stride=TILES), :] = field[t * TE + p]

    def clear_heat(at, carry):
        heat[pl.ds(pl.multiple_of(at * SUB, SUB), SUB), :] = zero
        return carry

    lax.fori_loop(0, heat.shape[0] // SUB, clear_heat, 0, unroll=8)

    def joule(ref, size, slots, p, x_p, sigma):
        slot, _, y_p, _, z_p = slots
        own = ref[slot * size + p]
        d_x = x_p - own
        d_y = y_plus(own, ref[y_p * size + p]) - own
        d_z = z_plus(own, ref[z_p * size + p]) - own
        return sigma * (d_x * d_x + d_y * d_y + d_z * d_z)

    first_cell = 2 * (2 * j)

    def put_heat(local, x, value):
        heat[pl.ds(pl.multiple_of((local * SLABX + x) * SUB, SUB), SUB), :] = value

    def heat_tile(slot, carry):
        for which in range(3):
            cell, *near = around(which, slot)
            slots = (slot, *near)
            local = cell - first_cell
            inside = (local >= 0) & (local < 8)
            if which > 0:
                row = i - 1 if which == 1 else i + 1
                inside = inside & (row >= 0) & (row < rows_gx)

            @pl.when(inside)
            def _():
                if which == 0:
                    above = cell_at[2, cell]
                    for p in range(TE):
                        x_p = field[slot * TE + p + 1] if p < TE - 1 else f_u[above * HIGH[0]]
                        put_heat(local, HALO + p, joule(field, TE, slots, p, x_p, g_c[slot * TE + p]))
                elif which == 1:
                    centre = cell_at[0, cell]
                    for p in range(2):
                        q = LOW[0] - 2 + p
                        x_p = f_l[slot * LOW[0] + q + 1] if p < 1 else field[centre * TE]
                        put_heat(local, HALO - 2 + p, joule(f_l, LOW[0], slots, q, x_p, g_l[slot * LOW[2] + p]))
                else:
                    for p in range(2):
                        x_p = f_u[slot * HIGH[0] + p + 1]
                        put_heat(local, HALO + TE + p, joule(f_u, HIGH[0], slots, p, x_p, g_u[slot * HIGH[2] + p]))

        return carry

    lax.fori_loop(0, tiles, heat_tile, 0)

    quarter = [(lane >= q * TE) & (lane < (q + 1) * TE) for q in range(3)]

    def pick(parts):
        return jnp.where(
            quarter[0], parts[0], jnp.where(quarter[1], parts[1], jnp.where(quarter[2], parts[2], parts[3]))
        )

    quads = (t_in.shape[1] - LANES) // (2 * LANES)
    for m in range(quads):
        y0 = 4 * m - 4 + TE
        col, yq = y0 // TE, y0 % TE // 4
        for g in range(SLABX // SUB):
            a = heat[pl.ds((2 * col * SLABX + g * SUB) * SUB + yq, SUB, stride=SUB), :]
            b = heat[pl.ds(((2 * col + 1) * SLABX + g * SUB) * SUB + yq, SUB, stride=SUB), :]
            rows = slice(g * SUB, (g + 1) * SUB)
            q_ext[rows, 2 * m * LANES : (2 * m + 1) * LANES] = pick(
                (a, roll(b, TE, 1), roll(a, TE, 1), roll(b, 2 * TE, 1))
            )
            q_ext[rows, (2 * m + 1) * LANES : (2 * m + 2) * LANES] = pick(
                (roll(a, 2 * TE, 1), roll(b, -TE, 1), roll(a, -TE, 1), b)
            )

    wide = (SLABX, LANES)
    lane_w = lax.broadcasted_iota(jnp.int32, wide, 1)
    row_w = lax.broadcasted_iota(jnp.int32, wide, 0)
    half = lane_w < NZ
    no_z = lane_w % NZ == NZ - 1
    no_x = ((row_w == HALO - 1) & (i == 0)) | ((row_w == HALO + TE - 1) & (i == rows_gx - 1))
    nothing = jnp.zeros(wide, jnp.float32)
    count = 2 * quads
    low_block, high_block = PAD // LANES - 1, count - PAD // LANES - 1

    def load(ref, at):
        return ref[:, pl.ds(pl.multiple_of(at * LANES, LANES), LANES)]

    for step in range(CSWEEPS):
        source = t_in if step == 0 else t_ext

        def conduct(temp, at):
            return load(k0_ext, at) / (1.0 + load(b_ext, at) * temp * temp)

        def advance(at, carry):
            temp, cond, temp_r, cond_r, flux_before = carry
            temp_n = load(source, at + 1)
            cond_n = conduct(temp_n, at + 1)
            temp_nr, cond_nr = roll(temp_n, NZ, 1), roll(cond_n, NZ, 1)
            flux_y = (cond + jnp.where(half, cond_r, cond_nr)) * (jnp.where(half, temp_r, temp_nr) - temp)
            closed = ((at == low_block) & (j == 0)) | ((at == high_block) & (j == width_gy - 1))
            flux_y = jnp.where((lane_w >= NZ) & closed, 0.0, flux_y)
            flux_yr = roll(flux_y, NZ, 1)
            div = flux_y - jnp.where(half, flux_before, flux_yr)
            flux_x = (cond + roll(cond, -1, 0)) * (roll(temp, -1, 0) - temp)
            flux_x = jnp.where(no_x, 0.0, flux_x)
            div = div + (flux_x - roll(flux_x, 1, 0))
            flux_z = (cond + roll(cond, -1, 1)) * (roll(temp, -1, 1) - temp)
            flux_z = jnp.where(no_z, 0.0, flux_z)
            div = div + (flux_z - roll(flux_z, 1, 1))
            t_ext[:, pl.ds(pl.multiple_of(at * LANES, LANES), LANES)] = temp + DT * (0.5 * div + load(q_ext, at))
            return temp_n, cond_n, temp_nr, cond_nr, flux_yr

        temp_0 = load(source, 0)
        cond_0 = conduct(temp_0, 0)
        lax.fori_loop(
            0, count, advance, (temp_0, cond_0, roll(temp_0, NZ, 1), roll(cond_0, NZ, 1), nothing)
        )
        t_ext[:, count * LANES :] = nothing

    temp_out[...] = t_ext[HALO : HALO + TE, PAD : PAD + temp_out.shape[1]]

    for m in range(quads - 2):
        col, yq = 4 * m // TE, 4 * m % TE // 4
        for g in range(TE // SUB):
            rows = slice(g * SUB, (g + 1) * SUB)
            v = temp_out[rows, 2 * m * LANES : (2 * m + 1) * LANES]
            w = temp_out[rows, (2 * m + 1) * LANES : (2 * m + 2) * LANES]
            a = pick((v, roll(v, -TE, 1), roll(w, 2 * TE, 1), roll(w, TE, 1)))
            b = pick((roll(v, -TE, 1), roll(v, 2 * TE, 1), roll(w, TE, 1), w))
            blocks[pl.ds((2 * col * TE + g * SUB) * SUB + yq, SUB, stride=SUB), :] = a
            blocks[pl.ds(((2 * col + 1) * TE + g * SUB) * SUB + yq, SUB, stride=SUB), :] = b
    for shift in range(width_gy):
        dev = lax.rem(j + shift, width_gy)
        for t in range(TILES):
            tile = i * tiles + dev * TILES + t
            col = pos[tile, 1] - 2 * j
            cell = jnp.clip(col, 0, 1) * 2 + pos[tile, 2]
            here = (col >= 0) & (col < 2)

            def plane(p, carry):
                value = blocks[pl.ds(pl.multiple_of((cell * TE + p) * SUB, SUB), SUB), :]
                value = jnp.where(here, value, 0.0)
                sends[shift][pl.ds(pl.multiple_of(p * ROW, ROW) + t, SUB, stride=TILES), :] = value
                return carry

            lax.fori_loop(0, TE, plane, 0, unroll=8)


def shifted(value, axis, by, wrap=False):
    count = lax.axis_size(axis)
    pairs = [(d, (d + by) % count) for d in range(count) if wrap or 0 <= d + by < count]
    return lax.ppermute(value, axis, pairs)


def from_mate(value):
    return lax.ppermute(value, "gy", [(d, d ^ 1) for d in range(lax.axis_size("gy"))])


def to_rows(value):
    return value.reshape(TILES, -1, LANES).transpose(1, 0, 2).reshape(-1, LANES)


def from_rows(value):
    return value.reshape(-1, TILES, LANES).transpose(1, 0, 2).reshape(TILES, -1)


def everyone(value, chips):
    mine = [value] + [shifted(value, "gy", 2 * d, True) for d in range(1, chips)]
    return mine + [from_mate(part) for part in mine]


VMEM = pl.BlockSpec(memory_space=pltpu.VMEM)
SMEM = pl.BlockSpec(memory_space=pltpu.SMEM)
PARAMS = pltpu.CompilerParams(vmem_limit_bytes=48 * 1024 * 1024)


def on_device(
    phi_init,
    source,
    tile_mat,
    tile_pos,
    neighbours,
    sigma_table,
    temp_init,
    slab_mat,
    k0_table,
    beta_table,
):
    f32 = jnp.float32
    width_gy = lax.axis_size("gy")
    chips = width_gy // 2
    tiles = width_gy * TILES
    size_x, width = temp_init.shape
    wide = width + 2 * PAD
    shape = jax.ShapeDtypeStruct

    body, up, down = pl.pallas_call(
        prep_kernel,
        out_shape=(
            shape((3 * TE * ROW, LANES), f32),
            shape((LOW_ROWS, LANES), f32),
            shape((HIGH_ROWS, LANES), f32),
        ),
        in_specs=[SMEM, VMEM, VMEM, VMEM],
        out_specs=(VMEM, VMEM, VMEM),
        compiler_params=PARAMS,
        name="prep",
    )(sigma_table, to_rows(phi_init), to_rows(source), to_rows(tile_mat))
    bodies = everyone(body, chips)
    halo = jnp.concatenate([shifted(up, "gx", 1), shifted(down, "gx", -1)])
    halos = everyone(halo, chips)

    edge = lambda lanes: jnp.stack([temp_init[:, lanes], slab_mat[:, lanes].astype(f32)])
    ylow = shifted(edge(slice(width - PAD, None)), "gy", 1)
    yhigh = shifted(edge(slice(0, PAD)), "gy", -1)

    def x_edge(rows):
        temp = jnp.concatenate([ylow[0, rows], temp_init[rows], yhigh[0, rows]], axis=1)
        mat = jnp.concatenate([ylow[1, rows], slab_mat[rows].astype(f32), yhigh[1, rows]], axis=1)
        return jnp.concatenate([temp, mat])

    xlow = shifted(x_edge(slice(size_x - HALO, None)), "gx", 1)
    xhigh = shifted(x_edge(slice(0, HALO)), "gx", -1)

    ext = shape((SLABX, wide + LANES), f32)

    t_ext, k0_ext, b_ext = pl.pallas_call(
        slab_kernel,
        out_shape=(ext, ext, ext),
        in_specs=[SMEM, SMEM] + [VMEM] * 6,
        out_specs=(VMEM, VMEM, VMEM),
        compiler_params=PARAMS,
        name="slab_prep",
    )(k0_table, beta_table, temp_init, slab_mat, ylow, yhigh, xlow, xhigh)

    plane = (SUB, LANES)

    def planes(count):
        return pltpu.VMEM(((tiles + 1) * count, *plane), f32)

    cells = 2 * (2 * width_gy + 2)
    tile_rows = shape((TE * ROW, LANES), f32)
    results = pl.pallas_call(
        functools.partial(step_kernel, chips),
        out_shape=(tile_rows, shape((size_x, width), f32)) + (tile_rows,) * width_gy,
        in_specs=[SMEM] + [VMEM] * (2 * width_gy + 3),
        out_specs=(VMEM,) * (2 + width_gy),
        scratch_shapes=[
            pltpu.SMEM((3, cells), jnp.int32),
            pltpu.SMEM((3, tiles), jnp.int32),
            planes(TE), planes(TE), planes(LOW[0]), planes(LOW[0]), planes(HIGH[0]), planes(HIGH[0]),
            planes(TE), planes(LOW[1]), planes(HIGH[1]),
            planes(TE), planes(LOW[2]), planes(HIGH[2]),
            pltpu.VMEM((8 * SLABX * SUB, LANES), f32),
            pltpu.VMEM((SLABX, wide), f32),
            pltpu.VMEM((SLABX, wide + LANES), f32),
            pltpu.VMEM((4 * TE * SUB, LANES), f32),
        ],
        compiler_params=PARAMS,
        name="step",
    )(tile_pos, *bodies, *halos, t_ext, k0_ext, b_ext)
    pot, temp, sends = results[0], results[1], results[2:]
    tile_temps = sends[0]
    for by in range(1, width_gy):
        tile_temps = tile_temps + shifted(sends[by], "gy", by, True)
    return from_rows(pot), temp, from_rows(tile_temps)


def solution(mesh):
    placed = (
        P(("gx", "gy"), None),
        P(("gx", "gy"), None),
        P(("gx", "gy"), None),
        P(),
        P(("gx", "gy"), None),
        P(),
        P("gx", "gy"),
        P("gx", "gy"),
        P(),
        P(),
    )
    return jax.shard_map(
        on_device,
        mesh=mesh,
        in_specs=placed,
        out_specs=(P(("gx", "gy"), None), P("gx", "gy"), P(("gx", "gy"), None)),
        check_vma=False,
    )
```

profile of v0, /device:TPU:21, one launch (start us, length us, event | category | flops | bytes accessed | tf_op | source)
XLA Modules:
  0.0 107.3 jit_solution(4454161806539474151)
XLA Ops:
  0.7 1.0 copy-done.2
  1.7 0.9 copy-done.3
  2.6 0.9 copy-done.4
  3.6 0.7 copy-done.14
  4.2 0.7 prep.1
  4.9 0.7 collective-permute-start.1
  5.6 1.2 %collective-permute-start = (f32[1536,128]{1,0:T(8,128)S(1)}, f32[1536,128]{1,0:T(8,128)S(1)}, u32[]{:S(2)}, u32[]{:S(2)}) collective-permute-start(f32[1536,128]{1,0:T(8,128)S(1)} %get-tuple-element.15.refs_0_), channel_id=1, source_target_pairs={{0,2},{1,3},{2,0},{3,1},{4,6},{5,7},{6,4},{7,5},{8,10},{9,11},{10,... | collective-permute-start | bytes 2359304 | tf_op jit(solution)/shard_map/ppermute | solution.py:383
  6.9 0.8 convert_bitcast_fusion
  7.7 2.4 %collective-permute-start.8 = (f32[2,32,256]{2,1,0:T(8,128)S(1)}, f32[2,32,256]{2,1,0:T(8,128)S(1)}, u32[]{:S(2)}, u32[]{:S(2)}) collective-permute-start(f32[2,32,256]{2,1,0:T(8,128)S(1)} %pad_maximum_fusion), channel_id=1, source_target_pairs={{0,1},{1,2},{2,3},{4,5},{5,6},{6,7},{8,9},{9,10},{10,11},{12,13},{... | collective-permute-start | bytes 196616 | tf_op jit(solution)/shard_map/ppermute | solution.py:383
  10.1 1.9 %collective-permute-start.9 = (f32[2,32,256]{2,1,0:T(8,128)S(1)}, f32[2,32,256]{2,1,0:T(8,128)S(1)}, u32[]{:S(2)}, u32[]{:S(2)}) collective-permute-start(f32[2,32,256]{2,1,0:T(8,128)S(1)} %pad_maximum_fusion.1), channel_id=1, source_target_pairs={{1,0},{2,1},{3,2},{5,4},{6,5},{7,6},{9,8},{10,9},{11,10},{13,12},{... | collective-permute-start | bytes 196616 | tf_op jit(solution)/shard_map/ppermute | solution.py:383
  12.0 3.1 %collective-permute-start.3 = (f32[208,128]{1,0:T(8,128)S(1)}, f32[208,128]{1,0:T(8,128)S(1)}, u32[]{:S(2)}, u32[]{:S(2)}) collective-permute-start(f32[208,128]{1,0:T(8,128)S(1)} %get-tuple-element.16), channel_id=1, source_target_pairs={{0,4},{4,8},{8,12},{12,16},{16,20},{20,24},{24,28},{1,5},{5,9},{9,... | collective-permute-start | bytes 319496 | tf_op jit(solution)/shard_map/ppermute | solution.py:383
  15.3 9.7 %collective-permute-done.8.ylow = f32[2,32,256]{2,1,0:T(8,128)S(1)} collective-permute-done((f32[2,32,256]{2,1,0:T(8,128)S(1)}, f32[2,32,256]{2,1,0:T(8,128)S(1)}, u32[]{:S(2)}, u32[]{:S(2)}) %collective-permute-start.8) | collective-permute-done | bytes 65568 | tf_op jit(solution)/shard_map/ppermute | solution.py:383
  24.9 2.1 %collective-permute-start.4 = (f32[240,128]{1,0:T(8,128)S(1)}, f32[240,128]{1,0:T(8,128)S(1)}, u32[]{:S(2)}, u32[]{:S(2)}) collective-permute-start(f32[240,128]{1,0:T(8,128)S(1)} %get-tuple-element.17), channel_id=1, source_target_pairs={{4,0},{8,4},{12,8},{16,12},{20,16},{24,20},{28,24},{5,1},{9,5},{13... | collective-permute-start | bytes 368648 | tf_op jit(solution)/shard_map/ppermute | solution.py:383
  27.7 3.7 %collective-permute-done.4 = f32[240,128]{1,0:T(8,128)S(1)} collective-permute-done((f32[240,128]{1,0:T(8,128)S(1)}, f32[240,128]{1,0:T(8,128)S(1)}, u32[]{:S(2)}, u32[]{:S(2)}) %collective-permute-start.4) | collective-permute-done | bytes 122912 | tf_op jit(solution)/shard_map/ppermute | solution.py:383
  31.5 4.0 %collective-permute-start.2 = (f32[1536,128]{1,0:T(8,128)S(1)}, f32[1536,128]{1,0:T(8,128)}, u32[]{:S(2)}, u32[]{:S(2)}) collective-permute-start(f32[1536,128]{1,0:T(8,128)S(1)} %collective-permute-done.refs_1_), channel_id=1, source_target_pairs={{0,1},{1,0},{2,3},{3,2},{4,5},{5,4},{6,7},{7,6},{8,9},{9,8},{10,11... | collective-permute-start | bytes 2359304 | tf_op jit(solution)/shard_map/ppermute | solution.py:387
  35.6 2.2 %collective-permute-start.10 = (f32[6,4608]{1,0:T(8,128)S(1)}, f32[6,4608]{1,0:T(8,128)S(1)}, u32[]{:S(2)}, u32[]{:S(2)}) collective-permute-start(f32[6,4608]{1,0:T(8,128)S(1)} %maximum_maximum_fusion), channel_id=1, source_target_pairs={{0,4},{4,8},{8,12},{12,16},{16,20},{20,24},{24,28},{1,5},{5,9},{9,... | collective-permute-start | bytes 331784 | tf_op jit(solution)/shard_map/ppermute | solution.py:383
  38.2 1.4 %collective-permute-start.7 = (f32[448,128]{1,0:T(8,128)S(1)}, f32[448,128]{1,0:T(8,128)S(1)}, u32[]{:S(2)}, u32[]{:S(2)}) collective-permute-start(f32[448,128]{1,0:T(8,128)S(1)} %collective-permute-done.5.refs_5_), channel_id=1, source_target_pairs={{0,1},{1,0},{2,3},{3,2},{4,5},{5,4},{6,7},{7,6},{8,9},{9,8},{10,11... | collective-permute-start | bytes 688136 | tf_op jit(solution)/shard_map/ppermute | solution.py:387
  39.5 0.7 maximum_maximum_fusion.1
  40.2 2.7 %collective-permute-done.10.xlow = f32[6,4608]{1,0:T(8,128)S(1)} collective-permute-done((f32[6,4608]{1,0:T(8,128)S(1)}, f32[6,4608]{1,0:T(8,128)S(1)}, u32[]{:S(2)}, u32[]{:S(2)}) %collective-permute-start.10) | collective-permute-done | bytes 110624 | tf_op jit(solution)/shard_map/ppermute | solution.py:383
  43.0 0.7 copy-done.5
  43.6 2.1 %collective-permute-start.11 = (f32[6,4608]{1,0:T(8,128)}, f32[6,4608]{1,0:T(8,128)}, u32[]{:S(2)}, u32[]{:S(2)}) collective-permute-start(f32[6,4608]{1,0:T(8,128)} %maximum_maximum_fusion.1), channel_id=1, source_target_pairs={{4,0},{8,4},{12,8},{16,12},{20,16},{24,20},{28,24},{5,1},{9,5},{13... | collective-permute-start | bytes 331784 | tf_op jit(solution)/shard_map/ppermute | solution.py:383
  45.8 0.7 copy.15.pos
  46.5 4.8 %collective-permute-done.11.xhigh = f32[6,4608]{1,0:T(8,128)} collective-permute-done((f32[6,4608]{1,0:T(8,128)}, f32[6,4608]{1,0:T(8,128)}, u32[]{:S(2)}, u32[]{:S(2)}) %collective-permute-start.11) | collective-permute-done | bytes 110624 | tf_op jit(solution)/shard_map/ppermute | solution.py:383
  51.3 0.9 copy-done.6
  52.2 0.8 copy-done.9
  53.1 0.8 copy-done.11
  53.9 1.6 %slab_prep.1 = (f32[40,4736]{1,0:T(8,128)S(1)}, f32[40,4736]{1,0:T(8,128)S(1)}, f32[40,4736]{1,0:T(8,128)S(1)}) custom-call(f32[4]{0:T(128)S(1)} %copy-done.12, f32[4]{0:T(128)S(1)} %copy-done.13, f32[32,4096]{1,0:T(8,128)S(1)} %copy-done, s32[32,4096]{1,0:T(8,128)S(1)} %copy-done.1, f32[2,32,256]{2,1,0:T(8,128)S(1)} %copy-done.9, ...), custom_call_target="tpu_custom_call" | custom-call | tf_op jit(solution)/shard_map/slab_prep/pallas_call | solution.py:458
  55.5 36.2 %step.1 = (f32[512,128]{1,0:T(8,128)}, f32[32,4096]{1,0:T(8,128)}, f32[512,128]{1,0:T(8,128)S(1)}, f32[512,128]{1,0:T(8,128)S(1)}, f32[512,128]{1,0:T(8,128)S(1)}, /*index=5*/f32[512,128]{1,0:T(8,128)S(1)}) custom-call(s32[64,3]{1,0:T(8,128)S(1)} %copy-done.7, f32[1536,128]{1,0:T(8,128)S(1)} %get-tuple-element.15.refs_0_, ...), custom_call_target="tpu_custom_call" | custom-call | tf_op jit(solution)/shard_map/step/pallas_call | solution.py:474
  92.3 2.0 %collective-permute-start.13 = (f32[512,128]{1,0:T(8,128)S(1)}, f32[512,128]{1,0:T(8,128)S(1)}, u32[]{:S(2)}, u32[]{:S(2)}) collective-permute-start(f32[512,128]{1,0:T(8,128)S(1)} %get-tuple-element.25), channel_id=1, source_target_pairs={{0,2},{1,3},{2,0},{3,1},{4,6},{5,7},{6,4},{7,5},{8,10},{9,11},{10,... | collective-permute-start | bytes 786440 | tf_op jit(solution)/shard_map/ppermute | solution.py:383
  94.4 3.3 %collective-permute-done.12 = f32[512,128]{1,0:T(8,128)S(1)} collective-permute-done((f32[512,128]{1,0:T(8,128)S(1)}, f32[512,128]{1,0:T(8,128)S(1)}, u32[]{:S(2)}, u32[]{:S(2)}) %collective-permute-start.12) | collective-permute-done | bytes 262176 | tf_op jit(solution)/shard_map/ppermute | solution.py:383
  97.6 8.4 %collective-permute-done.13 = f32[512,128]{1,0:T(8,128)S(1)} collective-permute-done((f32[512,128]{1,0:T(8,128)S(1)}, f32[512,128]{1,0:T(8,128)S(1)}, u32[]{:S(2)}, u32[]{:S(2)}) %collective-permute-start.13) | collective-permute-done | bytes 262176 | tf_op jit(solution)/shard_map/ppermute | solution.py:383
  106.5 0.8 add_add_fusion
  (47 shorter events, 2.4 us)
Async XLA Ops:
  0.6 6.2 %copy-start = (f32[32,4096]{1,0:T(8,128)S(1)}, f32[32,4096]{1,0:T(8,128)}, u32[]{:S(2)}) copy-start(f32[32,4096]{1,0:T(8,128)} %temp.1) | copy-start | bytes 1572868
  0.6 1.0 copy-start.2
  1.6 0.9 copy-start.3
  2.6 0.9 copy-start.4
  3.6 0.7 copy-start.14
  4.9 10.3 %copy-start.1 = (s32[32,4096]{1,0:T(8,128)S(1)}, s32[32,4096]{1,0:T(8,128)}, u32[]{:S(2)}) copy-start(s32[32,4096]{1,0:T(8,128)} %mat.1) | copy-start | bytes 1572868
  4.9 50.6 %collective-permute-start.1 = (f32[1536,128]{1,0:T(8,128)S(1)}, f32[1536,128]{1,0:T(8,128)}, u32[]{:S(2)}, u32[]{:S(2)}) collective-permute-start(f32[1536,128]{1,0:T(8,128)S(1)} %get-tuple-element.15.refs_0_), channel_id=1, source_target_pairs={{0,1},{1,0},{2,3},{3,2},{4,5},{5,4},{6,7},{7,6},{8,9},{9,8},{10,11... | collective-permute-start | bytes 2359304 | tf_op jit(solution)/shard_map/ppermute | solution.py:387
  5.6 25.9 %collective-permute-start = (f32[1536,128]{1,0:T(8,128)S(1)}, f32[1536,128]{1,0:T(8,128)S(1)}, u32[]{:S(2)}, u32[]{:S(2)}) collective-permute-start(f32[1536,128]{1,0:T(8,128)S(1)} %get-tuple-element.15.refs_0_), channel_id=1, source_target_pairs={{0,2},{1,3},{2,0},{3,1},{4,6},{5,7},{6,4},{7,5},{8,10},{9,11},{10,... | collective-permute-start | bytes 2359304 | tf_op jit(solution)/shard_map/ppermute | solution.py:383
  7.7 17.3 %collective-permute-start.8 = (f32[2,32,256]{2,1,0:T(8,128)S(1)}, f32[2,32,256]{2,1,0:T(8,128)S(1)}, u32[]{:S(2)}, u32[]{:S(2)}) collective-permute-start(f32[2,32,256]{2,1,0:T(8,128)S(1)} %pad_maximum_fusion), channel_id=1, source_target_pairs={{0,1},{1,2},{2,3},{4,5},{5,6},{6,7},{8,9},{9,10},{10,11},{12,13},{... | collective-permute-start | bytes 196616 | tf_op jit(solution)/shard_map/ppermute | solution.py:383
  10.1 17.0 %collective-permute-start.9 = (f32[2,32,256]{2,1,0:T(8,128)S(1)}, f32[2,32,256]{2,1,0:T(8,128)S(1)}, u32[]{:S(2)}, u32[]{:S(2)}) collective-permute-start(f32[2,32,256]{2,1,0:T(8,128)S(1)} %pad_maximum_fusion.1), channel_id=1, source_target_pairs={{1,0},{2,1},{3,2},{5,4},{6,5},{7,6},{9,8},{10,9},{11,10},{13,12},{... | collective-permute-start | bytes 196616 | tf_op jit(solution)/shard_map/ppermute | solution.py:383
  12.0 15.1 %collective-permute-start.3 = (f32[208,128]{1,0:T(8,128)S(1)}, f32[208,128]{1,0:T(8,128)S(1)}, u32[]{:S(2)}, u32[]{:S(2)}) collective-permute-start(f32[208,128]{1,0:T(8,128)S(1)} %get-tuple-element.16), channel_id=1, source_target_pairs={{0,4},{4,8},{8,12},{12,16},{16,20},{20,24},{24,28},{1,5},{5,9},{9,... | collective-permute-start | bytes 319496 | tf_op jit(solution)/shard_map/ppermute | solution.py:383
  24.9 2.2 %copy-start.8 = (f32[2,32,256]{2,1,0:T(8,128)}, f32[2,32,256]{2,1,0:T(8,128)S(1)}, u32[]{:S(2)}) copy-start(f32[2,32,256]{2,1,0:T(8,128)S(1)} %collective-permute-done.8.ylow) | copy-start | bytes 196612
  24.9 6.5 %collective-permute-start.4 = (f32[240,128]{1,0:T(8,128)S(1)}, f32[240,128]{1,0:T(8,128)S(1)}, u32[]{:S(2)}, u32[]{:S(2)}) collective-permute-start(f32[240,128]{1,0:T(8,128)S(1)} %get-tuple-element.17), channel_id=1, source_target_pairs={{4,0},{8,4},{12,8},{16,12},{20,16},{24,20},{28,24},{5,1},{9,5},{13... | collective-permute-start | bytes 368648 | tf_op jit(solution)/shard_map/ppermute | solution.py:383
  27.1 0.6 copy-start.10
  31.4 6.7 %collective-permute-start.5 = (f32[448,128]{1,0:T(8,128)S(1)}, f32[448,128]{1,0:T(8,128)S(1)}, u32[]{:S(2)}, u32[]{:S(2)}) collective-permute-start(f32[448,128]{1,0:T(8,128)S(1)} %constant_dynamic-update-slice_fusion.refs_4_), channel_id=1, source_target_pairs={{0,2},{1,3},{2,0},{3,1},{4,6},{5,7},{6,4},{7,5},{8,10},{9,11},{10,... | collective-permute-start | bytes 688136 | tf_op jit(solution)/shard_map/ppermute | solution.py:383
  31.5 24.0 %collective-permute-start.2 = (f32[1536,128]{1,0:T(8,128)S(1)}, f32[1536,128]{1,0:T(8,128)}, u32[]{:S(2)}, u32[]{:S(2)}) collective-permute-start(f32[1536,128]{1,0:T(8,128)S(1)} %collective-permute-done.refs_1_), channel_id=1, source_target_pairs={{0,1},{1,0},{2,3},{3,2},{4,5},{5,4},{6,7},{7,6},{8,9},{9,8},{10,11... | collective-permute-start | bytes 2359304 | tf_op jit(solution)/shard_map/ppermute | solution.py:387
  35.6 7.4 %collective-permute-start.10 = (f32[6,4608]{1,0:T(8,128)S(1)}, f32[6,4608]{1,0:T(8,128)S(1)}, u32[]{:S(2)}, u32[]{:S(2)}) collective-permute-start(f32[6,4608]{1,0:T(8,128)S(1)} %maximum_maximum_fusion), channel_id=1, source_target_pairs={{0,4},{4,8},{8,12},{12,16},{16,20},{20,24},{24,28},{1,5},{5,9},{9,... | collective-permute-start | bytes 331784 | tf_op jit(solution)/shard_map/ppermute | solution.py:383
  37.8 17.6 %collective-permute-start.6 = (f32[448,128]{1,0:T(8,128)S(1)}, f32[448,128]{1,0:T(8,128)S(1)}, u32[]{:S(2)}, u32[]{:S(2)}) collective-permute-start(f32[448,128]{1,0:T(8,128)S(1)} %constant_dynamic-update-slice_fusion.refs_4_), channel_id=1, source_target_pairs={{0,1},{1,0},{2,3},{3,2},{4,5},{5,4},{6,7},{7,6},{8,9},{9,8},{10,11... | collective-permute-start | bytes 688136 | tf_op jit(solution)/shard_map/ppermute | solution.py:387
  38.2 17.3 %collective-permute-start.7 = (f32[448,128]{1,0:T(8,128)S(1)}, f32[448,128]{1,0:T(8,128)S(1)}, u32[]{:S(2)}, u32[]{:S(2)}) collective-permute-start(f32[448,128]{1,0:T(8,128)S(1)} %collective-permute-done.5.refs_5_), channel_id=1, source_target_pairs={{0,1},{1,0},{2,3},{3,2},{4,5},{5,4},{6,7},{7,6},{8,9},{9,8},{10,11... | collective-permute-start | bytes 688136 | tf_op jit(solution)/shard_map/ppermute | solution.py:387
  39.5 6.2 %copy-start.15 = (s32[64,3]{0,1:T(4,128)S(1)}, s32[64,3]{0,1:T(4,128)}, u32[]{:S(2)}) copy-start(s32[64,3]{0,1:T(4,128)} %param.13) | copy-start | bytes 2308
  40.2 11.1 %copy-start.12 = (f32[4]{0:T(128)S(1)}, f32[4]{0:T(128)}, u32[]{:S(2)}) copy-start(f32[4]{0:T(128)} %k0_table.1) | copy-start | bytes 52
  40.2 11.1 %copy-start.13 = (f32[4]{0:T(128)S(1)}, f32[4]{0:T(128)}, u32[]{:S(2)}) copy-start(f32[4]{0:T(128)} %beta_table.1) | copy-start | bytes 52
  43.0 0.7 copy-start.5
  43.6 7.7 %collective-permute-start.11 = (f32[6,4608]{1,0:T(8,128)}, f32[6,4608]{1,0:T(8,128)}, u32[]{:S(2)}, u32[]{:S(2)}) collective-permute-start(f32[6,4608]{1,0:T(8,128)} %maximum_maximum_fusion.1), channel_id=1, source_target_pairs={{4,0},{8,4},{12,8},{16,12},{20,16},{24,20},{28,24},{5,1},{9,5},{13... | collective-permute-start | bytes 331784 | tf_op jit(solution)/shard_map/ppermute | solution.py:383
  51.3 0.9 copy-start.6
  52.2 0.8 copy-start.9
  53.1 0.8 copy-start.11
  53.9 1.6 %copy-start.7 = (s32[64,3]{1,0:T(8,128)S(1)}, s32[64,3]{1,0:T(8,128)}, u32[]{:S(2)}) copy-start(s32[64,3]{1,0:T(8,128)} %copy.15.pos) | copy-start | bytes 2308
  91.7 5.9 %collective-permute-start.12 = (f32[512,128]{1,0:T(8,128)S(1)}, f32[512,128]{1,0:T(8,128)S(1)}, u32[]{:S(2)}, u32[]{:S(2)}) collective-permute-start(f32[512,128]{1,0:T(8,128)S(1)} %get-tuple-element.24), channel_id=1, source_target_pairs={{0,1},{1,2},{2,3},{3,0},{4,5},{5,6},{6,7},{7,4},{8,9},{9,10},{10,1... | collective-permute-start | bytes 786440 | tf_op jit(solution)/shard_map/ppermute | solution.py:383
  92.3 13.6 %collective-permute-start.13 = (f32[512,128]{1,0:T(8,128)S(1)}, f32[512,128]{1,0:T(8,128)S(1)}, u32[]{:S(2)}, u32[]{:S(2)}) collective-permute-start(f32[512,128]{1,0:T(8,128)S(1)} %get-tuple-element.25), channel_id=1, source_target_pairs={{0,2},{1,3},{2,0},{3,1},{4,6},{5,7},{6,4},{7,5},{8,10},{9,11},{10,... | collective-permute-start | bytes 786440 | tf_op jit(solution)/shard_map/ppermute | solution.py:383
  94.4 12.2 %collective-permute-start.14 = (f32[512,128]{1,0:T(8,128)S(1)}, f32[512,128]{1,0:T(8,128)S(1)}, u32[]{:S(2)}, u32[]{:S(2)}) collective-permute-start(f32[512,128]{1,0:T(8,128)S(1)} %get-tuple-element.26), channel_id=1, source_target_pairs={{0,3},{1,0},{2,1},{3,2},{4,7},{5,4},{6,5},{7,6},{8,11},{9,8},{10,9... | collective-permute-start | bytes 786440 | tf_op jit(solution)/shard_map/ppermute | solution.py:383
where the time goes:
time: 108 us; the launch traced here: 107 us
  Pallas kernels  38.4 us (36%)
  waiting for transfers between devices  33.2 us (31%)
  starting transfers between devices  24.4 us (23%)
  local copies, waits for them, and re-layouts  8.16 us (8%)
  other arithmetic  2.3 us (2%)
    pallas_call x1, Pallas kernels, on_device(): pl.pallas_call(functools.partial(step_kernel, chips), out_shape=(tile_row...  36.2 us
    ppermute x11, waiting for transfers between devices, shifted(): return lax.ppermute(value, axis, pairs)  33.1 us
    ppermute x11, starting transfers between devices, shifted(): return lax.ppermute(value, axis, pairs)  17.9 us
    unnamed x34, local copies, waits for them, and re-layouts  8.1 us
    ppermute x4, starting transfers between devices, from_mate(): lax.ppermute(value, 'gy', [(d, d ^ 1) for d in range(lax.axis_size('gy'))])  6.45 us
  transfers between devices with their start and end apart: 15, of which 7 were waited for; matrix products, arithmetic and copies ran while one was open for 2% of the time, Pallas kernels for 1%

commit v1 on v0

--- a/solution.py
+++ b/solution.py
@@ -39,92 +39,125 @@
     return out
 
 
-def prep_kernel(table, phi, src, mat, body, up, down):
+def roll(value, by, axis):
+    return pltpu.roll(value, by % value.shape[axis], axis)
+
+
+def prep_kernel(table, phi, src, mat, temp, slab, body, sigma, up, down, src_v, mat_v, ends_t, ends_m, sems):
     rows = TE * ROW
-    sigma = lookup(table, mat[...])
-    s = src[...] / sigma
-    body[0:rows] = phi[...]
-    body[rows : 2 * rows] = s
-    body[2 * rows : 3 * rows] = sigma
+    size_x, width = temp.shape
+    moves = [(phi, body.at[0:rows]), (src, src_v), (mat, mat_v)]
+    for which, first in enumerate((0, size_x - SUB)):
+        moves.append((temp.at[first : first + SUB], ends_t.at[which]))
+        moves.append((slab.at[first : first + SUB], ends_m.at[which]))
+    moves = [pltpu.make_async_copy(*move, sems.at[at]) for at, move in enumerate(moves)]
+    for move in moves:
+        move.start()
+    for move in moves:
+        move.wait()
+    sigma[...] = lookup(table, mat_v[...])
+    body[rows : 2 * rows] = src_v[...] / sigma[...]
     at_up, at_down = 0, 0
-    for which in range(3):
+    for ref, first in ((body, 0), (body, rows), (sigma, 0)):
+        which = (first // rows) if ref is body else 2
         size = LOW[which] * ROW
-        up[at_up : at_up + size] = body[(which + 1) * rows - size : (which + 1) * rows]
+        up[at_up : at_up + size] = ref[first + rows - size : first + rows]
         at_up += size
         size = HIGH[which] * ROW
-        down[at_down : at_down + size] = body[which * rows : which * rows + size]
+        down[at_down : at_down + size] = ref[first : first + size]
         at_down += size
+    sub = lax.broadcasted_iota(jnp.int32, (SUB, LANES), 0)
+    for at in range(width // LANES):
+        lanes = slice(at * LANES, (at + 1) * LANES)
+        t_low, m_low = ends_t[0, :, lanes], ends_m[0, :, lanes].astype(jnp.float32)
+        t_high, m_high = ends_t[1, :, lanes], ends_m[1, :, lanes].astype(jnp.float32)
+        first = at * SUB
+        up[LOW_ROWS + first : LOW_ROWS + first + SUB] = jnp.where(sub < 4, roll(t_high, HALO, 0), roll(m_high, -1, 0))
+        down[HIGH_ROWS + first : HIGH_ROWS + first + SUB] = jnp.where(sub < 4, t_low, roll(m_low, 4, 0))
+
+
+def relay_kernel(low, high, temp, mat, halo, edge_low, edge_high):
+    halo[0:LOW_ROWS] = low[0:LOW_ROWS]
+    halo[LOW_ROWS : LOW_ROWS + HIGH_ROWS] = high[0:HIGH_ROWS]
+    blocks = temp.shape[1] // LANES
+    for edge, firsts in ((edge_low, (0, 1)), (edge_high, (blocks - 2, blocks - 1))):
+        for at, block in enumerate(firsts):
+            lanes = slice(at * LANES, (at + 1) * LANES)
+            own = slice(block * LANES, (block + 1) * LANES)
+            for which, value in enumerate((temp[:, own], mat[:, own].astype(jnp.float32))):
+                edge[which, HALO : HALO + TE, lanes] = value
+                first = LOW_ROWS + block * SUB + 4 * which
+                edge[which, 0:HALO, lanes] = low[first : first + HALO, :]
+                first = HIGH_ROWS + block * SUB + 4 * which
+                edge[which, HALO + TE : 2 * HALO + TE, lanes] = high[first : first + HALO, :]
+                rest = SLABX - TE - 2 * HALO
+                edge[which, SLABX - rest :, lanes] = jnp.zeros((rest, LANES), jnp.float32)
 
 
 def slab_kernel(k0_table, beta_table, temp, mat, ylow, yhigh, xlow, xhigh, t_ext, k0_ext, b_ext):
     width = temp.shape[1]
     inner = slice(HALO, HALO + TE)
     high = slice(HALO + TE, 2 * HALO + TE)
-
-    def fill(ref, which, own):
-        wide = width + 2 * PAD
-        ref[0:HALO, 0:wide] = xlow[which * HALO : (which + 1) * HALO, :]
-        ref[inner, 0:PAD] = ylow[which]
-        ref[inner, PAD : PAD + width] = own
-        ref[inner, PAD + width : wide] = yhigh[which]
-        ref[high, 0:wide] = xhigh[which * HALO : (which + 1) * HALO, :]
-        ref[2 * HALO + TE :, 0:wide] = jnp.zeros((SLABX - TE - 2 * HALO, wide), jnp.float32)
-        ref[:, wide:] = jnp.zeros((SLABX, ref.shape[1] - wide), jnp.float32)
-
-    fill(t_ext, 0, temp[...])
-    fill(b_ext, 1, mat[...].astype(jnp.float32))
-
-    def block(at, carry):
-        lanes = pl.ds(pl.multiple_of(at * LANES, LANES), LANES)
+    rest = slice(2 * HALO + TE, SLABX)
+    for which, (own, target) in enumerate(((temp, t_ext), (mat, b_ext))):
+        target[:, 0:PAD] = ylow[which]
+        target[:, PAD + width : 2 * PAD + width] = yhigh[which]
+        target[:, 2 * PAD + width :] = jnp.zeros((SLABX, LANES), jnp.float32)
+        target[rest, PAD : PAD + width] = jnp.zeros((SLABX - TE - 2 * HALO, width), jnp.float32)
+        for at in range(width // LANES):
+            lanes = slice(PAD + at * LANES, PAD + (at + 1) * LANES)
+            first = LOW_ROWS + at * SUB + 4 * which
+            target[0:HALO, lanes] = xlow[first : first + HALO, :]
+            first = HIGH_ROWS + at * SUB + 4 * which
+            target[high, lanes] = xhigh[first : first + HALO, :]
+            target[inner, lanes] = own[:, at * LANES : (at + 1) * LANES].astype(jnp.float32)
+    for at in range(t_ext.shape[1] // LANES):
+        lanes = slice(at * LANES, (at + 1) * LANES)
         ids = b_ext[:, lanes]
         k0_ext[:, lanes] = lookup(k0_table, ids)
         b_ext[:, lanes] = lookup(beta_table, ids)
-        return carry
-
-    lax.fori_loop(0, t_ext.shape[1] // LANES, block, 0)
-
-
-def roll(value, by, axis):
-    return pltpu.roll(value, by % value.shape[axis], axis)
-
-
-def step_kernel(chips, pos, *refs):
+
+
+def fill_maps(chips, pos, cell_at, cell_of):
+    width_gy = 2 * chips
+    tiles = width_gy * TILES
+    i = lax.axis_index("gx")
+    j = lax.axis_index("gy")
+    rows_gx = lax.axis_size("gx")
+    for at in range(2 * (2 * width_gy + 2)):
+        for which in range(3):
+            cell_at[which, at] = tiles
+    for which, by in enumerate((0, -1, 1)):
+        row = i + by
+        valid = (row >= 0) & (row < rows_gx)
+        first = jnp.clip(row, 0, rows_gx - 1) * tiles
+        for part in range(width_gy):
+            dev = part_device(part, chips, j)
+            for t in range(TILES):
+                tile = first + dev * TILES + t
+                cell = (pos[tile, 1] + 1) * 2 + pos[tile, 2]
+                slot = part * TILES + t
+                cell_of[which, slot] = cell
+                cell_at[which, cell] = jnp.where(valid, slot, tiles)
+
+
+def part_device(part, chips, j):
+    mate = j + 1 - 2 * lax.rem(j, 2)
+    base = j if part < chips else mate
+    return lax.rem(base - 2 * (part % chips) + 2 * chips, 2 * chips)
+
+
+def sweep_kernel(chips, pos, *refs):
     width_gy = 2 * chips
     tiles = width_gy * TILES
     none = tiles
     bodies = refs[:width_gy]
     halos = refs[width_gy : 2 * width_gy]
-    t_in, k0_ext, b_ext = refs[2 * width_gy : 2 * width_gy + 3]
-    outs = refs[2 * width_gy + 3 :]
-    pot, temp_out = outs[:2]
-    sends = outs[2 : 2 + width_gy]
-    cell_at, cell_of, pa, pb, la, lb, ua, ub, s_c, s_l, s_u, g_c, g_l, g_u, heat, q_ext, t_ext, blocks = outs[
-        2 + width_gy :
-    ]
+    pot, slope, cell_at, cell_of, pa, pb, la, lb, ua, ub, s_c, s_l, s_u = refs[2 * width_gy :]
     i = lax.axis_index("gx")
     j = lax.axis_index("gy")
     rows_gx = lax.axis_size("gx")
-
-    def clear_map(at, carry):
-        for which in range(3):
-            cell_at[which, at] = none
-        return carry
-
-    lax.fori_loop(0, 2 * (2 * width_gy + 2), clear_map, 0)
-    mate = j + 1 - 2 * lax.rem(j, 2)
-    for which, by in enumerate((0, -1, 1)):
-        row = i + by
-        valid = (row >= 0) & (row < rows_gx)
-        first = jnp.clip(row, 0, rows_gx - 1) * tiles
-        for part in range(width_gy):
-            base = j if part < chips else mate
-            dev = lax.rem(base - 2 * (part % chips) + width_gy, width_gy)
-            for t in range(TILES):
-                tile = first + dev * TILES + t
-                cell = (pos[tile, 1] + 1) * 2 + pos[tile, 2]
-                slot = part * TILES + t
-                cell_of[which, slot] = cell
-                cell_at[which, cell] = jnp.where(valid, slot, none)
+    fill_maps(chips, pos, cell_at, cell_of)
 
     zero = jnp.zeros((SUB, LANES), jnp.float32)
 
@@ -139,13 +172,14 @@
     for part in range(width_gy):
         for t in range(TILES):
             slot = part * TILES + t
-            for which, target in enumerate((pa, s_c, g_c)):
+            for which, target in enumerate((pa, s_c)):
                 unpack(bodies[part], which * TE * ROW, t, target, slot * TE, TE)
             at = 0
-            for which, target in enumerate((la, s_l, g_l)):
+            for which, target in enumerate((la, s_l)):
                 unpack(halos[part], at, t, target, slot * LOW[which], LOW[which])
                 at += LOW[which] * ROW
-            for which, target in enumerate((ua, s_u, g_u)):
+            at = LOW_ROWS
+            for which, target in enumerate((ua, s_u)):
                 unpack(halos[part], at, t, target, slot * HIGH[which], HIGH[which])
                 at += HIGH[which] * ROW
     for ref, count in ((pa, TE), (pb, TE), (la, LOW[0]), (lb, LOW[0]), (ua, HIGH[0]), (ub, HIGH[0])):
@@ -230,34 +264,28 @@
         for p in range(TE):
             pot[pl.ds(p * ROW + t, SUB, stride=TILES), :] = field[t * TE + p]
 
-    def clear_heat(at, carry):
-        heat[pl.ds(pl.multiple_of(at * SUB, SUB), SUB), :] = zero
+    def clear(at, carry):
+        slope[pl.ds(pl.multiple_of(at * SUB, SUB), SUB), :] = zero
         return carry
 
-    lax.fori_loop(0, heat.shape[0] // SUB, clear_heat, 0, unroll=8)
-
-    def joule(ref, size, slots, p, x_p, sigma):
+    lax.fori_loop(0, slope.shape[0] // SUB, clear, 0, unroll=8)
+
+    def squares(ref, size, slots, p, x_p):
         slot, _, y_p, _, z_p = slots
         own = ref[slot * size + p]
         d_x = x_p - own
         d_y = y_plus(own, ref[y_p * size + p]) - own
         d_z = z_plus(own, ref[z_p * size + p]) - own
-        return sigma * (d_x * d_x + d_y * d_y + d_z * d_z)
-
-    first_cell = 2 * (2 * j)
-
-    def put_heat(local, x, value):
-        heat[pl.ds(pl.multiple_of((local * SLABX + x) * SUB, SUB), SUB), :] = value
-
-    def heat_tile(slot, carry):
+        return d_x * d_x + d_y * d_y + d_z * d_z
+
+    def put(local, x, value):
+        slope[pl.ds(pl.multiple_of((local * SLABX + x) * SUB, SUB), SUB), :] = value
+
+    def slope_tile(slot, carry):
         for which in range(3):
             cell, *near = around(which, slot)
             slots = (slot, *near)
-            local = cell - first_cell
-            inside = (local >= 0) & (local < 8)
-            if which > 0:
-                row = i - 1 if which == 1 else i + 1
-                inside = inside & (row >= 0) & (row < rows_gx)
+            local, inside = window(which, cell, i, j, rows_gx)
 
             @pl.when(inside)
             def _():
@@ -265,21 +293,71 @@
                     above = cell_at[2, cell]
                     for p in range(TE):
                         x_p = field[slot * TE + p + 1] if p < TE - 1 else f_u[above * HIGH[0]]
-                        put_heat(local, HALO + p, joule(field, TE, slots, p, x_p, g_c[slot * TE + p]))
+                        put(local, HALO + p, squares(field, TE, slots, p, x_p))
                 elif which == 1:
                     centre = cell_at[0, cell]
                     for p in range(2):
                         q = LOW[0] - 2 + p
                         x_p = f_l[slot * LOW[0] + q + 1] if p < 1 else field[centre * TE]
-                        put_heat(local, HALO - 2 + p, joule(f_l, LOW[0], slots, q, x_p, g_l[slot * LOW[2] + p]))
+                        put(local, HALO - 2 + p, squares(f_l, LOW[0], slots, q, x_p))
                 else:
                     for p in range(2):
                         x_p = f_u[slot * HIGH[0] + p + 1]
-                        put_heat(local, HALO + TE + p, joule(f_u, HIGH[0], slots, p, x_p, g_u[slot * HIGH[2] + p]))
+                        put(local, HALO + TE + p, squares(f_u, HIGH[0], slots, p, x_p))
 
         return carry
 
-    lax.fori_loop(0, tiles, heat_tile, 0)
+    lax.fori_loop(0, tiles, slope_tile, 0)
+
+
+def window(which, cell, i, j, rows_gx):
+    local = cell - 4 * j
+    inside = (local >= 0) & (local < 8)
+    if which > 0:
+        row = i - 1 if which == 1 else i + 1
+        inside = inside & (row >= 0) & (row < rows_gx)
+    return local, inside
+
+
+def slab_steps_kernel(chips, pos, *refs):
+    width_gy = 2 * chips
+    tiles = width_gy * TILES
+    sigmas = refs[:width_gy]
+    halos = refs[width_gy : 2 * width_gy]
+    slope, t_in, k0_ext, b_ext, temp_out = refs[2 * width_gy : 2 * width_gy + 5]
+    sends = refs[2 * width_gy + 5 : 3 * width_gy + 5]
+    heat, q_ext, t_ext, blocks = refs[3 * width_gy + 5 :]
+    i = lax.axis_index("gx")
+    j = lax.axis_index("gy")
+    rows_gx = lax.axis_size("gx")
+    lane = lax.broadcasted_iota(jnp.int32, (SUB, LANES), 1)
+    zero = jnp.zeros((SUB, LANES), jnp.float32)
+
+    def clear(at, carry):
+        heat[pl.ds(pl.multiple_of(at * SUB, SUB), SUB), :] = zero
+        return carry
+
+    lax.fori_loop(0, heat.shape[0] // SUB, clear, 0, unroll=8)
+    low_at, high_at = (LOW[0] + LOW[1]) * ROW, LOW_ROWS + (HIGH[0] + HIGH[1]) * ROW
+    for part in range(width_gy):
+        dev = part_device(part, chips, j)
+        for t in range(TILES):
+            for which, by in enumerate((0, -1, 1)):
+                tile = jnp.clip(i + by, 0, rows_gx - 1) * tiles + dev * TILES + t
+                cell = (pos[tile, 1] + 1) * 2 + pos[tile, 2]
+                local, inside = window(which, cell, i, j, rows_gx)
+                source, start, x, count = (
+                    (sigmas[part], 0, HALO, TE),
+                    (halos[part], low_at, HALO - 2, 2),
+                    (halos[part], high_at, HALO + TE, 2),
+                )[which]
+
+                @pl.when(inside)
+                def _():
+                    for p in range(count):
+                        rows = pl.ds(pl.multiple_of((local * SLABX + x + p) * SUB, SUB), SUB)
+                        sigma = source[pl.ds(start + p * ROW + t, SUB, stride=TILES), :]
+                        heat[rows, :] = sigma * slope[rows, :]
 
     quarter = [(lane >= q * TE) & (lane < (q + 1) * TE) for q in range(3)]
 
@@ -314,38 +392,36 @@
     low_block, high_block = PAD // LANES - 1, count - PAD // LANES - 1
 
     def load(ref, at):
-        return ref[:, pl.ds(pl.multiple_of(at * LANES, LANES), LANES)]
+        return ref[:, at * LANES : (at + 1) * LANES]
 
     for step in range(CSWEEPS):
         source = t_in if step == 0 else t_ext
 
-        def conduct(temp, at):
-            return load(k0_ext, at) / (1.0 + load(b_ext, at) * temp * temp)
-
-        def advance(at, carry):
-            temp, cond, temp_r, cond_r, flux_before = carry
-            temp_n = load(source, at + 1)
-            cond_n = conduct(temp_n, at + 1)
-            temp_nr, cond_nr = roll(temp_n, NZ, 1), roll(cond_n, NZ, 1)
-            flux_y = (cond + jnp.where(half, cond_r, cond_nr)) * (jnp.where(half, temp_r, temp_nr) - temp)
-            closed = ((at == low_block) & (j == 0)) | ((at == high_block) & (j == width_gy - 1))
-            flux_y = jnp.where((lane_w >= NZ) & closed, 0.0, flux_y)
+        def fetch(at):
+            temp = load(source, at)
+            cond = load(k0_ext, at) / (1.0 + load(b_ext, at) * temp * temp)
+            return temp, cond, roll(temp, NZ, 1), roll(cond, NZ, 1)
+
+        ahead = fetch(0)
+        flux_before = nothing
+        for at in range(count):
+            temp, cond, temp_r, cond_r = ahead
+            ahead = fetch(at + 1)
+            flux_y = (cond + jnp.where(half, cond_r, ahead[3])) * (jnp.where(half, temp_r, ahead[2]) - temp)
+            if at == low_block:
+                flux_y = jnp.where((lane_w >= NZ) & (j == 0), 0.0, flux_y)
+            if at == high_block:
+                flux_y = jnp.where((lane_w >= NZ) & (j == width_gy - 1), 0.0, flux_y)
             flux_yr = roll(flux_y, NZ, 1)
             div = flux_y - jnp.where(half, flux_before, flux_yr)
+            flux_before = flux_yr
             flux_x = (cond + roll(cond, -1, 0)) * (roll(temp, -1, 0) - temp)
             flux_x = jnp.where(no_x, 0.0, flux_x)
             div = div + (flux_x - roll(flux_x, 1, 0))
             flux_z = (cond + roll(cond, -1, 1)) * (roll(temp, -1, 1) - temp)
             flux_z = jnp.where(no_z, 0.0, flux_z)
             div = div + (flux_z - roll(flux_z, 1, 1))
-            t_ext[:, pl.ds(pl.multiple_of(at * LANES, LANES), LANES)] = temp + DT * (0.5 * div + load(q_ext, at))
-            return temp_n, cond_n, temp_nr, cond_nr, flux_yr
-
-        temp_0 = load(source, 0)
-        cond_0 = conduct(temp_0, 0)
-        lax.fori_loop(
-            0, count, advance, (temp_0, cond_0, roll(temp_0, NZ, 1), roll(cond_0, NZ, 1), nothing)
-        )
+            t_ext[:, at * LANES : (at + 1) * LANES] = temp + DT * (0.5 * div + load(q_ext, at))
         t_ext[:, count * LANES :] = nothing
 
     temp_out[...] = t_ext[HALO : HALO + TE, PAD : PAD + temp_out.shape[1]]
@@ -367,14 +443,9 @@
             col = pos[tile, 1] - 2 * j
             cell = jnp.clip(col, 0, 1) * 2 + pos[tile, 2]
             here = (col >= 0) & (col < 2)
-
-            def plane(p, carry):
+            for p in range(TE):
                 value = blocks[pl.ds(pl.multiple_of((cell * TE + p) * SUB, SUB), SUB), :]
-                value = jnp.where(here, value, 0.0)
-                sends[shift][pl.ds(pl.multiple_of(p * ROW, ROW) + t, SUB, stride=TILES), :] = value
-                return carry
-
-            lax.fori_loop(0, TE, plane, 0, unroll=8)
+                sends[shift][pl.ds(p * ROW + t, SUB, stride=TILES), :] = jnp.where(here, value, 0.0)
 
 
 def shifted(value, axis, by, wrap=False):
@@ -400,8 +471,18 @@
     return mine + [from_mate(part) for part in mine]
 
 
+def everyone_direct(value, chips):
+    mine = [value] + [shifted(value, "gy", 2 * d, True) for d in range(1, chips)]
+    count = 2 * chips
+    for d in range(chips):
+        pairs = [(at, ((at ^ 1) + 2 * d) % count) for at in range(count)]
+        mine.append(lax.ppermute(value, "gy", pairs))
+    return mine
+
+
 VMEM = pl.BlockSpec(memory_space=pltpu.VMEM)
 SMEM = pl.BlockSpec(memory_space=pltpu.SMEM)
+HBM = pl.BlockSpec(memory_space=pltpu.HBM)
 PARAMS = pltpu.CompilerParams(vmem_limit_bytes=48 * 1024 * 1024)
 
 
@@ -423,38 +504,48 @@
     tiles = width_gy * TILES
     size_x, width = temp_init.shape
     wide = width + 2 * PAD
-    shape = jax.ShapeDtypeStruct
-
-    body, up, down = pl.pallas_call(
+    edge_rows = width // LANES * SUB
+
+    def rows(count):
+        return jax.ShapeDtypeStruct((count, LANES), f32)
+
+    body, sigma, up, down = pl.pallas_call(
         prep_kernel,
         out_shape=(
-            shape((3 * TE * ROW, LANES), f32),
-            shape((LOW_ROWS, LANES), f32),
-            shape((HIGH_ROWS, LANES), f32),
+            rows(2 * TE * ROW),
+            rows(TE * ROW),
+            rows(LOW_ROWS + edge_rows),
+            rows(HIGH_ROWS + edge_rows),
         ),
-        in_specs=[SMEM, VMEM, VMEM, VMEM],
-        out_specs=(VMEM, VMEM, VMEM),
+        in_specs=[SMEM] + [HBM] * 5,
+        out_specs=(VMEM,) * 4,
+        scratch_shapes=[
+            pltpu.VMEM((TE * ROW, LANES), f32),
+            pltpu.VMEM((TE * ROW, LANES), jnp.int32),
+            pltpu.VMEM((2, SUB, width), f32),
+            pltpu.VMEM((2, SUB, width), jnp.int32),
+            pltpu.SemaphoreType.DMA((7,)),
+        ],
         compiler_params=PARAMS,
         name="prep",
-    )(sigma_table, to_rows(phi_init), to_rows(source), to_rows(tile_mat))
+    )(sigma_table, to_rows(phi_init), to_rows(source), to_rows(tile_mat), temp_init, slab_mat)
     bodies = everyone(body, chips)
-    halo = jnp.concatenate([shifted(up, "gx", 1), shifted(down, "gx", -1)])
+    low, high = shifted(up, "gx", 1), shifted(down, "gx", -1)
+
+    edge = jax.ShapeDtypeStruct((2, SLABX, PAD), f32)
+    halo, edge_low, edge_high = pl.pallas_call(
+        relay_kernel,
+        out_shape=(rows(LOW_ROWS + HIGH_ROWS), edge, edge),
+        in_specs=[VMEM] * 4,
+        out_specs=(VMEM,) * 3,
+        compiler_params=PARAMS,
+        name="relay",
+    )(low, high, temp_init, slab_mat)
     halos = everyone(halo, chips)
-
-    edge = lambda lanes: jnp.stack([temp_init[:, lanes], slab_mat[:, lanes].astype(f32)])
-    ylow = shifted(edge(slice(width - PAD, None)), "gy", 1)
-    yhigh = shifted(edge(slice(0, PAD)), "gy", -1)
-
-    def x_edge(rows):
-        temp = jnp.concatenate([ylow[0, rows], temp_init[rows], yhigh[0, rows]], axis=1)
-        mat = jnp.concatenate([ylow[1, rows], slab_mat[rows].astype(f32), yhigh[1, rows]], axis=1)
-        return jnp.concatenate([temp, mat])
-
-    xlow = shifted(x_edge(slice(size_x - HALO, None)), "gx", 1)
-    xhigh = shifted(x_edge(slice(0, HALO)), "gx", -1)
-
-    ext = shape((SLABX, wide + LANES), f32)
-
+    ylow, yhigh = shifted(edge_high, "gy", 1), shifted(edge_low, "gy", -1)
+    sigmas = everyone_direct(sigma, chips)
+
+    ext = jax.ShapeDtypeStruct((SLABX, wide + LANES), f32)
     t_ext, k0_ext, b_ext = pl.pallas_call(
         slab_kernel,
         out_shape=(ext, ext, ext),
@@ -462,35 +553,40 @@
         out_specs=(VMEM, VMEM, VMEM),
         compiler_params=PARAMS,
         name="slab_prep",
-    )(k0_table, beta_table, temp_init, slab_mat, ylow, yhigh, xlow, xhigh)
-
-    plane = (SUB, LANES)
+    )(k0_table, beta_table, temp_init, slab_mat, ylow, yhigh, low, high)
 
     def planes(count):
-        return pltpu.VMEM(((tiles + 1) * count, *plane), f32)
-
-    cells = 2 * (2 * width_gy + 2)
-    tile_rows = shape((TE * ROW, LANES), f32)
-    results = pl.pallas_call(
-        functools.partial(step_kernel, chips),
-        out_shape=(tile_rows, shape((size_x, width), f32)) + (tile_rows,) * width_gy,
-        in_specs=[SMEM] + [VMEM] * (2 * width_gy + 3),
-        out_specs=(VMEM,) * (2 + width_gy),
+        return pltpu.VMEM(((tiles + 1) * count, SUB, LANES), f32)
+
+    pot, slope = pl.pallas_call(
+        functools.partial(sweep_kernel, chips),
+        out_shape=(rows(TE * ROW), rows(8 * SLABX * SUB)),
+        in_specs=[SMEM] + [VMEM] * (2 * width_gy),
+        out_specs=(VMEM,) * 2,
         scratch_shapes=[
-            pltpu.SMEM((3, cells), jnp.int32),
+            pltpu.SMEM((3, 2 * (2 * width_gy + 2)), jnp.int32),
             pltpu.SMEM((3, tiles), jnp.int32),
             planes(TE), planes(TE), planes(LOW[0]), planes(LOW[0]), planes(HIGH[0]), planes(HIGH[0]),
             planes(TE), planes(LOW[1]), planes(HIGH[1]),
-            planes(TE), planes(LOW[2]), planes(HIGH[2]),
+        ],
+        compiler_params=PARAMS,
+        name="sweeps",
+    )(tile_pos, *bodies, *halos)
+
+    temp, *sends = pl.pallas_call(
+        functools.partial(slab_steps_kernel, chips),
+        out_shape=(jax.ShapeDtypeStruct((size_x, width), f32),) + (rows(TE * ROW),) * width_gy,
+        in_specs=[SMEM] + [VMEM] * (2 * width_gy + 4),
+        out_specs=(VMEM,) * (1 + width_gy),
+        scratch_shapes=[
             pltpu.VMEM((8 * SLABX * SUB, LANES), f32),
             pltpu.VMEM((SLABX, wide), f32),
             pltpu.VMEM((SLABX, wide + LANES), f32),
             pltpu.VMEM((4 * TE * SUB, LANES), f32),
         ],
         compiler_params=PARAMS,
-        name="step",
-    )(tile_pos, *bodies, *halos, t_ext, k0_ext, b_ext)
-    pot, temp, sends = results[0], results[1], results[2:]
+        name="slab_steps",
+    )(tile_pos, *sigmas, *halos, slope, t_ext, k0_ext, b_ext)
     tile_temps = sends[0]
     for by in range(1, width_gy):
         tile_temps = tile_temps + shifted(sends[by], "gy", by, True)

time: 108 us -> 100 us (0.926)
  the two profiles are of different devices: /device:TPU:21 before, /device:TPU:5 now
where the time goes in v1:
time: 100 us; the launch traced here: 99.5 us
  Pallas kernels  39.6 us (40%)
  waiting for transfers between devices  28 us (28%)
  starting transfers between devices  19.7 us (20%)
  local copies, waits for them, and re-layouts  10.7 us (11%)
    ppermute x10, waiting for transfers between devices, shifted(): return lax.ppermute(value, axis, pairs)  27.9 us
    pallas_call x1, Pallas kernels, on_device(): pl.pallas_call(functools.partial(slab_steps_kernel, chips), out_shape=(ja...  21.6 us
    ppermute x10, starting transfers between devices, shifted(): return lax.ppermute(value, axis, pairs)  16.3 us
    pallas_call x1, Pallas kernels, on_device(): pl.pallas_call(functools.partial(sweep_kernel, chips), out_shape=(rows(TE...  14.8 us
    unnamed x37, local copies, waits for them, and re-layouts  10.7 us
    ppermute x4, starting transfers between devices, from_mate(): lax.ppermute(value, 'gy', [(d, d ^ 1) for d in range(lax.axis_size('gy'))])  3.38 us
    pallas_call x1, Pallas kernels, on_device(): pl.pallas_call(prep_kernel, out_shape=(rows(2 * TE * ROW), rows(TE * ROW)...  2.12 us
  transfers between devices with their start and end apart: 16, of which 7 were waited for; matrix products, arithmetic and copies ran while one was open for 0% of the time, Pallas kernels for 16%

profile of v1, /device:TPU:5, one launch (start us, length us, event | category | flops | bytes accessed | tf_op | source)
XLA Modules:
  0.0 99.5 jit_solution(17829623839382624042)
XLA Ops:
  0.6 1.0 %copy-done = f32[32,4096]{1,0:T(8,128)S(1)} copy-done((f32[32,4096]{1,0:T(8,128)S(1)}, f32[32,4096]{1,0:T(8,128)}, u32[]{:S(2)}) %copy-start) | copy-done | bytes 524312
  1.7 1.0 %copy-done.2 = s32[32,4096]{1,0:T(8,128)S(1)} copy-done((s32[32,4096]{1,0:T(8,128)S(1)}, s32[32,4096]{1,0:T(8,128)}, u32[]{:S(2)}) %copy-start.2) | copy-done | bytes 524312
  2.7 0.9 copy-done.7
  3.7 0.9 copy-done.8
  4.6 0.9 copy-done.9
  5.6 0.7 copy-done.16
  6.2 2.1 %prep.1 = (f32[1024,128]{1,0:T(8,128)S(1)}, f32[512,128]{1,0:T(8,128)}, f32[464,128]{1,0:T(8,128)S(1)}, f32[496,128]{1,0:T(8,128)S(1)}) custom-call(f32[4]{0:T(128)S(1)} %copy-done.16, f32[512,128]{1,0:T(8,128)S(1)} %bitcast.25, f32[512,128]{1,0:T(8,128)S(1)} %bitcast.26, s32[512,128]{1,0:T(8,128)S(1)} %bitcast.27, f32[32,4096]{1,0:T(8,128)S(1)} %copy-done, ...), custom_call_target="tpu_custom_call" | custom-call | tf_op jit(solution)/shard_map/prep/pallas_call | solution.py:512
  8.4 1.3 %collective-permute-start = (f32[1024,128]{1,0:T(8,128)S(1)}, f32[1024,128]{1,0:T(8,128)S(1)}, u32[]{:S(2)}, u32[]{:S(2)}) collective-permute-start(f32[1024,128]{1,0:T(8,128)S(1)} %get-tuple-element.20.refs_0_), channel_id=1, source_target_pairs={{0,2},{1,3},{2,0},{3,1},{4,6},{5,7},{6,4},{7,5},{8,10},{9,11},{10,... | collective-permute-start | bytes 1572872 | tf_op jit(solution)/shard_map/ppermute | solution.py:454
  9.7 1.0 collective-permute-start.1
  10.6 2.1 %collective-permute-start.4 = (f32[496,128]{1,0:T(8,128)S(1)}, f32[496,128]{1,0:T(8,128)S(1)}, u32[]{:S(2)}, u32[]{:S(2)}) collective-permute-start(f32[496,128]{1,0:T(8,128)S(1)} %get-tuple-element.22), channel_id=1, source_target_pairs={{4,0},{8,4},{12,8},{16,12},{20,16},{24,20},{28,24},{5,1},{9,5},{13... | collective-permute-start | bytes 761864 | tf_op jit(solution)/shard_map/ppermute | solution.py:454
  12.7 4.0 %collective-permute-start.3 = (f32[464,128]{1,0:T(8,128)S(1)}, f32[464,128]{1,0:T(8,128)S(1)}, u32[]{:S(2)}, u32[]{:S(2)}) collective-permute-start(f32[464,128]{1,0:T(8,128)S(1)} %get-tuple-element.21), channel_id=1, source_target_pairs={{0,4},{4,8},{8,12},{12,16},{16,20},{20,24},{24,28},{1,5},{5,9},{9,... | collective-permute-start | bytes 712712 | tf_op jit(solution)/shard_map/ppermute | solution.py:454
  16.8 4.4 %collective-permute-done.refs_1_ = f32[1024,128]{1,0:T(8,128)S(1)} collective-permute-done((f32[1024,128]{1,0:T(8,128)S(1)}, f32[1024,128]{1,0:T(8,128)S(1)}, u32[]{:S(2)}, u32[]{:S(2)}) %collective-permute-start) | collective-permute-done | bytes 524320 | tf_op jit(solution)/shard_map/ppermute | solution.py:454
  21.2 1.5 %collective-permute-start.2 = (f32[1024,128]{1,0:T(8,128)S(1)}, f32[1024,128]{1,0:T(8,128)}, u32[]{:S(2)}, u32[]{:S(2)}) collective-permute-start(f32[1024,128]{1,0:T(8,128)S(1)} %collective-permute-done.refs_1_), channel_id=1, source_target_pairs={{0,1},{1,0},{2,3},{3,2},{4,5},{5,4},{6,7},{7,6},{8,9},{9,8},{10,11... | collective-permute-start | bytes 1572872 | tf_op jit(solution)/shard_map/ppermute | solution.py:458
  22.8 3.8 %collective-permute-done.3.low.xlow = f32[464,128]{1,0:T(8,128)S(1)} collective-permute-done((f32[464,128]{1,0:T(8,128)S(1)}, f32[464,128]{1,0:T(8,128)S(1)}, u32[]{:S(2)}, u32[]{:S(2)}) %collective-permute-start.3) | collective-permute-done | bytes 237600 | tf_op jit(solution)/shard_map/ppermute | solution.py:454
  27.4 3.3 %collective-permute-start.11 = (f32[2,40,256]{2,1,0:T(8,128)S(1)}, f32[2,40,256]{2,1,0:T(8,128)S(1)}, u32[]{:S(2)}, u32[]{:S(2)}) collective-permute-start(f32[2,40,256]{2,1,0:T(8,128)S(1)} %get-tuple-element.27), channel_id=1, source_target_pairs={{0,1},{1,2},{2,3},{4,5},{5,6},{6,7},{8,9},{9,10},{10,11},{12,13},{... | collective-permute-start | bytes 245768 | tf_op jit(solution)/shard_map/ppermute | solution.py:454
  30.8 3.0 %collective-permute-done.11.ylow = f32[2,40,256]{2,1,0:T(8,128)S(1)} collective-permute-done((f32[2,40,256]{2,1,0:T(8,128)S(1)}, f32[2,40,256]{2,1,0:T(8,128)S(1)}, u32[]{:S(2)}, u32[]{:S(2)}) %collective-permute-start.11) | collective-permute-done | bytes 81952 | tf_op jit(solution)/shard_map/ppermute | solution.py:454
  34.4 1.9 %collective-permute-start.12 = (f32[2,40,256]{2,1,0:T(8,128)S(1)}, f32[2,40,256]{2,1,0:T(8,128)S(1)}, u32[]{:S(2)}, u32[]{:S(2)}) collective-permute-start(f32[2,40,256]{2,1,0:T(8,128)S(1)} %get-tuple-element.28), channel_id=1, source_target_pairs={{1,0},{2,1},{3,2},{5,4},{6,5},{7,6},{9,8},{10,9},{11,10},{13,12},{... | collective-permute-start | bytes 245768 | tf_op jit(solution)/shard_map/ppermute | solution.py:454
  36.3 4.6 %collective-permute-done.12.yhigh = f32[2,40,256]{2,1,0:T(8,128)S(1)} collective-permute-done((f32[2,40,256]{2,1,0:T(8,128)S(1)}, f32[2,40,256]{2,1,0:T(8,128)S(1)}, u32[]{:S(2)}, u32[]{:S(2)}) %collective-permute-start.12) | collective-permute-done | bytes 81952 | tf_op jit(solution)/shard_map/ppermute | solution.py:454
  40.9 0.6 copy-done.12
  41.5 1.8 %collective-permute-start.8 = (f32[512,128]{1,0:T(8,128)}, f32[512,128]{1,0:T(8,128)}, u32[]{:S(2)}, u32[]{:S(2)}) collective-permute-start(f32[512,128]{1,0:T(8,128)} %get-tuple-element.25.refs_0_), channel_id=1, source_target_pairs={{0,2},{1,3},{2,0},{3,1},{4,6},{5,7},{6,4},{7,5},{8,10},{9,11},{10,... | collective-permute-start | bytes 786440 | tf_op jit(solution)/shard_map/ppermute | solution.py:454
  43.4 0.8 copy-done.5
  44.6 0.9 copy-done.11
  45.5 0.9 copy-done.13
  46.4 0.9 slab_prep.1
  47.4 14.8 %sweeps.1 = (f32[512,128]{1,0:T(8,128)}, f32[2560,128]{1,0:T(8,128)S(1)}) custom-call(s32[64,3]{1,0:T(8,128)S(1)} %copy.15.pos, f32[1024,128]{1,0:T(8,128)S(1)} %get-tuple-element.20.refs_0_, f32[1024,128]{1,0:T(8,128)S(1)} %collective-permute-done.refs_1_, f32[1024,128]{1,0:T(8,128)S(1)} %copy-done.6, f32[1024,128]{1,0:T(8,128)} %collective-permute-done.2.refs_3_, ...), custom_call_target="tpu_custom_call" | custom-call | tf_op jit(solution)/shard_map/sweeps/pallas_call | solution.py:561
  62.3 1.1 %copy-done.4 = f32[2560,128]{1,0:T(8,128)} copy-done((f32[2560,128]{1,0:T(8,128)}, f32[2560,128]{1,0:T(8,128)S(1)}, u32[]{:S(2)}) %copy-start.4) | copy-done | bytes 1310744
  63.4 21.6 %slab_steps.1 = (f32[32,4096]{1,0:T(8,128)}, f32[512,128]{1,0:T(8,128)S(1)}, f32[512,128]{1,0:T(8,128)S(1)}, f32[512,128]{1,0:T(8,128)S(1)}, f32[512,128]{1,0:T(8,128)S(1)}) custom-call(s32[64,3]{1,0:T(8,128)S(1)} %copy.15.pos, f32[512,128]{1,0:T(8,128)} %get-tuple-element.25.refs_0_, f32[512,128]{1,0:T(8,128)} %collective-permute-done.8.refs_1_, ...), custom_call_target="tpu_custom_call" | custom-call | tf_op jit(solution)/shard_map/slab_steps/pallas_call | solution.py:576
  85.0 1.5 %collective-permute-start.14 = (f32[512,128]{1,0:T(8,128)S(1)}, f32[512,128]{1,0:T(8,128)S(1)}, u32[]{:S(2)}, u32[]{:S(2)}) collective-permute-start(f32[512,128]{1,0:T(8,128)S(1)} %get-tuple-element.35), channel_id=1, source_target_pairs={{0,2},{1,3},{2,0},{3,1},{4,6},{5,7},{6,4},{7,5},{8,10},{9,11},{10,... | collective-permute-start | bytes 786440 | tf_op jit(solution)/shard_map/ppermute | solution.py:454
  86.5 4.0 %collective-permute-done.13 = f32[512,128]{1,0:T(8,128)S(1)} collective-permute-done((f32[512,128]{1,0:T(8,128)S(1)}, f32[512,128]{1,0:T(8,128)S(1)}, u32[]{:S(2)}, u32[]{:S(2)}) %collective-permute-start.13) | collective-permute-done | bytes 262176 | tf_op jit(solution)/shard_map/ppermute | solution.py:454
  90.5 7.3 %collective-permute-done.14 = f32[512,128]{1,0:T(8,128)S(1)} collective-permute-done((f32[512,128]{1,0:T(8,128)S(1)}, f32[512,128]{1,0:T(8,128)S(1)}, u32[]{:S(2)}, u32[]{:S(2)}) %collective-permute-start.14) | collective-permute-done | bytes 262176 | tf_op jit(solution)/shard_map/ppermute | solution.py:454
  97.8 0.9 collective-permute-done.15
  98.7 0.8 add_add_fusion
  (43 shorter events, 2.1 us)
Async XLA Ops:
  0.6 1.0 %copy-start = (f32[32,4096]{1,0:T(8,128)S(1)}, f32[32,4096]{1,0:T(8,128)}, u32[]{:S(2)}) copy-start(f32[32,4096]{1,0:T(8,128)} %temp.5) | copy-start | bytes 1572868
  1.7 1.0 %copy-start.2 = (s32[32,4096]{1,0:T(8,128)S(1)}, s32[32,4096]{1,0:T(8,128)}, u32[]{:S(2)}) copy-start(s32[32,4096]{1,0:T(8,128)} %mat.3) | copy-start | bytes 1572868
  2.7 0.9 copy-start.7
  3.7 0.9 copy-start.8
  4.6 0.9 copy-start.9
  5.6 0.7 copy-start.16
  6.2 20.3 %copy-start.1 = (f32[32,4096]{1,0:T(8,128)S(1)}, f32[32,4096]{1,0:T(8,128)}, u32[]{:S(2)}) copy-start(f32[32,4096]{1,0:T(8,128)} %temp.5) | copy-start | bytes 1572868
  6.2 20.3 %copy-start.3 = (s32[32,4096]{1,0:T(8,128)S(1)}, s32[32,4096]{1,0:T(8,128)}, u32[]{:S(2)}) copy-start(s32[32,4096]{1,0:T(8,128)} %mat.3) | copy-start | bytes 1572868
  6.2 38.3 %copy-start.17 = (s32[64,3]{0,1:T(4,128)S(1)}, s32[64,3]{0,1:T(4,128)}, u32[]{:S(2)}) copy-start(s32[64,3]{0,1:T(4,128)} %param.13) | copy-start | bytes 2308
  6.2 38.4 %copy-start.14 = (f32[4]{0:T(128)S(1)}, f32[4]{0:T(128)}, u32[]{:S(2)}) copy-start(f32[4]{0:T(128)} %k0_table.1) | copy-start | bytes 52
  6.2 38.4 %copy-start.15 = (f32[4]{0:T(128)S(1)}, f32[4]{0:T(128)}, u32[]{:S(2)}) copy-start(f32[4]{0:T(128)} %beta_table.1) | copy-start | bytes 52
  8.4 12.9 %collective-permute-start = (f32[1024,128]{1,0:T(8,128)S(1)}, f32[1024,128]{1,0:T(8,128)S(1)}, u32[]{:S(2)}, u32[]{:S(2)}) collective-permute-start(f32[1024,128]{1,0:T(8,128)S(1)} %get-tuple-element.20.refs_0_), channel_id=1, source_target_pairs={{0,2},{1,3},{2,0},{3,1},{4,6},{5,7},{6,4},{7,5},{8,10},{9,11},{10,... | collective-permute-start | bytes 1572872 | tf_op jit(solution)/shard_map/ppermute | solution.py:454
  9.7 33.7 %collective-permute-start.1 = (f32[1024,128]{1,0:T(8,128)S(1)}, f32[1024,128]{1,0:T(8,128)S(1)}, u32[]{:S(2)}, u32[]{:S(2)}) collective-permute-start(f32[1024,128]{1,0:T(8,128)S(1)} %get-tuple-element.20.refs_0_), channel_id=1, source_target_pairs={{0,1},{1,0},{2,3},{3,2},{4,5},{5,4},{6,7},{7,6},{8,9},{9,8},{10,11... | collective-permute-start | bytes 1572872 | tf_op jit(solution)/shard_map/ppermute | solution.py:458
  10.6 16.0 %collective-permute-start.4 = (f32[496,128]{1,0:T(8,128)S(1)}, f32[496,128]{1,0:T(8,128)S(1)}, u32[]{:S(2)}, u32[]{:S(2)}) collective-permute-start(f32[496,128]{1,0:T(8,128)S(1)} %get-tuple-element.22), channel_id=1, source_target_pairs={{4,0},{8,4},{12,8},{16,12},{20,16},{24,20},{28,24},{5,1},{9,5},{13... | collective-permute-start | bytes 761864 | tf_op jit(solution)/shard_map/ppermute | solution.py:454
  12.7 13.8 %collective-permute-start.3 = (f32[464,128]{1,0:T(8,128)S(1)}, f32[464,128]{1,0:T(8,128)S(1)}, u32[]{:S(2)}, u32[]{:S(2)}) collective-permute-start(f32[464,128]{1,0:T(8,128)S(1)} %get-tuple-element.21), channel_id=1, source_target_pairs={{0,4},{4,8},{8,12},{12,16},{16,20},{20,24},{24,28},{1,5},{5,9},{9,... | collective-permute-start | bytes 712712 | tf_op jit(solution)/shard_map/ppermute | solution.py:454
  21.2 26.1 %collective-permute-start.2 = (f32[1024,128]{1,0:T(8,128)S(1)}, f32[1024,128]{1,0:T(8,128)}, u32[]{:S(2)}, u32[]{:S(2)}) collective-permute-start(f32[1024,128]{1,0:T(8,128)S(1)} %collective-permute-done.refs_1_), channel_id=1, source_target_pairs={{0,1},{1,0},{2,3},{3,2},{4,5},{5,4},{6,7},{7,6},{8,9},{9,8},{10,11... | collective-permute-start | bytes 1572872 | tf_op jit(solution)/shard_map/ppermute | solution.py:458
  26.6 14.9 %collective-permute-start.6 = (f32[448,128]{1,0:T(8,128)S(1)}, f32[448,128]{1,0:T(8,128)S(1)}, u32[]{:S(2)}, u32[]{:S(2)}) collective-permute-start(f32[448,128]{1,0:T(8,128)S(1)} %get-tuple-element.23.refs_4_), channel_id=1, source_target_pairs={{0,1},{1,0},{2,3},{3,2},{4,5},{5,4},{6,7},{7,6},{8,9},{9,8},{10,11... | collective-permute-start | bytes 688136 | tf_op jit(solution)/shard_map/ppermute | solution.py:458
  27.1 14.4 %collective-permute-start.5 = (f32[448,128]{1,0:T(8,128)S(1)}, f32[448,128]{1,0:T(8,128)S(1)}, u32[]{:S(2)}, u32[]{:S(2)}) collective-permute-start(f32[448,128]{1,0:T(8,128)S(1)} %get-tuple-element.23.refs_4_), channel_id=1, source_target_pairs={{0,2},{1,3},{2,0},{3,1},{4,6},{5,7},{6,4},{7,5},{8,10},{9,11},{10,... | collective-permute-start | bytes 688136 | tf_op jit(solution)/shard_map/ppermute | solution.py:454
  27.4 6.3 %collective-permute-start.11 = (f32[2,40,256]{2,1,0:T(8,128)S(1)}, f32[2,40,256]{2,1,0:T(8,128)S(1)}, u32[]{:S(2)}, u32[]{:S(2)}) collective-permute-start(f32[2,40,256]{2,1,0:T(8,128)S(1)} %get-tuple-element.27), channel_id=1, source_target_pairs={{0,1},{1,2},{2,3},{4,5},{5,6},{6,7},{8,9},{9,10},{10,11},{12,13},{... | collective-permute-start | bytes 245768 | tf_op jit(solution)/shard_map/ppermute | solution.py:454
  34.4 6.5 %collective-permute-start.12 = (f32[2,40,256]{2,1,0:T(8,128)S(1)}, f32[2,40,256]{2,1,0:T(8,128)S(1)}, u32[]{:S(2)}, u32[]{:S(2)}) collective-permute-start(f32[2,40,256]{2,1,0:T(8,128)S(1)} %get-tuple-element.28), channel_id=1, source_target_pairs={{1,0},{2,1},{3,2},{5,4},{6,5},{7,6},{9,8},{10,9},{11,10},{13,12},{... | collective-permute-start | bytes 245768 | tf_op jit(solution)/shard_map/ppermute | solution.py:454
  41.5 21.9 %collective-permute-start.10 = (f32[512,128]{1,0:T(8,128)}, f32[512,128]{1,0:T(8,128)}, u32[]{:S(2)}, u32[]{:S(2)}) collective-permute-start(f32[512,128]{1,0:T(8,128)} %get-tuple-element.25.refs_0_), channel_id=1, source_target_pairs={{0,3},{1,2},{2,1},{3,0},{4,7},{5,6},{6,5},{7,4},{8,11},{9,10},{10,... | collective-permute-start | bytes 786440 | tf_op jit(solution)/shard_map/ppermute | solution.py:479
  41.5 21.9 %collective-permute-start.9 = (f32[512,128]{1,0:T(8,128)}, f32[512,128]{1,0:T(8,128)}, u32[]{:S(2)}, u32[]{:S(2)}) collective-permute-start(f32[512,128]{1,0:T(8,128)} %get-tuple-element.25.refs_0_), channel_id=1, source_target_pairs={{0,1},{1,0},{2,3},{3,2},{4,5},{5,4},{6,7},{7,6},{8,9},{9,8},{10,11... | collective-permute-start | bytes 786440 | tf_op jit(solution)/shard_map/ppermute | solution.py:479
  41.5 21.8 %collective-permute-start.8 = (f32[512,128]{1,0:T(8,128)}, f32[512,128]{1,0:T(8,128)}, u32[]{:S(2)}, u32[]{:S(2)}) collective-permute-start(f32[512,128]{1,0:T(8,128)} %get-tuple-element.25.refs_0_), channel_id=1, source_target_pairs={{0,2},{1,3},{2,0},{3,1},{4,6},{5,7},{6,4},{7,5},{8,10},{9,11},{10,... | collective-permute-start | bytes 786440 | tf_op jit(solution)/shard_map/ppermute | solution.py:454
  43.4 0.8 copy-start.5
  44.2 3.2 %collective-permute-start.7 = (f32[448,128]{1,0:T(8,128)S(1)}, f32[448,128]{1,0:T(8,128)S(1)}, u32[]{:S(2)}, u32[]{:S(2)}) collective-permute-start(f32[448,128]{1,0:T(8,128)S(1)} %collective-permute-done.5.refs_5_), channel_id=1, source_target_pairs={{0,1},{1,0},{2,3},{3,2},{4,5},{5,4},{6,7},{7,6},{8,9},{9,8},{10,11... | collective-permute-start | bytes 688136 | tf_op jit(solution)/shard_map/ppermute | solution.py:458
  44.6 0.9 copy-start.11
  45.5 0.9 copy-start.13
  46.4 1.0 %copy-start.6 = (f32[1024,128]{1,0:T(8,128)S(1)}, f32[1024,128]{1,0:T(8,128)}, u32[]{:S(2)}) copy-start(f32[1024,128]{1,0:T(8,128)} %copy-done.5) | copy-start | bytes 1572868
  62.3 1.1 %copy-start.4 = (f32[2560,128]{1,0:T(8,128)}, f32[2560,128]{1,0:T(8,128)S(1)}, u32[]{:S(2)}) copy-start(f32[2560,128]{1,0:T(8,128)S(1)} %get-tuple-element.26.refs_8_) | copy-start | bytes 3932164
  85.0 5.5 %collective-permute-start.13 = (f32[512,128]{1,0:T(8,128)S(1)}, f32[512,128]{1,0:T(8,128)S(1)}, u32[]{:S(2)}, u32[]{:S(2)}) collective-permute-start(f32[512,128]{1,0:T(8,128)S(1)} %get-tuple-element.34), channel_id=1, source_target_pairs={{0,1},{1,2},{2,3},{3,0},{4,5},{5,6},{6,7},{7,4},{8,9},{9,10},{10,1... | collective-permute-start | bytes 786440 | tf_op jit(solution)/shard_map/ppermute | solution.py:454
  85.0 12.8 %collective-permute-start.14 = (f32[512,128]{1,0:T(8,128)S(1)}, f32[512,128]{1,0:T(8,128)S(1)}, u32[]{:S(2)}, u32[]{:S(2)}) collective-permute-start(f32[512,128]{1,0:T(8,128)S(1)} %get-tuple-element.35), channel_id=1, source_target_pairs={{0,2},{1,3},{2,0},{3,1},{4,6},{5,7},{6,4},{7,5},{8,10},{9,11},{10,... | collective-permute-start | bytes 786440 | tf_op jit(solution)/shard_map/ppermute | solution.py:454
  86.5 12.2 %collective-permute-start.15 = (f32[512,128]{1,0:T(8,128)S(1)}, f32[512,128]{1,0:T(8,128)S(1)}, u32[]{:S(2)}, u32[]{:S(2)}) collective-permute-start(f32[512,128]{1,0:T(8,128)S(1)} %get-tuple-element.36), channel_id=1, source_target_pairs={{0,3},{1,0},{2,1},{3,2},{4,7},{5,4},{6,5},{7,6},{8,11},{9,8},{10,9... | collective-permute-start | bytes 786440 | tf_op jit(solution)/shard_map/ppermute | solution.py:454
  (2 other events, 1.3 us)

commit v2 on v1

v2 whole, which is shorter than its diff:
```python
import functools
import math

import jax
import jax.numpy as jnp
from jax import lax
from jax.experimental import pallas as pl
from jax.experimental.pallas import tpu as pltpu
from jax.sharding import PartitionSpec as P

TE = 32
SWEEPS = 4
CSWEEPS = 3
NZ = 64
EPS = 2.0
DT = 0.15
LANES = 128
SUB = 8
TILES = 2
ROW = SUB * TILES

LOW = (SWEEPS + 2, SWEEPS + 1, 2)
HIGH = (SWEEPS + 3, SWEEPS + 2, 2)
LOW_ROWS = sum(LOW) * ROW
HIGH_ROWS = sum(HIGH) * ROW
SLABX = TE + SUB
HALO = CSWEEPS
HALF = TE
YBLOCKS = HALF + 2 * HALO
ROW0 = SUB
SLAB_ROWS = ROW0 + YBLOCKS * SLABX + SUB


def cheb_weight(step, count):
    return 1.0 / (1.0 + 0.75 * math.cos(math.pi * (2 * step + 1) / (2 * count)))


def lookup(table, ids):
    out = jnp.full(ids.shape, table[3], jnp.float32)
    for which in (2, 1, 0):
        out = jnp.where(ids == which, table[which], out)
    return out


def roll(value, by, axis):
    return pltpu.roll(value, by % value.shape[axis], axis)


def prep_kernel(table, phi, src, mat, temp, slab, body, sigma, up, down, src_v, mat_v, ends_t, ends_m, sems):
    rows = TE * ROW
    size_x, width = temp.shape
    moves = [(phi, body.at[0:rows]), (src, src_v), (mat, mat_v)]
    for which, first in enumerate((0, size_x - SUB)):
        moves.append((temp.at[first : first + SUB], ends_t.at[which]))
        moves.append((slab.at[first : first + SUB], ends_m.at[which]))
    moves = [pltpu.make_async_copy(*move, sems.at[at]) for at, move in enumerate(moves)]
    for move in moves:
        move.start()
    for move in moves:
        move.wait()
    sigma[...] = lookup(table, mat_v[...])
    body[rows : 2 * rows] = src_v[...] / sigma[...]
    at_up, at_down = 0, 0
    for ref, first in ((body, 0), (body, rows), (sigma, 0)):
        which = (first // rows) if ref is body else 2
        size = LOW[which] * ROW
        up[at_up : at_up + size] = ref[first + rows - size : first + rows]
        at_up += size
        size = HIGH[which] * ROW
        down[at_down : at_down + size] = ref[first : first + size]
        at_down += size
    sub = lax.broadcasted_iota(jnp.int32, (SUB, LANES), 0)
    for at in range(width // LANES):
        lanes = slice(at * LANES, (at + 1) * LANES)
        t_low, m_low = ends_t[0, :, lanes], ends_m[0, :, lanes].astype(jnp.float32)
        t_high, m_high = ends_t[1, :, lanes], ends_m[1, :, lanes].astype(jnp.float32)
        first = at * SUB
        up[LOW_ROWS + first : LOW_ROWS + first + SUB] = jnp.where(sub < 4, roll(t_high, HALO, 0), roll(m_high, -1, 0))
        down[HIGH_ROWS + first : HIGH_ROWS + first + SUB] = jnp.where(sub < 4, t_low, roll(m_low, 4, 0))


def relay_kernel(low, high, halo):
    halo[0:LOW_ROWS] = low[0:LOW_ROWS]
    halo[LOW_ROWS : LOW_ROWS + HIGH_ROWS] = high[0:HIGH_ROWS]


def loose(pos):
    return jnp.minimum(pos[0, 0], 0)


def slab_kernel(pos, k0_table, beta_table, temp, mat, low, high, t_ext, k0_ext, b_ext, edge_low, edge_high, native_t, native_m):
    start = loose(pos)
    blocks = temp.shape[1] // LANES
    half = lax.broadcasted_iota(jnp.int32, (SUB, LANES), 1) < NZ
    for which, (own, native) in enumerate(((temp, native_t), (mat, native_m))):
        for at in range(blocks):
            lanes = slice(at * LANES, (at + 1) * LANES)
            first = at * SLABX
            side = LOW_ROWS + at * SUB
            value = low[side : side + SUB, :]
            native[first : first + SUB, :] = roll(value, -4, 0) if which else value
            for g in range(TE // SUB):
                value = own[g * SUB : (g + 1) * SUB, lanes].astype(jnp.float32)
                native[pl.ds(start + first + HALO + g * SUB, SUB), :] = value
            side = HIGH_ROWS + at * SUB
            value = high[side : side + SUB, :]
            native[pl.ds(start + first + HALO + TE, SUB), :] = roll(value, -4, 0) if which else value
    for at in range(blocks // 2):
        for g in range(SLABX // SUB):
            halves = []
            for native in (native_t, native_m):
                lower = native[at * SLABX + g * SUB : at * SLABX + (g + 1) * SUB, :]
                upper_at = (blocks // 2 + at) * SLABX + g * SUB
                upper = native[upper_at : upper_at + SUB, :]
                lower_r, upper_r = roll(lower, NZ, 1), roll(upper, NZ, 1)
                halves.append((lower, lower_r, upper, upper_r))
            for odd in range(2):
                y = 2 * at + odd
                temps, mats = (jnp.where(half, v[odd], v[3 - odd]) for v in halves)
                places = [(y + HALO, temps, mats)]
                if y >= HALF - HALO:
                    places.append((y - HALF + HALO, halves[0][1 - odd], halves[1][1 - odd]))
                if y < HALO:
                    places.append((y + HALF + HALO, halves[0][2 + odd], halves[1][2 + odd]))
                for block, t, m in places:
                    rows = slice(ROW0 + block * SLABX + g * SUB, ROW0 + block * SLABX + (g + 1) * SUB)
                    t_ext[rows] = t
                    k0_ext[rows] = lookup(k0_table, m)
                    b_ext[rows] = lookup(beta_table, m)
                if y < HALO:
                    rows = slice(y * SLABX + g * SUB, y * SLABX + (g + 1) * SUB)
                    edge_low[rows] = jnp.where(half, halves[0][odd], halves[1][1 - odd])
                if y >= HALF - HALO:
                    first = (y - HALF + HALO) * SLABX + g * SUB
                    edge_high[first : first + SUB] = jnp.where(half, halves[0][2 + odd], halves[1][3 - odd])


def fill_maps(chips, pos, cell_at, cell_of):
    width_gy = 2 * chips
    tiles = width_gy * TILES
    i = lax.axis_index("gx")
    j = lax.axis_index("gy")
    rows_gx = lax.axis_size("gx")
    for at in range(2 * (2 * width_gy + 2)):
        for which in range(3):
            cell_at[which, at] = tiles
    for which, by in enumerate((0, -1, 1)):
        row = i + by
        valid = (row >= 0) & (row < rows_gx)
        first = jnp.clip(row, 0, rows_gx - 1) * tiles
        for part in range(width_gy):
            dev = part_device(part, chips, j)
            for t in range(TILES):
                tile = first + dev * TILES + t
                cell = (pos[tile, 1] + 1) * 2 + pos[tile, 2]
                slot = part * TILES + t
                cell_of[which, slot] = cell
                cell_at[which, cell] = jnp.where(valid, slot, tiles)


def part_device(part, chips, j):
    mate = j + 1 - 2 * lax.rem(j, 2)
    base = j if part < chips else mate
    return lax.rem(base - 2 * (part % chips) + 2 * chips, 2 * chips)


def sweep_kernel(chips, pos, *refs):
    width_gy = 2 * chips
    tiles = width_gy * TILES
    none = tiles
    bodies = refs[:width_gy]
    halos = refs[width_gy : 2 * width_gy]
    pot, slope, cell_at, cell_of, pa, pb, la, lb, ua, ub, s_c, s_l, s_u = refs[2 * width_gy :]
    i = lax.axis_index("gx")
    j = lax.axis_index("gy")
    rows_gx = lax.axis_size("gx")
    fill_maps(chips, pos, cell_at, cell_of)

    zero = jnp.zeros((SUB, LANES), jnp.float32)

    def plane_at(ref, at, shift=0):
        first = ROW0 + at * SUB
        return ref[pl.ds(pl.multiple_of(first, SUB) if shift == 0 else first + shift, SUB), :]

    def put_plane(ref, at, value):
        ref[pl.ds(pl.multiple_of(ROW0 + at * SUB, SUB), SUB), :] = value

    def unpack(source, start, t, target, first, count):
        def plane(p, carry):
            at = pl.multiple_of(p * ROW, ROW)
            value = source[pl.ds(start + at + t, SUB, stride=TILES), :]
            if len(target.shape) == 3:
                target[first + p] = value
            else:
                put_plane(target, first + p, value)
            return carry

        lax.fori_loop(0, count, plane, 0, unroll=min(count, 8))

    for part in range(width_gy):
        for t in range(TILES):
            slot = part * TILES + t
            for which, target in enumerate((pa, s_c)):
                unpack(bodies[part], which * TE * ROW, t, target, slot * TE, TE)
            at = 0
            for which, target in enumerate((la, s_l)):
                unpack(halos[part], at, t, target, slot * LOW[which], LOW[which])
                at += LOW[which] * ROW
            at = LOW_ROWS
            for which, target in enumerate((ua, s_u)):
                unpack(halos[part], at, t, target, slot * HIGH[which], HIGH[which])
                at += HIGH[which] * ROW
    for ref, count in ((pa, TE), (pb, TE), (la, LOW[0]), (lb, LOW[0]), (ua, HIGH[0]), (ub, HIGH[0])):
        for p in range(count):
            put_plane(ref, none * count + p, zero)

    lane = lax.broadcasted_iota(jnp.int32, (SUB, LANES), 1)
    sub = lax.broadcasted_iota(jnp.int32, (SUB, LANES), 0)
    depth = lane % TE
    first_y, last_y = lane < TE, lane >= LANES - TE
    first_sub, last_sub = sub == 0, sub == SUB - 1
    first_z, last_z = depth == 0, depth == TE - 1

    def y_plus(ref, own, at, ghost_at):
        turned = jnp.where(last_sub, plane_at(ref, ghost_at, 1 - SUB), plane_at(ref, at, 1))
        return roll(jnp.where(first_y, turned, own), -TE, 1)

    def y_minus(ref, own, at, ghost_at):
        turned = jnp.where(first_sub, plane_at(ref, ghost_at, SUB - 1), plane_at(ref, at, -1))
        return roll(jnp.where(last_y, turned, own), TE, 1)

    def around(which, slot):
        cell = cell_of[which, slot]
        upper = cell % 2
        y_m = cell_at[which, cell - 2]
        y_p = cell_at[which, cell + 2]
        z = cell_at[which, cell + 1 - 2 * upper]
        turn = jnp.where(upper == 1, LANES + 1 - TE, TE - 1)
        meets = jnp.where(upper == 1, 0, TE - 1) == depth
        return cell, (slot, y_m, y_p, z, turn, meets)

    bufs = ((pa, la, ua), (pb, lb, ub))
    for k in range(SWEEPS):
        weight = cheb_weight(k, SWEEPS)
        keep, gain = 1.0 - weight, weight / (6.0 + EPS)
        (c_src, l_src, u_src), (c_dst, l_dst, u_dst) = bufs[k % 2], bufs[(k + 1) % 2]

        def relax(field, size, slots, p, x_m, x_p, s):
            slot, y_m, y_p, z, turn, meets = slots
            at = slot * size + p
            own = plane_at(field, at)
            total = (x_m + x_p) + s
            total = total + y_minus(field, own, at, y_m * size + p)
            total = total + y_plus(field, own, at, y_p * size + p)
            total = total + jnp.where(last_z, 0.0, roll(own, -1, 1))
            total = total + jnp.where(first_z, 0.0, roll(own, 1, 1))
            total = total + jnp.where(meets, pltpu.roll(plane_at(field, z * size + p), turn, 1), 0.0)
            return keep * own + gain * total

        def sweep_tile(slot, carry):
            cell, slots = around(0, slot)
            below, above = cell_at[1, cell], cell_at[2, cell]
            for p in range(TE):
                x_m = plane_at(c_src, slot * TE + p - 1) if p > 0 else plane_at(l_src, below * LOW[0] + LOW[0] - 1)
                x_p = plane_at(c_src, slot * TE + p + 1) if p < TE - 1 else plane_at(u_src, above * HIGH[0])
                put_plane(c_dst, slot * TE + p, relax(c_src, TE, slots, p, x_m, x_p, s_c[slot * TE + p]))
            cell, slots = around(1, slot)
            centre = cell_at[0, cell]
            for p in range(k + 1, LOW[0]):
                x_m = plane_at(l_src, slot * LOW[0] + p - 1)
                x_p = plane_at(l_src, slot * LOW[0] + p + 1) if p < LOW[0] - 1 else plane_at(c_src, centre * TE)
                s = s_l[slot * LOW[1] + p - (LOW[0] - LOW[1])]
                put_plane(l_dst, slot * LOW[0] + p, relax(l_src, LOW[0], slots, p, x_m, x_p, s))
            cell, slots = around(2, slot)
            centre = cell_at[0, cell]
            for p in range(HIGH[0] - 1 - k):
                x_m = plane_at(u_src, slot * HIGH[0] + p - 1) if p > 0 else plane_at(c_src, centre * TE + TE - 1)
                x_p = plane_at(u_src, slot * HIGH[0] + p + 1)
                s = s_u[slot * HIGH[1] + p]
                put_plane(u_dst, slot * HIGH[0] + p, relax(u_src, HIGH[0], slots, p, x_m, x_p, s))
            return carry

        lax.fori_loop(0, tiles, sweep_tile, 0)

    field, f_l, f_u = bufs[SWEEPS % 2]
    for t in range(TILES):
        for p in range(TE):
            pot[pl.ds(p * ROW + t, SUB, stride=TILES), :] = plane_at(field, t * TE + p)

    def clear(at, carry):
        slope[pl.ds(pl.multiple_of(at * SUB, SUB), SUB), :] = zero
        return carry

    lax.fori_loop(0, slope.shape[0] // SUB, clear, 0, unroll=8)

    def squares(ref, size, slots, p, x_p):
        slot, _, y_p, z, turn, meets = slots
        at = slot * size + p
        own = plane_at(ref, at)
        d_x = x_p - own
        d_y = y_plus(ref, own, at, y_p * size + p) - own
        ghost = jnp.where(meets, pltpu.roll(plane_at(ref, z * size + p), turn, 1), 0.0)
        d_z = jnp.where(last_z, ghost, roll(own, -1, 1)) - own
        return d_x * d_x + d_y * d_y + d_z * d_z

    def put(local, x, value):
        slope[pl.ds(pl.multiple_of((local * SLABX + x) * SUB, SUB), SUB), :] = value

    def slope_tile(slot, carry):
        for which in range(3):
            cell, slots = around(which, slot)
            local, inside = window(which, cell, i, j, rows_gx)

            @pl.when(inside)
            def _():
                if which == 0:
                    above = cell_at[2, cell]
                    for p in range(TE):
                        x_p = plane_at(field, slot * TE + p + 1) if p < TE - 1 else plane_at(f_u, above * HIGH[0])
                        put(local, HALO + p, squares(field, TE, slots, p, x_p))
                elif which == 1:
                    centre = cell_at[0, cell]
                    for p in range(2):
                        q = LOW[0] - 2 + p
                        x_p = plane_at(f_l, slot * LOW[0] + q + 1) if p < 1 else plane_at(field, centre * TE)
                        put(local, HALO - 2 + p, squares(f_l, LOW[0], slots, q, x_p))
                else:
                    for p in range(2):
                        x_p = plane_at(f_u, slot * HIGH[0] + p + 1)
                        put(local, HALO + TE + p, squares(f_u, HIGH[0], slots, p, x_p))

        return carry

    lax.fori_loop(0, tiles, slope_tile, 0)


def window(which, cell, i, j, rows_gx):
    local = cell - 4 * j
    inside = (local >= 0) & (local < 8)
    if which > 0:
        row = i - 1 if which == 1 else i + 1
        inside = inside & (row >= 0) & (row < rows_gx)
    return local, inside


def slab_steps_kernel(chips, pos, k0_table, beta_table, *refs):
    width_gy = 2 * chips
    tiles = width_gy * TILES
    sigmas = refs[:width_gy]
    halos = refs[width_gy : 2 * width_gy]
    slope, t_in, k0_in, b_in, ylow, yhigh, temp_out = refs[2 * width_gy : 2 * width_gy + 7]
    sends = refs[2 * width_gy + 7 : 3 * width_gy + 7]
    heat, q_ext, temp_a, temp_b, cond_a, cond_b, k0_edge, b_edge, blocks = refs[3 * width_gy + 7 :]
    i = lax.axis_index("gx")
    j = lax.axis_index("gy")
    rows_gx = lax.axis_size("gx")
    lane = lax.broadcasted_iota(jnp.int32, (SUB, LANES), 1)
    zero = jnp.zeros((SUB, LANES), jnp.float32)

    def clear(at, carry):
        heat[pl.ds(pl.multiple_of(at * SUB, SUB), SUB), :] = zero
        return carry

    lax.fori_loop(0, heat.shape[0] // SUB, clear, 0, unroll=8)
    low_at, high_at = (LOW[0] + LOW[1]) * ROW, LOW_ROWS + (HIGH[0] + HIGH[1]) * ROW
    for part in range(width_gy):
        dev = part_device(part, chips, j)
        for t in range(TILES):
            for which, by in enumerate((0, -1, 1)):
                tile = jnp.clip(i + by, 0, rows_gx - 1) * tiles + dev * TILES + t
                cell = (pos[tile, 1] + 1) * 2 + pos[tile, 2]
                local, inside = window(which, cell, i, j, rows_gx)
                source, start, x, count = (
                    (sigmas[part], 0, HALO, TE),
                    (halos[part], low_at, HALO - 2, 2),
                    (halos[part], high_at, HALO + TE, 2),
                )[which]

                @pl.when(inside)
                def _():
                    for p in range(count):
                        rows = pl.ds(pl.multiple_of((local * SLABX + x + p) * SUB, SUB), SUB)
                        sigma = source[pl.ds(start + p * ROW + t, SUB, stride=TILES), :]
                        heat[rows, :] = sigma * slope[rows, :]

    quarter = [(lane >= q * TE) & (lane < (q + 1) * TE) for q in range(3)]

    def pick(parts):
        return jnp.where(
            quarter[0], parts[0], jnp.where(quarter[1], parts[1], jnp.where(quarter[2], parts[2], parts[3]))
        )

    def turned(value, by):
        return value if by % 4 == 0 else roll(value, by * TE, 1)

    def rows_of(block, g):
        first = ROW0 + block * SLABX + g * SUB
        return slice(first, first + SUB)

    groups = SLABX // SUB
    for first in range(-1, HALF // 4 + 1):
        col, yq = first * 4 // TE + 1, first * 4 % TE // 4
        for g in range(groups):
            cells = [
                heat[pl.ds(((2 * col + c) * SLABX + g * SUB) * SUB + yq, SUB, stride=SUB), :] for c in range(4)
            ]
            for r in range(4):
                block = 4 * first + r + HALO
                if 0 < block < YBLOCKS - 1:
                    q_ext[rows_of(block, g)] = pick([turned(cells[c], c - r) for c in range(4)])

    start = loose(pos)
    sub = lax.broadcasted_iota(jnp.int32, (SUB, LANES), 0)
    half = lane < NZ
    no_z = lane % NZ == NZ - 1
    low_x = (sub == HALO - 1) & (i == 0), (sub == HALO) & (i == 0)
    high_x = (sub == (HALO + TE - 1) % SUB) & (i == rows_gx - 1)
    low_y, high_y = half & (j == 0), (lane >= NZ) & (j == width_gy - 1)

    def beside(ref, block, g, by):
        return ref[pl.ds(start + (ROW0 + block * SLABX + g * SUB + by), SUB), :]

    edges = {}
    for e in range(HALO):
        edges[e] = (ylow, e)
        edges[YBLOCKS - HALO + e] = (yhigh, e)
    for block in range(YBLOCKS):
        for g in range(groups):
            rows = rows_of(block, g)
            temp, k0, beta = t_in[rows], k0_in[rows], b_in[rows]
            if block in edges:
                edge, e = edges[block]
                value = edge[e * SLABX + g * SUB : e * SLABX + (g + 1) * SUB]
                swapped = roll(value, NZ, 1)
                if edge is ylow:
                    temp = jnp.where(half, value, temp)
                    k0 = jnp.where(half, lookup(k0_table, swapped), k0)
                    beta = jnp.where(half, lookup(beta_table, swapped), beta)
                else:
                    temp = jnp.where(half, temp, swapped)
                    k0 = jnp.where(half, k0, lookup(k0_table, value))
                    beta = jnp.where(half, beta, lookup(beta_table, value))
                k0_edge[rows_of(list(edges).index(block), g)] = k0
                b_edge[rows_of(list(edges).index(block), g)] = beta
            temp_a[rows] = temp
            cond_a[rows] = k0 / (1.0 + beta * temp * temp)

    for step in range(CSWEEPS):
        (t_src, c_src), (t_dst, c_dst) = ((temp_a, cond_a), (temp_b, cond_b))[:: 1 if step % 2 == 0 else -1]
        for g in range(groups):
            now = t_src[rows_of(step, g)], c_src[rows_of(step, g)]
            ahead = t_src[rows_of(step + 1, g)], c_src[rows_of(step + 1, g)]
            flux_y = (now[1] + ahead[1]) * (ahead[0] - now[0])
            if step == HALO - 1:
                flux_y = jnp.where(low_y, 0.0, flux_y)
            for block in range(step + 1, YBLOCKS - 1 - step):
                (temp, cond), before = ahead, flux_y
                ahead = t_src[rows_of(block + 1, g)], c_src[rows_of(block + 1, g)]
                flux_y = (cond + ahead[1]) * (ahead[0] - temp)
                if block == HALO - 1:
                    flux_y = jnp.where(low_y, 0.0, flux_y)
                if block == HALO + HALF - 1:
                    flux_y = jnp.where(high_y, 0.0, flux_y)
                flux_p = (cond + beside(c_src, block, g, 1)) * (beside(t_src, block, g, 1) - temp)
                flux_m = (cond + beside(c_src, block, g, -1)) * (beside(t_src, block, g, -1) - temp)
                if g == 0:
                    flux_p = jnp.where(low_x[0], 0.0, flux_p)
                    flux_m = jnp.where(low_x[1], 0.0, flux_m)
                if g == groups - 1:
                    flux_p = jnp.where(high_x, 0.0, flux_p)
                flux_z = (cond + roll(cond, -1, 1)) * (roll(temp, -1, 1) - temp)
                flux_z = jnp.where(no_z, 0.0, flux_z)
                div = (flux_y - before) + (flux_p + flux_m) + (flux_z - roll(flux_z, 1, 1))
                rows = rows_of(block, g)
                new = temp + DT * (0.5 * div + q_ext[rows])
                t_dst[rows] = new
                if step < CSWEEPS - 1:
                    if block in edges:
                        at = list(edges).index(block)
                        k0, beta = k0_edge[rows_of(at, g)], b_edge[rows_of(at, g)]
                    else:
                        k0, beta = k0_in[rows], b_in[rows]
                    c_dst[rows] = k0 / (1.0 + beta * new * new)
    final = temp_b if CSWEEPS % 2 else temp_a

    for yq in range(HALF // 4):
        for g in range(TE // SUB):
            x = slice(g * SUB, (g + 1) * SUB)
            turns = []
            for r in range(4):
                value = beside(final, HALO + 4 * yq + r, g, HALO)
                turns.append([turned(value, by) for by in range(4)])
            for pair in range(2):
                even, odd = turns[2 * pair], turns[2 * pair + 1]
                lower = (2 * yq + pair) * LANES
                upper = lower + temp_out.shape[1] // 2
                temp_out[x, lower : lower + LANES] = jnp.where(half, even[0], odd[2])
                temp_out[x, upper : upper + LANES] = jnp.where(half, even[2], odd[0])
            for c in range(4):
                value = pick([turns[r][(r - c) % 4] for r in range(4)])
                blocks[pl.ds((c * TE + g * SUB) * SUB + yq, SUB, stride=SUB), :] = value
    for shift in range(width_gy):
        dev = lax.rem(j + shift, width_gy)
        for t in range(TILES):
            tile = i * tiles + dev * TILES + t
            col = pos[tile, 1] - 2 * j
            cell = jnp.clip(col, 0, 1) * 2 + pos[tile, 2]
            here = (col >= 0) & (col < 2)
            for p in range(TE):
                value = blocks[pl.ds(pl.multiple_of((cell * TE + p) * SUB, SUB), SUB), :]
                sends[shift][pl.ds(p * ROW + t, SUB, stride=TILES), :] = jnp.where(here, value, 0.0)


def shifted(value, axis, by, wrap=False):
    count = lax.axis_size(axis)
    pairs = [(d, (d + by) % count) for d in range(count) if wrap or 0 <= d + by < count]
    return lax.ppermute(value, axis, pairs)


def from_mate(value):
    return lax.ppermute(value, "gy", [(d, d ^ 1) for d in range(lax.axis_size("gy"))])


def to_rows(value):
    return value.reshape(TILES, -1, LANES).transpose(1, 0, 2).reshape(-1, LANES)


def from_rows(value):
    return value.reshape(-1, TILES, LANES).transpose(1, 0, 2).reshape(TILES, -1)


def everyone(value, chips):
    mine = [value] + [shifted(value, "gy", 2 * d, True) for d in range(1, chips)]
    return mine + [from_mate(part) for part in mine]


def everyone_direct(value, chips):
    mine = [value] + [shifted(value, "gy", 2 * d, True) for d in range(1, chips)]
    count = 2 * chips
    for d in range(chips):
        pairs = [(at, ((at ^ 1) + 2 * d) % count) for at in range(count)]
        mine.append(lax.ppermute(value, "gy", pairs))
    return mine


VMEM = pl.BlockSpec(memory_space=pltpu.VMEM)
SMEM = pl.BlockSpec(memory_space=pltpu.SMEM)
HBM = pl.BlockSpec(memory_space=pltpu.HBM)
PARAMS = pltpu.CompilerParams(vmem_limit_bytes=48 * 1024 * 1024)


def on_device(
    phi_init,
    source,
    tile_mat,
    tile_pos,
    neighbours,
    sigma_table,
    temp_init,
    slab_mat,
    k0_table,
    beta_table,
):
    f32 = jnp.float32
    width_gy = lax.axis_size("gy")
    chips = width_gy // 2
    tiles = width_gy * TILES
    size_x, width = temp_init.shape
    edge_rows = width // LANES * SUB

    def rows(count):
        return jax.ShapeDtypeStruct((count, LANES), f32)

    body, sigma, up, down = pl.pallas_call(
        prep_kernel,
        out_shape=(
            rows(2 * TE * ROW),
            rows(TE * ROW),
            rows(LOW_ROWS + edge_rows),
            rows(HIGH_ROWS + edge_rows),
        ),
        in_specs=[SMEM] + [HBM] * 5,
        out_specs=(VMEM,) * 4,
        scratch_shapes=[
            pltpu.VMEM((TE * ROW, LANES), f32),
            pltpu.VMEM((TE * ROW, LANES), jnp.int32),
            pltpu.VMEM((2, SUB, width), f32),
            pltpu.VMEM((2, SUB, width), jnp.int32),
            pltpu.SemaphoreType.DMA((7,)),
        ],
        compiler_params=pltpu.CompilerParams(vmem_limit_bytes=62 * 1024 * 1024),
        name="prep",
    )(sigma_table, to_rows(phi_init), to_rows(source), to_rows(tile_mat), temp_init, slab_mat)
    bodies = everyone(body, chips)
    low, high = shifted(up, "gx", 1), shifted(down, "gx", -1)

    halo = pl.pallas_call(
        relay_kernel,
        out_shape=rows(LOW_ROWS + HIGH_ROWS),
        in_specs=[VMEM] * 2,
        out_specs=VMEM,
        compiler_params=PARAMS,
        name="relay",
    )(low, high)
    halos = everyone(halo, chips)
    sigmas = everyone_direct(sigma, chips)

    native = pltpu.VMEM((width // LANES * SLABX + SUB, LANES), f32)
    t_ext, k0_ext, b_ext, edge_low, edge_high = pl.pallas_call(
        slab_kernel,
        out_shape=(rows(SLAB_ROWS),) * 3 + (rows(HALO * SLABX),) * 2,
        in_specs=[SMEM] * 3 + [VMEM] * 4,
        out_specs=(VMEM,) * 5,
        scratch_shapes=[native, native],
        compiler_params=PARAMS,
        name="slab_prep",
    )(tile_pos, k0_table, beta_table, temp_init, slab_mat, low, high)
    ylow, yhigh = shifted(edge_high, "gy", 1), shifted(edge_low, "gy", -1)

    def planes(count):
        return pltpu.VMEM(((tiles + 1) * count, SUB, LANES), f32)

    def fields(count):
        return pltpu.VMEM((2 * ROW0 + (tiles + 1) * count * SUB, LANES), f32)

    pot, slope = pl.pallas_call(
        functools.partial(sweep_kernel, chips),
        out_shape=(rows(TE * ROW), rows(8 * SLABX * SUB)),
        in_specs=[SMEM] + [VMEM] * (2 * width_gy),
        out_specs=(VMEM,) * 2,
        scratch_shapes=[
            pltpu.SMEM((3, 2 * (2 * width_gy + 2)), jnp.int32),
            pltpu.SMEM((3, tiles), jnp.int32),
            fields(TE), fields(TE), fields(LOW[0]), fields(LOW[0]), fields(HIGH[0]), fields(HIGH[0]),
            planes(TE), planes(LOW[1]), planes(HIGH[1]),
        ],
        compiler_params=PARAMS,
        name="sweeps",
    )(tile_pos, *bodies, *halos)

    temp, *sends = pl.pallas_call(
        functools.partial(slab_steps_kernel, chips),
        out_shape=(jax.ShapeDtypeStruct((size_x, width), f32),) + (rows(TE * ROW),) * width_gy,
        in_specs=[SMEM] * 3 + [VMEM] * (2 * width_gy + 6),
        out_specs=(VMEM,) * (1 + width_gy),
        scratch_shapes=[pltpu.VMEM((8 * SLABX * SUB, LANES), f32)]
        + [pltpu.VMEM((SLAB_ROWS, LANES), f32)] * 5
        + [pltpu.VMEM((ROW0 + 2 * HALO * SLABX, LANES), f32)] * 2
        + [pltpu.VMEM((4 * TE * SUB, LANES), f32)],
        compiler_params=PARAMS,
        name="slab_steps",
    )(tile_pos, k0_table, beta_table, *sigmas, *halos, slope, t_ext, k0_ext, b_ext, ylow, yhigh)
    tile_temps = sends[0]
    for by in range(1, width_gy):
        tile_temps = tile_temps + shifted(sends[by], "gy", by, True)
    return from_rows(pot), temp, from_rows(tile_temps)


def solution(mesh):
    placed = (
        P(("gx", "gy"), None),
        P(("gx", "gy"), None),
        P(("gx", "gy"), None),
        P(),
        P(("gx", "gy"), None),
        P(),
        P("gx", "gy"),
        P("gx", "gy"),
        P(),
        P(),
    )
    return jax.shard_map(
        on_device,
        mesh=mesh,
        in_specs=placed,
        out_specs=(P(("gx", "gy"), None), P("gx", "gy"), P(("gx", "gy"), None)),
        check_vma=False,
    )
```

time: 100 us -> 111 us (1.11)
  the two profiles are of different devices: /device:TPU:5 before, /device:TPU:0 now
where the time goes in v2:
time: 111 us; the launch traced here: 109 us
  Pallas kernels  59.2 us (53%)
  waiting for transfers between devices  27.2 us (25%)
  starting transfers between devices  19.4 us (17%)
  local copies, waits for them, and re-layouts  2.01 us (2%)
    pallas_call x1, Pallas kernels, on_device(): pl.pallas_call(functools.partial(slab_steps_kernel, chips), out_shape=(ja...  41 us
    ppermute x10, waiting for transfers between devices, shifted(): return lax.ppermute(value, axis, pairs)  27.2 us
    ppermute x10, starting transfers between devices, shifted(): return lax.ppermute(value, axis, pairs)  18.7 us
    pallas_call x1, Pallas kernels, on_device(): pl.pallas_call(functools.partial(sweep_kernel, chips), out_shape=(rows(TE...  13.3 us
    pallas_call x1, Pallas kernels, on_device(): pl.pallas_call(prep_kernel, out_shape=(rows(2 * TE * ROW), rows(TE * ROW)...  3.27 us
  transfers between devices with their start and end apart: 16, of which 6 were waited for; matrix products, arithmetic and copies ran while one was open for 0% of the time, Pallas kernels for 14%

profile of v2, /device:TPU:0, one launch (start us, length us, event | category | flops | bytes accessed | tf_op | source)
XLA Modules:
  0.0 109.5 jit_solution(1681824661139629038)
XLA Ops:
  0.7 3.3 %prep.1 = (f32[1024,128]{1,0:T(8,128)}, f32[512,128]{1,0:T(8,128)}, f32[464,128]{1,0:T(8,128)}, f32[496,128]{1,0:T(8,128)}) custom-call(f32[4]{0:T(128)} %table.1, f32[512,128]{1,0:T(8,128)} %bitcast.26, f32[512,128]{1,0:T(8,128)} %bitcast.27, s32[512,128]{1,0:T(8,128)} %bitcast.28, f32[32,4096]{1,0:T(8,128)} %temp.3, s32[32,4096]{1,0:T(8,128)} %mat.1), custom_call_target="tpu_custom_call" | custom-call | tf_op jit(solution)/shard_map/prep/pallas_call | solution.py:574
  4.0 0.0 copy-start.3
  4.0 3.0 %collective-permute-start = (f32[1024,128]{1,0:T(8,128)}, f32[1024,128]{1,0:T(8,128)}, u32[]{:S(2)}, u32[]{:S(2)}) collective-permute-start(f32[1024,128]{1,0:T(8,128)} %get-tuple-element.19.refs_0_), channel_id=1, source_target_pairs={{0,2},{1,3},{2,0},{3,1},{4,6},{5,7},{6,4},{7,5},{8,10},{9,11},{10,... | collective-permute-start | bytes 1572872 | tf_op jit(solution)/shard_map/ppermute | solution.py:517
  7.0 1.3 %collective-permute-start.4 = (f32[496,128]{1,0:T(8,128)}, f32[496,128]{1,0:T(8,128)S(1)}, u32[]{:S(2)}, u32[]{:S(2)}) collective-permute-start(f32[496,128]{1,0:T(8,128)} %get-tuple-element.21), channel_id=1, source_target_pairs={{4,0},{8,4},{12,8},{16,12},{20,16},{24,20},{28,24},{5,1},{9,5},{13... | collective-permute-start | bytes 761864 | tf_op jit(solution)/shard_map/ppermute | solution.py:517
  8.3 4.6 %collective-permute-start.3 = (f32[464,128]{1,0:T(8,128)}, f32[464,128]{1,0:T(8,128)S(1)}, u32[]{:S(2)}, u32[]{:S(2)}) collective-permute-start(f32[464,128]{1,0:T(8,128)} %get-tuple-element.20), channel_id=1, source_target_pairs={{0,4},{4,8},{8,12},{12,16},{16,20},{20,24},{24,28},{1,5},{5,9},{9,... | collective-permute-start | bytes 712712 | tf_op jit(solution)/shard_map/ppermute | solution.py:517
  12.8 6.4 %collective-permute-done.refs_1_ = f32[1024,128]{1,0:T(8,128)} collective-permute-done((f32[1024,128]{1,0:T(8,128)}, f32[1024,128]{1,0:T(8,128)}, u32[]{:S(2)}, u32[]{:S(2)}) %collective-permute-start) | collective-permute-done | bytes 524320 | tf_op jit(solution)/shard_map/ppermute | solution.py:517
  19.2 0.0 collective-permute-start.2
  19.2 3.5 %collective-permute-done.3.low = f32[464,128]{1,0:T(8,128)S(1)} collective-permute-done((f32[464,128]{1,0:T(8,128)}, f32[464,128]{1,0:T(8,128)S(1)}, u32[]{:S(2)}, u32[]{:S(2)}) %collective-permute-start.3) | collective-permute-done | bytes 237600 | tf_op jit(solution)/shard_map/ppermute | solution.py:517
  22.8 0.6 collective-permute-start.5
  23.4 7.0 %collective-permute-done.5.refs_5_ = f32[448,128]{1,0:T(8,128)S(1)} collective-permute-done((f32[448,128]{1,0:T(8,128)S(1)}, f32[448,128]{1,0:T(8,128)S(1)}, u32[]{:S(2)}, u32[]{:S(2)}) %collective-permute-start.5) | collective-permute-done | bytes 229408 | tf_op jit(solution)/shard_map/ppermute | solution.py:517
  30.4 0.0 collective-permute-start.7
  30.4 0.7 collective-permute-start.10
  31.1 0.0 collective-permute-start.9
  31.1 0.0 collective-permute-done.1.refs_2_
  31.1 0.8 copy-done.4
  31.9 1.5 %collective-permute-start.8 = (f32[512,128]{1,0:T(8,128)}, f32[512,128]{1,0:T(8,128)}, u32[]{:S(2)}, u32[]{:S(2)}) collective-permute-start(f32[512,128]{1,0:T(8,128)} %get-tuple-element.23.refs_0_), channel_id=1, source_target_pairs={{0,2},{1,3},{2,0},{3,1},{4,6},{5,7},{6,4},{7,5},{8,10},{9,11},{10,... | collective-permute-start | bytes 786440 | tf_op jit(solution)/shard_map/ppermute | solution.py:517
  33.4 0.1 copy.15.pos
  33.5 1.6 %slab_prep.1 = (f32[1536,128]{1,0:T(8,128)S(1)}, f32[1536,128]{1,0:T(8,128)S(1)}, f32[1536,128]{1,0:T(8,128)S(1)}, f32[120,128]{1,0:T(8,128)S(1)}, f32[120,128]{1,0:T(8,128)S(1)}) custom-call(s32[64,3]{1,0:T(8,128)S(1)} %copy.15.pos, f32[4]{0:T(128)S(1)} %copy-done.7, f32[4]{0:T(128)S(1)} %copy-done.8, f32[32,4096]{1,0:T(8,128)S(1)} %copy-done, ...), custom_call_target="tpu_custom_call" | custom-call | tf_op jit(solution)/shard_map/slab_prep/pallas_call | solution.py:609
  35.1 0.0 collective-permute-done.7.refs_7_
  35.1 2.1 %collective-permute-start.11 = (f32[120,128]{1,0:T(8,128)S(1)}, f32[120,128]{1,0:T(8,128)S(1)}, u32[]{:S(2)}, u32[]{:S(2)}) collective-permute-start(f32[120,128]{1,0:T(8,128)S(1)} %get-tuple-element.28), channel_id=1, source_target_pairs={{0,1},{1,2},{2,3},{4,5},{5,6},{6,7},{8,9},{9,10},{10,11},{12,13},{... | collective-permute-start | bytes 184328 | tf_op jit(solution)/shard_map/ppermute | solution.py:517
  37.3 0.0 copy-start.6
  37.3 1.4 %collective-permute-start.12 = (f32[120,128]{1,0:T(8,128)S(1)}, f32[120,128]{1,0:T(8,128)S(1)}, u32[]{:S(2)}, u32[]{:S(2)}) collective-permute-start(f32[120,128]{1,0:T(8,128)S(1)} %get-tuple-element.29), channel_id=1, source_target_pairs={{1,0},{2,1},{3,2},{5,4},{6,5},{7,6},{9,8},{10,9},{11,10},{13,12},{... | collective-permute-start | bytes 184328 | tf_op jit(solution)/shard_map/ppermute | solution.py:517
  38.8 13.3 %sweeps.1 = (f32[512,128]{1,0:T(8,128)}, f32[2560,128]{1,0:T(8,128)S(1)}) custom-call(s32[64,3]{1,0:T(8,128)S(1)} %copy.15.pos, f32[1024,128]{1,0:T(8,128)S(1)} %copy-done.3, f32[1024,128]{1,0:T(8,128)} %collective-permute-done.refs_1_, f32[1024,128]{1,0:T(8,128)S(1)} %copy-done.5, f32[1024,128]{1,0:T(8,128)} %collective-permute-done.2.refs_3_, ...), custom_call_target="tpu_custom_call" | custom-call | tf_op jit(solution)/shard_map/sweeps/pallas_call | solution.py:626
  52.0 1.1 copy-done.2
  53.2 41.0 %slab_steps.1 = (f32[32,4096]{1,0:T(8,128)}, f32[512,128]{1,0:T(8,128)S(1)}, f32[512,128]{1,0:T(8,128)S(1)}, f32[512,128]{1,0:T(8,128)S(1)}, f32[512,128]{1,0:T(8,128)S(1)}) custom-call(s32[64,3]{1,0:T(8,128)S(1)} %copy.15.pos, f32[4]{0:T(128)S(1)} %copy-done.7, f32[4]{0:T(128)S(1)} %copy-done.8, f32[512,128]{1,0:T(8,128)S(1)} %copy-done.6, ...), custom_call_target="tpu_custom_call" | custom-call | tf_op jit(solution)/shard_map/slab_steps/pallas_call | solution.py:641
  94.2 1.2 %collective-permute-start.13 = (f32[512,128]{1,0:T(8,128)S(1)}, f32[512,128]{1,0:T(8,128)S(1)}, u32[]{:S(2)}, u32[]{:S(2)}) collective-permute-start(f32[512,128]{1,0:T(8,128)S(1)} %get-tuple-element.32), channel_id=1, source_target_pairs={{0,1},{1,2},{2,3},{3,0},{4,5},{5,6},{6,7},{7,4},{8,9},{9,10},{10,1... | collective-permute-start | bytes 786440 | tf_op jit(solution)/shard_map/ppermute | solution.py:517
  95.4 1.6 %collective-permute-start.14 = (f32[512,128]{1,0:T(8,128)S(1)}, f32[512,128]{1,0:T(8,128)S(1)}, u32[]{:S(2)}, u32[]{:S(2)}) collective-permute-start(f32[512,128]{1,0:T(8,128)S(1)} %get-tuple-element.33), channel_id=1, source_target_pairs={{0,2},{1,3},{2,0},{3,1},{4,6},{5,7},{6,4},{7,5},{8,10},{9,11},{10,... | collective-permute-start | bytes 786440 | tf_op jit(solution)/shard_map/ppermute | solution.py:517
  97.0 1.4 %collective-permute-start.15 = (f32[512,128]{1,0:T(8,128)S(1)}, f32[512,128]{1,0:T(8,128)S(1)}, u32[]{:S(2)}, u32[]{:S(2)}) collective-permute-start(f32[512,128]{1,0:T(8,128)S(1)} %get-tuple-element.34), channel_id=1, source_target_pairs={{0,3},{1,0},{2,1},{3,2},{4,7},{5,4},{6,5},{7,6},{8,11},{9,8},{10,9... | collective-permute-start | bytes 786440 | tf_op jit(solution)/shard_map/ppermute | solution.py:517
  98.4 2.5 %collective-permute-done.13 = f32[512,128]{1,0:T(8,128)S(1)} collective-permute-done((f32[512,128]{1,0:T(8,128)S(1)}, f32[512,128]{1,0:T(8,128)S(1)}, u32[]{:S(2)}, u32[]{:S(2)}) %collective-permute-start.13) | collective-permute-done | bytes 262176 | tf_op jit(solution)/shard_map/ppermute | solution.py:517
  100.9 3.7 %collective-permute-done.14 = f32[512,128]{1,0:T(8,128)S(1)} collective-permute-done((f32[512,128]{1,0:T(8,128)S(1)}, f32[512,128]{1,0:T(8,128)S(1)}, u32[]{:S(2)}, u32[]{:S(2)}) %collective-permute-start.14) | collective-permute-done | bytes 262176 | tf_op jit(solution)/shard_map/ppermute | solution.py:517
  104.7 4.1 %collective-permute-done.15 = f32[512,128]{1,0:T(8,128)S(1)} collective-permute-done((f32[512,128]{1,0:T(8,128)S(1)}, f32[512,128]{1,0:T(8,128)S(1)}, u32[]{:S(2)}, u32[]{:S(2)}) %collective-permute-start.15) | collective-permute-done | bytes 262176 | tf_op jit(solution)/shard_map/ppermute | solution.py:517
  108.7 0.8 add_add_fusion
  (27 shorter events, 0.1 us)
Async XLA Ops:
  0.6 32.8 %copy-start.1 = (s32[32,4096]{1,0:T(8,128)S(1)}, s32[32,4096]{1,0:T(8,128)}, u32[]{:S(2)}) copy-start(s32[32,4096]{1,0:T(8,128)} %mat.1) | copy-start | bytes 1572868
  0.6 32.8 %copy-start = (f32[32,4096]{1,0:T(8,128)S(1)}, f32[32,4096]{1,0:T(8,128)}, u32[]{:S(2)}) copy-start(f32[32,4096]{1,0:T(8,128)} %temp.3) | copy-start | bytes 1572868
  0.7 32.7 %copy-start.9 = (s32[64,3]{0,1:T(4,128)S(1)}, s32[64,3]{0,1:T(4,128)}, u32[]{:S(2)}) copy-start(s32[64,3]{0,1:T(4,128)} %param.13) | copy-start | bytes 2308
  0.7 32.8 %copy-start.8 = (f32[4]{0:T(128)S(1)}, f32[4]{0:T(128)}, u32[]{:S(2)}) copy-start(f32[4]{0:T(128)} %beta_table.3) | copy-start | bytes 52
  0.7 32.8 %copy-start.7 = (f32[4]{0:T(128)S(1)}, f32[4]{0:T(128)}, u32[]{:S(2)}) copy-start(f32[4]{0:T(128)} %k0_table.3) | copy-start | bytes 52
  4.0 34.8 %copy-start.3 = (f32[1024,128]{1,0:T(8,128)S(1)}, f32[1024,128]{1,0:T(8,128)}, u32[]{:S(2)}) copy-start(f32[1024,128]{1,0:T(8,128)} %get-tuple-element.19.refs_0_) | copy-start | bytes 1572868
  4.0 15.2 %collective-permute-start = (f32[1024,128]{1,0:T(8,128)}, f32[1024,128]{1,0:T(8,128)}, u32[]{:S(2)}, u32[]{:S(2)}) collective-permute-start(f32[1024,128]{1,0:T(8,128)} %get-tuple-element.19.refs_0_), channel_id=1, source_target_pairs={{0,2},{1,3},{2,0},{3,1},{4,6},{5,7},{6,4},{7,5},{8,10},{9,11},{10,... | collective-permute-start | bytes 1572872 | tf_op jit(solution)/shard_map/ppermute | solution.py:517
  7.0 24.1 %collective-permute-start.1 = (f32[1024,128]{1,0:T(8,128)}, f32[1024,128]{1,0:T(8,128)S(1)}, u32[]{:S(2)}, u32[]{:S(2)}) collective-permute-start(f32[1024,128]{1,0:T(8,128)} %get-tuple-element.19.refs_0_), channel_id=1, source_target_pairs={{0,1},{1,0},{2,3},{3,2},{4,5},{5,4},{6,7},{7,6},{8,9},{9,8},{10,11... | collective-permute-start | bytes 1572872 | tf_op jit(solution)/shard_map/ppermute | solution.py:521
  7.0 15.8 %collective-permute-start.4 = (f32[496,128]{1,0:T(8,128)}, f32[496,128]{1,0:T(8,128)S(1)}, u32[]{:S(2)}, u32[]{:S(2)}) collective-permute-start(f32[496,128]{1,0:T(8,128)} %get-tuple-element.21), channel_id=1, source_target_pairs={{4,0},{8,4},{12,8},{16,12},{20,16},{24,20},{28,24},{5,1},{9,5},{13... | collective-permute-start | bytes 761864 | tf_op jit(solution)/shard_map/ppermute | solution.py:517
  8.3 14.5 %collective-permute-start.3 = (f32[464,128]{1,0:T(8,128)}, f32[464,128]{1,0:T(8,128)S(1)}, u32[]{:S(2)}, u32[]{:S(2)}) collective-permute-start(f32[464,128]{1,0:T(8,128)} %get-tuple-element.20), channel_id=1, source_target_pairs={{0,4},{4,8},{8,12},{12,16},{16,20},{20,24},{24,28},{1,5},{5,9},{9,... | collective-permute-start | bytes 712712 | tf_op jit(solution)/shard_map/ppermute | solution.py:517
  19.2 18.1 %collective-permute-start.2 = (f32[1024,128]{1,0:T(8,128)}, f32[1024,128]{1,0:T(8,128)}, u32[]{:S(2)}, u32[]{:S(2)}) collective-permute-start(f32[1024,128]{1,0:T(8,128)} %collective-permute-done.refs_1_), channel_id=1, source_target_pairs={{0,1},{1,0},{2,3},{3,2},{4,5},{5,4},{6,7},{7,6},{8,9},{9,8},{10,11... | collective-permute-start | bytes 1572872 | tf_op jit(solution)/shard_map/ppermute | solution.py:521
  22.8 7.6 %collective-permute-start.5 = (f32[448,128]{1,0:T(8,128)S(1)}, f32[448,128]{1,0:T(8,128)S(1)}, u32[]{:S(2)}, u32[]{:S(2)}) collective-permute-start(f32[448,128]{1,0:T(8,128)S(1)} %relay.1.refs_4_), channel_id=1, source_target_pairs={{0,2},{1,3},{2,0},{3,1},{4,6},{5,7},{6,4},{7,5},{8,10},{9,11},{10,... | collective-permute-start | bytes 688136 | tf_op jit(solution)/shard_map/ppermute | solution.py:517
  23.4 7.7 %collective-permute-start.6 = (f32[448,128]{1,0:T(8,128)S(1)}, f32[448,128]{1,0:T(8,128)S(1)}, u32[]{:S(2)}, u32[]{:S(2)}) collective-permute-start(f32[448,128]{1,0:T(8,128)S(1)} %relay.1.refs_4_), channel_id=1, source_target_pairs={{0,1},{1,0},{2,3},{3,2},{4,5},{5,4},{6,7},{7,6},{8,9},{9,8},{10,11... | collective-permute-start | bytes 688136 | tf_op jit(solution)/shard_map/ppermute | solution.py:521
  30.4 4.7 %collective-permute-start.7 = (f32[448,128]{1,0:T(8,128)S(1)}, f32[448,128]{1,0:T(8,128)S(1)}, u32[]{:S(2)}, u32[]{:S(2)}) collective-permute-start(f32[448,128]{1,0:T(8,128)S(1)} %collective-permute-done.5.refs_5_), channel_id=1, source_target_pairs={{0,1},{1,0},{2,3},{3,2},{4,5},{5,4},{6,7},{7,6},{8,9},{9,8},{10,11... | collective-permute-start | bytes 688136 | tf_op jit(solution)/shard_map/ppermute | solution.py:521
  30.4 22.7 %collective-permute-start.10 = (f32[512,128]{1,0:T(8,128)}, f32[512,128]{1,0:T(8,128)S(1)}, u32[]{:S(2)}, u32[]{:S(2)}) collective-permute-start(f32[512,128]{1,0:T(8,128)} %get-tuple-element.23.refs_0_), channel_id=1, source_target_pairs={{0,3},{1,2},{2,1},{3,0},{4,7},{5,6},{6,5},{7,4},{8,11},{9,10},{10,... | collective-permute-start | bytes 786440 | tf_op jit(solution)/shard_map/ppermute | solution.py:542
  31.1 22.0 %collective-permute-start.9 = (f32[512,128]{1,0:T(8,128)}, f32[512,128]{1,0:T(8,128)}, u32[]{:S(2)}, u32[]{:S(2)}) collective-permute-start(f32[512,128]{1,0:T(8,128)} %get-tuple-element.23.refs_0_), channel_id=1, source_target_pairs={{0,1},{1,0},{2,3},{3,2},{4,5},{5,4},{6,7},{7,6},{8,9},{9,8},{10,11... | collective-permute-start | bytes 786440 | tf_op jit(solution)/shard_map/ppermute | solution.py:542
  31.1 0.8 copy-start.4
  31.9 21.2 %collective-permute-start.8 = (f32[512,128]{1,0:T(8,128)}, f32[512,128]{1,0:T(8,128)}, u32[]{:S(2)}, u32[]{:S(2)}) collective-permute-start(f32[512,128]{1,0:T(8,128)} %get-tuple-element.23.refs_0_), channel_id=1, source_target_pairs={{0,2},{1,3},{2,0},{3,1},{4,6},{5,7},{6,4},{7,5},{8,10},{9,11},{10,... | collective-permute-start | bytes 786440 | tf_op jit(solution)/shard_map/ppermute | solution.py:517
  33.5 5.3 %copy-start.5 = (f32[1024,128]{1,0:T(8,128)S(1)}, f32[1024,128]{1,0:T(8,128)}, u32[]{:S(2)}) copy-start(f32[1024,128]{1,0:T(8,128)} %copy-done.4) | copy-start | bytes 1572868
  35.1 18.0 %collective-permute-start.11 = (f32[120,128]{1,0:T(8,128)S(1)}, f32[120,128]{1,0:T(8,128)S(1)}, u32[]{:S(2)}, u32[]{:S(2)}) collective-permute-start(f32[120,128]{1,0:T(8,128)S(1)} %get-tuple-element.28), channel_id=1, source_target_pairs={{0,1},{1,2},{2,3},{4,5},{5,6},{6,7},{8,9},{9,10},{10,11},{12,13},{... | collective-permute-start | bytes 184328 | tf_op jit(solution)/shard_map/ppermute | solution.py:517
  37.3 15.9 %copy-start.6 = (f32[512,128]{1,0:T(8,128)S(1)}, f32[512,128]{1,0:T(8,128)}, u32[]{:S(2)}) copy-start(f32[512,128]{1,0:T(8,128)} %get-tuple-element.23.refs_0_) | copy-start | bytes 786436
  37.3 15.8 %collective-permute-start.12 = (f32[120,128]{1,0:T(8,128)S(1)}, f32[120,128]{1,0:T(8,128)S(1)}, u32[]{:S(2)}, u32[]{:S(2)}) collective-permute-start(f32[120,128]{1,0:T(8,128)S(1)} %get-tuple-element.29), channel_id=1, source_target_pairs={{1,0},{2,1},{3,2},{5,4},{6,5},{7,6},{9,8},{10,9},{11,10},{13,12},{... | collective-permute-start | bytes 184328 | tf_op jit(solution)/shard_map/ppermute | solution.py:517
  52.0 1.1 copy-start.2
  94.2 6.7 %collective-permute-start.13 = (f32[512,128]{1,0:T(8,128)S(1)}, f32[512,128]{1,0:T(8,128)S(1)}, u32[]{:S(2)}, u32[]{:S(2)}) collective-permute-start(f32[512,128]{1,0:T(8,128)S(1)} %get-tuple-element.32), channel_id=1, source_target_pairs={{0,1},{1,2},{2,3},{3,0},{4,5},{5,6},{6,7},{7,4},{8,9},{9,10},{10,1... | collective-permute-start | bytes 786440 | tf_op jit(solution)/shard_map/ppermute | solution.py:517
  95.4 9.2 %collective-permute-start.14 = (f32[512,128]{1,0:T(8,128)S(1)}, f32[512,128]{1,0:T(8,128)S(1)}, u32[]{:S(2)}, u32[]{:S(2)}) collective-permute-start(f32[512,128]{1,0:T(8,128)S(1)} %get-tuple-element.33), channel_id=1, source_target_pairs={{0,2},{1,3},{2,0},{3,1},{4,6},{5,7},{6,4},{7,5},{8,10},{9,11},{10,... | collective-permute-start | bytes 786440 | tf_op jit(solution)/shard_map/ppermute | solution.py:517
  97.0 11.7 %collective-permute-start.15 = (f32[512,128]{1,0:T(8,128)S(1)}, f32[512,128]{1,0:T(8,128)S(1)}, u32[]{:S(2)}, u32[]{:S(2)}) collective-permute-start(f32[512,128]{1,0:T(8,128)S(1)} %get-tuple-element.34), channel_id=1, source_target_pairs={{0,3},{1,0},{2,1},{3,2},{4,7},{5,4},{6,5},{7,6},{8,11},{9,8},{10,9... | collective-permute-start | bytes 786440 | tf_op jit(solution)/shard_map/ppermute | solution.py:517

commit v3 on v2

--- a/solution.py
+++ b/solution.py
@@ -27,6 +27,7 @@
 HALO = CSWEEPS
 HALF = TE
 YBLOCKS = HALF + 2 * HALO
+BATCH = 8
 ROW0 = SUB
 SLAB_ROWS = ROW0 + YBLOCKS * SLABX + SUB
 
@@ -46,7 +47,7 @@
     return pltpu.roll(value, by % value.shape[axis], axis)
 
 
-def prep_kernel(table, phi, src, mat, temp, slab, body, sigma, up, down, src_v, mat_v, ends_t, ends_m, sems):
+def prep_kernel(table, phi, src, mat, temp, slab, body, sigma, up, down, up_t, down_t, src_v, mat_v, ends_t, ends_m, sems):
     rows = TE * ROW
     size_x, width = temp.shape
     moves = [(phi, body.at[0:rows]), (src, src_v), (mat, mat_v)]
@@ -75,13 +76,13 @@
         t_low, m_low = ends_t[0, :, lanes], ends_m[0, :, lanes].astype(jnp.float32)
         t_high, m_high = ends_t[1, :, lanes], ends_m[1, :, lanes].astype(jnp.float32)
         first = at * SUB
-        up[LOW_ROWS + first : LOW_ROWS + first + SUB] = jnp.where(sub < 4, roll(t_high, HALO, 0), roll(m_high, -1, 0))
-        down[HIGH_ROWS + first : HIGH_ROWS + first + SUB] = jnp.where(sub < 4, t_low, roll(m_low, 4, 0))
+        up_t[first : first + SUB] = jnp.where(sub < 4, roll(t_high, HALO, 0), roll(m_high, -1, 0))
+        down_t[first : first + SUB] = jnp.where(sub < 4, t_low, roll(m_low, 4, 0))
 
 
 def relay_kernel(low, high, halo):
-    halo[0:LOW_ROWS] = low[0:LOW_ROWS]
-    halo[LOW_ROWS : LOW_ROWS + HIGH_ROWS] = high[0:HIGH_ROWS]
+    halo[0:LOW_ROWS] = low[...]
+    halo[LOW_ROWS:] = high[...]
 
 
 def loose(pos):
@@ -96,13 +97,13 @@
         for at in range(blocks):
             lanes = slice(at * LANES, (at + 1) * LANES)
             first = at * SLABX
-            side = LOW_ROWS + at * SUB
+            side = at * SUB
             value = low[side : side + SUB, :]
             native[first : first + SUB, :] = roll(value, -4, 0) if which else value
             for g in range(TE // SUB):
                 value = own[g * SUB : (g + 1) * SUB, lanes].astype(jnp.float32)
                 native[pl.ds(start + first + HALO + g * SUB, SUB), :] = value
-            side = HIGH_ROWS + at * SUB
+            side = at * SUB
             value = high[side : side + SUB, :]
             native[pl.ds(start + first + HALO + TE, SUB), :] = roll(value, -4, 0) if which else value
     for at in range(blocks // 2):
@@ -260,24 +261,33 @@
         def sweep_tile(slot, carry):
             cell, slots = around(0, slot)
             below, above = cell_at[1, cell], cell_at[2, cell]
-            for p in range(TE):
-                x_m = plane_at(c_src, slot * TE + p - 1) if p > 0 else plane_at(l_src, below * LOW[0] + LOW[0] - 1)
-                x_p = plane_at(c_src, slot * TE + p + 1) if p < TE - 1 else plane_at(u_src, above * HIGH[0])
-                put_plane(c_dst, slot * TE + p, relax(c_src, TE, slots, p, x_m, x_p, s_c[slot * TE + p]))
+            for first in range(0, TE, BATCH):
+                results = []
+                for p in range(first, first + BATCH):
+                    x_m = plane_at(c_src, slot * TE + p - 1) if p > 0 else plane_at(l_src, below * LOW[0] + LOW[0] - 1)
+                    x_p = plane_at(c_src, slot * TE + p + 1) if p < TE - 1 else plane_at(u_src, above * HIGH[0])
+                    results.append(relax(c_src, TE, slots, p, x_m, x_p, s_c[slot * TE + p]))
+                for p in range(first, first + BATCH):
+                    put_plane(c_dst, slot * TE + p, results[p - first])
             cell, slots = around(1, slot)
             centre = cell_at[0, cell]
+            results = []
             for p in range(k + 1, LOW[0]):
                 x_m = plane_at(l_src, slot * LOW[0] + p - 1)
                 x_p = plane_at(l_src, slot * LOW[0] + p + 1) if p < LOW[0] - 1 else plane_at(c_src, centre * TE)
                 s = s_l[slot * LOW[1] + p - (LOW[0] - LOW[1])]
-                put_plane(l_dst, slot * LOW[0] + p, relax(l_src, LOW[0], slots, p, x_m, x_p, s))
+                results.append(relax(l_src, LOW[0], slots, p, x_m, x_p, s))
+            for p in range(k + 1, LOW[0]):
+                put_plane(l_dst, slot * LOW[0] + p, results[p - k - 1])
             cell, slots = around(2, slot)
             centre = cell_at[0, cell]
+            results = []
             for p in range(HIGH[0] - 1 - k):
                 x_m = plane_at(u_src, slot * HIGH[0] + p - 1) if p > 0 else plane_at(c_src, centre * TE + TE - 1)
                 x_p = plane_at(u_src, slot * HIGH[0] + p + 1)
-                s = s_u[slot * HIGH[1] + p]
-                put_plane(u_dst, slot * HIGH[0] + p, relax(u_src, HIGH[0], slots, p, x_m, x_p, s))
+                results.append(relax(u_src, HIGH[0], slots, p, x_m, x_p, s_u[slot * HIGH[1] + p]))
+            for p in range(HIGH[0] - 1 - k):
+                put_plane(u_dst, slot * HIGH[0] + p, results[p])
             return carry
 
         lax.fori_loop(0, tiles, sweep_tile, 0)
@@ -409,16 +419,30 @@
                 if 0 < block < YBLOCKS - 1:
                     q_ext[rows_of(block, g)] = pick([turned(cells[c], c - r) for c in range(4)])
 
-    start = loose(pos)
     sub = lax.broadcasted_iota(jnp.int32, (SUB, LANES), 0)
     half = lane < NZ
     no_z = lane % NZ == NZ - 1
-    low_x = (sub == HALO - 1) & (i == 0), (sub == HALO) & (i == 0)
+    low_x = (sub == HALO - 1) & (i == 0)
     high_x = (sub == (HALO + TE - 1) % SUB) & (i == rows_gx - 1)
     low_y, high_y = half & (j == 0), (lane >= NZ) & (j == width_gy - 1)
 
-    def beside(ref, block, g, by):
-        return ref[pl.ds(start + (ROW0 + block * SLABX + g * SUB + by), SUB), :]
+    first_sub, last_sub = sub == 0, sub == SUB - 1
+
+    def inverse(value):
+        near = pl.reciprocal(value, approx=True)
+        near = near * (2.0 - value * near)
+        return near * (2.0 - value * near)
+
+    def load(ref, block):
+        return [ref[rows_of(block, g)] for g in range(groups)]
+
+    def next_x(values):
+        up = [roll(v, -1, 0) for v in values]
+        return [jnp.where(last_sub, up[min(g + 1, groups - 1)], up[g]) for g in range(groups)]
+
+    def last_x(values):
+        down = [roll(v, 1, 0) for v in values]
+        return [jnp.where(first_sub, down[max(g - 1, 0)], down[g]) for g in range(groups)]
 
     edges = {}
     for e in range(HALO):
@@ -443,44 +467,47 @@
                 k0_edge[rows_of(list(edges).index(block), g)] = k0
                 b_edge[rows_of(list(edges).index(block), g)] = beta
             temp_a[rows] = temp
-            cond_a[rows] = k0 / (1.0 + beta * temp * temp)
+            cond_a[rows] = k0 * inverse(1.0 + beta * temp * temp)
 
     for step in range(CSWEEPS):
         (t_src, c_src), (t_dst, c_dst) = ((temp_a, cond_a), (temp_b, cond_b))[:: 1 if step % 2 == 0 else -1]
-        for g in range(groups):
-            now = t_src[rows_of(step, g)], c_src[rows_of(step, g)]
-            ahead = t_src[rows_of(step + 1, g)], c_src[rows_of(step + 1, g)]
-            flux_y = (now[1] + ahead[1]) * (ahead[0] - now[0])
-            if step == HALO - 1:
-                flux_y = jnp.where(low_y, 0.0, flux_y)
-            for block in range(step + 1, YBLOCKS - 1 - step):
-                (temp, cond), before = ahead, flux_y
-                ahead = t_src[rows_of(block + 1, g)], c_src[rows_of(block + 1, g)]
-                flux_y = (cond + ahead[1]) * (ahead[0] - temp)
-                if block == HALO - 1:
-                    flux_y = jnp.where(low_y, 0.0, flux_y)
-                if block == HALO + HALF - 1:
-                    flux_y = jnp.where(high_y, 0.0, flux_y)
-                flux_p = (cond + beside(c_src, block, g, 1)) * (beside(t_src, block, g, 1) - temp)
-                flux_m = (cond + beside(c_src, block, g, -1)) * (beside(t_src, block, g, -1) - temp)
-                if g == 0:
-                    flux_p = jnp.where(low_x[0], 0.0, flux_p)
-                    flux_m = jnp.where(low_x[1], 0.0, flux_m)
-                if g == groups - 1:
-                    flux_p = jnp.where(high_x, 0.0, flux_p)
-                flux_z = (cond + roll(cond, -1, 1)) * (roll(temp, -1, 1) - temp)
+        ahead, flux_y = None, None
+        for block in range(step, YBLOCKS - 1 - step):
+            temp, cond = ahead or (load(t_src, block), load(c_src, block))
+            ahead = load(t_src, block + 1), load(c_src, block + 1)
+            before = flux_y
+            flux_y = [(cond[g] + ahead[1][g]) * (ahead[0][g] - temp[g]) for g in range(groups)]
+            if block == HALO - 1:
+                flux_y = [jnp.where(low_y, 0.0, f) for f in flux_y]
+            if block == HALO + HALF - 1:
+                flux_y = [jnp.where(high_y, 0.0, f) for f in flux_y]
+            if before is None:
+                continue
+            temp_x, cond_x = next_x(temp), next_x(cond)
+            flux_x = [(cond[g] + cond_x[g]) * (temp_x[g] - temp[g]) for g in range(groups)]
+            flux_x[0] = jnp.where(low_x, 0.0, flux_x[0])
+            flux_x[-1] = jnp.where(high_x, 0.0, flux_x[-1])
+            back_x = last_x(flux_x)
+            results = []
+            for g in range(groups):
+                flux_z = (cond[g] + roll(cond[g], -1, 1)) * (roll(temp[g], -1, 1) - temp[g])
                 flux_z = jnp.where(no_z, 0.0, flux_z)
-                div = (flux_y - before) + (flux_p + flux_m) + (flux_z - roll(flux_z, 1, 1))
+                div = (flux_y[g] - before[g]) + (flux_x[g] - back_x[g]) + (flux_z - roll(flux_z, 1, 1))
                 rows = rows_of(block, g)
-                new = temp + DT * (0.5 * div + q_ext[rows])
-                t_dst[rows] = new
+                new = temp[g] + DT * (0.5 * div + q_ext[rows])
                 if step < CSWEEPS - 1:
                     if block in edges:
                         at = list(edges).index(block)
                         k0, beta = k0_edge[rows_of(at, g)], b_edge[rows_of(at, g)]
                     else:
                         k0, beta = k0_in[rows], b_in[rows]
-                    c_dst[rows] = k0 / (1.0 + beta * new * new)
+                    results.append((new, k0 * inverse(1.0 + beta * new * new)))
+                else:
+                    results.append((new, None))
+            for g in range(groups):
+                t_dst[rows_of(block, g)] = results[g][0]
+                if step < CSWEEPS - 1:
+                    c_dst[rows_of(block, g)] = results[g][1]
     final = temp_b if CSWEEPS % 2 else temp_a
 
     for yq in range(HALF // 4):
@@ -488,7 +515,8 @@
             x = slice(g * SUB, (g + 1) * SUB)
             turns = []
             for r in range(4):
-                value = beside(final, HALO + 4 * yq + r, g, HALO)
+                here, after = (final[rows_of(HALO + 4 * yq + r, at)] for at in (g, g + 1))
+                value = jnp.where(sub < SUB - HALO, roll(here, -HALO, 0), roll(after, -HALO, 0))
                 turns.append([turned(value, by) for by in range(4)])
             for pair in range(2):
                 even, odd = turns[2 * pair], turns[2 * pair + 1]
@@ -546,7 +574,7 @@
 VMEM = pl.BlockSpec(memory_space=pltpu.VMEM)
 SMEM = pl.BlockSpec(memory_space=pltpu.SMEM)
 HBM = pl.BlockSpec(memory_space=pltpu.HBM)
-PARAMS = pltpu.CompilerParams(vmem_limit_bytes=48 * 1024 * 1024)
+PARAMS = pltpu.CompilerParams(vmem_limit_bytes=32 * 1024 * 1024)
 
 
 def on_device(
@@ -571,16 +599,18 @@
     def rows(count):
         return jax.ShapeDtypeStruct((count, LANES), f32)
 
-    body, sigma, up, down = pl.pallas_call(
+    body, sigma, up, down, up_t, down_t = pl.pallas_call(
         prep_kernel,
         out_shape=(
             rows(2 * TE * ROW),
             rows(TE * ROW),
-            rows(LOW_ROWS + edge_rows),
-            rows(HIGH_ROWS + edge_rows),
+            rows(LOW_ROWS),
+            rows(HIGH_ROWS),
+            rows(edge_rows),
+            rows(edge_rows),
         ),
         in_specs=[SMEM] + [HBM] * 5,
-        out_specs=(VMEM,) * 4,
+        out_specs=(VMEM,) * 6,
         scratch_shapes=[
             pltpu.VMEM((TE * ROW, LANES), f32),
             pltpu.VMEM((TE * ROW, LANES), jnp.int32),
@@ -593,6 +623,7 @@
     )(sigma_table, to_rows(phi_init), to_rows(source), to_rows(tile_mat), temp_init, slab_mat)
     bodies = everyone(body, chips)
     low, high = shifted(up, "gx", 1), shifted(down, "gx", -1)
+    low_t, high_t = shifted(up_t, "gx", 1), shifted(down_t, "gx", -1)
 
     halo = pl.pallas_call(
         relay_kernel,
@@ -602,7 +633,7 @@
         compiler_params=PARAMS,
         name="relay",
     )(low, high)
-    halos = everyone(halo, chips)
+    halos = [halo] + [shifted(halo, "gy", 2 * d, True) for d in range(1, chips)]
     sigmas = everyone_direct(sigma, chips)
 
     native = pltpu.VMEM((width // LANES * SLABX + SUB, LANES), f32)
@@ -614,7 +645,9 @@
         scratch_shapes=[native, native],
         compiler_params=PARAMS,
         name="slab_prep",
-    )(tile_pos, k0_table, beta_table, temp_init, slab_mat, low, high)
+    )(tile_pos, k0_table, beta_table, temp_init, slab_mat, low_t, high_t)
+    *halos[1:], edge_low, edge_high = lax.optimization_barrier((*halos[1:], edge_low, edge_high))
+    halos = halos + [from_mate(part) for part in halos]
     ylow, yhigh = shifted(edge_high, "gy", 1), shifted(edge_low, "gy", -1)
 
     def planes(count):

time: 111 us -> 116 us (1.045)
  starting transfers between devices: 19.4 us -> 25.8 us
    ppermute x10 -> x12, starting transfers between devices: 18.7 us -> 25 us  [shifted(): return lax.ppermute(value, axis, pairs)]
    ppermute x10 -> x12, waiting for transfers between devices: 27.2 us -> 27.4 us  [shifted(): return lax.ppermute(value, axis, pairs)]
  transfers between devices with their start and end apart: 16 -> 18, of which waited for: 6 -> 5; matrix products, arithmetic and copies ran while one was open for 0% -> 0% of each run, Pallas kernels for 14% -> 13%
where the time goes in v3:
time: 116 us; the launch traced here: 115 us
  Pallas kernels  58.7 us (51%)
  waiting for transfers between devices  27.4 us (24%)
  starting transfers between devices  25.8 us (22%)
  local copies, waits for them, and re-layouts  1.68 us (1%)
    pallas_call x1, Pallas kernels, on_device(): pl.pallas_call(functools.partial(slab_steps_kernel, chips), out_shape=(ja...  40.7 us
    ppermute x12, waiting for transfers between devices, shifted(): return lax.ppermute(value, axis, pairs)  27.4 us
    ppermute x12, starting transfers between devices, shifted(): return lax.ppermute(value, axis, pairs)  25 us
    pallas_call x1, Pallas kernels, on_device(): pl.pallas_call(functools.partial(sweep_kernel, chips), out_shape=(rows(TE...  13.1 us
    pallas_call x1, Pallas kernels, on_device(): pl.pallas_call(prep_kernel, out_shape=(rows(2 * TE * ROW), rows(TE * ROW)...  3.27 us
  transfers between devices with their start and end apart: 18, of which 5 were waited for; matrix products, arithmetic and copies ran while one was open for 0% of the time, Pallas kernels for 13%

profile of v3, /device:TPU:0, one launch (start us, length us, event | category | flops | bytes accessed | tf_op | source)
XLA Modules:
  0.0 115.1 jit_solution(14269026021255993817)
XLA Ops:
  0.7 3.3 %prep.1 = (f32[1024,128]{1,0:T(8,128)}, f32[512,128]{1,0:T(8,128)}, f32[208,128]{1,0:T(8,128)}, f32[240,128]{1,0:T(8,128)}, f32[256,128]{1,0:T(8,128)}, /*index=5*/f32[256,128]{1,0:T(8,128)}) custom-call(f32[4]{0:T(128)} %table.1, f32[512,128]{1,0:T(8,128)} %bitcast.26, f32[512,128]{1,0:T(8,128)} %bitcast.27, s32[512,128]{1,0:T(8,128)} %bitcast.28, ...), custom_call_target="tpu_custom_call" | custom-call | tf_op jit(solution)/shard_map/prep/pallas_call | solution.py:602
  4.0 0.0 copy-start.3
  4.0 0.0 copy-start.2
  4.0 3.0 %collective-permute-start = (f32[1024,128]{1,0:T(8,128)}, f32[1024,128]{1,0:T(8,128)}, u32[]{:S(2)}, u32[]{:S(2)}) collective-permute-start(f32[1024,128]{1,0:T(8,128)} %get-tuple-element.24.refs_0_), channel_id=1, source_target_pairs={{0,2},{1,3},{2,0},{3,1},{4,6},{5,7},{6,4},{7,5},{8,10},{9,11},{10,... | collective-permute-start | bytes 1572872 | tf_op jit(solution)/shard_map/ppermute | solution.py:545
  7.0 0.0 collective-permute-start.1
  7.0 1.3 %collective-permute-start.4 = (f32[240,128]{1,0:T(8,128)}, f32[240,128]{1,0:T(8,128)S(1)}, u32[]{:S(2)}, u32[]{:S(2)}) collective-permute-start(f32[240,128]{1,0:T(8,128)} %get-tuple-element.26), channel_id=1, source_target_pairs={{4,0},{8,4},{12,8},{16,12},{20,16},{24,20},{28,24},{5,1},{9,5},{13... | collective-permute-start | bytes 368648 | tf_op jit(solution)/shard_map/ppermute | solution.py:545
  8.3 4.6 %collective-permute-start.3 = (f32[208,128]{1,0:T(8,128)}, f32[208,128]{1,0:T(8,128)S(1)}, u32[]{:S(2)}, u32[]{:S(2)}) collective-permute-start(f32[208,128]{1,0:T(8,128)} %get-tuple-element.25), channel_id=1, source_target_pairs={{0,4},{4,8},{8,12},{12,16},{16,20},{20,24},{24,28},{1,5},{5,9},{9,... | collective-permute-start | bytes 319496 | tf_op jit(solution)/shard_map/ppermute | solution.py:545
  12.8 6.4 %collective-permute-done.refs_1_ = f32[1024,128]{1,0:T(8,128)} collective-permute-done((f32[1024,128]{1,0:T(8,128)}, f32[1024,128]{1,0:T(8,128)}, u32[]{:S(2)}, u32[]{:S(2)}) %collective-permute-start) | collective-permute-done | bytes 524320 | tf_op jit(solution)/shard_map/ppermute | solution.py:545
  19.2 3.7 %collective-permute-start.6 = (f32[256,128]{1,0:T(8,128)}, f32[256,128]{1,0:T(8,128)S(1)}, u32[]{:S(2)}, u32[]{:S(2)}) collective-permute-start(f32[256,128]{1,0:T(8,128)} %get-tuple-element.27), channel_id=1, source_target_pairs={{0,4},{4,8},{8,12},{12,16},{16,20},{20,24},{24,28},{1,5},{5,9},{9,... | collective-permute-start | bytes 393224 | tf_op jit(solution)/shard_map/ppermute | solution.py:545
  22.9 0.0 collective-permute-done.4.high
  23.0 1.6 %collective-permute-start.5 = (f32[448,128]{1,0:T(8,128)S(1)}, f32[448,128]{1,0:T(8,128)S(1)}, u32[]{:S(2)}, u32[]{:S(2)}) collective-permute-start(f32[448,128]{1,0:T(8,128)S(1)} %relay.1.refs_4_), channel_id=1, source_target_pairs={{0,2},{1,3},{2,0},{3,1},{4,6},{5,7},{6,4},{7,5},{8,10},{9,11},{10,... | collective-permute-start | bytes 688136 | tf_op jit(solution)/shard_map/ppermute | solution.py:545
  24.5 2.1 %collective-permute-done.6.low = f32[256,128]{1,0:T(8,128)S(1)} collective-permute-done((f32[256,128]{1,0:T(8,128)}, f32[256,128]{1,0:T(8,128)S(1)}, u32[]{:S(2)}, u32[]{:S(2)}) %collective-permute-start.6) | collective-permute-done | bytes 131104 | tf_op jit(solution)/shard_map/ppermute | solution.py:545
  26.6 1.3 %collective-permute-start.7 = (f32[256,128]{1,0:T(8,128)}, f32[256,128]{1,0:T(8,128)S(1)}, u32[]{:S(2)}, u32[]{:S(2)}) collective-permute-start(f32[256,128]{1,0:T(8,128)} %get-tuple-element.28), channel_id=1, source_target_pairs={{4,0},{8,4},{12,8},{16,12},{20,16},{24,20},{28,24},{5,1},{9,5},{13... | collective-permute-start | bytes 393224 | tf_op jit(solution)/shard_map/ppermute | solution.py:545
  27.9 0.1 copy.16.pos
  28.0 6.5 %collective-permute-done.7.high = f32[256,128]{1,0:T(8,128)S(1)} collective-permute-done((f32[256,128]{1,0:T(8,128)}, f32[256,128]{1,0:T(8,128)S(1)}, u32[]{:S(2)}, u32[]{:S(2)}) %collective-permute-start.7) | collective-permute-done | bytes 131104 | tf_op jit(solution)/shard_map/ppermute | solution.py:545
  34.5 0.7 copy-done.4
  35.2 0.9 copy-done.5
  36.1 1.6 %slab_prep.1 = (f32[1536,128]{1,0:T(8,128)S(1)}, f32[1536,128]{1,0:T(8,128)S(1)}, f32[1536,128]{1,0:T(8,128)S(1)}, f32[120,128]{1,0:T(8,128)S(1)}, f32[120,128]{1,0:T(8,128)S(1)}) custom-call(s32[64,3]{1,0:T(8,128)S(1)} %copy.16.pos, f32[4]{0:T(128)S(1)} %copy-done.6, f32[4]{0:T(128)S(1)} %copy-done.7, f32[32,4096]{1,0:T(8,128)S(1)} %copy-done, ...), custom_call_target="tpu_custom_call" | custom-call | tf_op jit(solution)/shard_map/slab_prep/pallas_call | solution.py:640
  37.7 0.1 collective-permute-start.9
  37.8 1.6 %collective-permute-start.10 = (f32[512,128]{1,0:T(8,128)S(1)}, f32[512,128]{1,0:T(8,128)S(1)}, u32[]{:S(2)}, u32[]{:S(2)}) collective-permute-start(f32[512,128]{1,0:T(8,128)S(1)} %copy-done.3), channel_id=1, source_target_pairs={{0,2},{1,3},{2,0},{3,1},{4,6},{5,7},{6,4},{7,5},{8,10},{9,11},{10,... | collective-permute-start | bytes 786440 | tf_op jit(solution)/shard_map/ppermute | solution.py:545
  39.4 0.2 collective-permute-start.11
  39.5 0.5 collective-permute-start.12
  40.0 2.1 %collective-permute-start.13 = (f32[120,128]{1,0:T(8,128)S(1)}, f32[120,128]{1,0:T(8,128)S(1)}, u32[]{:S(2)}, u32[]{:S(2)}) collective-permute-start(f32[120,128]{1,0:T(8,128)S(1)} %get-tuple-element.38), channel_id=1, source_target_pairs={{0,1},{1,2},{2,3},{4,5},{5,6},{6,7},{8,9},{9,10},{10,11},{12,13},{... | collective-permute-start | bytes 184328 | tf_op jit(solution)/shard_map/ppermute | solution.py:545
  42.1 1.3 %collective-permute-start.14 = (f32[120,128]{1,0:T(8,128)S(1)}, f32[120,128]{1,0:T(8,128)S(1)}, u32[]{:S(2)}, u32[]{:S(2)}) collective-permute-start(f32[120,128]{1,0:T(8,128)S(1)} %get-tuple-element.39), channel_id=1, source_target_pairs={{1,0},{2,1},{3,2},{5,4},{6,5},{7,6},{9,8},{10,9},{11,10},{13,12},{... | collective-permute-start | bytes 184328 | tf_op jit(solution)/shard_map/ppermute | solution.py:545
  43.4 13.1 %sweeps.1 = (f32[512,128]{1,0:T(8,128)}, f32[2560,128]{1,0:T(8,128)S(1)}) custom-call(s32[64,3]{1,0:T(8,128)S(1)} %copy.16.pos, f32[1024,128]{1,0:T(8,128)S(1)} %copy-done.2, f32[1024,128]{1,0:T(8,128)} %collective-permute-done.refs_1_, f32[1024,128]{1,0:T(8,128)} %collective-permute-done.1.refs_2_, f32[1024,128]{1,0:T(8,128)} %collective-permute-done.2.refs_3_, ...), custom_call_target="tpu_custom_call" | custom-call | tf_op jit(solution)/shard_map/sweeps/pallas_call | solution.py:659
  56.5 40.7 %slab_steps.1 = (f32[32,4096]{1,0:T(8,128)}, f32[512,128]{1,0:T(8,128)S(1)}, f32[512,128]{1,0:T(8,128)S(1)}, f32[512,128]{1,0:T(8,128)S(1)}, f32[512,128]{1,0:T(8,128)S(1)}) custom-call(s32[64,3]{1,0:T(8,128)S(1)} %copy.16.pos, f32[4]{0:T(128)S(1)} %copy-done.6, f32[4]{0:T(128)S(1)} %copy-done.7, f32[512,128]{1,0:T(8,128)S(1)} %copy-done.3, ...), custom_call_target="tpu_custom_call" | custom-call | tf_op jit(solution)/shard_map/slab_steps/pallas_call | solution.py:674
  97.2 3.1 %collective-permute-start.17 = (f32[512,128]{1,0:T(8,128)S(1)}, f32[512,128]{1,0:T(8,128)S(1)}, u32[]{:S(2)}, u32[]{:S(2)}) collective-permute-start(f32[512,128]{1,0:T(8,128)S(1)} %get-tuple-element.44), channel_id=1, source_target_pairs={{0,3},{1,0},{2,1},{3,2},{4,7},{5,4},{6,5},{7,6},{8,11},{9,8},{10,9... | collective-permute-start | bytes 786440 | tf_op jit(solution)/shard_map/ppermute | solution.py:545
  100.4 1.4 %collective-permute-start.16 = (f32[512,128]{1,0:T(8,128)S(1)}, f32[512,128]{1,0:T(8,128)S(1)}, u32[]{:S(2)}, u32[]{:S(2)}) collective-permute-start(f32[512,128]{1,0:T(8,128)S(1)} %get-tuple-element.43), channel_id=1, source_target_pairs={{0,2},{1,3},{2,0},{3,1},{4,6},{5,7},{6,4},{7,5},{8,10},{9,11},{10,... | collective-permute-start | bytes 786440 | tf_op jit(solution)/shard_map/ppermute | solution.py:545
  101.8 0.2 collective-permute-start.15
  102.0 4.1 %collective-permute-done.17 = f32[512,128]{1,0:T(8,128)S(1)} collective-permute-done((f32[512,128]{1,0:T(8,128)S(1)}, f32[512,128]{1,0:T(8,128)S(1)}, u32[]{:S(2)}, u32[]{:S(2)}) %collective-permute-start.17) | collective-permute-done | bytes 262176 | tf_op jit(solution)/shard_map/ppermute | solution.py:545
  106.1 8.3 %collective-permute-done.16 = f32[512,128]{1,0:T(8,128)S(1)} collective-permute-done((f32[512,128]{1,0:T(8,128)S(1)}, f32[512,128]{1,0:T(8,128)S(1)}, u32[]{:S(2)}, u32[]{:S(2)}) %collective-permute-start.16) | collective-permute-done | bytes 262176 | tf_op jit(solution)/shard_map/ppermute | solution.py:545
  114.4 0.8 add_add_fusion
  (29 shorter events, 0.1 us)
Async XLA Ops:
  0.6 34.5 %copy-start = (f32[32,4096]{1,0:T(8,128)S(1)}, f32[32,4096]{1,0:T(8,128)}, u32[]{:S(2)}) copy-start(f32[32,4096]{1,0:T(8,128)} %temp.3) | copy-start | bytes 1572868
  0.6 34.5 %copy-start.1 = (s32[32,4096]{1,0:T(8,128)S(1)}, s32[32,4096]{1,0:T(8,128)}, u32[]{:S(2)}) copy-start(s32[32,4096]{1,0:T(8,128)} %mat.1) | copy-start | bytes 1572868
  0.7 27.3 %copy-start.8 = (s32[64,3]{0,1:T(4,128)S(1)}, s32[64,3]{0,1:T(4,128)}, u32[]{:S(2)}) copy-start(s32[64,3]{0,1:T(4,128)} %param.13) | copy-start | bytes 2308
  0.7 34.5 %copy-start.6 = (f32[4]{0:T(128)S(1)}, f32[4]{0:T(128)}, u32[]{:S(2)}) copy-start(f32[4]{0:T(128)} %k0_table.3) | copy-start | bytes 52
  0.7 34.5 %copy-start.7 = (f32[4]{0:T(128)S(1)}, f32[4]{0:T(128)}, u32[]{:S(2)}) copy-start(f32[4]{0:T(128)} %beta_table.3) | copy-start | bytes 52
  4.0 33.8 %copy-start.3 = (f32[512,128]{1,0:T(8,128)S(1)}, f32[512,128]{1,0:T(8,128)}, u32[]{:S(2)}) copy-start(f32[512,128]{1,0:T(8,128)} %get-tuple-element.33.refs_0_) | copy-start | bytes 786436
  4.0 39.4 %copy-start.2 = (f32[1024,128]{1,0:T(8,128)S(1)}, f32[1024,128]{1,0:T(8,128)}, u32[]{:S(2)}) copy-start(f32[1024,128]{1,0:T(8,128)} %get-tuple-element.24.refs_0_) | copy-start | bytes 1572868
  4.0 15.2 %collective-permute-start = (f32[1024,128]{1,0:T(8,128)}, f32[1024,128]{1,0:T(8,128)}, u32[]{:S(2)}, u32[]{:S(2)}) collective-permute-start(f32[1024,128]{1,0:T(8,128)} %get-tuple-element.24.refs_0_), channel_id=1, source_target_pairs={{0,2},{1,3},{2,0},{3,1},{4,6},{5,7},{6,4},{7,5},{8,10},{9,11},{10,... | collective-permute-start | bytes 1572872 | tf_op jit(solution)/shard_map/ppermute | solution.py:545
  7.0 32.5 %collective-permute-start.1 = (f32[1024,128]{1,0:T(8,128)}, f32[1024,128]{1,0:T(8,128)}, u32[]{:S(2)}, u32[]{:S(2)}) collective-permute-start(f32[1024,128]{1,0:T(8,128)} %get-tuple-element.24.refs_0_), channel_id=1, source_target_pairs={{0,1},{1,0},{2,3},{3,2},{4,5},{5,4},{6,7},{7,6},{8,9},{9,8},{10,11... | collective-permute-start | bytes 1572872 | tf_op jit(solution)/shard_map/ppermute | solution.py:549
  7.0 15.9 %collective-permute-start.4 = (f32[240,128]{1,0:T(8,128)}, f32[240,128]{1,0:T(8,128)S(1)}, u32[]{:S(2)}, u32[]{:S(2)}) collective-permute-start(f32[240,128]{1,0:T(8,128)} %get-tuple-element.26), channel_id=1, source_target_pairs={{4,0},{8,4},{12,8},{16,12},{20,16},{24,20},{28,24},{5,1},{9,5},{13... | collective-permute-start | bytes 368648 | tf_op jit(solution)/shard_map/ppermute | solution.py:545
  8.3 14.6 %collective-permute-start.3 = (f32[208,128]{1,0:T(8,128)}, f32[208,128]{1,0:T(8,128)S(1)}, u32[]{:S(2)}, u32[]{:S(2)}) collective-permute-start(f32[208,128]{1,0:T(8,128)} %get-tuple-element.25), channel_id=1, source_target_pairs={{0,4},{4,8},{8,12},{12,16},{16,20},{20,24},{24,28},{1,5},{5,9},{9,... | collective-permute-start | bytes 319496 | tf_op jit(solution)/shard_map/ppermute | solution.py:545
  19.2 22.8 %collective-permute-start.2 = (f32[1024,128]{1,0:T(8,128)}, f32[1024,128]{1,0:T(8,128)}, u32[]{:S(2)}, u32[]{:S(2)}) collective-permute-start(f32[1024,128]{1,0:T(8,128)} %collective-permute-done.refs_1_), channel_id=1, source_target_pairs={{0,1},{1,0},{2,3},{3,2},{4,5},{5,4},{6,7},{7,6},{8,9},{9,8},{10,11... | collective-permute-start | bytes 1572872 | tf_op jit(solution)/shard_map/ppermute | solution.py:549
  19.2 7.4 %collective-permute-start.6 = (f32[256,128]{1,0:T(8,128)}, f32[256,128]{1,0:T(8,128)S(1)}, u32[]{:S(2)}, u32[]{:S(2)}) collective-permute-start(f32[256,128]{1,0:T(8,128)} %get-tuple-element.27), channel_id=1, source_target_pairs={{0,4},{4,8},{8,12},{12,16},{16,20},{20,24},{24,28},{1,5},{5,9},{9,... | collective-permute-start | bytes 393224 | tf_op jit(solution)/shard_map/ppermute | solution.py:545
  23.0 14.7 %collective-permute-start.5 = (f32[448,128]{1,0:T(8,128)S(1)}, f32[448,128]{1,0:T(8,128)S(1)}, u32[]{:S(2)}, u32[]{:S(2)}) collective-permute-start(f32[448,128]{1,0:T(8,128)S(1)} %relay.1.refs_4_), channel_id=1, source_target_pairs={{0,2},{1,3},{2,0},{3,1},{4,6},{5,7},{6,4},{7,5},{8,10},{9,11},{10,... | collective-permute-start | bytes 688136 | tf_op jit(solution)/shard_map/ppermute | solution.py:545
  24.5 14.8 %collective-permute-start.8 = (f32[448,128]{1,0:T(8,128)S(1)}, f32[448,128]{1,0:T(8,128)S(1)}, u32[]{:S(2)}, u32[]{:S(2)}) collective-permute-start(f32[448,128]{1,0:T(8,128)S(1)} %relay.1.refs_4_), channel_id=1, source_target_pairs={{0,1},{1,0},{2,3},{3,2},{4,5},{5,4},{6,7},{7,6},{8,9},{9,8},{10,11... | collective-permute-start | bytes 688136 | tf_op jit(solution)/shard_map/ppermute | solution.py:549
  26.6 7.9 %collective-permute-start.7 = (f32[256,128]{1,0:T(8,128)}, f32[256,128]{1,0:T(8,128)S(1)}, u32[]{:S(2)}, u32[]{:S(2)}) collective-permute-start(f32[256,128]{1,0:T(8,128)} %get-tuple-element.28), channel_id=1, source_target_pairs={{4,0},{8,4},{12,8},{16,12},{20,16},{24,20},{28,24},{5,1},{9,5},{13... | collective-permute-start | bytes 393224 | tf_op jit(solution)/shard_map/ppermute | solution.py:545
  34.5 0.7 copy-start.4
  35.2 0.9 copy-start.5
  37.7 2.3 %collective-permute-start.9 = (f32[448,128]{1,0:T(8,128)S(1)}, f32[448,128]{1,0:T(8,128)S(1)}, u32[]{:S(2)}, u32[]{:S(2)}) collective-permute-start(f32[448,128]{1,0:T(8,128)S(1)} %collective-permute-done.5.refs_5_), channel_id=1, source_target_pairs={{0,1},{1,0},{2,3},{3,2},{4,5},{5,4},{6,7},{7,6},{8,9},{9,8},{10,11... | collective-permute-start | bytes 688136 | tf_op jit(solution)/shard_map/ppermute | solution.py:549
  37.8 18.7 %collective-permute-start.10 = (f32[512,128]{1,0:T(8,128)S(1)}, f32[512,128]{1,0:T(8,128)S(1)}, u32[]{:S(2)}, u32[]{:S(2)}) collective-permute-start(f32[512,128]{1,0:T(8,128)S(1)} %copy-done.3), channel_id=1, source_target_pairs={{0,2},{1,3},{2,0},{3,1},{4,6},{5,7},{6,4},{7,5},{8,10},{9,11},{10,... | collective-permute-start | bytes 786440 | tf_op jit(solution)/shard_map/ppermute | solution.py:545
  39.4 17.1 %collective-permute-start.11 = (f32[512,128]{1,0:T(8,128)S(1)}, f32[512,128]{1,0:T(8,128)S(1)}, u32[]{:S(2)}, u32[]{:S(2)}) collective-permute-start(f32[512,128]{1,0:T(8,128)S(1)} %copy-done.3), channel_id=1, source_target_pairs={{0,1},{1,0},{2,3},{3,2},{4,5},{5,4},{6,7},{7,6},{8,9},{9,8},{10,11... | collective-permute-start | bytes 786440 | tf_op jit(solution)/shard_map/ppermute | solution.py:570
  39.5 16.9 %collective-permute-start.12 = (f32[512,128]{1,0:T(8,128)S(1)}, f32[512,128]{1,0:T(8,128)S(1)}, u32[]{:S(2)}, u32[]{:S(2)}) collective-permute-start(f32[512,128]{1,0:T(8,128)S(1)} %copy-done.3), channel_id=1, source_target_pairs={{0,3},{1,2},{2,1},{3,0},{4,7},{5,6},{6,5},{7,4},{8,11},{9,10},{10,... | collective-permute-start | bytes 786440 | tf_op jit(solution)/shard_map/ppermute | solution.py:570
  40.0 16.5 %collective-permute-start.13 = (f32[120,128]{1,0:T(8,128)S(1)}, f32[120,128]{1,0:T(8,128)S(1)}, u32[]{:S(2)}, u32[]{:S(2)}) collective-permute-start(f32[120,128]{1,0:T(8,128)S(1)} %get-tuple-element.38), channel_id=1, source_target_pairs={{0,1},{1,2},{2,3},{4,5},{5,6},{6,7},{8,9},{9,10},{10,11},{12,13},{... | collective-permute-start | bytes 184328 | tf_op jit(solution)/shard_map/ppermute | solution.py:545
  42.1 14.4 %collective-permute-start.14 = (f32[120,128]{1,0:T(8,128)S(1)}, f32[120,128]{1,0:T(8,128)S(1)}, u32[]{:S(2)}, u32[]{:S(2)}) collective-permute-start(f32[120,128]{1,0:T(8,128)S(1)} %get-tuple-element.39), channel_id=1, source_target_pairs={{1,0},{2,1},{3,2},{5,4},{6,5},{7,6},{9,8},{10,9},{11,10},{13,12},{... | collective-permute-start | bytes 184328 | tf_op jit(solution)/shard_map/ppermute | solution.py:545
  97.2 8.8 %collective-permute-start.17 = (f32[512,128]{1,0:T(8,128)S(1)}, f32[512,128]{1,0:T(8,128)S(1)}, u32[]{:S(2)}, u32[]{:S(2)}) collective-permute-start(f32[512,128]{1,0:T(8,128)S(1)} %get-tuple-element.44), channel_id=1, source_target_pairs={{0,3},{1,0},{2,1},{3,2},{4,7},{5,4},{6,5},{7,6},{8,11},{9,8},{10,9... | collective-permute-start | bytes 786440 | tf_op jit(solution)/shard_map/ppermute | solution.py:545
  100.4 14.0 %collective-permute-start.16 = (f32[512,128]{1,0:T(8,128)S(1)}, f32[512,128]{1,0:T(8,128)S(1)}, u32[]{:S(2)}, u32[]{:S(2)}) collective-permute-start(f32[512,128]{1,0:T(8,128)S(1)} %get-tuple-element.43), channel_id=1, source_target_pairs={{0,2},{1,3},{2,0},{3,1},{4,6},{5,7},{6,4},{7,5},{8,10},{9,11},{10,... | collective-permute-start | bytes 786440 | tf_op jit(solution)/shard_map/ppermute | solution.py:545
  101.8 12.6 %collective-permute-start.15 = (f32[512,128]{1,0:T(8,128)S(1)}, f32[512,128]{1,0:T(8,128)S(1)}, u32[]{:S(2)}, u32[]{:S(2)}) collective-permute-start(f32[512,128]{1,0:T(8,128)S(1)} %get-tuple-element.42), channel_id=1, source_target_pairs={{0,1},{1,2},{2,3},{3,0},{4,5},{5,6},{6,7},{7,4},{8,9},{9,10},{10,1... | collective-permute-start | bytes 786440 | tf_op jit(solution)/shard_map/ppermute | solution.py:545

commit v4 on v3

--- a/solution.py
+++ b/solution.py
@@ -28,6 +28,7 @@
 HALF = TE
 YBLOCKS = HALF + 2 * HALO
 BATCH = 8
+C_SIZE, L_SIZE, U_SIZE = TE + 2, LOW[0] + 1, HIGH[0] + 1
 ROW0 = SUB
 SLAB_ROWS = ROW0 + YBLOCKS * SLABX + SUB
 
@@ -47,7 +48,7 @@
     return pltpu.roll(value, by % value.shape[axis], axis)
 
 
-def prep_kernel(table, phi, src, mat, temp, slab, body, sigma, up, down, up_t, down_t, src_v, mat_v, ends_t, ends_m, sems):
+def prep_kernel(table, phi, src, mat, temp, slab, body, sigma, up, down, src_v, mat_v, ends_t, ends_m, sems):
     rows = TE * ROW
     size_x, width = temp.shape
     moves = [(phi, body.at[0:rows]), (src, src_v), (mat, mat_v)]
@@ -76,13 +77,13 @@
         t_low, m_low = ends_t[0, :, lanes], ends_m[0, :, lanes].astype(jnp.float32)
         t_high, m_high = ends_t[1, :, lanes], ends_m[1, :, lanes].astype(jnp.float32)
         first = at * SUB
-        up_t[first : first + SUB] = jnp.where(sub < 4, roll(t_high, HALO, 0), roll(m_high, -1, 0))
-        down_t[first : first + SUB] = jnp.where(sub < 4, t_low, roll(m_low, 4, 0))
+        up[LOW_ROWS + first : LOW_ROWS + first + SUB] = jnp.where(sub < 4, roll(t_high, HALO, 0), roll(m_high, -1, 0))
+        down[HIGH_ROWS + first : HIGH_ROWS + first + SUB] = jnp.where(sub < 4, t_low, roll(m_low, 4, 0))
 
 
 def relay_kernel(low, high, halo):
-    halo[0:LOW_ROWS] = low[...]
-    halo[LOW_ROWS:] = high[...]
+    halo[0:LOW_ROWS] = low[0:LOW_ROWS]
+    halo[LOW_ROWS:] = high[0:HIGH_ROWS]
 
 
 def loose(pos):
@@ -97,13 +98,13 @@
         for at in range(blocks):
             lanes = slice(at * LANES, (at + 1) * LANES)
             first = at * SLABX
-            side = at * SUB
+            side = LOW_ROWS + at * SUB
             value = low[side : side + SUB, :]
             native[first : first + SUB, :] = roll(value, -4, 0) if which else value
             for g in range(TE // SUB):
                 value = own[g * SUB : (g + 1) * SUB, lanes].astype(jnp.float32)
                 native[pl.ds(start + first + HALO + g * SUB, SUB), :] = value
-            side = at * SUB
+            side = HIGH_ROWS + at * SUB
             value = high[side : side + SUB, :]
             native[pl.ds(start + first + HALO + TE, SUB), :] = roll(value, -4, 0) if which else value
     for at in range(blocks // 2):
@@ -201,17 +202,13 @@
     for part in range(width_gy):
         for t in range(TILES):
             slot = part * TILES + t
-            for which, target in enumerate((pa, s_c)):
-                unpack(bodies[part], which * TE * ROW, t, target, slot * TE, TE)
-            at = 0
-            for which, target in enumerate((la, s_l)):
-                unpack(halos[part], at, t, target, slot * LOW[which], LOW[which])
-                at += LOW[which] * ROW
-            at = LOW_ROWS
-            for which, target in enumerate((ua, s_u)):
-                unpack(halos[part], at, t, target, slot * HIGH[which], HIGH[which])
-                at += HIGH[which] * ROW
-    for ref, count in ((pa, TE), (pb, TE), (la, LOW[0]), (lb, LOW[0]), (ua, HIGH[0]), (ub, HIGH[0])):
+            unpack(bodies[part], 0, t, pa, slot * C_SIZE + 1, TE)
+            unpack(bodies[part], TE * ROW, t, s_c, slot * TE, TE)
+            unpack(halos[part], 0, t, la, slot * L_SIZE, LOW[0])
+            unpack(halos[part], LOW[0] * ROW, t, s_l, slot * LOW[1], LOW[1])
+            unpack(halos[part], LOW_ROWS, t, ua, slot * U_SIZE + 1, HIGH[0])
+            unpack(halos[part], LOW_ROWS + HIGH[0] * ROW, t, s_u, slot * HIGH[1], HIGH[1])
+    for ref, count in ((pa, C_SIZE), (pb, C_SIZE), (la, L_SIZE), (lb, L_SIZE), (ua, U_SIZE), (ub, U_SIZE)):
         for p in range(count):
             put_plane(ref, none * count + p, zero)
 
@@ -246,48 +243,47 @@
         keep, gain = 1.0 - weight, weight / (6.0 + EPS)
         (c_src, l_src, u_src), (c_dst, l_dst, u_dst) = bufs[k % 2], bufs[(k + 1) % 2]
 
-        def relax(field, size, slots, p, x_m, x_p, s):
+        def ghosts(slot, carry):
+            cell = cell_of[0, slot]
+            below, above = cell_at[1, cell], cell_at[2, cell]
+            put_plane(c_src, slot * C_SIZE, plane_at(l_src, below * L_SIZE + LOW[0] - 1))
+            put_plane(c_src, slot * C_SIZE + TE + 1, plane_at(u_src, above * U_SIZE + 1))
+            put_plane(l_src, slot * L_SIZE + LOW[0], plane_at(c_src, cell_at[0, cell_of[1, slot]] * C_SIZE + 1))
+            put_plane(u_src, slot * U_SIZE, plane_at(c_src, cell_at[0, cell_of[2, slot]] * C_SIZE + TE))
+            return carry
+
+        lax.fori_loop(0, tiles, ghosts, 0)
+
+        def relax(src, dst, size, slots, first, count, s_ref, s_at):
             slot, y_m, y_p, z, turn, meets = slots
-            at = slot * size + p
-            own = plane_at(field, at)
-            total = (x_m + x_p) + s
-            total = total + y_minus(field, own, at, y_m * size + p)
-            total = total + y_plus(field, own, at, y_p * size + p)
-            total = total + jnp.where(last_z, 0.0, roll(own, -1, 1))
-            total = total + jnp.where(first_z, 0.0, roll(own, 1, 1))
-            total = total + jnp.where(meets, pltpu.roll(plane_at(field, z * size + p), turn, 1), 0.0)
-            return keep * own + gain * total
+            results = []
+            for p in range(count):
+                at = slot * size + first + p
+                own = plane_at(src, at)
+                total = (plane_at(src, at - 1) + plane_at(src, at + 1)) + s_ref[s_at + p]
+                total = total + y_minus(src, own, at, y_m * size + first + p)
+                total = total + y_plus(src, own, at, y_p * size + first + p)
+                total = total + jnp.where(last_z, 0.0, roll(own, -1, 1))
+                total = total + jnp.where(first_z, 0.0, roll(own, 1, 1))
+                ghost = pltpu.roll(plane_at(src, z * size + first + p), turn, 1)
+                results.append(keep * own + gain * (total + jnp.where(meets, ghost, 0.0)))
+            for p in range(count):
+                put_plane(dst, slot * size + first + p, results[p])
 
         def sweep_tile(slot, carry):
-            cell, slots = around(0, slot)
-            below, above = cell_at[1, cell], cell_at[2, cell]
-            for first in range(0, TE, BATCH):
-                results = []
-                for p in range(first, first + BATCH):
-                    x_m = plane_at(c_src, slot * TE + p - 1) if p > 0 else plane_at(l_src, below * LOW[0] + LOW[0] - 1)
-                    x_p = plane_at(c_src, slot * TE + p + 1) if p < TE - 1 else plane_at(u_src, above * HIGH[0])
-                    results.append(relax(c_src, TE, slots, p, x_m, x_p, s_c[slot * TE + p]))
-                for p in range(first, first + BATCH):
-                    put_plane(c_dst, slot * TE + p, results[p - first])
-            cell, slots = around(1, slot)
-            centre = cell_at[0, cell]
-            results = []
-            for p in range(k + 1, LOW[0]):
-                x_m = plane_at(l_src, slot * LOW[0] + p - 1)
-                x_p = plane_at(l_src, slot * LOW[0] + p + 1) if p < LOW[0] - 1 else plane_at(c_src, centre * TE)
-                s = s_l[slot * LOW[1] + p - (LOW[0] - LOW[1])]
-                results.append(relax(l_src, LOW[0], slots, p, x_m, x_p, s))
-            for p in range(k + 1, LOW[0]):
-                put_plane(l_dst, slot * LOW[0] + p, results[p - k - 1])
-            cell, slots = around(2, slot)
-            centre = cell_at[0, cell]
-            results = []
-            for p in range(HIGH[0] - 1 - k):
-                x_m = plane_at(u_src, slot * HIGH[0] + p - 1) if p > 0 else plane_at(c_src, centre * TE + TE - 1)
-                x_p = plane_at(u_src, slot * HIGH[0] + p + 1)
-                results.append(relax(u_src, HIGH[0], slots, p, x_m, x_p, s_u[slot * HIGH[1] + p]))
-            for p in range(HIGH[0] - 1 - k):
-                put_plane(u_dst, slot * HIGH[0] + p, results[p])
+            _, slots = around(0, slot)
+
+            def group(at, carry):
+                first = at * BATCH
+                relax(c_src, c_dst, C_SIZE, slots, first + 1, BATCH, s_c, slot * TE + first)
+                return carry
+
+            lax.fori_loop(0, TE // BATCH, group, 0)
+            _, slots = around(1, slot)
+            count = LOW[0] - 1 - k
+            relax(l_src, l_dst, L_SIZE, slots, LOW[0] - count, count, s_l, (slot + 1) * LOW[1] - count)
+            _, slots = around(2, slot)
+            relax(u_src, u_dst, U_SIZE, slots, 1, HIGH[0] - 1 - k, s_u, slot * HIGH[1])
             return carry
 
         lax.fori_loop(0, tiles, sweep_tile, 0)
@@ -295,7 +291,7 @@
     field, f_l, f_u = bufs[SWEEPS % 2]
     for t in range(TILES):
         for p in range(TE):
-            pot[pl.ds(p * ROW + t, SUB, stride=TILES), :] = plane_at(field, t * TE + p)
+            pot[pl.ds(p * ROW + t, SUB, stride=TILES), :] = plane_at(field, t * C_SIZE + 1 + p)
 
     def clear(at, carry):
         slope[pl.ds(pl.multiple_of(at * SUB, SUB), SUB), :] = zero
@@ -307,7 +303,7 @@
         slot, _, y_p, z, turn, meets = slots
         at = slot * size + p
         own = plane_at(ref, at)
-        d_x = x_p - own
+        d_x = (plane_at(ref, at + 1) if x_p is None else x_p) - own
         d_y = y_plus(ref, own, at, y_p * size + p) - own
         ghost = jnp.where(meets, pltpu.roll(plane_at(ref, z * size + p), turn, 1), 0.0)
         d_z = jnp.where(last_z, ghost, roll(own, -1, 1)) - own
@@ -324,20 +320,23 @@
             @pl.when(inside)
             def _():
                 if which == 0:
-                    above = cell_at[2, cell]
-                    for p in range(TE):
-                        x_p = plane_at(field, slot * TE + p + 1) if p < TE - 1 else plane_at(f_u, above * HIGH[0])
-                        put(local, HALO + p, squares(field, TE, slots, p, x_p))
+                    put_plane(field, slot * C_SIZE + TE + 1, plane_at(f_u, cell_at[2, cell] * U_SIZE + 1))
+
+                    def group(at, carry):
+                        first = at * BATCH
+                        values = [squares(field, C_SIZE, slots, 1 + first + p, None) for p in range(BATCH)]
+                        for p in range(BATCH):
+                            put(local, HALO + first + p, values[p])
+                        return carry
+
+                    lax.fori_loop(0, TE // BATCH, group, 0)
                 elif which == 1:
-                    centre = cell_at[0, cell]
-                    for p in range(2):
-                        q = LOW[0] - 2 + p
-                        x_p = plane_at(f_l, slot * LOW[0] + q + 1) if p < 1 else plane_at(field, centre * TE)
-                        put(local, HALO - 2 + p, squares(f_l, LOW[0], slots, q, x_p))
+                    centre = plane_at(field, cell_at[0, cell] * C_SIZE + 1)
+                    put(local, HALO - 2, squares(f_l, L_SIZE, slots, LOW[0] - 2, None))
+                    put(local, HALO - 1, squares(f_l, L_SIZE, slots, LOW[0] - 1, centre))
                 else:
                     for p in range(2):
-                        x_p = plane_at(f_u, slot * HIGH[0] + p + 1)
-                        put(local, HALO + TE + p, squares(f_u, HIGH[0], slots, p, x_p))
+                        put(local, HALO + TE + p, squares(f_u, U_SIZE, slots, 1 + p, None))
 
         return carry
 
@@ -360,7 +359,7 @@
     halos = refs[width_gy : 2 * width_gy]
     slope, t_in, k0_in, b_in, ylow, yhigh, temp_out = refs[2 * width_gy : 2 * width_gy + 7]
     sends = refs[2 * width_gy + 7 : 3 * width_gy + 7]
-    heat, q_ext, temp_a, temp_b, cond_a, cond_b, k0_edge, b_edge, blocks = refs[3 * width_gy + 7 :]
+    heat, q_ext, temp_a, temp_b, cond_a, cond_b, k0_all, b_all, blocks = refs[3 * width_gy + 7 :]
     i = lax.axis_index("gx")
     j = lax.axis_index("gy")
     rows_gx = lax.axis_size("gx")
@@ -388,10 +387,14 @@
 
                 @pl.when(inside)
                 def _():
-                    for p in range(count):
+                    def plane(p, carry):
                         rows = pl.ds(pl.multiple_of((local * SLABX + x + p) * SUB, SUB), SUB)
-                        sigma = source[pl.ds(start + p * ROW + t, SUB, stride=TILES), :]
+                        at = pl.multiple_of(start + p * ROW, SUB)
+                        sigma = source[pl.ds(at + t, SUB, stride=TILES), :]
                         heat[rows, :] = sigma * slope[rows, :]
+                        return carry
+
+                    lax.fori_loop(0, count, plane, 0, unroll=min(count, 8))
 
     quarter = [(lane >= q * TE) & (lane < (q + 1) * TE) for q in range(3)]
 
@@ -405,19 +408,26 @@
 
     def rows_of(block, g):
         first = ROW0 + block * SLABX + g * SUB
-        return slice(first, first + SUB)
+        if not isinstance(first, int):
+            first = pl.multiple_of(first, SUB)
+        return pl.ds(first, SUB)
 
     groups = SLABX // SUB
-    for first in range(-1, HALF // 4 + 1):
-        col, yq = first * 4 // TE + 1, first * 4 % TE // 4
+
+    def place_heat(at, carry):
+        first = at - 1
+        col, yq = lax.div(first * 4 + TE, TE), lax.rem(first * 4 + TE, TE) // 4
         for g in range(groups):
             cells = [
-                heat[pl.ds(((2 * col + c) * SLABX + g * SUB) * SUB + yq, SUB, stride=SUB), :] for c in range(4)
+                heat[pl.ds(pl.multiple_of(((2 * col + c) * SLABX + g * SUB) * SUB, SUB) + yq, SUB, stride=SUB), :]
+                for c in range(4)
             ]
             for r in range(4):
-                block = 4 * first + r + HALO
-                if 0 < block < YBLOCKS - 1:
-                    q_ext[rows_of(block, g)] = pick([turned(cells[c], c - r) for c in range(4)])
+                block = 4 * first + r + HALO + 1
+                q_ext[rows_of(block, g)] = pick([turned(cells[c], c - r) for c in range(4)])
+        return carry
+
+    lax.fori_loop(0, HALF // 4 + 2, place_heat, 0)
 
     sub = lax.broadcasted_iota(jnp.int32, (SUB, LANES), 0)
     half = lane < NZ
@@ -444,17 +454,13 @@
         down = [roll(v, 1, 0) for v in values]
         return [jnp.where(first_sub, down[max(g - 1, 0)], down[g]) for g in range(groups)]
 
-    edges = {}
-    for e in range(HALO):
-        edges[e] = (ylow, e)
-        edges[YBLOCKS - HALO + e] = (yhigh, e)
-    for block in range(YBLOCKS):
+    def begin(block, edge, at):
+        values = []
         for g in range(groups):
             rows = rows_of(block, g)
             temp, k0, beta = t_in[rows], k0_in[rows], b_in[rows]
-            if block in edges:
-                edge, e = edges[block]
-                value = edge[e * SLABX + g * SUB : e * SLABX + (g + 1) * SUB]
+            if edge is not None:
+                value = edge[at * SLABX + g * SUB : at * SLABX + (g + 1) * SUB]
                 swapped = roll(value, NZ, 1)
                 if edge is ylow:
                     temp = jnp.where(half, value, temp)
@@ -464,25 +470,33 @@
                     temp = jnp.where(half, temp, swapped)
                     k0 = jnp.where(half, k0, lookup(k0_table, value))
                     beta = jnp.where(half, beta, lookup(beta_table, value))
-                k0_edge[rows_of(list(edges).index(block), g)] = k0
-                b_edge[rows_of(list(edges).index(block), g)] = beta
-            temp_a[rows] = temp
-            cond_a[rows] = k0 * inverse(1.0 + beta * temp * temp)
+            values.append((rows, temp, k0, beta, k0 * inverse(1.0 + beta * temp * temp)))
+        for rows, temp, k0, beta, cond in values:
+            temp_a[rows], k0_all[rows], b_all[rows], cond_a[rows] = temp, k0, beta, cond
+
+    for e in range(HALO):
+        begin(e, ylow, e)
+        begin(YBLOCKS - HALO + e, yhigh, e)
+
+    def begin_inner(block, carry):
+        begin(block, None, 0)
+        return carry
+
+    lax.fori_loop(HALO, YBLOCKS - HALO, begin_inner, 0, unroll=2)
 
     for step in range(CSWEEPS):
         (t_src, c_src), (t_dst, c_dst) = ((temp_a, cond_a), (temp_b, cond_b))[:: 1 if step % 2 == 0 else -1]
-        ahead, flux_y = None, None
-        for block in range(step, YBLOCKS - 1 - step):
-            temp, cond = ahead or (load(t_src, block), load(c_src, block))
-            ahead = load(t_src, block + 1), load(c_src, block + 1)
-            before = flux_y
-            flux_y = [(cond[g] + ahead[1][g]) * (ahead[0][g] - temp[g]) for g in range(groups)]
-            if block == HALO - 1:
-                flux_y = [jnp.where(low_y, 0.0, f) for f in flux_y]
-            if block == HALO + HALF - 1:
-                flux_y = [jnp.where(high_y, 0.0, f) for f in flux_y]
-            if before is None:
-                continue
+
+        def y_fluxes(block, temp, cond, temp_n, cond_n):
+            closed = (low_y & (block == HALO - 1)) | (high_y & (block == HALO + HALF - 1))
+            return [
+                jnp.where(closed, 0.0, (cond[g] + cond_n[g]) * (temp_n[g] - temp[g])) for g in range(groups)
+            ]
+
+        def advance(block, carry):
+            temp, cond, before = carry
+            temp_n, cond_n = load(t_src, block + 1), load(c_src, block + 1)
+            flux_y = y_fluxes(block, temp, cond, temp_n, cond_n)
             temp_x, cond_x = next_x(temp), next_x(cond)
             flux_x = [(cond[g] + cond_x[g]) * (temp_x[g] - temp[g]) for g in range(groups)]
             flux_x[0] = jnp.where(low_x, 0.0, flux_x[0])
@@ -493,24 +507,24 @@
                 flux_z = (cond[g] + roll(cond[g], -1, 1)) * (roll(temp[g], -1, 1) - temp[g])
                 flux_z = jnp.where(no_z, 0.0, flux_z)
                 div = (flux_y[g] - before[g]) + (flux_x[g] - back_x[g]) + (flux_z - roll(flux_z, 1, 1))
-                rows = rows_of(block, g)
-                new = temp[g] + DT * (0.5 * div + q_ext[rows])
+                new = temp[g] + DT * (0.5 * div + q_ext[rows_of(block + 1, g)])
                 if step < CSWEEPS - 1:
-                    if block in edges:
-                        at = list(edges).index(block)
-                        k0, beta = k0_edge[rows_of(at, g)], b_edge[rows_of(at, g)]
-                    else:
-                        k0, beta = k0_in[rows], b_in[rows]
-                    results.append((new, k0 * inverse(1.0 + beta * new * new)))
+                    rows = rows_of(block, g)
+                    results.append((new, k0_all[rows] * inverse(1.0 + b_all[rows] * new * new)))
                 else:
                     results.append((new, None))
             for g in range(groups):
                 t_dst[rows_of(block, g)] = results[g][0]
                 if step < CSWEEPS - 1:
                     c_dst[rows_of(block, g)] = results[g][1]
+            return temp_n, cond_n, flux_y
+
+        first = (load(t_src, 0), load(c_src, 0))
+        second = (load(t_src, 1), load(c_src, 1))
+        lax.fori_loop(1, YBLOCKS - 1, advance, (*second, y_fluxes(0, *first, *second)), unroll=2)
     final = temp_b if CSWEEPS % 2 else temp_a
 
-    for yq in range(HALF // 4):
+    def give_out(yq, carry):
         for g in range(TE // SUB):
             x = slice(g * SUB, (g + 1) * SUB)
             turns = []
@@ -522,21 +536,33 @@
                 even, odd = turns[2 * pair], turns[2 * pair + 1]
                 lower = (2 * yq + pair) * LANES
                 upper = lower + temp_out.shape[1] // 2
-                temp_out[x, lower : lower + LANES] = jnp.where(half, even[0], odd[2])
-                temp_out[x, upper : upper + LANES] = jnp.where(half, even[2], odd[0])
+                temp_out[x, pl.ds(pl.multiple_of(lower, LANES), LANES)] = jnp.where(half, even[0], odd[2])
+                temp_out[x, pl.ds(pl.multiple_of(upper, LANES), LANES)] = jnp.where(half, even[2], odd[0])
             for c in range(4):
                 value = pick([turns[r][(r - c) % 4] for r in range(4)])
                 blocks[pl.ds((c * TE + g * SUB) * SUB + yq, SUB, stride=SUB), :] = value
+        return carry
+
+    lax.fori_loop(0, HALF // 4, give_out, 0)
+    places = []
     for shift in range(width_gy):
         dev = lax.rem(j + shift, width_gy)
         for t in range(TILES):
             tile = i * tiles + dev * TILES + t
             col = pos[tile, 1] - 2 * j
             cell = jnp.clip(col, 0, 1) * 2 + pos[tile, 2]
-            here = (col >= 0) & (col < 2)
-            for p in range(TE):
-                value = blocks[pl.ds(pl.multiple_of((cell * TE + p) * SUB, SUB), SUB), :]
-                sends[shift][pl.ds(p * ROW + t, SUB, stride=TILES), :] = jnp.where(here, value, 0.0)
+            places.append((sends[shift], t, cell, (col >= 0) & (col < 2)))
+
+    def pack(p, carry):
+        values = []
+        for target, t, cell, here in places:
+            value = blocks[pl.ds(pl.multiple_of((cell * TE + p) * SUB, SUB), SUB), :]
+            values.append(jnp.where(here, value, 0.0))
+        for (target, t, cell, here), value in zip(places, values):
+            target[pl.ds(pl.multiple_of(p * ROW, ROW) + t, SUB, stride=TILES), :] = value
+        return carry
+
+    lax.fori_loop(0, TE, pack, 0, unroll=2)
 
 
 def shifted(value, axis, by, wrap=False):
@@ -599,18 +625,16 @@
     def rows(count):
         return jax.ShapeDtypeStruct((count, LANES), f32)
 
-    body, sigma, up, down, up_t, down_t = pl.pallas_call(
+    body, sigma, up, down = pl.pallas_call(
         prep_kernel,
         out_shape=(
             rows(2 * TE * ROW),
             rows(TE * ROW),
-            rows(LOW_ROWS),
-            rows(HIGH_ROWS),
-            rows(edge_rows),
-            rows(edge_rows),
+            rows(LOW_ROWS + edge_rows),
+            rows(HIGH_ROWS + edge_rows),
         ),
         in_specs=[SMEM] + [HBM] * 5,
-        out_specs=(VMEM,) * 6,
+        out_specs=(VMEM,) * 4,
         scratch_shapes=[
             pltpu.VMEM((TE * ROW, LANES), f32),
             pltpu.VMEM((TE * ROW, LANES), jnp.int32),
@@ -623,7 +647,6 @@
     )(sigma_table, to_rows(phi_init), to_rows(source), to_rows(tile_mat), temp_init, slab_mat)
     bodies = everyone(body, chips)
     low, high = shifted(up, "gx", 1), shifted(down, "gx", -1)
-    low_t, high_t = shifted(up_t, "gx", 1), shifted(down_t, "gx", -1)
 
     halo = pl.pallas_call(
         relay_kernel,
@@ -645,7 +668,7 @@
         scratch_shapes=[native, native],
         compiler_params=PARAMS,
         name="slab_prep",
-    )(tile_pos, k0_table, beta_table, temp_init, slab_mat, low_t, high_t)
+    )(tile_pos, k0_table, beta_table, temp_init, slab_mat, low, high)
     *halos[1:], edge_low, edge_high = lax.optimization_barrier((*halos[1:], edge_low, edge_high))
     halos = halos + [from_mate(part) for part in halos]
     ylow, yhigh = shifted(edge_high, "gy", 1), shifted(edge_low, "gy", -1)
@@ -664,7 +687,7 @@
         scratch_shapes=[
             pltpu.SMEM((3, 2 * (2 * width_gy + 2)), jnp.int32),
             pltpu.SMEM((3, tiles), jnp.int32),
-            fields(TE), fields(TE), fields(LOW[0]), fields(LOW[0]), fields(HIGH[0]), fields(HIGH[0]),
+            fields(C_SIZE), fields(C_SIZE), fields(L_SIZE), fields(L_SIZE), fields(U_SIZE), fields(U_SIZE),
             planes(TE), planes(LOW[1]), planes(HIGH[1]),
         ],
         compiler_params=PARAMS,
@@ -677,8 +700,8 @@
         in_specs=[SMEM] * 3 + [VMEM] * (2 * width_gy + 6),
         out_specs=(VMEM,) * (1 + width_gy),
         scratch_shapes=[pltpu.VMEM((8 * SLABX * SUB, LANES), f32)]
-        + [pltpu.VMEM((SLAB_ROWS, LANES), f32)] * 5
-        + [pltpu.VMEM((ROW0 + 2 * HALO * SLABX, LANES), f32)] * 2
+        + [pltpu.VMEM((SLAB_ROWS + 3 * SLABX, LANES), f32)]
+        + [pltpu.VMEM((SLAB_ROWS, LANES), f32)] * 6
         + [pltpu.VMEM((4 * TE * SUB, LANES), f32)],
         compiler_params=PARAMS,
         name="slab_steps",

time: 116 us -> 93 us (0.80)
  Pallas kernels: 58.7 us -> 45.6 us
  starting transfers between devices: 25.8 us -> 17.7 us
  local copies, waits for them, and re-layouts: 1.68 us -> 0.13 us
    pallas_call x1, Pallas kernels: 40.7 us -> 15.6 us  [on_device(): pl.pallas_call(functools.partial(slab_steps_kernel, chips), out_shape=(ja...]
    pallas_call x1, Pallas kernels: 13.1 us -> 25.1 us  [on_device(): pl.pallas_call(functools.partial(sweep_kernel, chips), out_shape=(rows(TE...]
    ppermute x12 -> x10, starting transfers between devices: 25 us -> 16.1 us  [shifted(): return lax.ppermute(value, axis, pairs)]
    unnamed x19 -> x15, local copies, waits for them, and re-layouts: 1.68 us -> 0.13 us
    ppermute x12 -> x10, waiting for transfers between devices: 27.4 us -> 27.4 us  [shifted(): return lax.ppermute(value, axis, pairs)]
  transfers between devices with their start and end apart: 18 -> 16, of which waited for: 5 -> 5; matrix products, arithmetic and copies ran while one was open for 0% -> 0% of each run, Pallas kernels for 13% -> 29%
where the time goes in v4:
time: 93 us; the launch traced here: 92.5 us
  Pallas kernels  45.6 us (49%)
  waiting for transfers between devices  27.4 us (29%)
  starting transfers between devices  17.7 us (19%)
    ppermute x10, waiting for transfers between devices, shifted(): return lax.ppermute(value, axis, pairs)  27.4 us
    pallas_call x1, Pallas kernels, on_device(): pl.pallas_call(functools.partial(sweep_kernel, chips), out_shape=(rows(TE...  25.1 us
    ppermute x10, starting transfers between devices, shifted(): return lax.ppermute(value, axis, pairs)  16.1 us
    pallas_call x1, Pallas kernels, on_device(): pl.pallas_call(functools.partial(slab_steps_kernel, chips), out_shape=(ja...  15.6 us
    pallas_call x1, Pallas kernels, on_device(): pl.pallas_call(prep_kernel, out_shape=(rows(2 * TE * ROW), rows(TE * ROW)...  3.28 us
  transfers between devices with their start and end apart: 16, of which 5 were waited for; matrix products, arithmetic and copies ran while one was open for 0% of the time, Pallas kernels for 29%

profile of v4, /device:TPU:0, one launch (start us, length us, event | category | flops | bytes accessed | tf_op | source)
XLA Modules:
  0.0 92.5 jit_solution(8509302390384303922)
XLA Ops:
  0.7 3.3 %prep.1 = (f32[1024,128]{1,0:T(8,128)}, f32[512,128]{1,0:T(8,128)}, f32[464,128]{1,0:T(8,128)}, f32[496,128]{1,0:T(8,128)}) custom-call(f32[4]{0:T(128)} %table.1, f32[512,128]{1,0:T(8,128)} %bitcast.26, f32[512,128]{1,0:T(8,128)} %bitcast.27, s32[512,128]{1,0:T(8,128)} %bitcast.28, f32[32,4096]{1,0:T(8,128)} %temp.3, s32[32,4096]{1,0:T(8,128)} %mat.1), custom_call_target="tpu_custom_call" | custom-call | tf_op jit(solution)/shard_map/prep/pallas_call | solution.py:628
  4.0 0.0 copy-start.3
  4.0 0.0 copy-start.2
  4.0 3.0 %collective-permute-start = (f32[1024,128]{1,0:T(8,128)}, f32[1024,128]{1,0:T(8,128)}, u32[]{:S(2)}, u32[]{:S(2)}) collective-permute-start(f32[1024,128]{1,0:T(8,128)} %get-tuple-element.22.refs_0_), channel_id=1, source_target_pairs={{0,2},{1,3},{2,0},{3,1},{4,6},{5,7},{6,4},{7,5},{8,10},{9,11},{10,... | collective-permute-start | bytes 1572872 | tf_op jit(solution)/shard_map/ppermute | solution.py:571
  7.0 0.0 collective-permute-start.1
  7.0 1.3 %collective-permute-start.4 = (f32[496,128]{1,0:T(8,128)}, f32[496,128]{1,0:T(8,128)S(1)}, u32[]{:S(2)}, u32[]{:S(2)}) collective-permute-start(f32[496,128]{1,0:T(8,128)} %get-tuple-element.24), channel_id=1, source_target_pairs={{4,0},{8,4},{12,8},{16,12},{20,16},{24,20},{28,24},{5,1},{9,5},{13... | collective-permute-start | bytes 761864 | tf_op jit(solution)/shard_map/ppermute | solution.py:571
  8.3 4.6 %collective-permute-start.3 = (f32[464,128]{1,0:T(8,128)}, f32[464,128]{1,0:T(8,128)S(1)}, u32[]{:S(2)}, u32[]{:S(2)}) collective-permute-start(f32[464,128]{1,0:T(8,128)} %get-tuple-element.23), channel_id=1, source_target_pairs={{0,4},{4,8},{8,12},{12,16},{16,20},{20,24},{24,28},{1,5},{5,9},{9,... | collective-permute-start | bytes 712712 | tf_op jit(solution)/shard_map/ppermute | solution.py:571
  12.9 6.4 %collective-permute-done.refs_1_ = f32[1024,128]{1,0:T(8,128)} collective-permute-done((f32[1024,128]{1,0:T(8,128)}, f32[1024,128]{1,0:T(8,128)}, u32[]{:S(2)}, u32[]{:S(2)}) %collective-permute-start) | collective-permute-done | bytes 524320 | tf_op jit(solution)/shard_map/ppermute | solution.py:571
  19.2 0.0 collective-permute-start.2
  19.2 3.5 %collective-permute-done.3.low = f32[464,128]{1,0:T(8,128)S(1)} collective-permute-done((f32[464,128]{1,0:T(8,128)}, f32[464,128]{1,0:T(8,128)S(1)}, u32[]{:S(2)}, u32[]{:S(2)}) %collective-permute-start.3) | collective-permute-done | bytes 237600 | tf_op jit(solution)/shard_map/ppermute | solution.py:571
  22.8 0.6 collective-permute-start.5
  23.4 0.0 collective-permute-start.6
  23.4 0.1 copy.16.pos
  23.5 1.6 %slab_prep.1 = (f32[1536,128]{1,0:T(8,128)S(1)}, f32[1536,128]{1,0:T(8,128)S(1)}, f32[1536,128]{1,0:T(8,128)S(1)}, f32[120,128]{1,0:T(8,128)S(1)}, f32[120,128]{1,0:T(8,128)S(1)}) custom-call(s32[64,3]{1,0:T(8,128)S(1)} %copy.16.pos, f32[4]{0:T(128)S(1)} %copy-done.4, f32[4]{0:T(128)S(1)} %copy-done.5, f32[32,4096]{1,0:T(8,128)S(1)} %copy-done, ...), custom_call_target="tpu_custom_call" | custom-call | tf_op jit(solution)/shard_map/slab_prep/pallas_call | solution.py:663
  25.2 5.2 %collective-permute-done.5.refs_5_ = f32[448,128]{1,0:T(8,128)S(1)} collective-permute-done((f32[448,128]{1,0:T(8,128)S(1)}, f32[448,128]{1,0:T(8,128)S(1)}, u32[]{:S(2)}, u32[]{:S(2)}) %collective-permute-start.5) | collective-permute-done | bytes 229408 | tf_op jit(solution)/shard_map/ppermute | solution.py:571
  30.4 0.0 collective-permute-start.7
  30.4 0.5 collective-permute-start.8
  31.0 0.0 collective-permute-done.6.refs_6_
  31.0 0.2 collective-permute-start.9
  31.2 1.4 %collective-permute-start.10 = (f32[512,128]{1,0:T(8,128)S(1)}, f32[512,128]{1,0:T(8,128)S(1)}, u32[]{:S(2)}, u32[]{:S(2)}) collective-permute-start(f32[512,128]{1,0:T(8,128)S(1)} %copy-done.3), channel_id=1, source_target_pairs={{0,3},{1,2},{2,1},{3,0},{4,7},{5,6},{6,5},{7,4},{8,11},{9,10},{10,... | collective-permute-start | bytes 786440 | tf_op jit(solution)/shard_map/ppermute | solution.py:596
  32.6 0.0 collective-permute-done.7.refs_7_
  32.6 2.1 %collective-permute-start.11 = (f32[120,128]{1,0:T(8,128)S(1)}, f32[120,128]{1,0:T(8,128)S(1)}, u32[]{:S(2)}, u32[]{:S(2)}) collective-permute-start(f32[120,128]{1,0:T(8,128)S(1)} %get-tuple-element.34), channel_id=1, source_target_pairs={{0,1},{1,2},{2,3},{4,5},{5,6},{6,7},{8,9},{9,10},{10,11},{12,13},{... | collective-permute-start | bytes 184328 | tf_op jit(solution)/shard_map/ppermute | solution.py:571
  34.7 1.3 %collective-permute-start.12 = (f32[120,128]{1,0:T(8,128)S(1)}, f32[120,128]{1,0:T(8,128)S(1)}, u32[]{:S(2)}, u32[]{:S(2)}) collective-permute-start(f32[120,128]{1,0:T(8,128)S(1)} %get-tuple-element.35), channel_id=1, source_target_pairs={{1,0},{2,1},{3,2},{5,4},{6,5},{7,6},{9,8},{10,9},{11,10},{13,12},{... | collective-permute-start | bytes 184328 | tf_op jit(solution)/shard_map/ppermute | solution.py:571
  36.0 25.1 %sweeps.1 = (f32[512,128]{1,0:T(8,128)}, f32[2560,128]{1,0:T(8,128)S(1)}) custom-call(s32[64,3]{1,0:T(8,128)S(1)} %copy.16.pos, f32[1024,128]{1,0:T(8,128)S(1)} %copy-done.2, f32[1024,128]{1,0:T(8,128)} %collective-permute-done.refs_1_, f32[1024,128]{1,0:T(8,128)} %collective-permute-done.1.refs_2_, f32[1024,128]{1,0:T(8,128)} %collective-permute-done.2.refs_3_, ...), custom_call_target="tpu_custom_call" | custom-call | tf_op jit(solution)/shard_map/sweeps/pallas_call | solution.py:682
  61.1 0.0 collective-permute-done.8.refs_1_
  61.1 0.0 collective-permute-done.9.refs_2_
  61.1 0.0 collective-permute-done.10.refs_3_
  61.2 15.6 %slab_steps.1 = (f32[32,4096]{1,0:T(8,128)}, f32[512,128]{1,0:T(8,128)S(1)}, f32[512,128]{1,0:T(8,128)S(1)}, f32[512,128]{1,0:T(8,128)S(1)}, f32[512,128]{1,0:T(8,128)S(1)}) custom-call(s32[64,3]{1,0:T(8,128)S(1)} %copy.16.pos, f32[4]{0:T(128)S(1)} %copy-done.4, f32[4]{0:T(128)S(1)} %copy-done.5, f32[512,128]{1,0:T(8,128)S(1)} %copy-done.3, ...), custom_call_target="tpu_custom_call" | custom-call | tf_op jit(solution)/shard_map/slab_steps/pallas_call | solution.py:697
  76.7 2.7 %collective-permute-start.14 = (f32[512,128]{1,0:T(8,128)S(1)}, f32[512,128]{1,0:T(8,128)S(1)}, u32[]{:S(2)}, u32[]{:S(2)}) collective-permute-start(f32[512,128]{1,0:T(8,128)S(1)} %get-tuple-element.39), channel_id=1, source_target_pairs={{0,2},{1,3},{2,0},{3,1},{4,6},{5,7},{6,4},{7,5},{8,10},{9,11},{10,... | collective-permute-start | bytes 786440 | tf_op jit(solution)/shard_map/ppermute | solution.py:571
  79.5 3.2 %collective-permute-done.15 = f32[512,128]{1,0:T(8,128)S(1)} collective-permute-done((f32[512,128]{1,0:T(8,128)S(1)}, f32[512,128]{1,0:T(8,128)S(1)}, u32[]{:S(2)}, u32[]{:S(2)}) %collective-permute-start.15) | collective-permute-done | bytes 262176 | tf_op jit(solution)/shard_map/ppermute | solution.py:571
  82.7 9.0 %collective-permute-done.14 = f32[512,128]{1,0:T(8,128)S(1)} collective-permute-done((f32[512,128]{1,0:T(8,128)S(1)}, f32[512,128]{1,0:T(8,128)S(1)}, u32[]{:S(2)}, u32[]{:S(2)}) %collective-permute-start.14) | collective-permute-done | bytes 262176 | tf_op jit(solution)/shard_map/ppermute | solution.py:571
  91.7 0.8 add_add_fusion
  (21 shorter events, 0.1 us)
Async XLA Ops:
  0.6 22.9 %copy-start = (f32[32,4096]{1,0:T(8,128)S(1)}, f32[32,4096]{1,0:T(8,128)}, u32[]{:S(2)}) copy-start(f32[32,4096]{1,0:T(8,128)} %temp.3) | copy-start | bytes 1572868
  0.6 22.9 %copy-start.1 = (s32[32,4096]{1,0:T(8,128)S(1)}, s32[32,4096]{1,0:T(8,128)}, u32[]{:S(2)}) copy-start(s32[32,4096]{1,0:T(8,128)} %mat.1) | copy-start | bytes 1572868
  0.7 22.7 %copy-start.6 = (s32[64,3]{0,1:T(4,128)S(1)}, s32[64,3]{0,1:T(4,128)}, u32[]{:S(2)}) copy-start(s32[64,3]{0,1:T(4,128)} %param.13) | copy-start | bytes 2308
  0.7 22.8 %copy-start.4 = (f32[4]{0:T(128)S(1)}, f32[4]{0:T(128)}, u32[]{:S(2)}) copy-start(f32[4]{0:T(128)} %k0_table.3) | copy-start | bytes 52
  0.7 22.8 %copy-start.5 = (f32[4]{0:T(128)S(1)}, f32[4]{0:T(128)}, u32[]{:S(2)}) copy-start(f32[4]{0:T(128)} %beta_table.3) | copy-start | bytes 52
  4.0 26.4 %copy-start.3 = (f32[512,128]{1,0:T(8,128)S(1)}, f32[512,128]{1,0:T(8,128)}, u32[]{:S(2)}) copy-start(f32[512,128]{1,0:T(8,128)} %get-tuple-element.29.refs_0_) | copy-start | bytes 786436
  4.0 32.0 %copy-start.2 = (f32[1024,128]{1,0:T(8,128)S(1)}, f32[1024,128]{1,0:T(8,128)}, u32[]{:S(2)}) copy-start(f32[1024,128]{1,0:T(8,128)} %get-tuple-element.22.refs_0_) | copy-start | bytes 1572868
  4.0 15.2 %collective-permute-start = (f32[1024,128]{1,0:T(8,128)}, f32[1024,128]{1,0:T(8,128)}, u32[]{:S(2)}, u32[]{:S(2)}) collective-permute-start(f32[1024,128]{1,0:T(8,128)} %get-tuple-element.22.refs_0_), channel_id=1, source_target_pairs={{0,2},{1,3},{2,0},{3,1},{4,6},{5,7},{6,4},{7,5},{8,10},{9,11},{10,... | collective-permute-start | bytes 1572872 | tf_op jit(solution)/shard_map/ppermute | solution.py:571
  7.0 24.2 %collective-permute-start.1 = (f32[1024,128]{1,0:T(8,128)}, f32[1024,128]{1,0:T(8,128)}, u32[]{:S(2)}, u32[]{:S(2)}) collective-permute-start(f32[1024,128]{1,0:T(8,128)} %get-tuple-element.22.refs_0_), channel_id=1, source_target_pairs={{0,1},{1,0},{2,3},{3,2},{4,5},{5,4},{6,7},{7,6},{8,9},{9,8},{10,11... | collective-permute-start | bytes 1572872 | tf_op jit(solution)/shard_map/ppermute | solution.py:575
  7.0 15.8 %collective-permute-start.4 = (f32[496,128]{1,0:T(8,128)}, f32[496,128]{1,0:T(8,128)S(1)}, u32[]{:S(2)}, u32[]{:S(2)}) collective-permute-start(f32[496,128]{1,0:T(8,128)} %get-tuple-element.24), channel_id=1, source_target_pairs={{4,0},{8,4},{12,8},{16,12},{20,16},{24,20},{28,24},{5,1},{9,5},{13... | collective-permute-start | bytes 761864 | tf_op jit(solution)/shard_map/ppermute | solution.py:571
  8.3 14.5 %collective-permute-start.3 = (f32[464,128]{1,0:T(8,128)}, f32[464,128]{1,0:T(8,128)S(1)}, u32[]{:S(2)}, u32[]{:S(2)}) collective-permute-start(f32[464,128]{1,0:T(8,128)} %get-tuple-element.23), channel_id=1, source_target_pairs={{0,4},{4,8},{8,12},{12,16},{16,20},{20,24},{24,28},{1,5},{5,9},{9,... | collective-permute-start | bytes 712712 | tf_op jit(solution)/shard_map/ppermute | solution.py:571
  19.2 15.5 %collective-permute-start.2 = (f32[1024,128]{1,0:T(8,128)}, f32[1024,128]{1,0:T(8,128)}, u32[]{:S(2)}, u32[]{:S(2)}) collective-permute-start(f32[1024,128]{1,0:T(8,128)} %collective-permute-done.refs_1_), channel_id=1, source_target_pairs={{0,1},{1,0},{2,3},{3,2},{4,5},{5,4},{6,7},{7,6},{8,9},{9,8},{10,11... | collective-permute-start | bytes 1572872 | tf_op jit(solution)/shard_map/ppermute | solution.py:575
  22.8 7.6 %collective-permute-start.5 = (f32[448,128]{1,0:T(8,128)S(1)}, f32[448,128]{1,0:T(8,128)S(1)}, u32[]{:S(2)}, u32[]{:S(2)}) collective-permute-start(f32[448,128]{1,0:T(8,128)S(1)} %relay.1.refs_4_), channel_id=1, source_target_pairs={{0,2},{1,3},{2,0},{3,1},{4,6},{5,7},{6,4},{7,5},{8,10},{9,11},{10,... | collective-permute-start | bytes 688136 | tf_op jit(solution)/shard_map/ppermute | solution.py:571
  23.4 7.6 %collective-permute-start.6 = (f32[448,128]{1,0:T(8,128)S(1)}, f32[448,128]{1,0:T(8,128)S(1)}, u32[]{:S(2)}, u32[]{:S(2)}) collective-permute-start(f32[448,128]{1,0:T(8,128)S(1)} %relay.1.refs_4_), channel_id=1, source_target_pairs={{0,1},{1,0},{2,3},{3,2},{4,5},{5,4},{6,7},{7,6},{8,9},{9,8},{10,11... | collective-permute-start | bytes 688136 | tf_op jit(solution)/shard_map/ppermute | solution.py:575
  30.4 2.2 %collective-permute-start.7 = (f32[448,128]{1,0:T(8,128)S(1)}, f32[448,128]{1,0:T(8,128)S(1)}, u32[]{:S(2)}, u32[]{:S(2)}) collective-permute-start(f32[448,128]{1,0:T(8,128)S(1)} %collective-permute-done.5.refs_5_), channel_id=1, source_target_pairs={{0,1},{1,0},{2,3},{3,2},{4,5},{5,4},{6,7},{7,6},{8,9},{9,8},{10,11... | collective-permute-start | bytes 688136 | tf_op jit(solution)/shard_map/ppermute | solution.py:575
  30.4 30.7 %collective-permute-start.8 = (f32[512,128]{1,0:T(8,128)S(1)}, f32[512,128]{1,0:T(8,128)S(1)}, u32[]{:S(2)}, u32[]{:S(2)}) collective-permute-start(f32[512,128]{1,0:T(8,128)S(1)} %copy-done.3), channel_id=1, source_target_pairs={{0,2},{1,3},{2,0},{3,1},{4,6},{5,7},{6,4},{7,5},{8,10},{9,11},{10,... | collective-permute-start | bytes 786440 | tf_op jit(solution)/shard_map/ppermute | solution.py:571
  31.0 30.2 %collective-permute-start.9 = (f32[512,128]{1,0:T(8,128)S(1)}, f32[512,128]{1,0:T(8,128)S(1)}, u32[]{:S(2)}, u32[]{:S(2)}) collective-permute-start(f32[512,128]{1,0:T(8,128)S(1)} %copy-done.3), channel_id=1, source_target_pairs={{0,1},{1,0},{2,3},{3,2},{4,5},{5,4},{6,7},{7,6},{8,9},{9,8},{10,11... | collective-permute-start | bytes 786440 | tf_op jit(solution)/shard_map/ppermute | solution.py:596
  31.2 29.9 %collective-permute-start.10 = (f32[512,128]{1,0:T(8,128)S(1)}, f32[512,128]{1,0:T(8,128)S(1)}, u32[]{:S(2)}, u32[]{:S(2)}) collective-permute-start(f32[512,128]{1,0:T(8,128)S(1)} %copy-done.3), channel_id=1, source_target_pairs={{0,3},{1,2},{2,1},{3,0},{4,7},{5,6},{6,5},{7,4},{8,11},{9,10},{10,... | collective-permute-start | bytes 786440 | tf_op jit(solution)/shard_map/ppermute | solution.py:596
  32.6 28.6 %collective-permute-start.11 = (f32[120,128]{1,0:T(8,128)S(1)}, f32[120,128]{1,0:T(8,128)S(1)}, u32[]{:S(2)}, u32[]{:S(2)}) collective-permute-start(f32[120,128]{1,0:T(8,128)S(1)} %get-tuple-element.34), channel_id=1, source_target_pairs={{0,1},{1,2},{2,3},{4,5},{5,6},{6,7},{8,9},{9,10},{10,11},{12,13},{... | collective-permute-start | bytes 184328 | tf_op jit(solution)/shard_map/ppermute | solution.py:571
  34.7 26.4 %collective-permute-start.12 = (f32[120,128]{1,0:T(8,128)S(1)}, f32[120,128]{1,0:T(8,128)S(1)}, u32[]{:S(2)}, u32[]{:S(2)}) collective-permute-start(f32[120,128]{1,0:T(8,128)S(1)} %get-tuple-element.35), channel_id=1, source_target_pairs={{1,0},{2,1},{3,2},{5,4},{6,5},{7,6},{9,8},{10,9},{11,10},{13,12},{... | collective-permute-start | bytes 184328 | tf_op jit(solution)/shard_map/ppermute | solution.py:571
  76.7 5.9 %collective-permute-start.15 = (f32[512,128]{1,0:T(8,128)S(1)}, f32[512,128]{1,0:T(8,128)S(1)}, u32[]{:S(2)}, u32[]{:S(2)}) collective-permute-start(f32[512,128]{1,0:T(8,128)S(1)} %get-tuple-element.40), channel_id=1, source_target_pairs={{0,3},{1,0},{2,1},{3,2},{4,7},{5,4},{6,5},{7,6},{8,11},{9,8},{10,9... | collective-permute-start | bytes 786440 | tf_op jit(solution)/shard_map/ppermute | solution.py:571
  76.7 15.0 %collective-permute-start.14 = (f32[512,128]{1,0:T(8,128)S(1)}, f32[512,128]{1,0:T(8,128)S(1)}, u32[]{:S(2)}, u32[]{:S(2)}) collective-permute-start(f32[512,128]{1,0:T(8,128)S(1)} %get-tuple-element.39), channel_id=1, source_target_pairs={{0,2},{1,3},{2,0},{3,1},{4,6},{5,7},{6,4},{7,5},{8,10},{9,11},{10,... | collective-permute-start | bytes 786440 | tf_op jit(solution)/shard_map/ppermute | solution.py:571
  79.5 12.2 %collective-permute-start.13 = (f32[512,128]{1,0:T(8,128)S(1)}, f32[512,128]{1,0:T(8,128)S(1)}, u32[]{:S(2)}, u32[]{:S(2)}) collective-permute-start(f32[512,128]{1,0:T(8,128)S(1)} %get-tuple-element.38), channel_id=1, source_target_pairs={{0,1},{1,2},{2,3},{3,0},{4,5},{5,6},{6,7},{7,4},{8,9},{9,10},{10,1... | collective-permute-start | bytes 786440 | tf_op jit(solution)/shard_map/ppermute | solution.py:571

commit v5 on v4

--- a/solution.py
+++ b/solution.py
@@ -23,11 +23,11 @@
 HIGH = (SWEEPS + 3, SWEEPS + 2, 2)
 LOW_ROWS = sum(LOW) * ROW
 HIGH_ROWS = sum(HIGH) * ROW
+SIDE_ROWS = max(LOW_ROWS, HIGH_ROWS)
 SLABX = TE + SUB
 HALO = CSWEEPS
 HALF = TE
 YBLOCKS = HALF + 2 * HALO
-BATCH = 8
 C_SIZE, L_SIZE, U_SIZE = TE + 2, LOW[0] + 1, HIGH[0] + 1
 ROW0 = SUB
 SLAB_ROWS = ROW0 + YBLOCKS * SLABX + SUB
@@ -48,7 +48,7 @@
     return pltpu.roll(value, by % value.shape[axis], axis)
 
 
-def prep_kernel(table, phi, src, mat, temp, slab, body, sigma, up, down, src_v, mat_v, ends_t, ends_m, sems):
+def prep_kernel(table, phi, src, mat, temp, slab, body, sigma, inner, outer, src_v, mat_v, ends_t, ends_m, sems):
     rows = TE * ROW
     size_x, width = temp.shape
     moves = [(phi, body.at[0:rows]), (src, src_v), (mat, mat_v)]
@@ -62,6 +62,20 @@
         move.wait()
     sigma[...] = lookup(table, mat_v[...])
     body[rows : 2 * rows] = src_v[...] / sigma[...]
+    even = lax.rem(lax.axis_index("gx"), 2) == 0
+
+    @pl.when(even)
+    def _():
+        fill_sides(body, sigma, ends_t, ends_m, inner, outer)
+
+    @pl.when(jnp.logical_not(even))
+    def _():
+        fill_sides(body, sigma, ends_t, ends_m, outer, inner)
+
+
+def fill_sides(body, sigma, ends_t, ends_m, up, down):
+    rows = TE * ROW
+    width = ends_t.shape[2]
     at_up, at_down = 0, 0
     for ref, first in ((body, 0), (body, rows), (sigma, 0)):
         which = (first // rows) if ref is body else 2
@@ -77,35 +91,40 @@
         t_low, m_low = ends_t[0, :, lanes], ends_m[0, :, lanes].astype(jnp.float32)
         t_high, m_high = ends_t[1, :, lanes], ends_m[1, :, lanes].astype(jnp.float32)
         first = at * SUB
-        up[LOW_ROWS + first : LOW_ROWS + first + SUB] = jnp.where(sub < 4, roll(t_high, HALO, 0), roll(m_high, -1, 0))
-        down[HIGH_ROWS + first : HIGH_ROWS + first + SUB] = jnp.where(sub < 4, t_low, roll(m_low, 4, 0))
-
-
-def relay_kernel(low, high, halo):
-    halo[0:LOW_ROWS] = low[0:LOW_ROWS]
-    halo[LOW_ROWS:] = high[0:HIGH_ROWS]
+        up[SIDE_ROWS + first : SIDE_ROWS + first + SUB] = jnp.where(sub < 4, roll(t_high, HALO, 0), roll(m_high, -1, 0))
+        down[SIDE_ROWS + first : SIDE_ROWS + first + SUB] = jnp.where(sub < 4, t_low, roll(m_low, 4, 0))
+
+
+def relay_kernel(inner, outer, halo):
+    def join(low, high):
+        halo[0:LOW_ROWS] = low[0:LOW_ROWS]
+        halo[LOW_ROWS:] = high[0:HIGH_ROWS]
+
+    even = lax.rem(lax.axis_index("gx"), 2) == 0
+    pl.when(even)(lambda: join(outer, inner))
+    pl.when(jnp.logical_not(even))(lambda: join(inner, outer))
 
 
 def loose(pos):
     return jnp.minimum(pos[0, 0], 0)
 
 
-def slab_kernel(pos, k0_table, beta_table, temp, mat, low, high, t_ext, k0_ext, b_ext, edge_low, edge_high, native_t, native_m):
+def slab_kernel(pos, k0_table, beta_table, temp, mat, inner, outer, t_ext, k0_ext, b_ext, edge_low, edge_high, native_t, native_m):
     start = loose(pos)
+    even = lax.rem(lax.axis_index("gx"), 2) == 0
     blocks = temp.shape[1] // LANES
     half = lax.broadcasted_iota(jnp.int32, (SUB, LANES), 1) < NZ
     for which, (own, native) in enumerate(((temp, native_t), (mat, native_m))):
         for at in range(blocks):
             lanes = slice(at * LANES, (at + 1) * LANES)
             first = at * SLABX
-            side = LOW_ROWS + at * SUB
-            value = low[side : side + SUB, :]
+            side = slice(SIDE_ROWS + at * SUB, SIDE_ROWS + (at + 1) * SUB)
+            value = jnp.where(even, outer[side, :], inner[side, :])
             native[first : first + SUB, :] = roll(value, -4, 0) if which else value
             for g in range(TE // SUB):
                 value = own[g * SUB : (g + 1) * SUB, lanes].astype(jnp.float32)
                 native[pl.ds(start + first + HALO + g * SUB, SUB), :] = value
-            side = HIGH_ROWS + at * SUB
-            value = high[side : side + SUB, :]
+            value = jnp.where(even, inner[side, :], outer[side, :])
             native[pl.ds(start + first + HALO + TE, SUB), :] = roll(value, -4, 0) if which else value
     for at in range(blocks // 2):
         for g in range(SLABX // SUB):
@@ -256,29 +275,22 @@
 
         def relax(src, dst, size, slots, first, count, s_ref, s_at):
             slot, y_m, y_p, z, turn, meets = slots
-            results = []
+            at = slot * size + first
+            before, own = plane_at(src, at - 1), plane_at(src, at)
             for p in range(count):
-                at = slot * size + first + p
-                own = plane_at(src, at)
-                total = (plane_at(src, at - 1) + plane_at(src, at + 1)) + s_ref[s_at + p]
-                total = total + y_minus(src, own, at, y_m * size + first + p)
-                total = total + y_plus(src, own, at, y_p * size + first + p)
+                after = plane_at(src, at + p + 1)
+                total = (before + after) + s_ref[s_at + p]
+                total = total + y_minus(src, own, at + p, y_m * size + first + p)
+                total = total + y_plus(src, own, at + p, y_p * size + first + p)
                 total = total + jnp.where(last_z, 0.0, roll(own, -1, 1))
                 total = total + jnp.where(first_z, 0.0, roll(own, 1, 1))
                 ghost = pltpu.roll(plane_at(src, z * size + first + p), turn, 1)
-                results.append(keep * own + gain * (total + jnp.where(meets, ghost, 0.0)))
-            for p in range(count):
-                put_plane(dst, slot * size + first + p, results[p])
+                put_plane(dst, at + p, keep * own + gain * (total + jnp.where(meets, ghost, 0.0)))
+                before, own = own, after
 
         def sweep_tile(slot, carry):
             _, slots = around(0, slot)
-
-            def group(at, carry):
-                first = at * BATCH
-                relax(c_src, c_dst, C_SIZE, slots, first + 1, BATCH, s_c, slot * TE + first)
-                return carry
-
-            lax.fori_loop(0, TE // BATCH, group, 0)
+            relax(c_src, c_dst, C_SIZE, slots, 1, TE, s_c, slot * TE)
             _, slots = around(1, slot)
             count = LOW[0] - 1 - k
             relax(l_src, l_dst, L_SIZE, slots, LOW[0] - count, count, s_l, (slot + 1) * LOW[1] - count)
@@ -322,14 +334,8 @@
                 if which == 0:
                     put_plane(field, slot * C_SIZE + TE + 1, plane_at(f_u, cell_at[2, cell] * U_SIZE + 1))
 
-                    def group(at, carry):
-                        first = at * BATCH
-                        values = [squares(field, C_SIZE, slots, 1 + first + p, None) for p in range(BATCH)]
-                        for p in range(BATCH):
-                            put(local, HALO + first + p, values[p])
-                        return carry
-
-                    lax.fori_loop(0, TE // BATCH, group, 0)
+                    for p in range(TE):
+                        put(local, HALO + p, squares(field, C_SIZE, slots, 1 + p, None))
                 elif which == 1:
                     centre = plane_at(field, cell_at[0, cell] * C_SIZE + 1)
                     put(local, HALO - 2, squares(f_l, L_SIZE, slots, LOW[0] - 2, None))
@@ -394,7 +400,7 @@
                         heat[rows, :] = sigma * slope[rows, :]
                         return carry
 
-                    lax.fori_loop(0, count, plane, 0, unroll=min(count, 8))
+                    lax.fori_loop(0, count, plane, 0, unroll=count)
 
     quarter = [(lane >= q * TE) & (lane < (q + 1) * TE) for q in range(3)]
 
@@ -427,7 +433,7 @@
                 q_ext[rows_of(block, g)] = pick([turned(cells[c], c - r) for c in range(4)])
         return carry
 
-    lax.fori_loop(0, HALF // 4 + 2, place_heat, 0)
+    lax.fori_loop(0, HALF // 4 + 2, place_heat, 0, unroll=2)
 
     sub = lax.broadcasted_iota(jnp.int32, (SUB, LANES), 0)
     half = lane < NZ
@@ -482,7 +488,7 @@
         begin(block, None, 0)
         return carry
 
-    lax.fori_loop(HALO, YBLOCKS - HALO, begin_inner, 0, unroll=2)
+    lax.fori_loop(HALO, YBLOCKS - HALO, begin_inner, 0, unroll=4)
 
     for step in range(CSWEEPS):
         (t_src, c_src), (t_dst, c_dst) = ((temp_a, cond_a), (temp_b, cond_b))[:: 1 if step % 2 == 0 else -1]
@@ -521,7 +527,7 @@
 
         first = (load(t_src, 0), load(c_src, 0))
         second = (load(t_src, 1), load(c_src, 1))
-        lax.fori_loop(1, YBLOCKS - 1, advance, (*second, y_fluxes(0, *first, *second)), unroll=2)
+        lax.fori_loop(1, YBLOCKS - 1, advance, (*second, y_fluxes(0, *first, *second)), unroll=6)
     final = temp_b if CSWEEPS % 2 else temp_a
 
     def give_out(yq, carry):
@@ -543,7 +549,7 @@
                 blocks[pl.ds((c * TE + g * SUB) * SUB + yq, SUB, stride=SUB), :] = value
         return carry
 
-    lax.fori_loop(0, HALF // 4, give_out, 0)
+    lax.fori_loop(0, HALF // 4, give_out, 0, unroll=2)
     places = []
     for shift in range(width_gy):
         dev = lax.rem(j + shift, width_gy)
@@ -562,13 +568,19 @@
             target[pl.ds(pl.multiple_of(p * ROW, ROW) + t, SUB, stride=TILES), :] = value
         return carry
 
-    lax.fori_loop(0, TE, pack, 0, unroll=2)
+    lax.fori_loop(0, TE, pack, 0, unroll=4)
 
 
 def shifted(value, axis, by, wrap=False):
     count = lax.axis_size(axis)
     pairs = [(d, (d + by) % count) for d in range(count) if wrap or 0 <= d + by < count]
     return lax.ppermute(value, axis, pairs)
+
+
+def with_partner(value, axis, first):
+    count = lax.axis_size(axis)
+    pairs = [(d, d + 1) for d in range(first, count - 1, 2)]
+    return lax.ppermute(value, axis, pairs + [(high, low) for low, high in pairs])
 
 
 def from_mate(value):
@@ -625,13 +637,13 @@
     def rows(count):
         return jax.ShapeDtypeStruct((count, LANES), f32)
 
-    body, sigma, up, down = pl.pallas_call(
+    body, sigma, inner, outer = pl.pallas_call(
         prep_kernel,
         out_shape=(
             rows(2 * TE * ROW),
             rows(TE * ROW),
-            rows(LOW_ROWS + edge_rows),
-            rows(HIGH_ROWS + edge_rows),
+            rows(SIDE_ROWS + edge_rows),
+            rows(SIDE_ROWS + edge_rows),
         ),
         in_specs=[SMEM] + [HBM] * 5,
         out_specs=(VMEM,) * 4,
@@ -646,7 +658,7 @@
         name="prep",
     )(sigma_table, to_rows(phi_init), to_rows(source), to_rows(tile_mat), temp_init, slab_mat)
     bodies = everyone(body, chips)
-    low, high = shifted(up, "gx", 1), shifted(down, "gx", -1)
+    inner, outer = with_partner(inner, "gx", 0), with_partner(outer, "gx", 1)
 
     halo = pl.pallas_call(
         relay_kernel,
@@ -655,7 +667,7 @@
         out_specs=VMEM,
         compiler_params=PARAMS,
         name="relay",
-    )(low, high)
+    )(inner, outer)
     halos = [halo] + [shifted(halo, "gy", 2 * d, True) for d in range(1, chips)]
     sigmas = everyone_direct(sigma, chips)
 
@@ -668,7 +680,7 @@
         scratch_shapes=[native, native],
         compiler_params=PARAMS,
         name="slab_prep",
-    )(tile_pos, k0_table, beta_table, temp_init, slab_mat, low, high)
+    )(tile_pos, k0_table, beta_table, temp_init, slab_mat, inner, outer)
     *halos[1:], edge_low, edge_high = lax.optimization_barrier((*halos[1:], edge_low, edge_high))
     halos = halos + [from_mate(part) for part in halos]
     ylow, yhigh = shifted(edge_high, "gy", 1), shifted(edge_low, "gy", -1)

time: 93 us -> 74.4 us (0.80)
  Pallas kernels: 45.6 us -> 28.2 us
  starting transfers between devices: 17.7 us -> 16.1 us
    pallas_call x1, Pallas kernels: 25.1 us -> 14 us  [on_device(): pl.pallas_call(functools.partial(sweep_kernel, chips), out_shape=(rows(TE...]
    pallas_call x1, Pallas kernels: 15.6 us -> 9.18 us  [on_device(): pl.pallas_call(functools.partial(slab_steps_kernel, chips), out_shape=(ja...]
    ppermute x10 -> x8, starting transfers between devices: 16.1 us -> 13 us  [shifted(): return lax.ppermute(value, axis, pairs)]
    ppermute x0 -> x2, starting transfers between devices: none -> 2.19 us  [with_partner(): lax.ppermute(value, axis, pairs + [(high, low) for low, high in pairs])]
    ppermute x0 -> x2, waiting for transfers between devices: none -> 1.11 us  [with_partner(): lax.ppermute(value, axis, pairs + [(high, low) for low, high in pairs])]
    ppermute x10 -> x8, waiting for transfers between devices: 27.4 us -> 27 us  [shifted(): return lax.ppermute(value, axis, pairs)]
  transfers between devices with their start and end apart: 16 -> 16, of which waited for: 5 -> 5; matrix products, arithmetic and copies ran while one was open for 0% -> 0% of each run, Pallas kernels for 29% -> 21%
where the time goes in v5:
time: 74.4 us; the launch traced here: 74.2 us
  Pallas kernels  28.2 us (38%)
  waiting for transfers between devices  28.2 us (38%)
  starting transfers between devices  16.1 us (22%)
  between operations  0.81 us (1%)
  other arithmetic  0.78 us (1%)
    ppermute x8, waiting for transfers between devices, shifted(): return lax.ppermute(value, axis, pairs)  27 us
    pallas_call x1, Pallas kernels, on_device(): pl.pallas_call(functools.partial(sweep_kernel, chips), out_shape=(rows(TE...  14 us
    ppermute x8, starting transfers between devices, shifted(): return lax.ppermute(value, axis, pairs)  13 us
    pallas_call x1, Pallas kernels, on_device(): pl.pallas_call(functools.partial(slab_steps_kernel, chips), out_shape=(ja...  9.18 us
    pallas_call x1, Pallas kernels, on_device(): pl.pallas_call(prep_kernel, out_shape=(rows(2 * TE * ROW), rows(TE * ROW)...  3.35 us
    ppermute x2, starting transfers between devices, with_partner(): lax.ppermute(value, axis, pairs + [(high, low) for low, high in pairs])  2.19 us
    pallas_call x1, Pallas kernels, on_device(): pl.pallas_call(slab_kernel, out_shape=(rows(SLAB_ROWS),) * 3 + (rows(HALO...  1.61 us
  transfers between devices with their start and end apart: 16, of which 5 were waited for; matrix products, arithmetic and copies ran while one was open for 0% of the time, Pallas kernels for 21%

profile of v5, /device:TPU:0, one launch (start us, length us, event | category | flops | bytes accessed | tf_op | source)
XLA Modules:
  0.0 74.2 jit_solution(15436413076383287469)
XLA Ops:
  0.7 3.4 %prep.1 = (f32[1024,128]{1,0:T(8,128)}, f32[512,128]{1,0:T(8,128)}, f32[496,128]{1,0:T(8,128)}, f32[496,128]{1,0:T(8,128)}) custom-call(f32[4]{0:T(128)} %table.1, f32[512,128]{1,0:T(8,128)} %bitcast.26, f32[512,128]{1,0:T(8,128)} %bitcast.27, s32[512,128]{1,0:T(8,128)} %bitcast.28, f32[32,4096]{1,0:T(8,128)} %temp.3, s32[32,4096]{1,0:T(8,128)} %mat.1), custom_call_target="tpu_custom_call" | custom-call | tf_op jit(solution)/shard_map/prep/pallas_call | solution.py:640
  4.0 0.0 copy-start.3
  4.1 0.0 copy-start.2
  4.1 3.0 %collective-permute-start = (f32[1024,128]{1,0:T(8,128)}, f32[1024,128]{1,0:T(8,128)}, u32[]{:S(2)}, u32[]{:S(2)}) collective-permute-start(f32[1024,128]{1,0:T(8,128)} %get-tuple-element.22.refs_0_), channel_id=1, source_target_pairs={{0,2},{1,3},{2,0},{3,1},{4,6},{5,7},{6,4},{7,5},{8,10},{9,11},{10,... | collective-permute-start | bytes 1572872 | tf_op jit(solution)/shard_map/ppermute | solution.py:577
  7.1 0.0 collective-permute-start.1
  7.1 1.5 %collective-permute-start.3 = (f32[496,128]{1,0:T(8,128)}, f32[496,128]{1,0:T(8,128)S(1)}, u32[]{:S(2)}, u32[]{:S(2)}) collective-permute-start(f32[496,128]{1,0:T(8,128)} %get-tuple-element.23), channel_id=1, source_target_pairs={{0,4},{8,12},{16,20},{24,28},{4,0},{12,8},{20,16},{28,24},{1,5},{9... | collective-permute-start | bytes 761864 | tf_op jit(solution)/shard_map/ppermute | solution.py:583
  8.6 0.7 collective-permute-start.4
  9.3 10.0 %collective-permute-done.refs_1_ = f32[1024,128]{1,0:T(8,128)} collective-permute-done((f32[1024,128]{1,0:T(8,128)}, f32[1024,128]{1,0:T(8,128)}, u32[]{:S(2)}, u32[]{:S(2)}) %collective-permute-start) | collective-permute-done | bytes 524320 | tf_op jit(solution)/shard_map/ppermute | solution.py:577
  19.3 1.1 %collective-permute-done.3.inner = f32[496,128]{1,0:T(8,128)S(1)} collective-permute-done((f32[496,128]{1,0:T(8,128)}, f32[496,128]{1,0:T(8,128)S(1)}, u32[]{:S(2)}, u32[]{:S(2)}) %collective-permute-start.3) | collective-permute-done | bytes 253984 | tf_op jit(solution)/shard_map/ppermute | solution.py:583
  20.4 0.7 collective-permute-start.5
  21.2 0.2 collective-permute-start.6
  21.4 0.1 copy.16.pos
  21.5 1.6 %slab_prep.1 = (f32[1536,128]{1,0:T(8,128)S(1)}, f32[1536,128]{1,0:T(8,128)S(1)}, f32[1536,128]{1,0:T(8,128)S(1)}, f32[120,128]{1,0:T(8,128)S(1)}, f32[120,128]{1,0:T(8,128)S(1)}) custom-call(s32[64,3]{1,0:T(8,128)S(1)} %copy.16.pos, f32[4]{0:T(128)S(1)} %copy-done.4, f32[4]{0:T(128)S(1)} %copy-done.5, f32[32,4096]{1,0:T(8,128)S(1)} %copy-done, ...), custom_call_target="tpu_custom_call" | custom-call | tf_op jit(solution)/shard_map/slab_prep/pallas_call | solution.py:675
  23.1 4.6 %collective-permute-done.5.refs_5_ = f32[448,128]{1,0:T(8,128)S(1)} collective-permute-done((f32[448,128]{1,0:T(8,128)S(1)}, f32[448,128]{1,0:T(8,128)S(1)}, u32[]{:S(2)}, u32[]{:S(2)}) %collective-permute-start.5) | collective-permute-done | bytes 229408 | tf_op jit(solution)/shard_map/ppermute | solution.py:577
  27.8 1.4 %collective-permute-start.8 = (f32[512,128]{1,0:T(8,128)S(1)}, f32[512,128]{1,0:T(8,128)S(1)}, u32[]{:S(2)}, u32[]{:S(2)}) collective-permute-start(f32[512,128]{1,0:T(8,128)S(1)} %copy-done.3), channel_id=1, source_target_pairs={{0,2},{1,3},{2,0},{3,1},{4,6},{5,7},{6,4},{7,5},{8,10},{9,11},{10,... | collective-permute-start | bytes 786440 | tf_op jit(solution)/shard_map/ppermute | solution.py:577
  29.2 0.0 collective-permute-done.6.refs_6_
  29.2 0.2 collective-permute-start.9
  29.4 0.5 collective-permute-start.10
  29.9 2.1 %collective-permute-start.11 = (f32[120,128]{1,0:T(8,128)S(1)}, f32[120,128]{1,0:T(8,128)S(1)}, u32[]{:S(2)}, u32[]{:S(2)}) collective-permute-start(f32[120,128]{1,0:T(8,128)S(1)} %get-tuple-element.34), channel_id=1, source_target_pairs={{0,1},{1,2},{2,3},{4,5},{5,6},{6,7},{8,9},{9,10},{10,11},{12,13},{... | collective-permute-start | bytes 184328 | tf_op jit(solution)/shard_map/ppermute | solution.py:577
  32.0 0.0 collective-permute-done.2.refs_3_
  32.1 1.3 %collective-permute-start.12 = (f32[120,128]{1,0:T(8,128)S(1)}, f32[120,128]{1,0:T(8,128)S(1)}, u32[]{:S(2)}, u32[]{:S(2)}) collective-permute-start(f32[120,128]{1,0:T(8,128)S(1)} %get-tuple-element.35), channel_id=1, source_target_pairs={{1,0},{2,1},{3,2},{5,4},{6,5},{7,6},{9,8},{10,9},{11,10},{13,12},{... | collective-permute-start | bytes 184328 | tf_op jit(solution)/shard_map/ppermute | solution.py:577
  33.4 14.0 %sweeps.1 = (f32[512,128]{1,0:T(8,128)}, f32[2560,128]{1,0:T(8,128)S(1)}) custom-call(s32[64,3]{1,0:T(8,128)S(1)} %copy.16.pos, f32[1024,128]{1,0:T(8,128)S(1)} %copy-done.2, f32[1024,128]{1,0:T(8,128)} %collective-permute-done.refs_1_, f32[1024,128]{1,0:T(8,128)} %collective-permute-done.1.refs_2_, f32[1024,128]{1,0:T(8,128)} %collective-permute-done.2.refs_3_, ...), custom_call_target="tpu_custom_call" | custom-call | tf_op jit(solution)/shard_map/sweeps/pallas_call | solution.py:694
  47.4 0.0 collective-permute-done.8.refs_1_
  47.4 0.0 collective-permute-done.9.refs_2_
  47.4 0.0 collective-permute-done.10.refs_3_
  47.4 9.2 %slab_steps.1 = (f32[32,4096]{1,0:T(8,128)}, f32[512,128]{1,0:T(8,128)S(1)}, f32[512,128]{1,0:T(8,128)S(1)}, f32[512,128]{1,0:T(8,128)S(1)}, f32[512,128]{1,0:T(8,128)S(1)}) custom-call(s32[64,3]{1,0:T(8,128)S(1)} %copy.16.pos, f32[4]{0:T(128)S(1)} %copy-done.4, f32[4]{0:T(128)S(1)} %copy-done.5, f32[512,128]{1,0:T(8,128)S(1)} %copy-done.3, ...), custom_call_target="tpu_custom_call" | custom-call | tf_op jit(solution)/shard_map/slab_steps/pallas_call | solution.py:709
  56.6 2.0 %collective-permute-start.15 = (f32[512,128]{1,0:T(8,128)S(1)}, f32[512,128]{1,0:T(8,128)S(1)}, u32[]{:S(2)}, u32[]{:S(2)}) collective-permute-start(f32[512,128]{1,0:T(8,128)S(1)} %get-tuple-element.40), channel_id=1, source_target_pairs={{0,3},{1,0},{2,1},{3,2},{4,7},{5,4},{6,5},{7,6},{8,11},{9,8},{10,9... | collective-permute-start | bytes 786440 | tf_op jit(solution)/shard_map/ppermute | solution.py:577
  58.5 2.3 %collective-permute-start.14 = (f32[512,128]{1,0:T(8,128)S(1)}, f32[512,128]{1,0:T(8,128)S(1)}, u32[]{:S(2)}, u32[]{:S(2)}) collective-permute-start(f32[512,128]{1,0:T(8,128)S(1)} %get-tuple-element.39), channel_id=1, source_target_pairs={{0,2},{1,3},{2,0},{3,1},{4,6},{5,7},{6,4},{7,5},{8,10},{9,11},{10,... | collective-permute-start | bytes 786440 | tf_op jit(solution)/shard_map/ppermute | solution.py:577
  60.8 0.2 collective-permute-start.13
  61.0 2.3 %collective-permute-done.15 = f32[512,128]{1,0:T(8,128)S(1)} collective-permute-done((f32[512,128]{1,0:T(8,128)S(1)}, f32[512,128]{1,0:T(8,128)S(1)}, u32[]{:S(2)}, u32[]{:S(2)}) %collective-permute-start.15) | collective-permute-done | bytes 262176 | tf_op jit(solution)/shard_map/ppermute | solution.py:577
  63.4 10.0 %collective-permute-done.14 = f32[512,128]{1,0:T(8,128)S(1)} collective-permute-done((f32[512,128]{1,0:T(8,128)S(1)}, f32[512,128]{1,0:T(8,128)S(1)}, u32[]{:S(2)}, u32[]{:S(2)}) %collective-permute-start.14) | collective-permute-done | bytes 262176 | tf_op jit(solution)/shard_map/ppermute | solution.py:577
  73.4 0.8 %add_add_fusion = f32[512,128]{1,0:T(8,128)} fusion(f32[512,128]{1,0:T(8,128)S(1)} %collective-permute-done.15, f32[512,128]{1,0:T(8,128)S(1)} %collective-permute-done.14, f32[512,128]{1,0:T(8,128)S(1)} %get-tuple-element.37, f32[512,128]{1,0:T(8,128)S(1)} %collective-permute-done.13), kind=kLoop, calls=%fused_computation | loop fusion | flops 196608 | bytes 1310720 | tf_op jit(solution)/shard_map/add | solution.py:723
  (21 shorter events, 0.1 us)
Async XLA Ops:
  0.6 20.8 %copy-start = (f32[32,4096]{1,0:T(8,128)S(1)}, f32[32,4096]{1,0:T(8,128)}, u32[]{:S(2)}) copy-start(f32[32,4096]{1,0:T(8,128)} %temp.3) | copy-start | bytes 1572868
  0.6 20.8 %copy-start.1 = (s32[32,4096]{1,0:T(8,128)S(1)}, s32[32,4096]{1,0:T(8,128)}, u32[]{:S(2)}) copy-start(s32[32,4096]{1,0:T(8,128)} %mat.1) | copy-start | bytes 1572868
  0.7 20.7 %copy-start.6 = (s32[64,3]{0,1:T(4,128)S(1)}, s32[64,3]{0,1:T(4,128)}, u32[]{:S(2)}) copy-start(s32[64,3]{0,1:T(4,128)} %param.13) | copy-start | bytes 2308
  0.7 20.8 %copy-start.4 = (f32[4]{0:T(128)S(1)}, f32[4]{0:T(128)}, u32[]{:S(2)}) copy-start(f32[4]{0:T(128)} %k0_table.3) | copy-start | bytes 52
  0.7 20.8 %copy-start.5 = (f32[4]{0:T(128)S(1)}, f32[4]{0:T(128)}, u32[]{:S(2)}) copy-start(f32[4]{0:T(128)} %beta_table.3) | copy-start | bytes 52
  4.0 23.7 %copy-start.3 = (f32[512,128]{1,0:T(8,128)S(1)}, f32[512,128]{1,0:T(8,128)}, u32[]{:S(2)}) copy-start(f32[512,128]{1,0:T(8,128)} %get-tuple-element.29.refs_0_) | copy-start | bytes 786436
  4.1 29.3 %copy-start.2 = (f32[1024,128]{1,0:T(8,128)S(1)}, f32[1024,128]{1,0:T(8,128)}, u32[]{:S(2)}) copy-start(f32[1024,128]{1,0:T(8,128)} %get-tuple-element.22.refs_0_) | copy-start | bytes 1572868
  4.1 15.2 %collective-permute-start = (f32[1024,128]{1,0:T(8,128)}, f32[1024,128]{1,0:T(8,128)}, u32[]{:S(2)}, u32[]{:S(2)}) collective-permute-start(f32[1024,128]{1,0:T(8,128)} %get-tuple-element.22.refs_0_), channel_id=1, source_target_pairs={{0,2},{1,3},{2,0},{3,1},{4,6},{5,7},{6,4},{7,5},{8,10},{9,11},{10,... | collective-permute-start | bytes 1572872 | tf_op jit(solution)/shard_map/ppermute | solution.py:577
  7.1 22.3 %collective-permute-start.1 = (f32[1024,128]{1,0:T(8,128)}, f32[1024,128]{1,0:T(8,128)}, u32[]{:S(2)}, u32[]{:S(2)}) collective-permute-start(f32[1024,128]{1,0:T(8,128)} %get-tuple-element.22.refs_0_), channel_id=1, source_target_pairs={{0,1},{1,0},{2,3},{3,2},{4,5},{5,4},{6,7},{7,6},{8,9},{9,8},{10,11... | collective-permute-start | bytes 1572872 | tf_op jit(solution)/shard_map/ppermute | solution.py:587
  7.1 13.3 %collective-permute-start.3 = (f32[496,128]{1,0:T(8,128)}, f32[496,128]{1,0:T(8,128)S(1)}, u32[]{:S(2)}, u32[]{:S(2)}) collective-permute-start(f32[496,128]{1,0:T(8,128)} %get-tuple-element.23), channel_id=1, source_target_pairs={{0,4},{8,12},{16,20},{24,28},{4,0},{12,8},{20,16},{28,24},{1,5},{9... | collective-permute-start | bytes 761864 | tf_op jit(solution)/shard_map/ppermute | solution.py:583
  8.6 11.8 %collective-permute-start.4 = (f32[496,128]{1,0:T(8,128)}, f32[496,128]{1,0:T(8,128)S(1)}, u32[]{:S(2)}, u32[]{:S(2)}) collective-permute-start(f32[496,128]{1,0:T(8,128)} %get-tuple-element.24), channel_id=1, source_target_pairs={{4,8},{12,16},{20,24},{8,4},{16,12},{24,20},{5,9},{13,17},{21,25},... | collective-permute-start | bytes 761864 | tf_op jit(solution)/shard_map/ppermute | solution.py:583
  19.3 12.7 %collective-permute-start.2 = (f32[1024,128]{1,0:T(8,128)}, f32[1024,128]{1,0:T(8,128)}, u32[]{:S(2)}, u32[]{:S(2)}) collective-permute-start(f32[1024,128]{1,0:T(8,128)} %collective-permute-done.refs_1_), channel_id=1, source_target_pairs={{0,1},{1,0},{2,3},{3,2},{4,5},{5,4},{6,7},{7,6},{8,9},{9,8},{10,11... | collective-permute-start | bytes 1572872 | tf_op jit(solution)/shard_map/ppermute | solution.py:587
  20.4 7.3 %collective-permute-start.5 = (f32[448,128]{1,0:T(8,128)S(1)}, f32[448,128]{1,0:T(8,128)S(1)}, u32[]{:S(2)}, u32[]{:S(2)}) collective-permute-start(f32[448,128]{1,0:T(8,128)S(1)} %relay.1.refs_4_), channel_id=1, source_target_pairs={{0,2},{1,3},{2,0},{3,1},{4,6},{5,7},{6,4},{7,5},{8,10},{9,11},{10,... | collective-permute-start | bytes 688136 | tf_op jit(solution)/shard_map/ppermute | solution.py:577
  21.2 8.0 %collective-permute-start.6 = (f32[448,128]{1,0:T(8,128)S(1)}, f32[448,128]{1,0:T(8,128)S(1)}, u32[]{:S(2)}, u32[]{:S(2)}) collective-permute-start(f32[448,128]{1,0:T(8,128)S(1)} %relay.1.refs_4_), channel_id=1, source_target_pairs={{0,1},{1,0},{2,3},{3,2},{4,5},{5,4},{6,7},{7,6},{8,9},{9,8},{10,11... | collective-permute-start | bytes 688136 | tf_op jit(solution)/shard_map/ppermute | solution.py:587
  27.8 2.2 %collective-permute-start.7 = (f32[448,128]{1,0:T(8,128)S(1)}, f32[448,128]{1,0:T(8,128)S(1)}, u32[]{:S(2)}, u32[]{:S(2)}) collective-permute-start(f32[448,128]{1,0:T(8,128)S(1)} %collective-permute-done.5.refs_5_), channel_id=1, source_target_pairs={{0,1},{1,0},{2,3},{3,2},{4,5},{5,4},{6,7},{7,6},{8,9},{9,8},{10,11... | collective-permute-start | bytes 688136 | tf_op jit(solution)/shard_map/ppermute | solution.py:587
  27.8 19.6 %collective-permute-start.8 = (f32[512,128]{1,0:T(8,128)S(1)}, f32[512,128]{1,0:T(8,128)S(1)}, u32[]{:S(2)}, u32[]{:S(2)}) collective-permute-start(f32[512,128]{1,0:T(8,128)S(1)} %copy-done.3), channel_id=1, source_target_pairs={{0,2},{1,3},{2,0},{3,1},{4,6},{5,7},{6,4},{7,5},{8,10},{9,11},{10,... | collective-permute-start | bytes 786440 | tf_op jit(solution)/shard_map/ppermute | solution.py:577
  29.2 18.2 %collective-permute-start.9 = (f32[512,128]{1,0:T(8,128)S(1)}, f32[512,128]{1,0:T(8,128)S(1)}, u32[]{:S(2)}, u32[]{:S(2)}) collective-permute-start(f32[512,128]{1,0:T(8,128)S(1)} %copy-done.3), channel_id=1, source_target_pairs={{0,1},{1,0},{2,3},{3,2},{4,5},{5,4},{6,7},{7,6},{8,9},{9,8},{10,11... | collective-permute-start | bytes 786440 | tf_op jit(solution)/shard_map/ppermute | solution.py:608
  29.4 18.0 %collective-permute-start.10 = (f32[512,128]{1,0:T(8,128)S(1)}, f32[512,128]{1,0:T(8,128)S(1)}, u32[]{:S(2)}, u32[]{:S(2)}) collective-permute-start(f32[512,128]{1,0:T(8,128)S(1)} %copy-done.3), channel_id=1, source_target_pairs={{0,3},{1,2},{2,1},{3,0},{4,7},{5,6},{6,5},{7,4},{8,11},{9,10},{10,... | collective-permute-start | bytes 786440 | tf_op jit(solution)/shard_map/ppermute | solution.py:608
  29.9 17.5 %collective-permute-start.11 = (f32[120,128]{1,0:T(8,128)S(1)}, f32[120,128]{1,0:T(8,128)S(1)}, u32[]{:S(2)}, u32[]{:S(2)}) collective-permute-start(f32[120,128]{1,0:T(8,128)S(1)} %get-tuple-element.34), channel_id=1, source_target_pairs={{0,1},{1,2},{2,3},{4,5},{5,6},{6,7},{8,9},{9,10},{10,11},{12,13},{... | collective-permute-start | bytes 184328 | tf_op jit(solution)/shard_map/ppermute | solution.py:577
  32.1 15.3 %collective-permute-start.12 = (f32[120,128]{1,0:T(8,128)S(1)}, f32[120,128]{1,0:T(8,128)S(1)}, u32[]{:S(2)}, u32[]{:S(2)}) collective-permute-start(f32[120,128]{1,0:T(8,128)S(1)} %get-tuple-element.35), channel_id=1, source_target_pairs={{1,0},{2,1},{3,2},{5,4},{6,5},{7,6},{9,8},{10,9},{11,10},{13,12},{... | collective-permute-start | bytes 184328 | tf_op jit(solution)/shard_map/ppermute | solution.py:577
  56.6 6.8 %collective-permute-start.15 = (f32[512,128]{1,0:T(8,128)S(1)}, f32[512,128]{1,0:T(8,128)S(1)}, u32[]{:S(2)}, u32[]{:S(2)}) collective-permute-start(f32[512,128]{1,0:T(8,128)S(1)} %get-tuple-element.40), channel_id=1, source_target_pairs={{0,3},{1,0},{2,1},{3,2},{4,7},{5,4},{6,5},{7,6},{8,11},{9,8},{10,9... | collective-permute-start | bytes 786440 | tf_op jit(solution)/shard_map/ppermute | solution.py:577
  58.5 14.9 %collective-permute-start.14 = (f32[512,128]{1,0:T(8,128)S(1)}, f32[512,128]{1,0:T(8,128)S(1)}, u32[]{:S(2)}, u32[]{:S(2)}) collective-permute-start(f32[512,128]{1,0:T(8,128)S(1)} %get-tuple-element.39), channel_id=1, source_target_pairs={{0,2},{1,3},{2,0},{3,1},{4,6},{5,7},{6,4},{7,5},{8,10},{9,11},{10,... | collective-permute-start | bytes 786440 | tf_op jit(solution)/shard_map/ppermute | solution.py:577
  60.8 12.6 %collective-permute-start.13 = (f32[512,128]{1,0:T(8,128)S(1)}, f32[512,128]{1,0:T(8,128)S(1)}, u32[]{:S(2)}, u32[]{:S(2)}) collective-permute-start(f32[512,128]{1,0:T(8,128)S(1)} %get-tuple-element.38), channel_id=1, source_target_pairs={{0,1},{1,2},{2,3},{3,0},{4,5},{5,6},{6,7},{7,4},{8,9},{9,10},{10,1... | collective-permute-start | bytes 786440 | tf_op jit(solution)/shard_map/ppermute | solution.py:577

commit v6 on v5

--- a/solution.py
+++ b/solution.py
@@ -109,7 +109,7 @@
     return jnp.minimum(pos[0, 0], 0)
 
 
-def slab_kernel(pos, k0_table, beta_table, temp, mat, inner, outer, t_ext, k0_ext, b_ext, edge_low, edge_high, native_t, native_m):
+def slab_kernel(pos, k0_table, beta_table, temp, mat, inner, outer, t_ext, k0_ext, b_ext, edge_in, edge_out, native_t, native_m, edge_low, edge_high):
     start = loose(pos)
     even = lax.rem(lax.axis_index("gx"), 2) == 0
     blocks = temp.shape[1] // LANES
@@ -154,6 +154,9 @@
                 if y >= HALF - HALO:
                     first = (y - HALF + HALO) * SLABX + g * SUB
                     edge_high[first : first + SUB] = jnp.where(half, halves[0][2 + odd], halves[1][3 - odd])
+    even = lax.rem(lax.axis_index("gy"), 2) == 0
+    edge_in[...] = jnp.where(even, edge_high[...], edge_low[...])
+    edge_out[...] = jnp.where(even, edge_low[...], edge_high[...])
 
 
 def fill_maps(chips, pos, cell_at, cell_of):
@@ -199,24 +202,25 @@
 
     zero = jnp.zeros((SUB, LANES), jnp.float32)
 
-    def plane_at(ref, at, shift=0):
-        first = ROW0 + at * SUB
-        return ref[pl.ds(pl.multiple_of(first, SUB) if shift == 0 else first + shift, SUB), :]
-
-    def put_plane(ref, at, value):
-        ref[pl.ds(pl.multiple_of(ROW0 + at * SUB, SUB), SUB), :] = value
+    def row_of(at):
+        return ROW0 + at * SUB
+
+    def plane_at(ref, row):
+        return ref[pl.ds(pl.multiple_of(row, SUB), SUB), :]
+
+    def loose_at(ref, row):
+        return ref[pl.ds(row, SUB), :]
+
+    def put_plane(ref, row, value):
+        ref[pl.ds(pl.multiple_of(row, SUB), SUB), :] = value
 
     def unpack(source, start, t, target, first, count):
         def plane(p, carry):
-            at = pl.multiple_of(p * ROW, ROW)
-            value = source[pl.ds(start + at + t, SUB, stride=TILES), :]
-            if len(target.shape) == 3:
-                target[first + p] = value
-            else:
-                put_plane(target, first + p, value)
+            value = source[pl.ds(pl.multiple_of(p * ROW, ROW) + (start + t), SUB, stride=TILES), :]
+            put_plane(target, p * SUB + row_of(first), value)
             return carry
 
-        lax.fori_loop(0, count, plane, 0, unroll=min(count, 8))
+        lax.fori_loop(0, count, plane, 0, unroll=min(count, 16))
 
     for part in range(width_gy):
         for t in range(TILES):
@@ -229,7 +233,7 @@
             unpack(halos[part], LOW_ROWS + HIGH[0] * ROW, t, s_u, slot * HIGH[1], HIGH[1])
     for ref, count in ((pa, C_SIZE), (pb, C_SIZE), (la, L_SIZE), (lb, L_SIZE), (ua, U_SIZE), (ub, U_SIZE)):
         for p in range(count):
-            put_plane(ref, none * count + p, zero)
+            put_plane(ref, row_of(none * count + p), zero)
 
     lane = lax.broadcasted_iota(jnp.int32, (SUB, LANES), 1)
     sub = lax.broadcasted_iota(jnp.int32, (SUB, LANES), 0)
@@ -238,12 +242,12 @@
     first_sub, last_sub = sub == 0, sub == SUB - 1
     first_z, last_z = depth == 0, depth == TE - 1
 
-    def y_plus(ref, own, at, ghost_at):
-        turned = jnp.where(last_sub, plane_at(ref, ghost_at, 1 - SUB), plane_at(ref, at, 1))
+    def y_plus(ref, own, row, ghost_row):
+        turned = jnp.where(last_sub, loose_at(ref, ghost_row), loose_at(ref, row))
         return roll(jnp.where(first_y, turned, own), -TE, 1)
 
-    def y_minus(ref, own, at, ghost_at):
-        turned = jnp.where(first_sub, plane_at(ref, ghost_at, SUB - 1), plane_at(ref, at, -1))
+    def y_minus(ref, own, row, ghost_row):
+        turned = jnp.where(first_sub, loose_at(ref, ghost_row), loose_at(ref, row))
         return roll(jnp.where(last_y, turned, own), TE, 1)
 
     def around(which, slot):
@@ -265,27 +269,32 @@
         def ghosts(slot, carry):
             cell = cell_of[0, slot]
             below, above = cell_at[1, cell], cell_at[2, cell]
-            put_plane(c_src, slot * C_SIZE, plane_at(l_src, below * L_SIZE + LOW[0] - 1))
-            put_plane(c_src, slot * C_SIZE + TE + 1, plane_at(u_src, above * U_SIZE + 1))
-            put_plane(l_src, slot * L_SIZE + LOW[0], plane_at(c_src, cell_at[0, cell_of[1, slot]] * C_SIZE + 1))
-            put_plane(u_src, slot * U_SIZE, plane_at(c_src, cell_at[0, cell_of[2, slot]] * C_SIZE + TE))
+            own = slot * C_SIZE
+            over, under = cell_at[0, cell_of[1, slot]], cell_at[0, cell_of[2, slot]]
+            put_plane(c_src, row_of(own), plane_at(l_src, row_of(below * L_SIZE + LOW[0] - 1)))
+            put_plane(c_src, row_of(own + TE + 1), plane_at(u_src, row_of(above * U_SIZE + 1)))
+            put_plane(l_src, row_of(slot * L_SIZE + LOW[0]), plane_at(c_src, row_of(over * C_SIZE + 1)))
+            put_plane(u_src, row_of(slot * U_SIZE), plane_at(c_src, row_of(under * C_SIZE + TE)))
             return carry
 
         lax.fori_loop(0, tiles, ghosts, 0)
 
         def relax(src, dst, size, slots, first, count, s_ref, s_at):
             slot, y_m, y_p, z, turn, meets = slots
-            at = slot * size + first
-            before, own = plane_at(src, at - 1), plane_at(src, at)
-            for p in range(count):
-                after = plane_at(src, at + p + 1)
-                total = (before + after) + s_ref[s_at + p]
-                total = total + y_minus(src, own, at + p, y_m * size + first + p)
-                total = total + y_plus(src, own, at + p, y_p * size + first + p)
+            row, s_row = row_of(slot * size + first), row_of(s_at)
+            up, down = row + 1, row - 1
+            row_m, row_p = row_of(y_m * size + first) + (SUB - 1), row_of(y_p * size + first) - (SUB - 1)
+            row_z = row_of(z * size + first)
+            before, own = plane_at(src, row - SUB), plane_at(src, row)
+            for step in range(0, count * SUB, SUB):
+                after = plane_at(src, row + (step + SUB))
+                total = (before + after) + plane_at(s_ref, s_row + step)
+                total = total + y_minus(src, own, down + step, row_m + step)
+                total = total + y_plus(src, own, up + step, row_p + step)
                 total = total + jnp.where(last_z, 0.0, roll(own, -1, 1))
                 total = total + jnp.where(first_z, 0.0, roll(own, 1, 1))
-                ghost = pltpu.roll(plane_at(src, z * size + first + p), turn, 1)
-                put_plane(dst, at + p, keep * own + gain * (total + jnp.where(meets, ghost, 0.0)))
+                ghost = pltpu.roll(plane_at(src, row_z + step), turn, 1)
+                put_plane(dst, row + step, keep * own + gain * (total + jnp.where(meets, ghost, 0.0)))
                 before, own = own, after
 
         def sweep_tile(slot, carry):
@@ -303,7 +312,7 @@
     field, f_l, f_u = bufs[SWEEPS % 2]
     for t in range(TILES):
         for p in range(TE):
-            pot[pl.ds(p * ROW + t, SUB, stride=TILES), :] = plane_at(field, t * C_SIZE + 1 + p)
+            pot[pl.ds(p * ROW + t, SUB, stride=TILES), :] = plane_at(field, row_of(t * C_SIZE + 1 + p))
 
     def clear(at, carry):
         slope[pl.ds(pl.multiple_of(at * SUB, SUB), SUB), :] = zero
@@ -311,18 +320,21 @@
 
     lax.fori_loop(0, slope.shape[0] // SUB, clear, 0, unroll=8)
 
-    def squares(ref, size, slots, p, x_p):
+    def squares(ref, size, slots, local, x, first, count, x_last=None):
         slot, _, y_p, z, turn, meets = slots
-        at = slot * size + p
-        own = plane_at(ref, at)
-        d_x = (plane_at(ref, at + 1) if x_p is None else x_p) - own
-        d_y = y_plus(ref, own, at, y_p * size + p) - own
-        ghost = jnp.where(meets, pltpu.roll(plane_at(ref, z * size + p), turn, 1), 0.0)
-        d_z = jnp.where(last_z, ghost, roll(own, -1, 1)) - own
-        return d_x * d_x + d_y * d_y + d_z * d_z
-
-    def put(local, x, value):
-        slope[pl.ds(pl.multiple_of((local * SLABX + x) * SUB, SUB), SUB), :] = value
+        row = row_of(slot * size + first)
+        up, row_p, row_z = row + 1, row_of(y_p * size + first) - (SUB - 1), row_of(z * size + first)
+        target = (local * SLABX + x) * SUB
+        own = plane_at(ref, row)
+        for step in range(0, count * SUB, SUB):
+            last = step == (count - 1) * SUB and x_last is not None
+            after = x_last if last else plane_at(ref, row + (step + SUB))
+            d_x = after - own
+            d_y = y_plus(ref, own, up + step, row_p + step) - own
+            ghost = jnp.where(meets, pltpu.roll(plane_at(ref, row_z + step), turn, 1), 0.0)
+            d_z = jnp.where(last_z, ghost, roll(own, -1, 1)) - own
+            put_plane(slope, target + step, d_x * d_x + d_y * d_y + d_z * d_z)
+            own = after
 
     def slope_tile(slot, carry):
         for which in range(3):
@@ -332,17 +344,13 @@
             @pl.when(inside)
             def _():
                 if which == 0:
-                    put_plane(field, slot * C_SIZE + TE + 1, plane_at(f_u, cell_at[2, cell] * U_SIZE + 1))
-
-                    for p in range(TE):
-                        put(local, HALO + p, squares(field, C_SIZE, slots, 1 + p, None))
+                    above = plane_at(f_u, row_of(cell_at[2, cell] * U_SIZE + 1))
+                    squares(field, C_SIZE, slots, local, HALO, 1, TE, above)
                 elif which == 1:
-                    centre = plane_at(field, cell_at[0, cell] * C_SIZE + 1)
-                    put(local, HALO - 2, squares(f_l, L_SIZE, slots, LOW[0] - 2, None))
-                    put(local, HALO - 1, squares(f_l, L_SIZE, slots, LOW[0] - 1, centre))
+                    centre = plane_at(field, row_of(cell_at[0, cell] * C_SIZE + 1))
+                    squares(f_l, L_SIZE, slots, local, HALO - 2, LOW[0] - 2, 2, centre)
                 else:
-                    for p in range(2):
-                        put(local, HALO + TE + p, squares(f_u, U_SIZE, slots, 1 + p, None))
+                    squares(f_u, U_SIZE, slots, local, HALO + TE, 1, 2)
 
         return carry
 
@@ -363,7 +371,7 @@
     tiles = width_gy * TILES
     sigmas = refs[:width_gy]
     halos = refs[width_gy : 2 * width_gy]
-    slope, t_in, k0_in, b_in, ylow, yhigh, temp_out = refs[2 * width_gy : 2 * width_gy + 7]
+    slope, t_in, k0_in, b_in, y_in, y_out, temp_out = refs[2 * width_gy : 2 * width_gy + 7]
     sends = refs[2 * width_gy + 7 : 3 * width_gy + 7]
     heat, q_ext, temp_a, temp_b, cond_a, cond_b, k0_all, b_all, blocks = refs[3 * width_gy + 7 :]
     i = lax.axis_index("gx")
@@ -460,15 +468,18 @@
         down = [roll(v, 1, 0) for v in values]
         return [jnp.where(first_sub, down[max(g - 1, 0)], down[g]) for g in range(groups)]
 
-    def begin(block, edge, at):
+    even = lax.rem(j, 2) == 0
+
+    def begin(block, low, at):
         values = []
         for g in range(groups):
             rows = rows_of(block, g)
             temp, k0, beta = t_in[rows], k0_in[rows], b_in[rows]
-            if edge is not None:
-                value = edge[at * SLABX + g * SUB : at * SLABX + (g + 1) * SUB]
+            if low is not None:
+                place = slice(at * SLABX + g * SUB, at * SLABX + (g + 1) * SUB)
+                value = jnp.where(even, *((y_out[place], y_in[place])[:: 1 if low else -1]))
                 swapped = roll(value, NZ, 1)
-                if edge is ylow:
+                if low:
                     temp = jnp.where(half, value, temp)
                     k0 = jnp.where(half, lookup(k0_table, swapped), k0)
                     beta = jnp.where(half, lookup(beta_table, swapped), beta)
@@ -481,8 +492,8 @@
             temp_a[rows], k0_all[rows], b_all[rows], cond_a[rows] = temp, k0, beta, cond
 
     for e in range(HALO):
-        begin(e, ylow, e)
-        begin(YBLOCKS - HALO + e, yhigh, e)
+        begin(e, True, e)
+        begin(YBLOCKS - HALO + e, False, e)
 
     def begin_inner(block, carry):
         begin(block, None, 0)
@@ -672,21 +683,18 @@
     sigmas = everyone_direct(sigma, chips)
 
     native = pltpu.VMEM((width // LANES * SLABX + SUB, LANES), f32)
-    t_ext, k0_ext, b_ext, edge_low, edge_high = pl.pallas_call(
+    t_ext, k0_ext, b_ext, edge_in, edge_out = pl.pallas_call(
         slab_kernel,
         out_shape=(rows(SLAB_ROWS),) * 3 + (rows(HALO * SLABX),) * 2,
         in_specs=[SMEM] * 3 + [VMEM] * 4,
         out_specs=(VMEM,) * 5,
-        scratch_shapes=[native, native],
+        scratch_shapes=[native, native] + [pltpu.VMEM((HALO * SLABX, LANES), f32)] * 2,
         compiler_params=PARAMS,
         name="slab_prep",
     )(tile_pos, k0_table, beta_table, temp_init, slab_mat, inner, outer)
-    *halos[1:], edge_low, edge_high = lax.optimization_barrier((*halos[1:], edge_low, edge_high))
+    y_in, y_out = with_partner(edge_in, "gy", 0), with_partner(edge_out, "gy", 1)
+    *halos[1:], y_in, y_out = lax.optimization_barrier((*halos[1:], y_in, y_out))
     halos = halos + [from_mate(part) for part in halos]
-    ylow, yhigh = shifted(edge_high, "gy", 1), shifted(edge_low, "gy", -1)
-
-    def planes(count):
-        return pltpu.VMEM(((tiles + 1) * count, SUB, LANES), f32)
 
     def fields(count):
         return pltpu.VMEM((2 * ROW0 + (tiles + 1) * count * SUB, LANES), f32)
@@ -700,7 +708,7 @@
             pltpu.SMEM((3, 2 * (2 * width_gy + 2)), jnp.int32),
             pltpu.SMEM((3, tiles), jnp.int32),
             fields(C_SIZE), fields(C_SIZE), fields(L_SIZE), fields(L_SIZE), fields(U_SIZE), fields(U_SIZE),
-            planes(TE), planes(LOW[1]), planes(HIGH[1]),
+            fields(TE), fields(LOW[1]), fields(HIGH[1]),
         ],
         compiler_params=PARAMS,
         name="sweeps",
@@ -717,7 +725,7 @@
         + [pltpu.VMEM((4 * TE * SUB, LANES), f32)],
         compiler_params=PARAMS,
         name="slab_steps",
-    )(tile_pos, k0_table, beta_table, *sigmas, *halos, slope, t_ext, k0_ext, b_ext, ylow, yhigh)
+    )(tile_pos, k0_table, beta_table, *sigmas, *halos, slope, t_ext, k0_ext, b_ext, y_in, y_out)
     tile_temps = sends[0]
     for by in range(1, width_gy):
         tile_temps = tile_temps + shifted(sends[by], "gy", by, True)

time: 74.4 us -> 72.2 us (0.970)
  waiting for transfers between devices: 28.2 us -> 25.5 us
    ppermute x8 -> x6, waiting for transfers between devices: 27 us -> 22.3 us  [shifted(): return lax.ppermute(value, axis, pairs)]
    ppermute x4, waiting for transfers between devices: 0.01 us -> 1.12 us  [from_mate(): lax.ppermute(value, 'gy', [(d, d ^ 1) for d in range(lax.axis_size('gy'))])]
    ppermute x2 -> x4, starting transfers between devices: 2.19 us -> 3.21 us  [with_partner(): lax.ppermute(value, axis, pairs + [(high, low) for low, high in pairs])]
    ppermute x8 -> x6, starting transfers between devices: 13 us -> 12 us  [shifted(): return lax.ppermute(value, axis, pairs)]
    ppermute x2 -> x4, waiting for transfers between devices: 1.11 us -> 2.05 us  [with_partner(): lax.ppermute(value, axis, pairs + [(high, low) for low, high in pairs])]
  transfers between devices with their start and end apart: 16 -> 16, of which waited for: 5 -> 6; matrix products, arithmetic and copies ran while one was open for 0% -> 0% of each run, Pallas kernels for 21% -> 22%
where the time goes in v6:
time: 72.2 us; the launch traced here: 71.8 us
  Pallas kernels  28.4 us (39%)
  waiting for transfers between devices  25.5 us (35%)
  starting transfers between devices  16.3 us (23%)
  between operations  0.79 us (1%)
  other arithmetic  0.78 us (1%)
    ppermute x6, waiting for transfers between devices, shifted(): return lax.ppermute(value, axis, pairs)  22.3 us
    pallas_call x1, Pallas kernels, on_device(): pl.pallas_call(functools.partial(sweep_kernel, chips), out_shape=(rows(TE...  14.2 us
    ppermute x6, starting transfers between devices, shifted(): return lax.ppermute(value, axis, pairs)  12 us
    pallas_call x1, Pallas kernels, on_device(): pl.pallas_call(functools.partial(slab_steps_kernel, chips), out_shape=(ja...  9.24 us
    pallas_call x1, Pallas kernels, on_device(): pl.pallas_call(prep_kernel, out_shape=(rows(2 * TE * ROW), rows(TE * ROW)...  3.35 us
    ppermute x4, starting transfers between devices, with_partner(): lax.ppermute(value, axis, pairs + [(high, low) for low, high in pairs])  3.21 us
    ppermute x4, waiting for transfers between devices, with_partner(): lax.ppermute(value, axis, pairs + [(high, low) for low, high in pairs])  2.05 us
    pallas_call x1, Pallas kernels, on_device(): pl.pallas_call(slab_kernel, out_shape=(rows(SLAB_ROWS),) * 3 + (rows(HALO...  1.61 us
  transfers between devices with their start and end apart: 16, of which 6 were waited for; matrix products, arithmetic and copies ran while one was open for 0% of the time, Pallas kernels for 22%

profile of v6, /device:TPU:0, one launch (start us, length us, event | category | flops | bytes accessed | tf_op | source)
XLA Modules:
  0.0 71.8 jit_solution(10166359260600417430)
XLA Ops:
  0.7 3.4 %prep.1 = (f32[1024,128]{1,0:T(8,128)}, f32[512,128]{1,0:T(8,128)}, f32[496,128]{1,0:T(8,128)}, f32[496,128]{1,0:T(8,128)}) custom-call(f32[4]{0:T(128)} %table.1, f32[512,128]{1,0:T(8,128)} %bitcast.26, f32[512,128]{1,0:T(8,128)} %bitcast.27, s32[512,128]{1,0:T(8,128)} %bitcast.28, f32[32,4096]{1,0:T(8,128)} %temp.3, s32[32,4096]{1,0:T(8,128)} %mat.1), custom_call_target="tpu_custom_call" | custom-call | tf_op jit(solution)/shard_map/prep/pallas_call | solution.py:651
  4.0 0.0 copy-start.3
  4.1 0.0 copy-start.2
  4.1 3.0 %collective-permute-start = (f32[1024,128]{1,0:T(8,128)}, f32[1024,128]{1,0:T(8,128)}, u32[]{:S(2)}, u32[]{:S(2)}) collective-permute-start(f32[1024,128]{1,0:T(8,128)} %get-tuple-element.22.refs_0_), channel_id=1, source_target_pairs={{0,2},{1,3},{2,0},{3,1},{4,6},{5,7},{6,4},{7,5},{8,10},{9,11},{10,... | collective-permute-start | bytes 1572872 | tf_op jit(solution)/shard_map/ppermute | solution.py:588
  7.1 1.5 %collective-permute-start.3 = (f32[496,128]{1,0:T(8,128)}, f32[496,128]{1,0:T(8,128)S(1)}, u32[]{:S(2)}, u32[]{:S(2)}) collective-permute-start(f32[496,128]{1,0:T(8,128)} %get-tuple-element.23), channel_id=1, source_target_pairs={{0,4},{8,12},{16,20},{24,28},{4,0},{12,8},{20,16},{28,24},{1,5},{9... | collective-permute-start | bytes 761864 | tf_op jit(solution)/shard_map/ppermute | solution.py:594
  8.6 0.7 collective-permute-start.4
  9.3 10.0 %collective-permute-done.refs_1_ = f32[1024,128]{1,0:T(8,128)} collective-permute-done((f32[1024,128]{1,0:T(8,128)}, f32[1024,128]{1,0:T(8,128)}, u32[]{:S(2)}, u32[]{:S(2)}) %collective-permute-start) | collective-permute-done | bytes 524320 | tf_op jit(solution)/shard_map/ppermute | solution.py:588
  19.3 0.0 collective-permute-start.2
  19.3 1.1 %collective-permute-done.3.inner = f32[496,128]{1,0:T(8,128)S(1)} collective-permute-done((f32[496,128]{1,0:T(8,128)}, f32[496,128]{1,0:T(8,128)S(1)}, u32[]{:S(2)}, u32[]{:S(2)}) %collective-permute-start.3) | collective-permute-done | bytes 253984 | tf_op jit(solution)/shard_map/ppermute | solution.py:594
  20.4 0.0 collective-permute-done.4.outer
  20.4 0.7 %collective-permute-start.5 = (f32[448,128]{1,0:T(8,128)S(1)}, f32[448,128]{1,0:T(8,128)S(1)}, u32[]{:S(2)}, u32[]{:S(2)}) collective-permute-start(f32[448,128]{1,0:T(8,128)S(1)} %relay.1.refs_4_), channel_id=1, source_target_pairs={{0,2},{1,3},{2,0},{3,1},{4,6},{5,7},{6,4},{7,5},{8,10},{9,11},{10,... | collective-permute-start | bytes 688136 | tf_op jit(solution)/shard_map/ppermute | solution.py:588
  21.2 0.2 collective-permute-start.8
  21.4 0.1 copy.16.pos
  21.5 1.6 %slab_prep.1 = (f32[1536,128]{1,0:T(8,128)S(1)}, f32[1536,128]{1,0:T(8,128)S(1)}, f32[1536,128]{1,0:T(8,128)S(1)}, f32[120,128]{1,0:T(8,128)S(1)}, f32[120,128]{1,0:T(8,128)S(1)}) custom-call(s32[64,3]{1,0:T(8,128)S(1)} %copy.16.pos, f32[4]{0:T(128)S(1)} %copy-done.4, f32[4]{0:T(128)S(1)} %copy-done.5, f32[32,4096]{1,0:T(8,128)S(1)} %copy-done, ...), custom_call_target="tpu_custom_call" | custom-call | tf_op jit(solution)/shard_map/slab_prep/pallas_call | solution.py:686
  23.1 0.4 collective-permute-start.6
  23.5 0.9 %collective-permute-done.6.refs_12_ = f32[120,128]{1,0:T(8,128)S(1)} collective-permute-done((f32[120,128]{1,0:T(8,128)S(1)}, f32[120,128]{1,0:T(8,128)S(1)}, u32[]{:S(2)}, u32[]{:S(2)}) %collective-permute-start.6) | collective-permute-done | bytes 61472 | tf_op jit(solution)/shard_map/ppermute | solution.py:594
  24.4 0.7 collective-permute-start.7
  25.1 6.2 %collective-permute-start.10 = (f32[512,128]{1,0:T(8,128)S(1)}, f32[512,128]{1,0:T(8,128)S(1)}, u32[]{:S(2)}, u32[]{:S(2)}) collective-permute-start(f32[512,128]{1,0:T(8,128)S(1)} %copy-done.3), channel_id=1, source_target_pairs={{0,2},{1,3},{2,0},{3,1},{4,6},{5,7},{6,4},{7,5},{8,10},{9,11},{10,... | collective-permute-start | bytes 786440 | tf_op jit(solution)/shard_map/ppermute | solution.py:588
  31.3 0.0 collective-permute-done.5.refs_5_
  31.3 0.0 collective-permute-start.11
  31.3 0.0 collective-permute-done.8.refs_6_
  31.3 0.4 collective-permute-start.12
  31.7 0.0 collective-permute-done.1.refs_2_
  31.7 0.4 collective-permute-start.9
  32.2 1.1 %collective-permute-done.9.refs_7_ = f32[448,128]{1,0:T(8,128)S(1)} collective-permute-done((f32[448,128]{1,0:T(8,128)S(1)}, f32[448,128]{1,0:T(8,128)S(1)}, u32[]{:S(2)}, u32[]{:S(2)}) %collective-permute-start.9) | collective-permute-done | bytes 229408 | tf_op jit(solution)/shard_map/ppermute | solution.py:598
  33.3 14.2 %sweeps.1 = (f32[512,128]{1,0:T(8,128)}, f32[2560,128]{1,0:T(8,128)S(1)}) custom-call(s32[64,3]{1,0:T(8,128)S(1)} %copy.16.pos, f32[1024,128]{1,0:T(8,128)S(1)} %copy-done.2, f32[1024,128]{1,0:T(8,128)} %collective-permute-done.refs_1_, f32[1024,128]{1,0:T(8,128)} %collective-permute-done.1.refs_2_, f32[1024,128]{1,0:T(8,128)} %collective-permute-done.2.refs_3_, ...), custom_call_target="tpu_custom_call" | custom-call | tf_op jit(solution)/shard_map/sweeps/pallas_call | solution.py:702
  47.4 9.2 %slab_steps.1 = (f32[32,4096]{1,0:T(8,128)}, f32[512,128]{1,0:T(8,128)S(1)}, f32[512,128]{1,0:T(8,128)S(1)}, f32[512,128]{1,0:T(8,128)S(1)}, f32[512,128]{1,0:T(8,128)S(1)}) custom-call(s32[64,3]{1,0:T(8,128)S(1)} %copy.16.pos, f32[4]{0:T(128)S(1)} %copy-done.4, f32[4]{0:T(128)S(1)} %copy-done.5, f32[512,128]{1,0:T(8,128)S(1)} %copy-done.3, ...), custom_call_target="tpu_custom_call" | custom-call | tf_op jit(solution)/shard_map/slab_steps/pallas_call | solution.py:717
  56.7 0.9 %collective-permute-start.15 = (f32[512,128]{1,0:T(8,128)S(1)}, f32[512,128]{1,0:T(8,128)S(1)}, u32[]{:S(2)}, u32[]{:S(2)}) collective-permute-start(f32[512,128]{1,0:T(8,128)S(1)} %get-tuple-element.40), channel_id=1, source_target_pairs={{0,3},{1,0},{2,1},{3,2},{4,7},{5,4},{6,5},{7,6},{8,11},{9,8},{10,9... | collective-permute-start | bytes 786440 | tf_op jit(solution)/shard_map/ppermute | solution.py:588
  57.6 1.2 %collective-permute-start.14 = (f32[512,128]{1,0:T(8,128)S(1)}, f32[512,128]{1,0:T(8,128)S(1)}, u32[]{:S(2)}, u32[]{:S(2)}) collective-permute-start(f32[512,128]{1,0:T(8,128)S(1)} %get-tuple-element.39), channel_id=1, source_target_pairs={{0,2},{1,3},{2,0},{3,1},{4,6},{5,7},{6,4},{7,5},{8,10},{9,11},{10,... | collective-permute-start | bytes 786440 | tf_op jit(solution)/shard_map/ppermute | solution.py:588
  58.8 5.2 %collective-permute-done.15 = f32[512,128]{1,0:T(8,128)S(1)} collective-permute-done((f32[512,128]{1,0:T(8,128)S(1)}, f32[512,128]{1,0:T(8,128)S(1)}, u32[]{:S(2)}, u32[]{:S(2)}) %collective-permute-start.15) | collective-permute-done | bytes 262176 | tf_op jit(solution)/shard_map/ppermute | solution.py:588
  64.0 7.0 %collective-permute-done.14 = f32[512,128]{1,0:T(8,128)S(1)} collective-permute-done((f32[512,128]{1,0:T(8,128)S(1)}, f32[512,128]{1,0:T(8,128)S(1)}, u32[]{:S(2)}, u32[]{:S(2)}) %collective-permute-start.14) | collective-permute-done | bytes 262176 | tf_op jit(solution)/shard_map/ppermute | solution.py:588
  71.0 0.8 %add_add_fusion = f32[512,128]{1,0:T(8,128)} fusion(f32[512,128]{1,0:T(8,128)S(1)} %collective-permute-done.15, f32[512,128]{1,0:T(8,128)S(1)} %collective-permute-done.14, f32[512,128]{1,0:T(8,128)S(1)} %get-tuple-element.37, f32[512,128]{1,0:T(8,128)S(1)} %collective-permute-done.13), kind=kLoop, calls=%fused_computation | loop fusion | flops 196608 | bytes 1310720 | tf_op jit(solution)/shard_map/add | solution.py:731
  (21 shorter events, 0.1 us)
Async XLA Ops:
  0.6 20.8 %copy-start = (f32[32,4096]{1,0:T(8,128)S(1)}, f32[32,4096]{1,0:T(8,128)}, u32[]{:S(2)}) copy-start(f32[32,4096]{1,0:T(8,128)} %temp.3) | copy-start | bytes 1572868
  0.6 20.8 %copy-start.1 = (s32[32,4096]{1,0:T(8,128)S(1)}, s32[32,4096]{1,0:T(8,128)}, u32[]{:S(2)}) copy-start(s32[32,4096]{1,0:T(8,128)} %mat.1) | copy-start | bytes 1572868
  0.7 20.7 %copy-start.6 = (s32[64,3]{0,1:T(4,128)S(1)}, s32[64,3]{0,1:T(4,128)}, u32[]{:S(2)}) copy-start(s32[64,3]{0,1:T(4,128)} %param.13) | copy-start | bytes 2308
  0.7 20.8 %copy-start.4 = (f32[4]{0:T(128)S(1)}, f32[4]{0:T(128)}, u32[]{:S(2)}) copy-start(f32[4]{0:T(128)} %k0_table.3) | copy-start | bytes 52
  0.7 20.8 %copy-start.5 = (f32[4]{0:T(128)S(1)}, f32[4]{0:T(128)}, u32[]{:S(2)}) copy-start(f32[4]{0:T(128)} %beta_table.3) | copy-start | bytes 52
  4.0 21.1 %copy-start.3 = (f32[512,128]{1,0:T(8,128)S(1)}, f32[512,128]{1,0:T(8,128)}, u32[]{:S(2)}) copy-start(f32[512,128]{1,0:T(8,128)} %get-tuple-element.29.refs_0_) | copy-start | bytes 786436
  4.1 29.2 %copy-start.2 = (f32[1024,128]{1,0:T(8,128)S(1)}, f32[1024,128]{1,0:T(8,128)}, u32[]{:S(2)}) copy-start(f32[1024,128]{1,0:T(8,128)} %get-tuple-element.22.refs_0_) | copy-start | bytes 1572868
  4.1 15.2 %collective-permute-start = (f32[1024,128]{1,0:T(8,128)}, f32[1024,128]{1,0:T(8,128)}, u32[]{:S(2)}, u32[]{:S(2)}) collective-permute-start(f32[1024,128]{1,0:T(8,128)} %get-tuple-element.22.refs_0_), channel_id=1, source_target_pairs={{0,2},{1,3},{2,0},{3,1},{4,6},{5,7},{6,4},{7,5},{8,10},{9,11},{10,... | collective-permute-start | bytes 1572872 | tf_op jit(solution)/shard_map/ppermute | solution.py:588
  7.1 24.6 %collective-permute-start.1 = (f32[1024,128]{1,0:T(8,128)}, f32[1024,128]{1,0:T(8,128)}, u32[]{:S(2)}, u32[]{:S(2)}) collective-permute-start(f32[1024,128]{1,0:T(8,128)} %get-tuple-element.22.refs_0_), channel_id=1, source_target_pairs={{0,1},{1,0},{2,3},{3,2},{4,5},{5,4},{6,7},{7,6},{8,9},{9,8},{10,11... | collective-permute-start | bytes 1572872 | tf_op jit(solution)/shard_map/ppermute | solution.py:598
  7.1 13.3 %collective-permute-start.3 = (f32[496,128]{1,0:T(8,128)}, f32[496,128]{1,0:T(8,128)S(1)}, u32[]{:S(2)}, u32[]{:S(2)}) collective-permute-start(f32[496,128]{1,0:T(8,128)} %get-tuple-element.23), channel_id=1, source_target_pairs={{0,4},{8,12},{16,20},{24,28},{4,0},{12,8},{20,16},{28,24},{1,5},{9... | collective-permute-start | bytes 761864 | tf_op jit(solution)/shard_map/ppermute | solution.py:594
  8.6 11.8 %collective-permute-start.4 = (f32[496,128]{1,0:T(8,128)}, f32[496,128]{1,0:T(8,128)S(1)}, u32[]{:S(2)}, u32[]{:S(2)}) collective-permute-start(f32[496,128]{1,0:T(8,128)} %get-tuple-element.24), channel_id=1, source_target_pairs={{4,8},{12,16},{20,24},{8,4},{16,12},{24,20},{5,9},{13,17},{21,25},... | collective-permute-start | bytes 761864 | tf_op jit(solution)/shard_map/ppermute | solution.py:594
  19.3 14.0 %collective-permute-start.2 = (f32[1024,128]{1,0:T(8,128)}, f32[1024,128]{1,0:T(8,128)}, u32[]{:S(2)}, u32[]{:S(2)}) collective-permute-start(f32[1024,128]{1,0:T(8,128)} %collective-permute-done.refs_1_), channel_id=1, source_target_pairs={{0,1},{1,0},{2,3},{3,2},{4,5},{5,4},{6,7},{7,6},{8,9},{9,8},{10,11... | collective-permute-start | bytes 1572872 | tf_op jit(solution)/shard_map/ppermute | solution.py:598
  20.4 10.8 %collective-permute-start.5 = (f32[448,128]{1,0:T(8,128)S(1)}, f32[448,128]{1,0:T(8,128)S(1)}, u32[]{:S(2)}, u32[]{:S(2)}) collective-permute-start(f32[448,128]{1,0:T(8,128)S(1)} %relay.1.refs_4_), channel_id=1, source_target_pairs={{0,2},{1,3},{2,0},{3,1},{4,6},{5,7},{6,4},{7,5},{8,10},{9,11},{10,... | collective-permute-start | bytes 688136 | tf_op jit(solution)/shard_map/ppermute | solution.py:588
  21.2 10.1 %collective-permute-start.8 = (f32[448,128]{1,0:T(8,128)S(1)}, f32[448,128]{1,0:T(8,128)S(1)}, u32[]{:S(2)}, u32[]{:S(2)}) collective-permute-start(f32[448,128]{1,0:T(8,128)S(1)} %relay.1.refs_4_), channel_id=1, source_target_pairs={{0,1},{1,0},{2,3},{3,2},{4,5},{5,4},{6,7},{7,6},{8,9},{9,8},{10,11... | collective-permute-start | bytes 688136 | tf_op jit(solution)/shard_map/ppermute | solution.py:598
  23.1 1.3 %collective-permute-start.6 = (f32[120,128]{1,0:T(8,128)S(1)}, f32[120,128]{1,0:T(8,128)S(1)}, u32[]{:S(2)}, u32[]{:S(2)}) collective-permute-start(f32[120,128]{1,0:T(8,128)S(1)} %get-tuple-element.25), channel_id=1, source_target_pairs={{0,1},{2,3},{1,0},{3,2},{4,5},{6,7},{5,4},{7,6},{8,9},{10,11},{9,8... | collective-permute-start | bytes 184328 | tf_op jit(solution)/shard_map/ppermute | solution.py:594
  24.4 0.7 collective-permute-start.7
  25.1 22.3 %collective-permute-start.10 = (f32[512,128]{1,0:T(8,128)S(1)}, f32[512,128]{1,0:T(8,128)S(1)}, u32[]{:S(2)}, u32[]{:S(2)}) collective-permute-start(f32[512,128]{1,0:T(8,128)S(1)} %copy-done.3), channel_id=1, source_target_pairs={{0,2},{1,3},{2,0},{3,1},{4,6},{5,7},{6,4},{7,5},{8,10},{9,11},{10,... | collective-permute-start | bytes 786440 | tf_op jit(solution)/shard_map/ppermute | solution.py:588
  31.3 16.1 %collective-permute-start.11 = (f32[512,128]{1,0:T(8,128)S(1)}, f32[512,128]{1,0:T(8,128)S(1)}, u32[]{:S(2)}, u32[]{:S(2)}) collective-permute-start(f32[512,128]{1,0:T(8,128)S(1)} %copy-done.3), channel_id=1, source_target_pairs={{0,1},{1,0},{2,3},{3,2},{4,5},{5,4},{6,7},{7,6},{8,9},{9,8},{10,11... | collective-permute-start | bytes 786440 | tf_op jit(solution)/shard_map/ppermute | solution.py:619
  31.3 16.1 %collective-permute-start.12 = (f32[512,128]{1,0:T(8,128)S(1)}, f32[512,128]{1,0:T(8,128)S(1)}, u32[]{:S(2)}, u32[]{:S(2)}) collective-permute-start(f32[512,128]{1,0:T(8,128)S(1)} %copy-done.3), channel_id=1, source_target_pairs={{0,3},{1,2},{2,1},{3,0},{4,7},{5,6},{6,5},{7,4},{8,11},{9,10},{10,... | collective-permute-start | bytes 786440 | tf_op jit(solution)/shard_map/ppermute | solution.py:619
  31.7 1.6 %collective-permute-start.9 = (f32[448,128]{1,0:T(8,128)S(1)}, f32[448,128]{1,0:T(8,128)S(1)}, u32[]{:S(2)}, u32[]{:S(2)}) collective-permute-start(f32[448,128]{1,0:T(8,128)S(1)} %collective-permute-done.5.refs_5_), channel_id=1, source_target_pairs={{0,1},{1,0},{2,3},{3,2},{4,5},{5,4},{6,7},{7,6},{8,9},{9,8},{10,11... | collective-permute-start | bytes 688136 | tf_op jit(solution)/shard_map/ppermute | solution.py:598
  56.7 7.3 %collective-permute-start.15 = (f32[512,128]{1,0:T(8,128)S(1)}, f32[512,128]{1,0:T(8,128)S(1)}, u32[]{:S(2)}, u32[]{:S(2)}) collective-permute-start(f32[512,128]{1,0:T(8,128)S(1)} %get-tuple-element.40), channel_id=1, source_target_pairs={{0,3},{1,0},{2,1},{3,2},{4,7},{5,4},{6,5},{7,6},{8,11},{9,8},{10,9... | collective-permute-start | bytes 786440 | tf_op jit(solution)/shard_map/ppermute | solution.py:588
  57.6 13.5 %collective-permute-start.14 = (f32[512,128]{1,0:T(8,128)S(1)}, f32[512,128]{1,0:T(8,128)S(1)}, u32[]{:S(2)}, u32[]{:S(2)}) collective-permute-start(f32[512,128]{1,0:T(8,128)S(1)} %get-tuple-element.39), channel_id=1, source_target_pairs={{0,2},{1,3},{2,0},{3,1},{4,6},{5,7},{6,4},{7,5},{8,10},{9,11},{10,... | collective-permute-start | bytes 786440 | tf_op jit(solution)/shard_map/ppermute | solution.py:588
  58.8 12.2 %collective-permute-start.13 = (f32[512,128]{1,0:T(8,128)S(1)}, f32[512,128]{1,0:T(8,128)S(1)}, u32[]{:S(2)}, u32[]{:S(2)}) collective-permute-start(f32[512,128]{1,0:T(8,128)S(1)} %get-tuple-element.38), channel_id=1, source_target_pairs={{0,1},{1,2},{2,3},{3,0},{4,5},{5,6},{6,7},{7,4},{8,9},{9,10},{10,1... | collective-permute-start | bytes 786440 | tf_op jit(solution)/shard_map/ppermute | solution.py:588

commit v7 on v6

--- a/solution.py
+++ b/solution.py
@@ -29,8 +29,8 @@
 HALF = TE
 YBLOCKS = HALF + 2 * HALO
 C_SIZE, L_SIZE, U_SIZE = TE + 2, LOW[0] + 1, HIGH[0] + 1
-ROW0 = SUB
-SLAB_ROWS = ROW0 + YBLOCKS * SLABX + SUB
+ROW0 = ROW
+SLAB_ROWS = ROW0 + YBLOCKS * SLABX + ROW0
 
 
 def cheb_weight(step, count):
@@ -194,46 +194,58 @@
     none = tiles
     bodies = refs[:width_gy]
     halos = refs[width_gy : 2 * width_gy]
-    pot, slope, cell_at, cell_of, pa, pb, la, lb, ua, ub, s_c, s_l, s_u = refs[2 * width_gy :]
+    pot, slope, cell_at, cell_of, pa, pb, la, lb, ua, ub, s_c, s_l, s_u, sems, pot_sem = refs[2 * width_gy :]
     i = lax.axis_index("gx")
     j = lax.axis_index("gy")
     rows_gx = lax.axis_size("gx")
+    zero = jnp.zeros((SUB, LANES), jnp.float32)
+
+    moves = []
+    for part in range(width_gy):
+        at = 0
+        pieces = [(bodies[part], 0, pa, part * C_SIZE + 1, TE), (bodies[part], TE * ROW, s_c, part * TE, TE)]
+        for target, first, count in (
+            (la, part * L_SIZE, LOW[0]),
+            (s_l, part * LOW[1], LOW[1]),
+            (None, 0, LOW[2]),
+            (ua, part * U_SIZE + 1, HIGH[0]),
+            (s_u, part * HIGH[1], HIGH[1]),
+        ):
+            if target is not None:
+                pieces.append((halos[part], at, target, first, count))
+            at += count * ROW
+        for source, start, target, first, count in pieces:
+            move = pltpu.make_async_copy(
+                source.at[start : start + count * ROW],
+                target.at[ROW0 + first * ROW : ROW0 + (first + count) * ROW],
+                sems.at[len(moves)],
+            )
+            move.start()
+            moves.append(move)
+
     fill_maps(chips, pos, cell_at, cell_of)
 
-    zero = jnp.zeros((SUB, LANES), jnp.float32)
-
-    def row_of(at):
-        return ROW0 + at * SUB
+    def row_of(slot, size, plane):
+        return ROW0 + (lax.div(slot, TILES) * size + plane) * ROW + lax.rem(slot, TILES)
 
     def plane_at(ref, row):
-        return ref[pl.ds(pl.multiple_of(row, SUB), SUB), :]
-
-    def loose_at(ref, row):
-        return ref[pl.ds(row, SUB), :]
+        return ref[pl.ds(row, SUB, stride=TILES), :]
 
     def put_plane(ref, row, value):
-        ref[pl.ds(pl.multiple_of(row, SUB), SUB), :] = value
-
-    def unpack(source, start, t, target, first, count):
-        def plane(p, carry):
-            value = source[pl.ds(pl.multiple_of(p * ROW, ROW) + (start + t), SUB, stride=TILES), :]
-            put_plane(target, p * SUB + row_of(first), value)
-            return carry
-
-        lax.fori_loop(0, count, plane, 0, unroll=min(count, 16))
-
-    for part in range(width_gy):
-        for t in range(TILES):
-            slot = part * TILES + t
-            unpack(bodies[part], 0, t, pa, slot * C_SIZE + 1, TE)
-            unpack(bodies[part], TE * ROW, t, s_c, slot * TE, TE)
-            unpack(halos[part], 0, t, la, slot * L_SIZE, LOW[0])
-            unpack(halos[part], LOW[0] * ROW, t, s_l, slot * LOW[1], LOW[1])
-            unpack(halos[part], LOW_ROWS, t, ua, slot * U_SIZE + 1, HIGH[0])
-            unpack(halos[part], LOW_ROWS + HIGH[0] * ROW, t, s_u, slot * HIGH[1], HIGH[1])
+        ref[pl.ds(row, SUB, stride=TILES), :] = value
+
     for ref, count in ((pa, C_SIZE), (pb, C_SIZE), (la, L_SIZE), (lb, L_SIZE), (ua, U_SIZE), (ub, U_SIZE)):
-        for p in range(count):
-            put_plane(ref, row_of(none * count + p), zero)
+        first = ROW0 + width_gy * count * ROW
+        for row in range(first, first + count * ROW, SUB):
+            ref[row : row + SUB] = zero
+
+    def clear(at, carry):
+        slope[pl.ds(pl.multiple_of(at * SUB, SUB), SUB), :] = zero
+        return carry
+
+    lax.fori_loop(0, slope.shape[0] // SUB, clear, 0, unroll=8)
+    for move in moves:
+        move.wait()
 
     lane = lax.broadcasted_iota(jnp.int32, (SUB, LANES), 1)
     sub = lax.broadcasted_iota(jnp.int32, (SUB, LANES), 0)
@@ -243,11 +255,11 @@
     first_z, last_z = depth == 0, depth == TE - 1
 
     def y_plus(ref, own, row, ghost_row):
-        turned = jnp.where(last_sub, loose_at(ref, ghost_row), loose_at(ref, row))
+        turned = jnp.where(last_sub, plane_at(ref, ghost_row), plane_at(ref, row))
         return roll(jnp.where(first_y, turned, own), -TE, 1)
 
     def y_minus(ref, own, row, ghost_row):
-        turned = jnp.where(first_sub, loose_at(ref, ghost_row), loose_at(ref, row))
+        turned = jnp.where(first_sub, plane_at(ref, ghost_row), plane_at(ref, row))
         return roll(jnp.where(last_y, turned, own), TE, 1)
 
     def around(which, slot):
@@ -269,25 +281,24 @@
         def ghosts(slot, carry):
             cell = cell_of[0, slot]
             below, above = cell_at[1, cell], cell_at[2, cell]
-            own = slot * C_SIZE
             over, under = cell_at[0, cell_of[1, slot]], cell_at[0, cell_of[2, slot]]
-            put_plane(c_src, row_of(own), plane_at(l_src, row_of(below * L_SIZE + LOW[0] - 1)))
-            put_plane(c_src, row_of(own + TE + 1), plane_at(u_src, row_of(above * U_SIZE + 1)))
-            put_plane(l_src, row_of(slot * L_SIZE + LOW[0]), plane_at(c_src, row_of(over * C_SIZE + 1)))
-            put_plane(u_src, row_of(slot * U_SIZE), plane_at(c_src, row_of(under * C_SIZE + TE)))
+            put_plane(c_src, row_of(slot, C_SIZE, 0), plane_at(l_src, row_of(below, L_SIZE, LOW[0] - 1)))
+            put_plane(c_src, row_of(slot, C_SIZE, TE + 1), plane_at(u_src, row_of(above, U_SIZE, 1)))
+            put_plane(l_src, row_of(slot, L_SIZE, LOW[0]), plane_at(c_src, row_of(over, C_SIZE, 1)))
+            put_plane(u_src, row_of(slot, U_SIZE, 0), plane_at(c_src, row_of(under, C_SIZE, TE)))
             return carry
 
         lax.fori_loop(0, tiles, ghosts, 0)
 
-        def relax(src, dst, size, slots, first, count, s_ref, s_at):
+        def relax(src, dst, size, slots, first, count, s_ref, s_size, s_first):
             slot, y_m, y_p, z, turn, meets = slots
-            row, s_row = row_of(slot * size + first), row_of(s_at)
-            up, down = row + 1, row - 1
-            row_m, row_p = row_of(y_m * size + first) + (SUB - 1), row_of(y_p * size + first) - (SUB - 1)
-            row_z = row_of(z * size + first)
-            before, own = plane_at(src, row - SUB), plane_at(src, row)
-            for step in range(0, count * SUB, SUB):
-                after = plane_at(src, row + (step + SUB))
+            row, s_row = row_of(slot, size, first), row_of(slot, s_size, s_first)
+            up, down = row + TILES, row - TILES
+            row_m, row_p = row_of(y_m, size, first) + (ROW - TILES), row_of(y_p, size, first) - (ROW - TILES)
+            row_z = row_of(z, size, first)
+            before, own = plane_at(src, row - ROW), plane_at(src, row)
+            for step in range(0, count * ROW, ROW):
+                after = plane_at(src, row + (step + ROW))
                 total = (before + after) + plane_at(s_ref, s_row + step)
                 total = total + y_minus(src, own, down + step, row_m + step)
                 total = total + y_plus(src, own, up + step, row_p + step)
@@ -299,41 +310,35 @@
 
         def sweep_tile(slot, carry):
             _, slots = around(0, slot)
-            relax(c_src, c_dst, C_SIZE, slots, 1, TE, s_c, slot * TE)
+            relax(c_src, c_dst, C_SIZE, slots, 1, TE, s_c, TE, 0)
             _, slots = around(1, slot)
             count = LOW[0] - 1 - k
-            relax(l_src, l_dst, L_SIZE, slots, LOW[0] - count, count, s_l, (slot + 1) * LOW[1] - count)
+            relax(l_src, l_dst, L_SIZE, slots, LOW[0] - count, count, s_l, LOW[1], LOW[1] - count)
             _, slots = around(2, slot)
-            relax(u_src, u_dst, U_SIZE, slots, 1, HIGH[0] - 1 - k, s_u, slot * HIGH[1])
+            relax(u_src, u_dst, U_SIZE, slots, 1, HIGH[0] - 1 - k, s_u, HIGH[1], 0)
             return carry
 
         lax.fori_loop(0, tiles, sweep_tile, 0)
 
     field, f_l, f_u = bufs[SWEEPS % 2]
-    for t in range(TILES):
-        for p in range(TE):
-            pot[pl.ds(p * ROW + t, SUB, stride=TILES), :] = plane_at(field, row_of(t * C_SIZE + 1 + p))
-
-    def clear(at, carry):
-        slope[pl.ds(pl.multiple_of(at * SUB, SUB), SUB), :] = zero
-        return carry
-
-    lax.fori_loop(0, slope.shape[0] // SUB, clear, 0, unroll=8)
+    pot_move = pltpu.make_async_copy(field.at[ROW0 + ROW : ROW0 + (TE + 1) * ROW], pot, pot_sem.at[0])
+    pot_move.start()
 
     def squares(ref, size, slots, local, x, first, count, x_last=None):
         slot, _, y_p, z, turn, meets = slots
-        row = row_of(slot * size + first)
-        up, row_p, row_z = row + 1, row_of(y_p * size + first) - (SUB - 1), row_of(z * size + first)
+        row = row_of(slot, size, first)
+        up, row_p, row_z = row + TILES, row_of(y_p, size, first) - (ROW - TILES), row_of(z, size, first)
         target = (local * SLABX + x) * SUB
         own = plane_at(ref, row)
-        for step in range(0, count * SUB, SUB):
-            last = step == (count - 1) * SUB and x_last is not None
-            after = x_last if last else plane_at(ref, row + (step + SUB))
+        for p in range(count):
+            last = p == count - 1 and x_last is not None
+            after = x_last if last else plane_at(ref, row + (p + 1) * ROW)
             d_x = after - own
-            d_y = y_plus(ref, own, up + step, row_p + step) - own
-            ghost = jnp.where(meets, pltpu.roll(plane_at(ref, row_z + step), turn, 1), 0.0)
+            d_y = y_plus(ref, own, up + p * ROW, row_p + p * ROW) - own
+            ghost = jnp.where(meets, pltpu.roll(plane_at(ref, row_z + p * ROW), turn, 1), 0.0)
             d_z = jnp.where(last_z, ghost, roll(own, -1, 1)) - own
-            put_plane(slope, target + step, d_x * d_x + d_y * d_y + d_z * d_z)
+            rows = pl.ds(pl.multiple_of(target + p * SUB, SUB), SUB)
+            slope[rows, :] = d_x * d_x + d_y * d_y + d_z * d_z
             own = after
 
     def slope_tile(slot, carry):
@@ -344,10 +349,10 @@
             @pl.when(inside)
             def _():
                 if which == 0:
-                    above = plane_at(f_u, row_of(cell_at[2, cell] * U_SIZE + 1))
+                    above = plane_at(f_u, row_of(cell_at[2, cell], U_SIZE, 1))
                     squares(field, C_SIZE, slots, local, HALO, 1, TE, above)
                 elif which == 1:
-                    centre = plane_at(field, row_of(cell_at[0, cell] * C_SIZE + 1))
+                    centre = plane_at(field, row_of(cell_at[0, cell], C_SIZE, 1))
                     squares(f_l, L_SIZE, slots, local, HALO - 2, LOW[0] - 2, 2, centre)
                 else:
                     squares(f_u, U_SIZE, slots, local, HALO + TE, 1, 2)
@@ -355,6 +360,7 @@
         return carry
 
     lax.fori_loop(0, tiles, slope_tile, 0)
+    pot_move.wait()
 
 
 def window(which, cell, i, j, rows_gx):
@@ -623,6 +629,7 @@
 VMEM = pl.BlockSpec(memory_space=pltpu.VMEM)
 SMEM = pl.BlockSpec(memory_space=pltpu.SMEM)
 HBM = pl.BlockSpec(memory_space=pltpu.HBM)
+ANY = pl.BlockSpec(memory_space=pl.ANY)
 PARAMS = pltpu.CompilerParams(vmem_limit_bytes=32 * 1024 * 1024)
 
 
@@ -697,18 +704,20 @@
     halos = halos + [from_mate(part) for part in halos]
 
     def fields(count):
-        return pltpu.VMEM((2 * ROW0 + (tiles + 1) * count * SUB, LANES), f32)
+        return pltpu.VMEM((2 * ROW0 + (width_gy + 1) * count * ROW, LANES), f32)
 
     pot, slope = pl.pallas_call(
         functools.partial(sweep_kernel, chips),
         out_shape=(rows(TE * ROW), rows(8 * SLABX * SUB)),
-        in_specs=[SMEM] + [VMEM] * (2 * width_gy),
-        out_specs=(VMEM,) * 2,
+        in_specs=[SMEM] + [ANY] * (2 * width_gy),
+        out_specs=(ANY, VMEM),
         scratch_shapes=[
             pltpu.SMEM((3, 2 * (2 * width_gy + 2)), jnp.int32),
             pltpu.SMEM((3, tiles), jnp.int32),
             fields(C_SIZE), fields(C_SIZE), fields(L_SIZE), fields(L_SIZE), fields(U_SIZE), fields(U_SIZE),
             fields(TE), fields(LOW[1]), fields(HIGH[1]),
+            pltpu.SemaphoreType.DMA((6 * width_gy,)),
+            pltpu.SemaphoreType.DMA((1,)),
         ],
         compiler_params=PARAMS,
         name="sweeps",

time: 72.2 us -> 72.6 us (level)
  no operation moved by 1% of the time
where the time goes in v7:
time: 72.6 us; the launch traced here: 72.2 us
  Pallas kernels  28.7 us (40%)
  waiting for transfers between devices  25.5 us (35%)
  starting transfers between devices  16.4 us (23%)
  between operations  0.82 us (1%)
  other arithmetic  0.75 us (1%)
    ppermute x6, waiting for transfers between devices, shifted(): return lax.ppermute(value, axis, pairs)  22.3 us
    pallas_call x1, Pallas kernels, on_device(): pl.pallas_call(functools.partial(sweep_kernel, chips), out_shape=(rows(TE...  14.5 us
    ppermute x6, starting transfers between devices, shifted(): return lax.ppermute(value, axis, pairs)  12.1 us
    pallas_call x1, Pallas kernels, on_device(): pl.pallas_call(functools.partial(slab_steps_kernel, chips), out_shape=(ja...  9.27 us
    pallas_call x1, Pallas kernels, on_device(): pl.pallas_call(prep_kernel, out_shape=(rows(2 * TE * ROW), rows(TE * ROW)...  3.35 us
    ppermute x4, starting transfers between devices, with_partner(): lax.ppermute(value, axis, pairs + [(high, low) for low, high in pairs])  3.21 us
    ppermute x4, waiting for transfers between devices, with_partner(): lax.ppermute(value, axis, pairs + [(high, low) for low, high in pairs])  2.05 us
    pallas_call x1, Pallas kernels, on_device(): pl.pallas_call(slab_kernel, out_shape=(rows(SLAB_ROWS),) * 3 + (rows(HALO...  1.61 us
  transfers between devices with their start and end apart: 16, of which 6 were waited for; matrix products, arithmetic and copies ran while one was open for 0% of the time, Pallas kernels for 22%

profile of v7, /device:TPU:0, one launch (start us, length us, event | category | flops | bytes accessed | tf_op | source)
XLA Modules:
  0.0 72.2 jit_solution(215678743010556417)
XLA Ops:
  0.7 3.4 %prep.1 = (f32[1024,128]{1,0:T(8,128)}, f32[512,128]{1,0:T(8,128)}, f32[496,128]{1,0:T(8,128)}, f32[496,128]{1,0:T(8,128)}) custom-call(f32[4]{0:T(128)} %table.1, f32[512,128]{1,0:T(8,128)} %bitcast.26, f32[512,128]{1,0:T(8,128)} %bitcast.27, s32[512,128]{1,0:T(8,128)} %bitcast.28, f32[32,4096]{1,0:T(8,128)} %temp.3, s32[32,4096]{1,0:T(8,128)} %mat.1), custom_call_target="tpu_custom_call" | custom-call | tf_op jit(solution)/shard_map/prep/pallas_call | solution.py:658
  4.0 0.0 copy-start.3
  4.1 0.0 copy-start.2
  4.1 3.0 %collective-permute-start = (f32[1024,128]{1,0:T(8,128)}, f32[1024,128]{1,0:T(8,128)}, u32[]{:S(2)}, u32[]{:S(2)}) collective-permute-start(f32[1024,128]{1,0:T(8,128)} %get-tuple-element.22.refs_0_), channel_id=1, source_target_pairs={{0,2},{1,3},{2,0},{3,1},{4,6},{5,7},{6,4},{7,5},{8,10},{9,11},{10,... | collective-permute-start | bytes 1572872 | tf_op jit(solution)/shard_map/ppermute | solution.py:594
  7.1 0.0 collective-permute-start.1
  7.1 1.5 %collective-permute-start.3 = (f32[496,128]{1,0:T(8,128)}, f32[496,128]{1,0:T(8,128)S(1)}, u32[]{:S(2)}, u32[]{:S(2)}) collective-permute-start(f32[496,128]{1,0:T(8,128)} %get-tuple-element.23), channel_id=1, source_target_pairs={{0,4},{8,12},{16,20},{24,28},{4,0},{12,8},{20,16},{28,24},{1,5},{9... | collective-permute-start | bytes 761864 | tf_op jit(solution)/shard_map/ppermute | solution.py:600
  8.6 0.7 collective-permute-start.4
  9.3 10.0 %collective-permute-done.refs_1_ = f32[1024,128]{1,0:T(8,128)} collective-permute-done((f32[1024,128]{1,0:T(8,128)}, f32[1024,128]{1,0:T(8,128)}, u32[]{:S(2)}, u32[]{:S(2)}) %collective-permute-start) | collective-permute-done | bytes 524320 | tf_op jit(solution)/shard_map/ppermute | solution.py:594
  19.3 1.1 %collective-permute-done.3.inner = f32[496,128]{1,0:T(8,128)S(1)} collective-permute-done((f32[496,128]{1,0:T(8,128)}, f32[496,128]{1,0:T(8,128)S(1)}, u32[]{:S(2)}, u32[]{:S(2)}) %collective-permute-start.3) | collective-permute-done | bytes 253984 | tf_op jit(solution)/shard_map/ppermute | solution.py:600
  20.4 0.7 %collective-permute-start.5 = (f32[448,128]{1,0:T(8,128)S(1)}, f32[448,128]{1,0:T(8,128)S(1)}, u32[]{:S(2)}, u32[]{:S(2)}) collective-permute-start(f32[448,128]{1,0:T(8,128)S(1)} %relay.1.refs_4_), channel_id=1, source_target_pairs={{0,2},{1,3},{2,0},{3,1},{4,6},{5,7},{6,4},{7,5},{8,10},{9,11},{10,... | collective-permute-start | bytes 688136 | tf_op jit(solution)/shard_map/ppermute | solution.py:594
  21.2 0.2 collective-permute-start.8
  21.4 0.1 copy.16.pos
  21.5 1.6 %slab_prep.1 = (f32[1552,128]{1,0:T(8,128)S(1)}, f32[1552,128]{1,0:T(8,128)S(1)}, f32[1552,128]{1,0:T(8,128)S(1)}, f32[120,128]{1,0:T(8,128)S(1)}, f32[120,128]{1,0:T(8,128)S(1)}) custom-call(s32[64,3]{1,0:T(8,128)S(1)} %copy.16.pos, f32[4]{0:T(128)S(1)} %copy-done.4, f32[4]{0:T(128)S(1)} %copy-done.5, f32[32,4096]{1,0:T(8,128)S(1)} %copy-done, ...), custom_call_target="tpu_custom_call" | custom-call | tf_op jit(solution)/shard_map/slab_prep/pallas_call | solution.py:693
  23.1 0.4 collective-permute-start.6
  23.5 0.9 %collective-permute-done.6.refs_12_ = f32[120,128]{1,0:T(8,128)S(1)} collective-permute-done((f32[120,128]{1,0:T(8,128)S(1)}, f32[120,128]{1,0:T(8,128)S(1)}, u32[]{:S(2)}, u32[]{:S(2)}) %collective-permute-start.6) | collective-permute-done | bytes 61472 | tf_op jit(solution)/shard_map/ppermute | solution.py:600
  24.4 0.7 collective-permute-start.7
  25.1 0.0 collective-permute-done.7.refs_13_
  25.1 6.2 %collective-permute-start.10 = (f32[512,128]{1,0:T(8,128)S(1)}, f32[512,128]{1,0:T(8,128)S(1)}, u32[]{:S(2)}, u32[]{:S(2)}) collective-permute-start(f32[512,128]{1,0:T(8,128)S(1)} %copy-done.3), channel_id=1, source_target_pairs={{0,2},{1,3},{2,0},{3,1},{4,6},{5,7},{6,4},{7,5},{8,10},{9,11},{10,... | collective-permute-start | bytes 786440 | tf_op jit(solution)/shard_map/ppermute | solution.py:594
  31.3 0.0 collective-permute-done.5.refs_5_
  31.3 0.0 collective-permute-start.11
  31.3 0.4 collective-permute-start.12
  31.7 0.0 collective-permute-done.1.refs_2_
  31.7 0.4 collective-permute-start.9
  32.2 1.1 %collective-permute-done.9.refs_7_ = f32[448,128]{1,0:T(8,128)S(1)} collective-permute-done((f32[448,128]{1,0:T(8,128)S(1)}, f32[448,128]{1,0:T(8,128)S(1)}, u32[]{:S(2)}, u32[]{:S(2)}) %collective-permute-start.9) | collective-permute-done | bytes 229408 | tf_op jit(solution)/shard_map/ppermute | solution.py:604
  33.3 14.5 %sweeps.1 = (f32[512,128]{1,0:T(8,128)}, f32[2560,128]{1,0:T(8,128)S(1)}) custom-call(s32[64,3]{1,0:T(8,128)S(1)} %copy.16.pos, f32[1024,128]{1,0:T(8,128)S(1)} %copy-done.2, f32[1024,128]{1,0:T(8,128)} %collective-permute-done.refs_1_, f32[1024,128]{1,0:T(8,128)} %collective-permute-done.1.refs_2_, f32[1024,128]{1,0:T(8,128)} %collective-permute-done.2.refs_3_, ...), custom_call_target="tpu_custom_call" | custom-call | tf_op jit(solution)/shard_map/sweeps/pallas_call | solution.py:709
  47.7 0.0 collective-permute-done.10.refs_1_
  47.8 9.3 %slab_steps.1 = (f32[32,4096]{1,0:T(8,128)}, f32[512,128]{1,0:T(8,128)S(1)}, f32[512,128]{1,0:T(8,128)S(1)}, f32[512,128]{1,0:T(8,128)S(1)}, f32[512,128]{1,0:T(8,128)S(1)}) custom-call(s32[64,3]{1,0:T(8,128)S(1)} %copy.16.pos, f32[4]{0:T(128)S(1)} %copy-done.4, f32[4]{0:T(128)S(1)} %copy-done.5, f32[512,128]{1,0:T(8,128)S(1)} %copy-done.3, ...), custom_call_target="tpu_custom_call" | custom-call | tf_op jit(solution)/shard_map/slab_steps/pallas_call | solution.py:726
  57.0 1.5 %collective-permute-start.15 = (f32[512,128]{1,0:T(8,128)S(1)}, f32[512,128]{1,0:T(8,128)S(1)}, u32[]{:S(2)}, u32[]{:S(2)}) collective-permute-start(f32[512,128]{1,0:T(8,128)S(1)} %get-tuple-element.40), channel_id=1, source_target_pairs={{0,3},{1,0},{2,1},{3,2},{4,7},{5,4},{6,5},{7,6},{8,11},{9,8},{10,9... | collective-permute-start | bytes 786440 | tf_op jit(solution)/shard_map/ppermute | solution.py:594
  58.5 0.7 %collective-permute-start.14 = (f32[512,128]{1,0:T(8,128)S(1)}, f32[512,128]{1,0:T(8,128)S(1)}, u32[]{:S(2)}, u32[]{:S(2)}) collective-permute-start(f32[512,128]{1,0:T(8,128)S(1)} %get-tuple-element.39), channel_id=1, source_target_pairs={{0,2},{1,3},{2,0},{3,1},{4,6},{5,7},{6,4},{7,5},{8,10},{9,11},{10,... | collective-permute-start | bytes 786440 | tf_op jit(solution)/shard_map/ppermute | solution.py:594
  59.2 6.0 %collective-permute-done.15 = f32[512,128]{1,0:T(8,128)S(1)} collective-permute-done((f32[512,128]{1,0:T(8,128)S(1)}, f32[512,128]{1,0:T(8,128)S(1)}, u32[]{:S(2)}, u32[]{:S(2)}) %collective-permute-start.15) | collective-permute-done | bytes 262176 | tf_op jit(solution)/shard_map/ppermute | solution.py:594
  65.2 6.3 %collective-permute-done.14 = f32[512,128]{1,0:T(8,128)S(1)} collective-permute-done((f32[512,128]{1,0:T(8,128)S(1)}, f32[512,128]{1,0:T(8,128)S(1)}, u32[]{:S(2)}, u32[]{:S(2)}) %collective-permute-start.14) | collective-permute-done | bytes 262176 | tf_op jit(solution)/shard_map/ppermute | solution.py:594
  71.5 0.8 %add_add_fusion = f32[512,128]{1,0:T(8,128)} fusion(f32[512,128]{1,0:T(8,128)S(1)} %collective-permute-done.15, f32[512,128]{1,0:T(8,128)S(1)} %collective-permute-done.14, f32[512,128]{1,0:T(8,128)S(1)} %get-tuple-element.37, f32[512,128]{1,0:T(8,128)S(1)} %collective-permute-done.13), kind=kLoop, calls=%fused_computation | loop fusion | flops 196608 | bytes 1310720 | tf_op jit(solution)/shard_map/add | solution.py:740
  (21 shorter events, 0.1 us)
Async XLA Ops:
  0.6 20.8 %copy-start = (f32[32,4096]{1,0:T(8,128)S(1)}, f32[32,4096]{1,0:T(8,128)}, u32[]{:S(2)}) copy-start(f32[32,4096]{1,0:T(8,128)} %temp.3) | copy-start | bytes 1572868
  0.6 20.8 %copy-start.1 = (s32[32,4096]{1,0:T(8,128)S(1)}, s32[32,4096]{1,0:T(8,128)}, u32[]{:S(2)}) copy-start(s32[32,4096]{1,0:T(8,128)} %mat.1) | copy-start | bytes 1572868
  0.7 20.7 %copy-start.6 = (s32[64,3]{0,1:T(4,128)S(1)}, s32[64,3]{0,1:T(4,128)}, u32[]{:S(2)}) copy-start(s32[64,3]{0,1:T(4,128)} %param.13) | copy-start | bytes 2308
  0.7 20.8 %copy-start.4 = (f32[4]{0:T(128)S(1)}, f32[4]{0:T(128)}, u32[]{:S(2)}) copy-start(f32[4]{0:T(128)} %k0_table.3) | copy-start | bytes 52
  0.7 20.8 %copy-start.5 = (f32[4]{0:T(128)S(1)}, f32[4]{0:T(128)}, u32[]{:S(2)}) copy-start(f32[4]{0:T(128)} %beta_table.3) | copy-start | bytes 52
  4.0 21.1 %copy-start.3 = (f32[512,128]{1,0:T(8,128)S(1)}, f32[512,128]{1,0:T(8,128)}, u32[]{:S(2)}) copy-start(f32[512,128]{1,0:T(8,128)} %get-tuple-element.29.refs_0_) | copy-start | bytes 786436
  4.1 29.2 %copy-start.2 = (f32[1024,128]{1,0:T(8,128)S(1)}, f32[1024,128]{1,0:T(8,128)}, u32[]{:S(2)}) copy-start(f32[1024,128]{1,0:T(8,128)} %get-tuple-element.22.refs_0_) | copy-start | bytes 1572868
  4.1 15.2 %collective-permute-start = (f32[1024,128]{1,0:T(8,128)}, f32[1024,128]{1,0:T(8,128)}, u32[]{:S(2)}, u32[]{:S(2)}) collective-permute-start(f32[1024,128]{1,0:T(8,128)} %get-tuple-element.22.refs_0_), channel_id=1, source_target_pairs={{0,2},{1,3},{2,0},{3,1},{4,6},{5,7},{6,4},{7,5},{8,10},{9,11},{10,... | collective-permute-start | bytes 1572872 | tf_op jit(solution)/shard_map/ppermute | solution.py:594
  7.1 24.6 %collective-permute-start.1 = (f32[1024,128]{1,0:T(8,128)}, f32[1024,128]{1,0:T(8,128)}, u32[]{:S(2)}, u32[]{:S(2)}) collective-permute-start(f32[1024,128]{1,0:T(8,128)} %get-tuple-element.22.refs_0_), channel_id=1, source_target_pairs={{0,1},{1,0},{2,3},{3,2},{4,5},{5,4},{6,7},{7,6},{8,9},{9,8},{10,11... | collective-permute-start | bytes 1572872 | tf_op jit(solution)/shard_map/ppermute | solution.py:604
  7.1 13.3 %collective-permute-start.3 = (f32[496,128]{1,0:T(8,128)}, f32[496,128]{1,0:T(8,128)S(1)}, u32[]{:S(2)}, u32[]{:S(2)}) collective-permute-start(f32[496,128]{1,0:T(8,128)} %get-tuple-element.23), channel_id=1, source_target_pairs={{0,4},{8,12},{16,20},{24,28},{4,0},{12,8},{20,16},{28,24},{1,5},{9... | collective-permute-start | bytes 761864 | tf_op jit(solution)/shard_map/ppermute | solution.py:600
  8.6 11.8 %collective-permute-start.4 = (f32[496,128]{1,0:T(8,128)}, f32[496,128]{1,0:T(8,128)S(1)}, u32[]{:S(2)}, u32[]{:S(2)}) collective-permute-start(f32[496,128]{1,0:T(8,128)} %get-tuple-element.24), channel_id=1, source_target_pairs={{4,8},{12,16},{20,24},{8,4},{16,12},{24,20},{5,9},{13,17},{21,25},... | collective-permute-start | bytes 761864 | tf_op jit(solution)/shard_map/ppermute | solution.py:600
  19.3 14.0 %collective-permute-start.2 = (f32[1024,128]{1,0:T(8,128)}, f32[1024,128]{1,0:T(8,128)}, u32[]{:S(2)}, u32[]{:S(2)}) collective-permute-start(f32[1024,128]{1,0:T(8,128)} %collective-permute-done.refs_1_), channel_id=1, source_target_pairs={{0,1},{1,0},{2,3},{3,2},{4,5},{5,4},{6,7},{7,6},{8,9},{9,8},{10,11... | collective-permute-start | bytes 1572872 | tf_op jit(solution)/shard_map/ppermute | solution.py:604
  20.4 10.8 %collective-permute-start.5 = (f32[448,128]{1,0:T(8,128)S(1)}, f32[448,128]{1,0:T(8,128)S(1)}, u32[]{:S(2)}, u32[]{:S(2)}) collective-permute-start(f32[448,128]{1,0:T(8,128)S(1)} %relay.1.refs_4_), channel_id=1, source_target_pairs={{0,2},{1,3},{2,0},{3,1},{4,6},{5,7},{6,4},{7,5},{8,10},{9,11},{10,... | collective-permute-start | bytes 688136 | tf_op jit(solution)/shard_map/ppermute | solution.py:594
  21.2 10.1 %collective-permute-start.8 = (f32[448,128]{1,0:T(8,128)S(1)}, f32[448,128]{1,0:T(8,128)S(1)}, u32[]{:S(2)}, u32[]{:S(2)}) collective-permute-start(f32[448,128]{1,0:T(8,128)S(1)} %relay.1.refs_4_), channel_id=1, source_target_pairs={{0,1},{1,0},{2,3},{3,2},{4,5},{5,4},{6,7},{7,6},{8,9},{9,8},{10,11... | collective-permute-start | bytes 688136 | tf_op jit(solution)/shard_map/ppermute | solution.py:604
  23.1 1.3 %collective-permute-start.6 = (f32[120,128]{1,0:T(8,128)S(1)}, f32[120,128]{1,0:T(8,128)S(1)}, u32[]{:S(2)}, u32[]{:S(2)}) collective-permute-start(f32[120,128]{1,0:T(8,128)S(1)} %get-tuple-element.25), channel_id=1, source_target_pairs={{0,1},{2,3},{1,0},{3,2},{4,5},{6,7},{5,4},{7,6},{8,9},{10,11},{9,8... | collective-permute-start | bytes 184328 | tf_op jit(solution)/shard_map/ppermute | solution.py:600
  24.4 0.7 collective-permute-start.7
  25.1 22.6 %collective-permute-start.10 = (f32[512,128]{1,0:T(8,128)S(1)}, f32[512,128]{1,0:T(8,128)S(1)}, u32[]{:S(2)}, u32[]{:S(2)}) collective-permute-start(f32[512,128]{1,0:T(8,128)S(1)} %copy-done.3), channel_id=1, source_target_pairs={{0,2},{1,3},{2,0},{3,1},{4,6},{5,7},{6,4},{7,5},{8,10},{9,11},{10,... | collective-permute-start | bytes 786440 | tf_op jit(solution)/shard_map/ppermute | solution.py:594
  31.3 16.4 %collective-permute-start.11 = (f32[512,128]{1,0:T(8,128)S(1)}, f32[512,128]{1,0:T(8,128)S(1)}, u32[]{:S(2)}, u32[]{:S(2)}) collective-permute-start(f32[512,128]{1,0:T(8,128)S(1)} %copy-done.3), channel_id=1, source_target_pairs={{0,1},{1,0},{2,3},{3,2},{4,5},{5,4},{6,7},{7,6},{8,9},{9,8},{10,11... | collective-permute-start | bytes 786440 | tf_op jit(solution)/shard_map/ppermute | solution.py:625
  31.3 16.5 %collective-permute-start.12 = (f32[512,128]{1,0:T(8,128)S(1)}, f32[512,128]{1,0:T(8,128)S(1)}, u32[]{:S(2)}, u32[]{:S(2)}) collective-permute-start(f32[512,128]{1,0:T(8,128)S(1)} %copy-done.3), channel_id=1, source_target_pairs={{0,3},{1,2},{2,1},{3,0},{4,7},{5,6},{6,5},{7,4},{8,11},{9,10},{10,... | collective-permute-start | bytes 786440 | tf_op jit(solution)/shard_map/ppermute | solution.py:625
  31.7 1.6 %collective-permute-start.9 = (f32[448,128]{1,0:T(8,128)S(1)}, f32[448,128]{1,0:T(8,128)S(1)}, u32[]{:S(2)}, u32[]{:S(2)}) collective-permute-start(f32[448,128]{1,0:T(8,128)S(1)} %collective-permute-done.5.refs_5_), channel_id=1, source_target_pairs={{0,1},{1,0},{2,3},{3,2},{4,5},{5,4},{6,7},{7,6},{8,9},{9,8},{10,11... | collective-permute-start | bytes 688136 | tf_op jit(solution)/shard_map/ppermute | solution.py:604
  57.0 8.2 %collective-permute-start.15 = (f32[512,128]{1,0:T(8,128)S(1)}, f32[512,128]{1,0:T(8,128)S(1)}, u32[]{:S(2)}, u32[]{:S(2)}) collective-permute-start(f32[512,128]{1,0:T(8,128)S(1)} %get-tuple-element.40), channel_id=1, source_target_pairs={{0,3},{1,0},{2,1},{3,2},{4,7},{5,4},{6,5},{7,6},{8,11},{9,8},{10,9... | collective-permute-start | bytes 786440 | tf_op jit(solution)/shard_map/ppermute | solution.py:594
  58.5 13.0 %collective-permute-start.14 = (f32[512,128]{1,0:T(8,128)S(1)}, f32[512,128]{1,0:T(8,128)S(1)}, u32[]{:S(2)}, u32[]{:S(2)}) collective-permute-start(f32[512,128]{1,0:T(8,128)S(1)} %get-tuple-element.39), channel_id=1, source_target_pairs={{0,2},{1,3},{2,0},{3,1},{4,6},{5,7},{6,4},{7,5},{8,10},{9,11},{10,... | collective-permute-start | bytes 786440 | tf_op jit(solution)/shard_map/ppermute | solution.py:594
  59.2 12.2 %collective-permute-start.13 = (f32[512,128]{1,0:T(8,128)S(1)}, f32[512,128]{1,0:T(8,128)S(1)}, u32[]{:S(2)}, u32[]{:S(2)}) collective-permute-start(f32[512,128]{1,0:T(8,128)S(1)} %get-tuple-element.38), channel_id=1, source_target_pairs={{0,1},{1,2},{2,3},{3,0},{4,5},{5,6},{6,7},{7,4},{8,9},{9,10},{10,1... | collective-permute-start | bytes 786440 | tf_op jit(solution)/shard_map/ppermute | solution.py:594

commit v8 on v7

--- a/solution.py
+++ b/solution.py
@@ -48,7 +48,7 @@
     return pltpu.roll(value, by % value.shape[axis], axis)
 
 
-def prep_kernel(table, phi, src, mat, temp, slab, body, sigma, inner, outer, src_v, mat_v, ends_t, ends_m, sems):
+def prep_kernel(table, phi, src, mat, temp, slab, body, s, sigma, inner, outer, src_v, mat_v, ends_t, ends_m, sems):
     rows = TE * ROW
     size_x, width = temp.shape
     moves = [(phi, body.at[0:rows]), (src, src_v), (mat, mat_v)]
@@ -61,7 +61,9 @@
     for move in moves:
         move.wait()
     sigma[...] = lookup(table, mat_v[...])
-    body[rows : 2 * rows] = src_v[...] / sigma[...]
+    s[...] = src_v[...] / sigma[...]
+    body[rows : 2 * rows] = s[...]
+    body[2 * rows : 3 * rows] = sigma[...]
     even = lax.rem(lax.axis_index("gx"), 2) == 0
 
     @pl.when(even)
@@ -192,9 +194,13 @@
     width_gy = 2 * chips
     tiles = width_gy * TILES
     none = tiles
-    bodies = refs[:width_gy]
-    halos = refs[width_gy : 2 * width_gy]
-    pot, slope, cell_at, cell_of, pa, pb, la, lb, ua, ub, s_c, s_l, s_u, sems, pot_sem = refs[2 * width_gy :]
+    half = 2 * chips - 1
+    halos = refs[2 * half : 2 * half + width_gy]
+    pot, slope, cell_at, cell_of, pa, pb, la, lb, ua, ub, s_c, s_l, s_u, sems, pot_sem = refs[2 * half + width_gy :]
+    bodies = []
+    for side in (refs[:half], refs[half : 2 * half]):
+        bodies.append(((side[0], 0), (side[0], TE * ROW)))
+        bodies += [((side[at], 0), (side[at + 1], 0)) for at in range(1, half, 2)]
     i = lax.axis_index("gx")
     j = lax.axis_index("gy")
     rows_gx = lax.axis_size("gx")
@@ -203,7 +209,7 @@
     moves = []
     for part in range(width_gy):
         at = 0
-        pieces = [(bodies[part], 0, pa, part * C_SIZE + 1, TE), (bodies[part], TE * ROW, s_c, part * TE, TE)]
+        pieces = [(*bodies[part][0], pa, part * C_SIZE + 1, TE), (*bodies[part][1], s_c, part * TE, TE)]
         for target, first, count in (
             (la, part * L_SIZE, LOW[0]),
             (s_l, part * LOW[1], LOW[1]),
@@ -375,47 +381,22 @@
 def slab_steps_kernel(chips, pos, k0_table, beta_table, *refs):
     width_gy = 2 * chips
     tiles = width_gy * TILES
-    sigmas = refs[:width_gy]
     halos = refs[width_gy : 2 * width_gy]
     slope, t_in, k0_in, b_in, y_in, y_out, temp_out = refs[2 * width_gy : 2 * width_gy + 7]
     sends = refs[2 * width_gy + 7 : 3 * width_gy + 7]
-    heat, q_ext, temp_a, temp_b, cond_a, cond_b, k0_all, b_all, blocks = refs[3 * width_gy + 7 :]
+    heat, q_ext, temp_a, temp_b, cond_a, cond_b, k0_all, b_all, blocks, sigmas, sems = refs[3 * width_gy + 7 :]
+    moves = []
+    for part in range(width_gy):
+        start = 2 * TE * ROW if part % chips == 0 else 0
+        source = refs[part].at[start : start + TE * ROW]
+        moves.append(pltpu.make_async_copy(source, sigmas.at[part], sems.at[part]))
+        moves[-1].start()
     i = lax.axis_index("gx")
     j = lax.axis_index("gy")
     rows_gx = lax.axis_size("gx")
     lane = lax.broadcasted_iota(jnp.int32, (SUB, LANES), 1)
     zero = jnp.zeros((SUB, LANES), jnp.float32)
 
-    def clear(at, carry):
-        heat[pl.ds(pl.multiple_of(at * SUB, SUB), SUB), :] = zero
-        return carry
-
-    lax.fori_loop(0, heat.shape[0] // SUB, clear, 0, unroll=8)
-    low_at, high_at = (LOW[0] + LOW[1]) * ROW, LOW_ROWS + (HIGH[0] + HIGH[1]) * ROW
-    for part in range(width_gy):
-        dev = part_device(part, chips, j)
-        for t in range(TILES):
-            for which, by in enumerate((0, -1, 1)):
-                tile = jnp.clip(i + by, 0, rows_gx - 1) * tiles + dev * TILES + t
-                cell = (pos[tile, 1] + 1) * 2 + pos[tile, 2]
-                local, inside = window(which, cell, i, j, rows_gx)
-                source, start, x, count = (
-                    (sigmas[part], 0, HALO, TE),
-                    (halos[part], low_at, HALO - 2, 2),
-                    (halos[part], high_at, HALO + TE, 2),
-                )[which]
-
-                @pl.when(inside)
-                def _():
-                    def plane(p, carry):
-                        rows = pl.ds(pl.multiple_of((local * SLABX + x + p) * SUB, SUB), SUB)
-                        at = pl.multiple_of(start + p * ROW, SUB)
-                        sigma = source[pl.ds(at + t, SUB, stride=TILES), :]
-                        heat[rows, :] = sigma * slope[rows, :]
-                        return carry
-
-                    lax.fori_loop(0, count, plane, 0, unroll=count)
-
     quarter = [(lane >= q * TE) & (lane < (q + 1) * TE) for q in range(3)]
 
     def pick(parts):
@@ -433,21 +414,6 @@
         return pl.ds(first, SUB)
 
     groups = SLABX // SUB
-
-    def place_heat(at, carry):
-        first = at - 1
-        col, yq = lax.div(first * 4 + TE, TE), lax.rem(first * 4 + TE, TE) // 4
-        for g in range(groups):
-            cells = [
-                heat[pl.ds(pl.multiple_of(((2 * col + c) * SLABX + g * SUB) * SUB, SUB) + yq, SUB, stride=SUB), :]
-                for c in range(4)
-            ]
-            for r in range(4):
-                block = 4 * first + r + HALO + 1
-                q_ext[rows_of(block, g)] = pick([turned(cells[c], c - r) for c in range(4)])
-        return carry
-
-    lax.fori_loop(0, HALF // 4 + 2, place_heat, 0, unroll=2)
 
     sub = lax.broadcasted_iota(jnp.int32, (SUB, LANES), 0)
     half = lane < NZ
@@ -506,6 +472,53 @@
         return carry
 
     lax.fori_loop(HALO, YBLOCKS - HALO, begin_inner, 0, unroll=4)
+
+    def clear(at, carry):
+        heat[pl.ds(pl.multiple_of(at * SUB, SUB), SUB), :] = zero
+        return carry
+
+    lax.fori_loop(0, heat.shape[0] // SUB, clear, 0, unroll=8)
+    for move in moves:
+        move.wait()
+    low_at, high_at = (LOW[0] + LOW[1]) * ROW, LOW_ROWS + (HIGH[0] + HIGH[1]) * ROW
+    for part in range(width_gy):
+        dev = part_device(part, chips, j)
+        for t in range(TILES):
+            for which, by in enumerate((0, -1, 1)):
+                tile = jnp.clip(i + by, 0, rows_gx - 1) * tiles + dev * TILES + t
+                cell = (pos[tile, 1] + 1) * 2 + pos[tile, 2]
+                local, inside = window(which, cell, i, j, rows_gx)
+                source, start, x, count = (
+                    (sigmas.at[part], 0, HALO, TE),
+                    (halos[part], low_at, HALO - 2, 2),
+                    (halos[part], high_at, HALO + TE, 2),
+                )[which]
+
+                @pl.when(inside)
+                def _():
+                    def plane(p, carry):
+                        rows = pl.ds(pl.multiple_of((local * SLABX + x + p) * SUB, SUB), SUB)
+                        at = pl.multiple_of(start + p * ROW, SUB)
+                        sigma = source[pl.ds(at + t, SUB, stride=TILES), :]
+                        heat[rows, :] = sigma * slope[rows, :]
+                        return carry
+
+                    lax.fori_loop(0, count, plane, 0, unroll=count)
+
+    def place_heat(at, carry):
+        first = at - 1
+        col, yq = lax.div(first * 4 + TE, TE), lax.rem(first * 4 + TE, TE) // 4
+        for g in range(groups):
+            cells = [
+                heat[pl.ds(pl.multiple_of(((2 * col + c) * SLABX + g * SUB) * SUB, SUB) + yq, SUB, stride=SUB), :]
+                for c in range(4)
+            ]
+            for r in range(4):
+                block = 4 * first + r + HALO + 1
+                q_ext[rows_of(block, g)] = pick([turned(cells[c], c - r) for c in range(4)])
+        return carry
+
+    lax.fori_loop(0, HALF // 4 + 2, place_heat, 0, unroll=2)
 
     for step in range(CSWEEPS):
         (t_src, c_src), (t_dst, c_dst) = ((temp_a, cond_a), (temp_b, cond_b))[:: 1 if step % 2 == 0 else -1]
@@ -612,18 +625,9 @@
     return value.reshape(-1, TILES, LANES).transpose(1, 0, 2).reshape(TILES, -1)
 
 
-def everyone(value, chips):
-    mine = [value] + [shifted(value, "gy", 2 * d, True) for d in range(1, chips)]
-    return mine + [from_mate(part) for part in mine]
-
-
-def everyone_direct(value, chips):
-    mine = [value] + [shifted(value, "gy", 2 * d, True) for d in range(1, chips)]
-    count = 2 * chips
-    for d in range(chips):
-        pairs = [(at, ((at ^ 1) + 2 * d) % count) for at in range(count)]
-        mine.append(lax.ppermute(value, "gy", pairs))
-    return mine
+def to_other_core(value, by):
+    count = lax.axis_size("gy")
+    return lax.ppermute(value, "gy", [(at, ((at ^ 1) + 2 * by) % count) for at in range(count)])
 
 
 VMEM = pl.BlockSpec(memory_space=pltpu.VMEM)
@@ -655,16 +659,19 @@
     def rows(count):
         return jax.ShapeDtypeStruct((count, LANES), f32)
 
-    body, sigma, inner, outer = pl.pallas_call(
+    phi = to_rows(phi_init)
+    phis = [shifted(phi, "gy", 2 * d, True) for d in range(1, chips)]
+    body, s, sigma, inner, outer = pl.pallas_call(
         prep_kernel,
         out_shape=(
-            rows(2 * TE * ROW),
+            rows(3 * TE * ROW),
+            rows(TE * ROW),
             rows(TE * ROW),
             rows(SIDE_ROWS + edge_rows),
             rows(SIDE_ROWS + edge_rows),
         ),
         in_specs=[SMEM] + [HBM] * 5,
-        out_specs=(VMEM,) * 4,
+        out_specs=(VMEM,) * 5,
         scratch_shapes=[
             pltpu.VMEM((TE * ROW, LANES), f32),
             pltpu.VMEM((TE * ROW, LANES), jnp.int32),
@@ -674,8 +681,11 @@
         ],
         compiler_params=pltpu.CompilerParams(vmem_limit_bytes=62 * 1024 * 1024),
         name="prep",
-    )(sigma_table, to_rows(phi_init), to_rows(source), to_rows(tile_mat), temp_init, slab_mat)
-    bodies = everyone(body, chips)
+    )(sigma_table, phi, to_rows(source), to_rows(tile_mat), temp_init, slab_mat)
+    bodies = [body]
+    for there, d in zip(phis, range(1, chips)):
+        bodies += [there, shifted(s, "gy", 2 * d, True)]
+    bodies += [from_mate(part) for part in bodies]
     inner, outer = with_partner(inner, "gx", 0), with_partner(outer, "gx", 1)
 
     halo = pl.pallas_call(
@@ -687,7 +697,8 @@
         name="relay",
     )(inner, outer)
     halos = [halo] + [shifted(halo, "gy", 2 * d, True) for d in range(1, chips)]
-    sigmas = everyone_direct(sigma, chips)
+    sigmas = [bodies[0]] + [shifted(sigma, "gy", 2 * d, True) for d in range(1, chips)]
+    sigmas += [bodies[2 * chips - 1]] + [to_other_core(sigma, d) for d in range(1, chips)]
 
     native = pltpu.VMEM((width // LANES * SLABX + SUB, LANES), f32)
     t_ext, k0_ext, b_ext, edge_in, edge_out = pl.pallas_call(
@@ -700,7 +711,7 @@
         name="slab_prep",
     )(tile_pos, k0_table, beta_table, temp_init, slab_mat, inner, outer)
     y_in, y_out = with_partner(edge_in, "gy", 0), with_partner(edge_out, "gy", 1)
-    *halos[1:], y_in, y_out = lax.optimization_barrier((*halos[1:], y_in, y_out))
+    *halos[1:], y_in = lax.optimization_barrier((*halos[1:], y_in))
     halos = halos + [from_mate(part) for part in halos]
 
     def fields(count):
@@ -709,7 +720,7 @@
     pot, slope = pl.pallas_call(
         functools.partial(sweep_kernel, chips),
         out_shape=(rows(TE * ROW), rows(8 * SLABX * SUB)),
-        in_specs=[SMEM] + [ANY] * (2 * width_gy),
+        in_specs=[SMEM] + [ANY] * (len(bodies) + width_gy),
         out_specs=(ANY, VMEM),
         scratch_shapes=[
             pltpu.SMEM((3, 2 * (2 * width_gy + 2)), jnp.int32),
@@ -726,12 +737,13 @@
     temp, *sends = pl.pallas_call(
         functools.partial(slab_steps_kernel, chips),
         out_shape=(jax.ShapeDtypeStruct((size_x, width), f32),) + (rows(TE * ROW),) * width_gy,
-        in_specs=[SMEM] * 3 + [VMEM] * (2 * width_gy + 6),
+        in_specs=[SMEM] * 3 + [ANY] * width_gy + [VMEM] * (width_gy + 6),
         out_specs=(VMEM,) * (1 + width_gy),
         scratch_shapes=[pltpu.VMEM((8 * SLABX * SUB, LANES), f32)]
         + [pltpu.VMEM((SLAB_ROWS + 3 * SLABX, LANES), f32)]
         + [pltpu.VMEM((SLAB_ROWS, LANES), f32)] * 6
-        + [pltpu.VMEM((4 * TE * SUB, LANES), f32)],
+        + [pltpu.VMEM((4 * TE * SUB, LANES), f32), pltpu.VMEM((width_gy, TE * ROW, LANES), f32)]
+        + [pltpu.SemaphoreType.DMA((width_gy,))],
         compiler_params=PARAMS,
         name="slab_steps",
     )(tile_pos, k0_table, beta_table, *sigmas, *halos, slope, t_ext, k0_ext, b_ext, y_in, y_out)

time: 72.6 us -> 70.9 us (0.977)
  starting transfers between devices: 16.4 us -> 13.5 us
  waiting for transfers between devices: 25.5 us -> 26.9 us
    ppermute x6 -> x7, starting transfers between devices: 12.1 us -> 7.61 us  [shifted(): return lax.ppermute(value, axis, pairs)]
    ppermute x4, waiting for transfers between devices: 2.05 us -> 6.42 us  [with_partner(): lax.ppermute(value, axis, pairs + [(high, low) for low, high in pairs])]
    ppermute x6 -> x7, waiting for transfers between devices: 22.3 us -> 19.8 us  [shifted(): return lax.ppermute(value, axis, pairs)]
    ppermute x4 -> x5, starting transfers between devices: 0.65 us -> 2.48 us  [from_mate(): lax.ppermute(value, 'gy', [(d, d ^ 1) for d in range(lax.axis_size('gy'))])]
  transfers between devices with their start and end apart: 16 -> 17, of which waited for: 6 -> 7; matrix products, arithmetic and copies ran while one was open for 0% -> 0% of each run, Pallas kernels for 22% -> 22%
where the time goes in v8:
time: 70.9 us; the launch traced here: 70.4 us
  Pallas kernels  28.4 us (40%)
  waiting for transfers between devices  26.9 us (38%)
  starting transfers between devices  13.5 us (19%)
  between operations  0.82 us (1%)
  other arithmetic  0.75 us (1%)
    ppermute x7, waiting for transfers between devices, shifted(): return lax.ppermute(value, axis, pairs)  19.8 us
    pallas_call x1, Pallas kernels, on_device(): pl.pallas_call(functools.partial(sweep_kernel, chips), out_shape=(rows(TE...  13.9 us
    pallas_call x1, Pallas kernels, on_device(): pl.pallas_call(functools.partial(slab_steps_kernel, chips), out_shape=(ja...  9.31 us
    ppermute x7, starting transfers between devices, shifted(): return lax.ppermute(value, axis, pairs)  7.61 us
    ppermute x4, waiting for transfers between devices, with_partner(): lax.ppermute(value, axis, pairs + [(high, low) for low, high in pairs])  6.42 us
    pallas_call x1, Pallas kernels, on_device(): pl.pallas_call(prep_kernel, out_shape=(rows(3 * TE * ROW), rows(TE * ROW)...  3.55 us
    ppermute x4, starting transfers between devices, with_partner(): lax.ppermute(value, axis, pairs + [(high, low) for low, high in pairs])  3.41 us
    ppermute x5, starting transfers between devices, from_mate(): lax.ppermute(value, 'gy', [(d, d ^ 1) for d in range(lax.axis_size('gy'))])  2.48 us
  transfers between devices with their start and end apart: 17, of which 7 were waited for; matrix products, arithmetic and copies ran while one was open for 0% of the time, Pallas kernels for 22%

profile of v8, /device:TPU:0, one launch (start us, length us, event | category | flops | bytes accessed | tf_op | source)
XLA Modules:
  0.0 70.4 jit_solution(15020311174938774195)
XLA Ops:
  0.7 3.6 %prep.1 = (f32[1536,128]{1,0:T(8,128)}, f32[512,128]{1,0:T(8,128)}, f32[512,128]{1,0:T(8,128)}, f32[496,128]{1,0:T(8,128)}, f32[496,128]{1,0:T(8,128)}) custom-call(f32[4]{0:T(128)} %table.1, f32[512,128]{1,0:T(8,128)} %bitcast.2.phi, f32[512,128]{1,0:T(8,128)} %bitcast.26, s32[512,128]{1,0:T(8,128)} %bitcast.27, f32[32,4096]{1,0:T(8,128)} %temp.3, ...), custom_call_target="tpu_custom_call" | custom-call | tf_op jit(solution)/shard_map/prep/pallas_call | solution.py:664
  4.3 0.5 collective-permute-start.2
  4.8 2.6 %collective-permute-start = (f32[512,128]{1,0:T(8,128)}, f32[512,128]{1,0:T(8,128)}, u32[]{:S(2)}, u32[]{:S(2)}) collective-permute-start(f32[512,128]{1,0:T(8,128)} %bitcast.2.phi), channel_id=1, source_target_pairs={{0,2},{1,3},{2,0},{3,1},{4,6},{5,7},{6,4},{7,5},{8,10},{9,11},{10,... | collective-permute-start | bytes 786440 | tf_op jit(solution)/shard_map/ppermute | solution.py:607
  7.3 1.5 %collective-permute-start.5 = (f32[496,128]{1,0:T(8,128)}, f32[496,128]{1,0:T(8,128)S(1)}, u32[]{:S(2)}, u32[]{:S(2)}) collective-permute-start(f32[496,128]{1,0:T(8,128)} %get-tuple-element.24), channel_id=1, source_target_pairs={{0,4},{8,12},{16,20},{24,28},{4,0},{12,8},{20,16},{28,24},{1,5},{9... | collective-permute-start | bytes 761864 | tf_op jit(solution)/shard_map/ppermute | solution.py:613
  8.9 0.7 collective-permute-start.6
  9.5 0.6 collective-permute-start.1
  10.1 4.7 %collective-permute-done.refs_1_ = f32[512,128]{1,0:T(8,128)} collective-permute-done((f32[512,128]{1,0:T(8,128)}, f32[512,128]{1,0:T(8,128)}, u32[]{:S(2)}, u32[]{:S(2)}) %collective-permute-start) | collective-permute-done | bytes 262176 | tf_op jit(solution)/shard_map/ppermute | solution.py:607
  14.8 0.0 collective-permute-start.3
  14.8 5.5 %collective-permute-done.5.inner = f32[496,128]{1,0:T(8,128)S(1)} collective-permute-done((f32[496,128]{1,0:T(8,128)}, f32[496,128]{1,0:T(8,128)S(1)}, u32[]{:S(2)}, u32[]{:S(2)}) %collective-permute-start.5) | collective-permute-done | bytes 253984 | tf_op jit(solution)/shard_map/ppermute | solution.py:613
  20.4 0.6 collective-permute-start.7
  21.0 0.1 copy.16.pos
  21.1 0.0 copy-start.6
  21.1 1.6 %slab_prep.1 = (f32[1552,128]{1,0:T(8,128)S(1)}, f32[1552,128]{1,0:T(8,128)S(1)}, f32[1552,128]{1,0:T(8,128)S(1)}, f32[120,128]{1,0:T(8,128)S(1)}, f32[120,128]{1,0:T(8,128)S(1)}) custom-call(s32[64,3]{1,0:T(8,128)S(1)} %copy.16.pos, f32[4]{0:T(128)S(1)} %copy-done.3, f32[4]{0:T(128)S(1)} %copy-done.4, f32[32,4096]{1,0:T(8,128)S(1)} %copy-done.1, ...), custom_call_target="tpu_custom_call" | custom-call | tf_op jit(solution)/shard_map/slab_prep/pallas_call | solution.py:704
  22.7 0.6 collective-permute-start.8
  23.3 0.9 %collective-permute-done.8.refs_12_ = f32[120,128]{1,0:T(8,128)S(1)} collective-permute-done((f32[120,128]{1,0:T(8,128)S(1)}, f32[120,128]{1,0:T(8,128)S(1)}, u32[]{:S(2)}, u32[]{:S(2)}) %collective-permute-start.8) | collective-permute-done | bytes 61472 | tf_op jit(solution)/shard_map/ppermute | solution.py:613
  24.2 0.4 collective-permute-start.4
  24.6 2.8 %collective-permute-done.7.refs_7_.refs_5_ = f32[448,128]{1,0:T(8,128)} collective-permute-done((f32[448,128]{1,0:T(8,128)S(1)}, f32[448,128]{1,0:T(8,128)}, u32[]{:S(2)}, u32[]{:S(2)}) %collective-permute-start.7) | collective-permute-done | bytes 229408 | tf_op jit(solution)/shard_map/ppermute | solution.py:607
  27.4 0.5 collective-permute-start.11
  27.9 0.0 collective-permute-done.9.refs_8_.refs_6_
  27.9 0.0 collective-permute-start.12
  27.9 1.6 %collective-permute-start.10 = (f32[448,128]{1,0:T(8,128)}, f32[448,128]{1,0:T(8,128)S(1)}, u32[]{:S(2)}, u32[]{:S(2)}) collective-permute-start(f32[448,128]{1,0:T(8,128)} %collective-permute-done.7.refs_7_.refs_5_), channel_id=1, source_target_pairs={{0,1},{1,0},{2,3},{3,2},{4,5},{5,4},{6,7},{7,6},{8,9},{9,8},{10,11... | collective-permute-start | bytes 688136 | tf_op jit(solution)/shard_map/ppermute | solution.py:617
  29.5 0.7 collective-permute-start.13
  30.2 0.7 collective-permute-done.10.refs_9_.refs_7_
  30.9 13.9 %sweeps.1 = (f32[512,128]{1,0:T(8,128)}, f32[2560,128]{1,0:T(8,128)S(1)}) custom-call(s32[64,3]{1,0:T(8,128)S(1)} %copy.16.pos, f32[1536,128]{1,0:T(8,128)S(1)} %copy-done, f32[512,128]{1,0:T(8,128)} %collective-permute-done.refs_1_, f32[512,128]{1,0:T(8,128)} %collective-permute-done.1.refs_2_, f32[1536,128]{1,0:T(8,128)S(1)} %collective-permute-done.2.refs_3_.refs_2_, ...), custom_call_target="tpu_custom_call" | custom-call | tf_op jit(solution)/shard_map/sweeps/pallas_call | solution.py:720
  44.7 0.0 collective-permute-done.11.refs_1_
  44.8 9.3 %slab_steps.1 = (f32[32,4096]{1,0:T(8,128)}, f32[512,128]{1,0:T(8,128)S(1)}, f32[512,128]{1,0:T(8,128)S(1)}, f32[512,128]{1,0:T(8,128)S(1)}, f32[512,128]{1,0:T(8,128)S(1)}) custom-call(s32[64,3]{1,0:T(8,128)S(1)} %copy.16.pos, f32[4]{0:T(128)S(1)} %copy-done.3, f32[4]{0:T(128)S(1)} %copy-done.4, f32[1536,128]{1,0:T(8,128)S(1)} %copy-done, ...), custom_call_target="tpu_custom_call" | custom-call | tf_op jit(solution)/shard_map/slab_steps/pallas_call | solution.py:737
  54.1 1.1 %collective-permute-start.16 = (f32[512,128]{1,0:T(8,128)S(1)}, f32[512,128]{1,0:T(8,128)S(1)}, u32[]{:S(2)}, u32[]{:S(2)}) collective-permute-start(f32[512,128]{1,0:T(8,128)S(1)} %get-tuple-element.40), channel_id=1, source_target_pairs={{0,3},{1,0},{2,1},{3,2},{4,7},{5,4},{6,5},{7,6},{8,11},{9,8},{10,9... | collective-permute-start | bytes 786440 | tf_op jit(solution)/shard_map/ppermute | solution.py:607
  55.2 2.2 %collective-permute-start.15 = (f32[512,128]{1,0:T(8,128)S(1)}, f32[512,128]{1,0:T(8,128)S(1)}, u32[]{:S(2)}, u32[]{:S(2)}) collective-permute-start(f32[512,128]{1,0:T(8,128)S(1)} %get-tuple-element.39), channel_id=1, source_target_pairs={{0,2},{1,3},{2,0},{3,1},{4,6},{5,7},{6,4},{7,5},{8,10},{9,11},{10,... | collective-permute-start | bytes 786440 | tf_op jit(solution)/shard_map/ppermute | solution.py:607
  57.4 0.0 collective-permute-start.14
  57.4 3.3 %collective-permute-done.16 = f32[512,128]{1,0:T(8,128)S(1)} collective-permute-done((f32[512,128]{1,0:T(8,128)S(1)}, f32[512,128]{1,0:T(8,128)S(1)}, u32[]{:S(2)}, u32[]{:S(2)}) %collective-permute-start.16) | collective-permute-done | bytes 262176 | tf_op jit(solution)/shard_map/ppermute | solution.py:607
  60.7 9.0 %collective-permute-done.15 = f32[512,128]{1,0:T(8,128)S(1)} collective-permute-done((f32[512,128]{1,0:T(8,128)S(1)}, f32[512,128]{1,0:T(8,128)S(1)}, u32[]{:S(2)}, u32[]{:S(2)}) %collective-permute-start.15) | collective-permute-done | bytes 262176 | tf_op jit(solution)/shard_map/ppermute | solution.py:607
  69.7 0.8 %add_add_fusion = f32[512,128]{1,0:T(8,128)} fusion(f32[512,128]{1,0:T(8,128)S(1)} %collective-permute-done.16, f32[512,128]{1,0:T(8,128)S(1)} %collective-permute-done.15, f32[512,128]{1,0:T(8,128)S(1)} %get-tuple-element.37, f32[512,128]{1,0:T(8,128)S(1)} %collective-permute-done.14), kind=kLoop, calls=%fused_computation | loop fusion | flops 196608 | bytes 1310720 | tf_op jit(solution)/shard_map/add | solution.py:752
  (23 shorter events, 0.1 us)
Async XLA Ops:
  0.6 20.4 %copy-start.1 = (f32[32,4096]{1,0:T(8,128)S(1)}, f32[32,4096]{1,0:T(8,128)}, u32[]{:S(2)}) copy-start(f32[32,4096]{1,0:T(8,128)} %temp.3) | copy-start | bytes 1572868
  0.6 20.4 %copy-start.2 = (s32[32,4096]{1,0:T(8,128)S(1)}, s32[32,4096]{1,0:T(8,128)}, u32[]{:S(2)}) copy-start(s32[32,4096]{1,0:T(8,128)} %mat.1) | copy-start | bytes 1572868
  0.7 20.3 %copy-start.5 = (s32[64,3]{0,1:T(4,128)S(1)}, s32[64,3]{0,1:T(4,128)}, u32[]{:S(2)}) copy-start(s32[64,3]{0,1:T(4,128)} %param.13) | copy-start | bytes 2308
  0.7 20.4 %copy-start.3 = (f32[4]{0:T(128)S(1)}, f32[4]{0:T(128)}, u32[]{:S(2)}) copy-start(f32[4]{0:T(128)} %k0_table.3) | copy-start | bytes 52
  0.7 20.4 %copy-start.4 = (f32[4]{0:T(128)S(1)}, f32[4]{0:T(128)}, u32[]{:S(2)}) copy-start(f32[4]{0:T(128)} %beta_table.3) | copy-start | bytes 52
  4.2 26.6 %copy-start = (f32[1536,128]{1,0:T(8,128)S(1)}, f32[1536,128]{1,0:T(8,128)}, u32[]{:S(2)}) copy-start(f32[1536,128]{1,0:T(8,128)} %get-tuple-element.22.refs_0_) | copy-start | bytes 2359300
  4.3 26.6 %collective-permute-start.2 = (f32[1536,128]{1,0:T(8,128)}, f32[1536,128]{1,0:T(8,128)S(1)}, u32[]{:S(2)}, u32[]{:S(2)}) collective-permute-start(f32[1536,128]{1,0:T(8,128)} %get-tuple-element.22.refs_0_), channel_id=1, source_target_pairs={{0,1},{1,0},{2,3},{3,2},{4,5},{5,4},{6,7},{7,6},{8,9},{9,8},{10,11... | collective-permute-start | bytes 2359304 | tf_op jit(solution)/shard_map/ppermute | solution.py:617
  4.8 10.0 %collective-permute-start = (f32[512,128]{1,0:T(8,128)}, f32[512,128]{1,0:T(8,128)}, u32[]{:S(2)}, u32[]{:S(2)}) collective-permute-start(f32[512,128]{1,0:T(8,128)} %bitcast.2.phi), channel_id=1, source_target_pairs={{0,2},{1,3},{2,0},{3,1},{4,6},{5,7},{6,4},{7,5},{8,10},{9,11},{10,... | collective-permute-start | bytes 786440 | tf_op jit(solution)/shard_map/ppermute | solution.py:607
  7.3 13.0 %collective-permute-start.5 = (f32[496,128]{1,0:T(8,128)}, f32[496,128]{1,0:T(8,128)S(1)}, u32[]{:S(2)}, u32[]{:S(2)}) collective-permute-start(f32[496,128]{1,0:T(8,128)} %get-tuple-element.24), channel_id=1, source_target_pairs={{0,4},{8,12},{16,20},{24,28},{4,0},{12,8},{20,16},{28,24},{1,5},{9... | collective-permute-start | bytes 761864 | tf_op jit(solution)/shard_map/ppermute | solution.py:613
  8.9 11.5 %collective-permute-start.6 = (f32[496,128]{1,0:T(8,128)}, f32[496,128]{1,0:T(8,128)S(1)}, u32[]{:S(2)}, u32[]{:S(2)}) collective-permute-start(f32[496,128]{1,0:T(8,128)} %get-tuple-element.25), channel_id=1, source_target_pairs={{4,8},{12,16},{20,24},{8,4},{16,12},{24,20},{5,9},{13,17},{21,25},... | collective-permute-start | bytes 761864 | tf_op jit(solution)/shard_map/ppermute | solution.py:613
  9.5 13.2 %collective-permute-start.1 = (f32[512,128]{1,0:T(8,128)}, f32[512,128]{1,0:T(8,128)}, u32[]{:S(2)}, u32[]{:S(2)}) collective-permute-start(f32[512,128]{1,0:T(8,128)} %get-tuple-element.23), channel_id=1, source_target_pairs={{0,2},{1,3},{2,0},{3,1},{4,6},{5,7},{6,4},{7,5},{8,10},{9,11},{10,... | collective-permute-start | bytes 786440 | tf_op jit(solution)/shard_map/ppermute | solution.py:607
  14.8 13.1 %collective-permute-start.3 = (f32[512,128]{1,0:T(8,128)}, f32[512,128]{1,0:T(8,128)}, u32[]{:S(2)}, u32[]{:S(2)}) collective-permute-start(f32[512,128]{1,0:T(8,128)} %collective-permute-done.refs_1_), channel_id=1, source_target_pairs={{0,1},{1,0},{2,3},{3,2},{4,5},{5,4},{6,7},{7,6},{8,9},{9,8},{10,11... | collective-permute-start | bytes 786440 | tf_op jit(solution)/shard_map/ppermute | solution.py:617
  20.4 7.0 %collective-permute-start.7 = (f32[448,128]{1,0:T(8,128)S(1)}, f32[448,128]{1,0:T(8,128)}, u32[]{:S(2)}, u32[]{:S(2)}) collective-permute-start(f32[448,128]{1,0:T(8,128)S(1)} %relay.1.refs_6_.refs_4_), channel_id=1, source_target_pairs={{0,2},{1,3},{2,0},{3,1},{4,6},{5,7},{6,4},{7,5},{8,10},{9,11},{10,... | collective-permute-start | bytes 688136 | tf_op jit(solution)/shard_map/ppermute | solution.py:607
  21.0 7.0 %collective-permute-start.9 = (f32[448,128]{1,0:T(8,128)S(1)}, f32[448,128]{1,0:T(8,128)}, u32[]{:S(2)}, u32[]{:S(2)}) collective-permute-start(f32[448,128]{1,0:T(8,128)S(1)} %relay.1.refs_6_.refs_4_), channel_id=1, source_target_pairs={{0,1},{1,0},{2,3},{3,2},{4,5},{5,4},{6,7},{7,6},{8,9},{9,8},{10,11... | collective-permute-start | bytes 688136 | tf_op jit(solution)/shard_map/ppermute | solution.py:617
  21.1 6.3 %copy-start.6 = (f32[512,128]{1,0:T(8,128)S(1)}, f32[512,128]{1,0:T(8,128)}, u32[]{:S(2)}) copy-start(f32[512,128]{1,0:T(8,128)} %get-tuple-element.29) | copy-start | bytes 786436
  22.7 1.5 %collective-permute-start.8 = (f32[120,128]{1,0:T(8,128)S(1)}, f32[120,128]{1,0:T(8,128)S(1)}, u32[]{:S(2)}, u32[]{:S(2)}) collective-permute-start(f32[120,128]{1,0:T(8,128)S(1)} %get-tuple-element.26), channel_id=1, source_target_pairs={{0,1},{2,3},{1,0},{3,2},{4,5},{6,7},{5,4},{7,6},{8,9},{10,11},{9,8... | collective-permute-start | bytes 184328 | tf_op jit(solution)/shard_map/ppermute | solution.py:613
  24.2 5.3 %collective-permute-start.4 = (f32[512,128]{1,0:T(8,128)}, f32[512,128]{1,0:T(8,128)S(1)}, u32[]{:S(2)}, u32[]{:S(2)}) collective-permute-start(f32[512,128]{1,0:T(8,128)} %collective-permute-done.1.refs_2_), channel_id=1, source_target_pairs={{0,1},{1,0},{2,3},{3,2},{4,5},{5,4},{6,7},{7,6},{8,9},{9,8},{10,11... | collective-permute-start | bytes 786440 | tf_op jit(solution)/shard_map/ppermute | solution.py:617
  27.4 17.4 %collective-permute-start.11 = (f32[512,128]{1,0:T(8,128)S(1)}, f32[512,128]{1,0:T(8,128)S(1)}, u32[]{:S(2)}, u32[]{:S(2)}) collective-permute-start(f32[512,128]{1,0:T(8,128)S(1)} %copy-done.6), channel_id=1, source_target_pairs={{0,2},{1,3},{2,0},{3,1},{4,6},{5,7},{6,4},{7,5},{8,10},{9,11},{10,... | collective-permute-start | bytes 786440 | tf_op jit(solution)/shard_map/ppermute | solution.py:607
  27.9 16.8 %collective-permute-start.12 = (f32[512,128]{1,0:T(8,128)S(1)}, f32[512,128]{1,0:T(8,128)S(1)}, u32[]{:S(2)}, u32[]{:S(2)}) collective-permute-start(f32[512,128]{1,0:T(8,128)S(1)} %copy-done.6), channel_id=1, source_target_pairs={{0,3},{1,2},{2,1},{3,0},{4,7},{5,6},{6,5},{7,4},{8,11},{9,10},{10,... | collective-permute-start | bytes 786440 | tf_op jit(solution)/shard_map/ppermute | solution.py:630
  27.9 2.9 %collective-permute-start.10 = (f32[448,128]{1,0:T(8,128)}, f32[448,128]{1,0:T(8,128)S(1)}, u32[]{:S(2)}, u32[]{:S(2)}) collective-permute-start(f32[448,128]{1,0:T(8,128)} %collective-permute-done.7.refs_7_.refs_5_), channel_id=1, source_target_pairs={{0,1},{1,0},{2,3},{3,2},{4,5},{5,4},{6,7},{7,6},{8,9},{9,8},{10,11... | collective-permute-start | bytes 688136 | tf_op jit(solution)/shard_map/ppermute | solution.py:617
  29.5 15.2 %collective-permute-start.13 = (f32[120,128]{1,0:T(8,128)S(1)}, f32[120,128]{1,0:T(8,128)S(1)}, u32[]{:S(2)}, u32[]{:S(2)}) collective-permute-start(f32[120,128]{1,0:T(8,128)S(1)} %get-tuple-element.35), channel_id=1, source_target_pairs={{1,2},{2,1},{5,6},{6,5},{9,10},{10,9},{13,14},{14,13},{17,18},{18,... | collective-permute-start | bytes 184328 | tf_op jit(solution)/shard_map/ppermute | solution.py:613
  54.1 6.6 %collective-permute-start.16 = (f32[512,128]{1,0:T(8,128)S(1)}, f32[512,128]{1,0:T(8,128)S(1)}, u32[]{:S(2)}, u32[]{:S(2)}) collective-permute-start(f32[512,128]{1,0:T(8,128)S(1)} %get-tuple-element.40), channel_id=1, source_target_pairs={{0,3},{1,0},{2,1},{3,2},{4,7},{5,4},{6,5},{7,6},{8,11},{9,8},{10,9... | collective-permute-start | bytes 786440 | tf_op jit(solution)/shard_map/ppermute | solution.py:607
  55.2 14.5 %collective-permute-start.15 = (f32[512,128]{1,0:T(8,128)S(1)}, f32[512,128]{1,0:T(8,128)S(1)}, u32[]{:S(2)}, u32[]{:S(2)}) collective-permute-start(f32[512,128]{1,0:T(8,128)S(1)} %get-tuple-element.39), channel_id=1, source_target_pairs={{0,2},{1,3},{2,0},{3,1},{4,6},{5,7},{6,4},{7,5},{8,10},{9,11},{10,... | collective-permute-start | bytes 786440 | tf_op jit(solution)/shard_map/ppermute | solution.py:607
  57.4 12.3 %collective-permute-start.14 = (f32[512,128]{1,0:T(8,128)S(1)}, f32[512,128]{1,0:T(8,128)S(1)}, u32[]{:S(2)}, u32[]{:S(2)}) collective-permute-start(f32[512,128]{1,0:T(8,128)S(1)} %get-tuple-element.38), channel_id=1, source_target_pairs={{0,1},{1,2},{2,3},{3,0},{4,5},{5,6},{6,7},{7,4},{8,9},{9,10},{10,1... | collective-permute-start | bytes 786440 | tf_op jit(solution)/shard_map/ppermute | solution.py:607

commit v9 on v8

--- a/solution.py
+++ b/solution.py
@@ -383,8 +383,9 @@
     tiles = width_gy * TILES
     halos = refs[width_gy : 2 * width_gy]
     slope, t_in, k0_in, b_in, y_in, y_out, temp_out = refs[2 * width_gy : 2 * width_gy + 7]
-    sends = refs[2 * width_gy + 7 : 3 * width_gy + 7]
-    heat, q_ext, temp_a, temp_b, cond_a, cond_b, k0_all, b_all, blocks, sigmas, sems = refs[3 * width_gy + 7 :]
+    mine, bundle = refs[2 * width_gy + 7 : 2 * width_gy + 9]
+    across = refs[2 * width_gy + 9 : 2 * width_gy + 8 + chips]
+    heat, q_ext, state_a, state_b, k0_all, b_all, blocks, sigmas, sems = refs[2 * width_gy + 8 + chips :]
     moves = []
     for part in range(width_gy):
         start = 2 * TE * ROW if part % chips == 0 else 0
@@ -418,27 +419,28 @@
     sub = lax.broadcasted_iota(jnp.int32, (SUB, LANES), 0)
     half = lane < NZ
     no_z = lane % NZ == NZ - 1
-    low_x = (sub == HALO - 1) & (i == 0)
+    low_x = (sub == HALO - 1) & (i == 0), (sub == HALO) & (i == 0)
     high_x = (sub == (HALO + TE - 1) % SUB) & (i == rows_gx - 1)
     low_y, high_y = half & (j == 0), (lane >= NZ) & (j == width_gy - 1)
-
-    first_sub, last_sub = sub == 0, sub == SUB - 1
 
     def inverse(value):
         near = pl.reciprocal(value, approx=True)
         near = near * (2.0 - value * near)
         return near * (2.0 - value * near)
 
-    def load(ref, block):
-        return [ref[rows_of(block, g)] for g in range(groups)]
-
-    def next_x(values):
-        up = [roll(v, -1, 0) for v in values]
-        return [jnp.where(last_sub, up[min(g + 1, groups - 1)], up[g]) for g in range(groups)]
-
-    def last_x(values):
-        down = [roll(v, 1, 0) for v in values]
-        return [jnp.where(first_sub, down[max(g - 1, 0)], down[g]) for g in range(groups)]
+    def both_of(block, g, by=0):
+        first = 2 * (ROW0 + block * SLABX + g * SUB + by)
+        return pl.ds(first, SUB, stride=2), pl.ds(first + 1, SUB, stride=2)
+
+    def load(ref, block, by=0):
+        places = [both_of(block, g, by) for g in range(groups)]
+        return [ref[at, :] for at, _ in places], [ref[at, :] for _, at in places]
+
+    def store(ref, block, g, temp, cond=None):
+        first, second = both_of(block, g)
+        ref[first, :] = temp
+        if cond is not None:
+            ref[second, :] = cond
 
     even = lax.rem(j, 2) == 0
 
@@ -460,8 +462,9 @@
                     k0 = jnp.where(half, k0, lookup(k0_table, value))
                     beta = jnp.where(half, beta, lookup(beta_table, value))
             values.append((rows, temp, k0, beta, k0 * inverse(1.0 + beta * temp * temp)))
-        for rows, temp, k0, beta, cond in values:
-            temp_a[rows], k0_all[rows], b_all[rows], cond_a[rows] = temp, k0, beta, cond
+        for g, (rows, temp, k0, beta, cond) in enumerate(values):
+            k0_all[rows], b_all[rows] = k0, beta
+            store(state_a, block, g, temp, cond)
 
     for e in range(HALO):
         begin(e, True, e)
@@ -521,52 +524,49 @@
     lax.fori_loop(0, HALF // 4 + 2, place_heat, 0, unroll=2)
 
     for step in range(CSWEEPS):
-        (t_src, c_src), (t_dst, c_dst) = ((temp_a, cond_a), (temp_b, cond_b))[:: 1 if step % 2 == 0 else -1]
-
-        def y_fluxes(block, temp, cond, temp_n, cond_n):
+        src, dst = (state_a, state_b)[:: 1 if step % 2 == 0 else -1]
+
+        def y_fluxes(block, now, ahead):
             closed = (low_y & (block == HALO - 1)) | (high_y & (block == HALO + HALF - 1))
-            return [
-                jnp.where(closed, 0.0, (cond[g] + cond_n[g]) * (temp_n[g] - temp[g])) for g in range(groups)
-            ]
+            return [flux(now, ahead, g, closed) for g in range(groups)]
+
+        def flux(now, other, g, closed=None):
+            value = (now[1][g] + other[1][g]) * (other[0][g] - now[0][g])
+            return value if closed is None else jnp.where(closed, 0.0, value)
 
         def advance(block, carry):
-            temp, cond, before = carry
-            temp_n, cond_n = load(t_src, block + 1), load(c_src, block + 1)
-            flux_y = y_fluxes(block, temp, cond, temp_n, cond_n)
-            temp_x, cond_x = next_x(temp), next_x(cond)
-            flux_x = [(cond[g] + cond_x[g]) * (temp_x[g] - temp[g]) for g in range(groups)]
-            flux_x[0] = jnp.where(low_x, 0.0, flux_x[0])
-            flux_x[-1] = jnp.where(high_x, 0.0, flux_x[-1])
-            back_x = last_x(flux_x)
+            now, before = carry
+            ahead = load(src, block + 1)
+            flux_y = y_fluxes(block, now, ahead)
+            x_p, x_m = load(src, block, 1), load(src, block, -1)
             results = []
             for g in range(groups):
-                flux_z = (cond[g] + roll(cond[g], -1, 1)) * (roll(temp[g], -1, 1) - temp[g])
+                temp, cond = now[0][g], now[1][g]
+                up = flux(now, x_p, g, {0: low_x[0], groups - 1: high_x}.get(g))
+                down = flux(now, x_m, g, {0: low_x[1]}.get(g))
+                flux_z = (cond + roll(cond, -1, 1)) * (roll(temp, -1, 1) - temp)
                 flux_z = jnp.where(no_z, 0.0, flux_z)
-                div = (flux_y[g] - before[g]) + (flux_x[g] - back_x[g]) + (flux_z - roll(flux_z, 1, 1))
-                new = temp[g] + DT * (0.5 * div + q_ext[rows_of(block + 1, g)])
+                div = (flux_y[g] - before[g]) + (up + down) + (flux_z - roll(flux_z, 1, 1))
+                new = temp + DT * (0.5 * div + q_ext[rows_of(block + 1, g)])
                 if step < CSWEEPS - 1:
                     rows = rows_of(block, g)
                     results.append((new, k0_all[rows] * inverse(1.0 + b_all[rows] * new * new)))
                 else:
-                    results.append((new, None))
+                    results.append((new,))
             for g in range(groups):
-                t_dst[rows_of(block, g)] = results[g][0]
-                if step < CSWEEPS - 1:
-                    c_dst[rows_of(block, g)] = results[g][1]
-            return temp_n, cond_n, flux_y
-
-        first = (load(t_src, 0), load(c_src, 0))
-        second = (load(t_src, 1), load(c_src, 1))
-        lax.fori_loop(1, YBLOCKS - 1, advance, (*second, y_fluxes(0, *first, *second)), unroll=6)
-    final = temp_b if CSWEEPS % 2 else temp_a
+                store(dst, block, g, *results[g])
+            return ahead, flux_y
+
+        first, second = load(src, 0), load(src, 1)
+        lax.fori_loop(1, YBLOCKS - 1, advance, (second, y_fluxes(0, first, second)), unroll=6)
+    final = state_b if CSWEEPS % 2 else state_a
 
     def give_out(yq, carry):
         for g in range(TE // SUB):
             x = slice(g * SUB, (g + 1) * SUB)
             turns = []
             for r in range(4):
-                here, after = (final[rows_of(HALO + 4 * yq + r, at)] for at in (g, g + 1))
-                value = jnp.where(sub < SUB - HALO, roll(here, -HALO, 0), roll(after, -HALO, 0))
+                value = final[both_of(HALO + 4 * yq + r, g, HALO)[0], :]
                 turns.append([turned(value, by) for by in range(4)])
             for pair in range(2):
                 even, odd = turns[2 * pair], turns[2 * pair + 1]
@@ -581,21 +581,24 @@
 
     lax.fori_loop(0, HALF // 4, give_out, 0, unroll=2)
     places = []
-    for shift in range(width_gy):
-        dev = lax.rem(j + shift, width_gy)
+    mate = j + 1 - 2 * lax.rem(j, 2)
+    targets = [(mine, 0, j)] + [(across[d - 1], 0, j + 2 * d) for d in range(1, chips)]
+    targets += [(bundle, d * TE * ROW, mate + 2 * d) for d in range(chips)]
+    for target, first, to in targets:
+        dev = lax.rem(to, width_gy)
         for t in range(TILES):
             tile = i * tiles + dev * TILES + t
             col = pos[tile, 1] - 2 * j
             cell = jnp.clip(col, 0, 1) * 2 + pos[tile, 2]
-            places.append((sends[shift], t, cell, (col >= 0) & (col < 2)))
+            places.append((target, first + t, cell, (col >= 0) & (col < 2)))
 
     def pack(p, carry):
         values = []
-        for target, t, cell, here in places:
+        for _, _, cell, here in places:
             value = blocks[pl.ds(pl.multiple_of((cell * TE + p) * SUB, SUB), SUB), :]
             values.append(jnp.where(here, value, 0.0))
-        for (target, t, cell, here), value in zip(places, values):
-            target[pl.ds(pl.multiple_of(p * ROW, ROW) + t, SUB, stride=TILES), :] = value
+        for (target, first, _, _), value in zip(places, values):
+            target[pl.ds(pl.multiple_of(p * ROW, ROW) + first, SUB, stride=TILES), :] = value
         return carry
 
     lax.fori_loop(0, TE, pack, 0, unroll=4)
@@ -734,22 +737,25 @@
         name="sweeps",
     )(tile_pos, *bodies, *halos)
 
-    temp, *sends = pl.pallas_call(
+    temp, mine, bundle, *across = pl.pallas_call(
         functools.partial(slab_steps_kernel, chips),
-        out_shape=(jax.ShapeDtypeStruct((size_x, width), f32),) + (rows(TE * ROW),) * width_gy,
+        out_shape=(jax.ShapeDtypeStruct((size_x, width), f32), rows(TE * ROW), rows(chips * TE * ROW))
+        + (rows(TE * ROW),) * (chips - 1),
         in_specs=[SMEM] * 3 + [ANY] * width_gy + [VMEM] * (width_gy + 6),
-        out_specs=(VMEM,) * (1 + width_gy),
+        out_specs=(VMEM,) * (2 + chips),
         scratch_shapes=[pltpu.VMEM((8 * SLABX * SUB, LANES), f32)]
         + [pltpu.VMEM((SLAB_ROWS + 3 * SLABX, LANES), f32)]
-        + [pltpu.VMEM((SLAB_ROWS, LANES), f32)] * 6
+        + [pltpu.VMEM((2 * SLAB_ROWS, LANES), f32)] * 2
+        + [pltpu.VMEM((SLAB_ROWS, LANES), f32)] * 2
         + [pltpu.VMEM((4 * TE * SUB, LANES), f32), pltpu.VMEM((width_gy, TE * ROW, LANES), f32)]
         + [pltpu.SemaphoreType.DMA((width_gy,))],
         compiler_params=PARAMS,
         name="slab_steps",
     )(tile_pos, k0_table, beta_table, *sigmas, *halos, slope, t_ext, k0_ext, b_ext, y_in, y_out)
-    tile_temps = sends[0]
-    for by in range(1, width_gy):
-        tile_temps = tile_temps + shifted(sends[by], "gy", by, True)
+    got = from_mate(bundle).reshape(chips, TE * ROW, LANES)
+    tile_temps = mine + got[0]
+    for d in range(1, chips):
+        tile_temps = tile_temps + shifted(across[d - 1] + got[d], "gy", 2 * d, True)
     return from_rows(pot), temp, from_rows(tile_temps)
 
 

time: 70.9 us -> 67.3 us (0.949)
  waiting for transfers between devices: 26.9 us -> 23.6 us
    ppermute x7 -> x5, waiting for transfers between devices: 19.8 us -> 15 us  [shifted(): return lax.ppermute(value, axis, pairs)]
    ppermute x7 -> x5, starting transfers between devices: 7.61 us -> 5.51 us  [shifted(): return lax.ppermute(value, axis, pairs)]
    ppermute x5 -> x6, waiting for transfers between devices: 0.67 us -> 2.21 us  [from_mate(): lax.ppermute(value, 'gy', [(d, d ^ 1) for d in range(lax.axis_size('gy'))])]
    ppermute x5 -> x6, starting transfers between devices: 2.48 us -> 3.89 us  [from_mate(): lax.ppermute(value, 'gy', [(d, d ^ 1) for d in range(lax.axis_size('gy'))])]
  transfers between devices with their start and end apart: 17 -> 16, of which waited for: 7 -> 7; matrix products, arithmetic and copies ran while one was open for 0% -> 0% of each run, Pallas kernels for 22% -> 24%
where the time goes in v9:
time: 67.3 us; the launch traced here: 67 us
  Pallas kernels  28.9 us (43%)
  waiting for transfers between devices  23.6 us (35%)
  starting transfers between devices  12.8 us (19%)
  between operations  0.82 us (1%)
  other arithmetic  0.79 us (1%)
    ppermute x5, waiting for transfers between devices, shifted(): return lax.ppermute(value, axis, pairs)  15 us
    pallas_call x1, Pallas kernels, on_device(): pl.pallas_call(functools.partial(sweep_kernel, chips), out_shape=(rows(TE...  14.4 us
    pallas_call x1, Pallas kernels, on_device(): pl.pallas_call(functools.partial(slab_steps_kernel, chips), out_shape=(ja...  9.37 us
    ppermute x4, waiting for transfers between devices, with_partner(): lax.ppermute(value, axis, pairs + [(high, low) for low, high in pairs])  6.42 us
    ppermute x5, starting transfers between devices, shifted(): return lax.ppermute(value, axis, pairs)  5.51 us
    ppermute x6, starting transfers between devices, from_mate(): lax.ppermute(value, 'gy', [(d, d ^ 1) for d in range(lax.axis_size('gy'))])  3.89 us
    pallas_call x1, Pallas kernels, on_device(): pl.pallas_call(prep_kernel, out_shape=(rows(3 * TE * ROW), rows(TE * ROW)...  3.54 us
    ppermute x4, starting transfers between devices, with_partner(): lax.ppermute(value, axis, pairs + [(high, low) for low, high in pairs])  3.41 us
  transfers between devices with their start and end apart: 16, of which 7 were waited for; matrix products, arithmetic and copies ran while one was open for 0% of the time, Pallas kernels for 24%

profile of v9, /device:TPU:0, one launch (start us, length us, event | category | flops | bytes accessed | tf_op | source)
XLA Modules:
  0.0 67.0 jit_solution(9781077200206221300)
XLA Ops:
  0.7 3.5 %prep.1 = (f32[1536,128]{1,0:T(8,128)}, f32[512,128]{1,0:T(8,128)}, f32[512,128]{1,0:T(8,128)}, f32[496,128]{1,0:T(8,128)}, f32[496,128]{1,0:T(8,128)}) custom-call(f32[4]{0:T(128)} %table.1, f32[512,128]{1,0:T(8,128)} %bitcast.2.phi, f32[512,128]{1,0:T(8,128)} %bitcast.25, s32[512,128]{1,0:T(8,128)} %bitcast.26, f32[32,4096]{1,0:T(8,128)} %temp.3, ...), custom_call_target="tpu_custom_call" | custom-call | tf_op jit(solution)/shard_map/prep/pallas_call | solution.py:667
  4.2 0.5 collective-permute-start.2
  4.8 2.6 %collective-permute-start = (f32[512,128]{1,0:T(8,128)}, f32[512,128]{1,0:T(8,128)}, u32[]{:S(2)}, u32[]{:S(2)}) collective-permute-start(f32[512,128]{1,0:T(8,128)} %bitcast.2.phi), channel_id=1, source_target_pairs={{0,2},{1,3},{2,0},{3,1},{4,6},{5,7},{6,4},{7,5},{8,10},{9,11},{10,... | collective-permute-start | bytes 786440 | tf_op jit(solution)/shard_map/ppermute | solution.py:610
  7.3 1.5 %collective-permute-start.5 = (f32[496,128]{1,0:T(8,128)}, f32[496,128]{1,0:T(8,128)S(1)}, u32[]{:S(2)}, u32[]{:S(2)}) collective-permute-start(f32[496,128]{1,0:T(8,128)} %get-tuple-element.23), channel_id=1, source_target_pairs={{0,4},{8,12},{16,20},{24,28},{4,0},{12,8},{20,16},{28,24},{1,5},{9... | collective-permute-start | bytes 761864 | tf_op jit(solution)/shard_map/ppermute | solution.py:616
  8.8 0.7 collective-permute-start.6
  9.5 0.6 collective-permute-start.1
  10.1 4.7 %collective-permute-done.refs_1_ = f32[512,128]{1,0:T(8,128)} collective-permute-done((f32[512,128]{1,0:T(8,128)}, f32[512,128]{1,0:T(8,128)}, u32[]{:S(2)}, u32[]{:S(2)}) %collective-permute-start) | collective-permute-done | bytes 262176 | tf_op jit(solution)/shard_map/ppermute | solution.py:610
  14.8 5.5 %collective-permute-done.5.inner = f32[496,128]{1,0:T(8,128)S(1)} collective-permute-done((f32[496,128]{1,0:T(8,128)}, f32[496,128]{1,0:T(8,128)S(1)}, u32[]{:S(2)}, u32[]{:S(2)}) %collective-permute-start.5) | collective-permute-done | bytes 253984 | tf_op jit(solution)/shard_map/ppermute | solution.py:616
  20.3 0.0 collective-permute-done.6.outer
  20.4 0.6 collective-permute-start.7
  21.0 0.0 collective-permute-start.9
  21.0 0.1 copy.16.pos
  21.1 0.0 copy-start.6
  21.1 1.6 %slab_prep.1 = (f32[1552,128]{1,0:T(8,128)S(1)}, f32[1552,128]{1,0:T(8,128)S(1)}, f32[1552,128]{1,0:T(8,128)S(1)}, f32[120,128]{1,0:T(8,128)S(1)}, f32[120,128]{1,0:T(8,128)S(1)}) custom-call(s32[64,3]{1,0:T(8,128)S(1)} %copy.16.pos, f32[4]{0:T(128)S(1)} %copy-done.3, f32[4]{0:T(128)S(1)} %copy-done.4, f32[32,4096]{1,0:T(8,128)S(1)} %copy-done.1, ...), custom_call_target="tpu_custom_call" | custom-call | tf_op jit(solution)/shard_map/slab_prep/pallas_call | solution.py:707
  22.7 0.0 collective-permute-done.1.refs_2_
  22.7 0.6 collective-permute-start.8
  23.3 0.9 %collective-permute-done.8.refs_12_ = f32[120,128]{1,0:T(8,128)S(1)} collective-permute-done((f32[120,128]{1,0:T(8,128)S(1)}, f32[120,128]{1,0:T(8,128)S(1)}, u32[]{:S(2)}, u32[]{:S(2)}) %collective-permute-start.8) | collective-permute-done | bytes 61472 | tf_op jit(solution)/shard_map/ppermute | solution.py:616
  24.2 0.4 collective-permute-start.4
  24.5 2.8 %collective-permute-done.7.refs_7_.refs_5_ = f32[448,128]{1,0:T(8,128)} collective-permute-done((f32[448,128]{1,0:T(8,128)S(1)}, f32[448,128]{1,0:T(8,128)}, u32[]{:S(2)}, u32[]{:S(2)}) %collective-permute-start.7) | collective-permute-done | bytes 229408 | tf_op jit(solution)/shard_map/ppermute | solution.py:610
  27.4 0.5 collective-permute-start.11
  27.9 0.0 collective-permute-done.3.refs_4_
  27.9 1.6 %collective-permute-start.10 = (f32[448,128]{1,0:T(8,128)}, f32[448,128]{1,0:T(8,128)S(1)}, u32[]{:S(2)}, u32[]{:S(2)}) collective-permute-start(f32[448,128]{1,0:T(8,128)} %collective-permute-done.7.refs_7_.refs_5_), channel_id=1, source_target_pairs={{0,1},{1,0},{2,3},{3,2},{4,5},{5,4},{6,7},{7,6},{8,9},{9,8},{10,11... | collective-permute-start | bytes 688136 | tf_op jit(solution)/shard_map/ppermute | solution.py:620
  29.5 0.0 collective-permute-done.4.refs_5_
  29.5 0.7 collective-permute-start.13
  30.2 0.7 collective-permute-done.10.refs_9_.refs_7_
  30.9 14.4 %sweeps.1 = (f32[512,128]{1,0:T(8,128)}, f32[2560,128]{1,0:T(8,128)S(1)}) custom-call(s32[64,3]{1,0:T(8,128)S(1)} %copy.16.pos, f32[1536,128]{1,0:T(8,128)S(1)} %copy-done, f32[512,128]{1,0:T(8,128)} %collective-permute-done.refs_1_, f32[512,128]{1,0:T(8,128)} %collective-permute-done.1.refs_2_, f32[1536,128]{1,0:T(8,128)S(1)} %collective-permute-done.2.refs_3_.refs_2_, ...), custom_call_target="tpu_custom_call" | custom-call | tf_op jit(solution)/shard_map/sweeps/pallas_call | solution.py:723
  45.3 9.4 %slab_steps.1 = (f32[32,4096]{1,0:T(8,128)}, f32[512,128]{1,0:T(8,128)S(1)}, f32[1024,128]{1,0:T(8,128)S(1)}, f32[512,128]{1,0:T(8,128)S(1)}) custom-call(s32[64,3]{1,0:T(8,128)S(1)} %copy.16.pos, f32[4]{0:T(128)S(1)} %copy-done.3, f32[4]{0:T(128)S(1)} %copy-done.4, f32[1536,128]{1,0:T(8,128)S(1)} %copy-done, ...), custom_call_target="tpu_custom_call" | custom-call | tf_op jit(solution)/shard_map/slab_steps/pallas_call | solution.py:740
  54.7 1.4 %collective-permute-start.14 = (f32[1024,128]{1,0:T(8,128)S(1)}, f32[1024,128]{1,0:T(8,128)S(1)}, u32[]{:S(2)}, u32[]{:S(2)}) collective-permute-start(f32[1024,128]{1,0:T(8,128)S(1)} %get-tuple-element.37), channel_id=1, source_target_pairs={{0,1},{1,0},{2,3},{3,2},{4,5},{5,4},{6,7},{7,6},{8,9},{9,8},{10,11... | collective-permute-start | bytes 1572872 | tf_op jit(solution)/shard_map/ppermute | solution.py:620
  56.1 1.5 %collective-permute-done.14 = f32[1024,128]{1,0:T(8,128)S(1)} collective-permute-done((f32[1024,128]{1,0:T(8,128)S(1)}, f32[1024,128]{1,0:T(8,128)S(1)}, u32[]{:S(2)}, u32[]{:S(2)}) %collective-permute-start.14) | collective-permute-done | bytes 524320 | tf_op jit(solution)/shard_map/ppermute | solution.py:620
  57.6 1.2 %collective-permute-start.15 = (f32[512,128]{1,0:T(8,128)S(1)}, f32[512,128]{1,0:T(8,128)S(1)}, u32[]{:S(2)}, u32[]{:S(2)}) collective-permute-start(f32[512,128]{1,0:T(8,128)S(1)} %slice_add_fusion), channel_id=1, source_target_pairs={{0,2},{1,3},{2,0},{3,1},{4,6},{5,7},{6,4},{7,5},{8,10},{9,11},{10,... | collective-permute-start | bytes 786440 | tf_op jit(solution)/shard_map/ppermute | solution.py:610
  58.9 7.4 %collective-permute-done.15 = f32[512,128]{1,0:T(8,128)S(1)} collective-permute-done((f32[512,128]{1,0:T(8,128)S(1)}, f32[512,128]{1,0:T(8,128)S(1)}, u32[]{:S(2)}, u32[]{:S(2)}) %collective-permute-start.15) | collective-permute-done | bytes 262176 | tf_op jit(solution)/shard_map/ppermute | solution.py:610
  66.3 0.7 %fusion = f32[512,128]{1,0:T(8,128)} fusion(f32[512,128]{1,0:T(8,128)S(1)} %collective-permute-done.15, f32[512,128]{1,0:T(8,128)S(1)} %get-tuple-element.36, f32[1024,128]{1,0:T(8,128)S(1)} %collective-permute-done.14), kind=kLoop, calls=%fused_computation.2 | loop fusion | flops 131072 | bytes 1048576 | tf_op jit(solution)/shard_map/add | solution.py:758
  (22 shorter events, 0.1 us)
Async XLA Ops:
  0.6 20.4 %copy-start.1 = (f32[32,4096]{1,0:T(8,128)S(1)}, f32[32,4096]{1,0:T(8,128)}, u32[]{:S(2)}) copy-start(f32[32,4096]{1,0:T(8,128)} %temp.3) | copy-start | bytes 1572868
  0.6 20.4 %copy-start.2 = (s32[32,4096]{1,0:T(8,128)S(1)}, s32[32,4096]{1,0:T(8,128)}, u32[]{:S(2)}) copy-start(s32[32,4096]{1,0:T(8,128)} %mat.1) | copy-start | bytes 1572868
  0.7 20.3 %copy-start.5 = (s32[64,3]{0,1:T(4,128)S(1)}, s32[64,3]{0,1:T(4,128)}, u32[]{:S(2)}) copy-start(s32[64,3]{0,1:T(4,128)} %param.13) | copy-start | bytes 2308
  0.7 20.4 %copy-start.3 = (f32[4]{0:T(128)S(1)}, f32[4]{0:T(128)}, u32[]{:S(2)}) copy-start(f32[4]{0:T(128)} %k0_table.3) | copy-start | bytes 52
  0.7 20.4 %copy-start.4 = (f32[4]{0:T(128)S(1)}, f32[4]{0:T(128)}, u32[]{:S(2)}) copy-start(f32[4]{0:T(128)} %beta_table.3) | copy-start | bytes 52
  4.2 26.6 %copy-start = (f32[1536,128]{1,0:T(8,128)S(1)}, f32[1536,128]{1,0:T(8,128)}, u32[]{:S(2)}) copy-start(f32[1536,128]{1,0:T(8,128)} %get-tuple-element.21.refs_0_) | copy-start | bytes 2359300
  4.2 26.6 %collective-permute-start.2 = (f32[1536,128]{1,0:T(8,128)}, f32[1536,128]{1,0:T(8,128)S(1)}, u32[]{:S(2)}, u32[]{:S(2)}) collective-permute-start(f32[1536,128]{1,0:T(8,128)} %get-tuple-element.21.refs_0_), channel_id=1, source_target_pairs={{0,1},{1,0},{2,3},{3,2},{4,5},{5,4},{6,7},{7,6},{8,9},{9,8},{10,11... | collective-permute-start | bytes 2359304 | tf_op jit(solution)/shard_map/ppermute | solution.py:620
  4.8 10.0 %collective-permute-start = (f32[512,128]{1,0:T(8,128)}, f32[512,128]{1,0:T(8,128)}, u32[]{:S(2)}, u32[]{:S(2)}) collective-permute-start(f32[512,128]{1,0:T(8,128)} %bitcast.2.phi), channel_id=1, source_target_pairs={{0,2},{1,3},{2,0},{3,1},{4,6},{5,7},{6,4},{7,5},{8,10},{9,11},{10,... | collective-permute-start | bytes 786440 | tf_op jit(solution)/shard_map/ppermute | solution.py:610
  7.3 13.0 %collective-permute-start.5 = (f32[496,128]{1,0:T(8,128)}, f32[496,128]{1,0:T(8,128)S(1)}, u32[]{:S(2)}, u32[]{:S(2)}) collective-permute-start(f32[496,128]{1,0:T(8,128)} %get-tuple-element.23), channel_id=1, source_target_pairs={{0,4},{8,12},{16,20},{24,28},{4,0},{12,8},{20,16},{28,24},{1,5},{9... | collective-permute-start | bytes 761864 | tf_op jit(solution)/shard_map/ppermute | solution.py:616
  8.8 11.5 %collective-permute-start.6 = (f32[496,128]{1,0:T(8,128)}, f32[496,128]{1,0:T(8,128)S(1)}, u32[]{:S(2)}, u32[]{:S(2)}) collective-permute-start(f32[496,128]{1,0:T(8,128)} %get-tuple-element.24), channel_id=1, source_target_pairs={{4,8},{12,16},{20,24},{8,4},{16,12},{24,20},{5,9},{13,17},{21,25},... | collective-permute-start | bytes 761864 | tf_op jit(solution)/shard_map/ppermute | solution.py:616
  9.5 13.2 %collective-permute-start.1 = (f32[512,128]{1,0:T(8,128)}, f32[512,128]{1,0:T(8,128)}, u32[]{:S(2)}, u32[]{:S(2)}) collective-permute-start(f32[512,128]{1,0:T(8,128)} %get-tuple-element.22), channel_id=1, source_target_pairs={{0,2},{1,3},{2,0},{3,1},{4,6},{5,7},{6,4},{7,5},{8,10},{9,11},{10,... | collective-permute-start | bytes 786440 | tf_op jit(solution)/shard_map/ppermute | solution.py:610
  14.8 13.1 %collective-permute-start.3 = (f32[512,128]{1,0:T(8,128)}, f32[512,128]{1,0:T(8,128)}, u32[]{:S(2)}, u32[]{:S(2)}) collective-permute-start(f32[512,128]{1,0:T(8,128)} %collective-permute-done.refs_1_), channel_id=1, source_target_pairs={{0,1},{1,0},{2,3},{3,2},{4,5},{5,4},{6,7},{7,6},{8,9},{9,8},{10,11... | collective-permute-start | bytes 786440 | tf_op jit(solution)/shard_map/ppermute | solution.py:620
  20.4 7.0 %collective-permute-start.7 = (f32[448,128]{1,0:T(8,128)S(1)}, f32[448,128]{1,0:T(8,128)}, u32[]{:S(2)}, u32[]{:S(2)}) collective-permute-start(f32[448,128]{1,0:T(8,128)S(1)} %relay.1.refs_6_.refs_4_), channel_id=1, source_target_pairs={{0,2},{1,3},{2,0},{3,1},{4,6},{5,7},{6,4},{7,5},{8,10},{9,11},{10,... | collective-permute-start | bytes 688136 | tf_op jit(solution)/shard_map/ppermute | solution.py:610
  21.0 7.0 %collective-permute-start.9 = (f32[448,128]{1,0:T(8,128)S(1)}, f32[448,128]{1,0:T(8,128)}, u32[]{:S(2)}, u32[]{:S(2)}) collective-permute-start(f32[448,128]{1,0:T(8,128)S(1)} %relay.1.refs_6_.refs_4_), channel_id=1, source_target_pairs={{0,1},{1,0},{2,3},{3,2},{4,5},{5,4},{6,7},{7,6},{8,9},{9,8},{10,11... | collective-permute-start | bytes 688136 | tf_op jit(solution)/shard_map/ppermute | solution.py:620
  21.1 6.3 %copy-start.6 = (f32[512,128]{1,0:T(8,128)S(1)}, f32[512,128]{1,0:T(8,128)}, u32[]{:S(2)}) copy-start(f32[512,128]{1,0:T(8,128)} %get-tuple-element.28) | copy-start | bytes 786436
  22.7 1.5 %collective-permute-start.8 = (f32[120,128]{1,0:T(8,128)S(1)}, f32[120,128]{1,0:T(8,128)S(1)}, u32[]{:S(2)}, u32[]{:S(2)}) collective-permute-start(f32[120,128]{1,0:T(8,128)S(1)} %get-tuple-element.25), channel_id=1, source_target_pairs={{0,1},{2,3},{1,0},{3,2},{4,5},{6,7},{5,4},{7,6},{8,9},{10,11},{9,8... | collective-permute-start | bytes 184328 | tf_op jit(solution)/shard_map/ppermute | solution.py:616
  24.2 5.3 %collective-permute-start.4 = (f32[512,128]{1,0:T(8,128)}, f32[512,128]{1,0:T(8,128)S(1)}, u32[]{:S(2)}, u32[]{:S(2)}) collective-permute-start(f32[512,128]{1,0:T(8,128)} %collective-permute-done.1.refs_2_), channel_id=1, source_target_pairs={{0,1},{1,0},{2,3},{3,2},{4,5},{5,4},{6,7},{7,6},{8,9},{9,8},{10,11... | collective-permute-start | bytes 786440 | tf_op jit(solution)/shard_map/ppermute | solution.py:620
  27.4 17.9 %collective-permute-start.11 = (f32[512,128]{1,0:T(8,128)S(1)}, f32[512,128]{1,0:T(8,128)S(1)}, u32[]{:S(2)}, u32[]{:S(2)}) collective-permute-start(f32[512,128]{1,0:T(8,128)S(1)} %copy-done.6), channel_id=1, source_target_pairs={{0,2},{1,3},{2,0},{3,1},{4,6},{5,7},{6,4},{7,5},{8,10},{9,11},{10,... | collective-permute-start | bytes 786440 | tf_op jit(solution)/shard_map/ppermute | solution.py:610
  27.9 17.3 %collective-permute-start.12 = (f32[512,128]{1,0:T(8,128)S(1)}, f32[512,128]{1,0:T(8,128)S(1)}, u32[]{:S(2)}, u32[]{:S(2)}) collective-permute-start(f32[512,128]{1,0:T(8,128)S(1)} %copy-done.6), channel_id=1, source_target_pairs={{0,3},{1,2},{2,1},{3,0},{4,7},{5,6},{6,5},{7,4},{8,11},{9,10},{10,... | collective-permute-start | bytes 786440 | tf_op jit(solution)/shard_map/ppermute | solution.py:633
  27.9 2.9 %collective-permute-start.10 = (f32[448,128]{1,0:T(8,128)}, f32[448,128]{1,0:T(8,128)S(1)}, u32[]{:S(2)}, u32[]{:S(2)}) collective-permute-start(f32[448,128]{1,0:T(8,128)} %collective-permute-done.7.refs_7_.refs_5_), channel_id=1, source_target_pairs={{0,1},{1,0},{2,3},{3,2},{4,5},{5,4},{6,7},{7,6},{8,9},{9,8},{10,11... | collective-permute-start | bytes 688136 | tf_op jit(solution)/shard_map/ppermute | solution.py:620
  29.5 15.7 %collective-permute-start.13 = (f32[120,128]{1,0:T(8,128)S(1)}, f32[120,128]{1,0:T(8,128)S(1)}, u32[]{:S(2)}, u32[]{:S(2)}) collective-permute-start(f32[120,128]{1,0:T(8,128)S(1)} %get-tuple-element.34), channel_id=1, source_target_pairs={{1,2},{2,1},{5,6},{6,5},{9,10},{10,9},{13,14},{14,13},{17,18},{18,... | collective-permute-start | bytes 184328 | tf_op jit(solution)/shard_map/ppermute | solution.py:616
  54.7 3.0 %collective-permute-start.14 = (f32[1024,128]{1,0:T(8,128)S(1)}, f32[1024,128]{1,0:T(8,128)S(1)}, u32[]{:S(2)}, u32[]{:S(2)}) collective-permute-start(f32[1024,128]{1,0:T(8,128)S(1)} %get-tuple-element.37), channel_id=1, source_target_pairs={{0,1},{1,0},{2,3},{3,2},{4,5},{5,4},{6,7},{7,6},{8,9},{9,8},{10,11... | collective-permute-start | bytes 1572872 | tf_op jit(solution)/shard_map/ppermute | solution.py:620
  57.6 8.6 %collective-permute-start.15 = (f32[512,128]{1,0:T(8,128)S(1)}, f32[512,128]{1,0:T(8,128)S(1)}, u32[]{:S(2)}, u32[]{:S(2)}) collective-permute-start(f32[512,128]{1,0:T(8,128)S(1)} %slice_add_fusion), channel_id=1, source_target_pairs={{0,2},{1,3},{2,0},{3,1},{4,6},{5,7},{6,4},{7,5},{8,10},{9,11},{10,... | collective-permute-start | bytes 786440 | tf_op jit(solution)/shard_map/ppermute | solution.py:610

commit v10 on v9

--- a/solution.py
+++ b/solution.py
@@ -48,7 +48,7 @@
     return pltpu.roll(value, by % value.shape[axis], axis)
 
 
-def prep_kernel(table, phi, src, mat, temp, slab, body, s, sigma, inner, outer, src_v, mat_v, ends_t, ends_m, sems):
+def prep_kernel(table, pos, phi, src, mat, temp, slab, body, ready, sigma, inner, outer, src_v, mat_v, ends_t, ends_m, sems):
     rows = TE * ROW
     size_x, width = temp.shape
     moves = [(phi, body.at[0:rows]), (src, src_v), (mat, mat_v)]
@@ -61,8 +61,21 @@
     for move in moves:
         move.wait()
     sigma[...] = lookup(table, mat_v[...])
-    s[...] = src_v[...] / sigma[...]
-    body[rows : 2 * rows] = s[...]
+    body[rows : 2 * rows] = src_v[...] / sigma[...]
+    first = (lax.axis_index("gx") * lax.axis_size("gy") + lax.axis_index("gy")) * TILES
+    for t in range(TILES):
+
+        @pl.when(pos[2, first + t] == 1)
+        def _():
+            def plane(p, carry):
+                for ref, start in ((body, 0), (body, rows), (sigma, 0)):
+                    at = pl.ds(pl.multiple_of(p * ROW, ROW) + (start + t), SUB, stride=TILES)
+                    ref[at, :] = roll(ref[at, :], TE, 1)
+                return carry
+
+            lax.fori_loop(0, TE, plane, 0, unroll=8)
+
+    ready[...] = body[0 : 2 * rows]
     body[2 * rows : 3 * rows] = sigma[...]
     even = lax.rem(lax.axis_index("gx"), 2) == 0
 
@@ -178,7 +191,7 @@
             dev = part_device(part, chips, j)
             for t in range(TILES):
                 tile = first + dev * TILES + t
-                cell = (pos[tile, 1] + 1) * 2 + pos[tile, 2]
+                cell = (pos[1, tile] + 1) * 2 + pos[2, tile]
                 slot = part * TILES + t
                 cell_of[which, slot] = cell
                 cell_at[which, cell] = jnp.where(valid, slot, tiles)
@@ -194,13 +207,8 @@
     width_gy = 2 * chips
     tiles = width_gy * TILES
     none = tiles
-    half = 2 * chips - 1
-    halos = refs[2 * half : 2 * half + width_gy]
-    pot, slope, cell_at, cell_of, pa, pb, la, lb, ua, ub, s_c, s_l, s_u, sems, pot_sem = refs[2 * half + width_gy :]
-    bodies = []
-    for side in (refs[:half], refs[half : 2 * half]):
-        bodies.append(((side[0], 0), (side[0], TE * ROW)))
-        bodies += [((side[at], 0), (side[at + 1], 0)) for at in range(1, half, 2)]
+    bodies, halos = refs[:width_gy], refs[width_gy : 2 * width_gy]
+    pot, slope, cell_at, cell_of, pa, pb, la, lb, ua, ub, s_c, s_l, s_u, sems = refs[2 * width_gy :]
     i = lax.axis_index("gx")
     j = lax.axis_index("gy")
     rows_gx = lax.axis_size("gx")
@@ -209,7 +217,7 @@
     moves = []
     for part in range(width_gy):
         at = 0
-        pieces = [(*bodies[part][0], pa, part * C_SIZE + 1, TE), (*bodies[part][1], s_c, part * TE, TE)]
+        pieces = [(bodies[part], 0, pa, part * C_SIZE + 1, TE), (bodies[part], TE * ROW, s_c, part * TE, TE)]
         for target, first, count in (
             (la, part * L_SIZE, LOW[0]),
             (s_l, part * LOW[1], LOW[1]),
@@ -256,27 +264,31 @@
     lane = lax.broadcasted_iota(jnp.int32, (SUB, LANES), 1)
     sub = lax.broadcasted_iota(jnp.int32, (SUB, LANES), 0)
     depth = lane % TE
-    first_y, last_y = lane < TE, lane >= LANES - TE
     first_sub, last_sub = sub == 0, sub == SUB - 1
     first_z, last_z = depth == 0, depth == TE - 1
 
-    def y_plus(ref, own, row, ghost_row):
+    def y_plus(ref, own, first_y, row, ghost_row):
         turned = jnp.where(last_sub, plane_at(ref, ghost_row), plane_at(ref, row))
         return roll(jnp.where(first_y, turned, own), -TE, 1)
 
-    def y_minus(ref, own, row, ghost_row):
+    def y_minus(ref, own, last_y, row, ghost_row):
         turned = jnp.where(first_sub, plane_at(ref, ghost_row), plane_at(ref, row))
         return roll(jnp.where(last_y, turned, own), TE, 1)
+
+    def z_plus(ref, own, ghost_row):
+        return roll(jnp.where(first_z, plane_at(ref, ghost_row), own), -1, 1)
+
+    def z_minus(ref, own, ghost_row):
+        return roll(jnp.where(last_z, plane_at(ref, ghost_row), own), 1, 1)
 
     def around(which, slot):
         cell = cell_of[which, slot]
         upper = cell % 2
-        y_m = cell_at[which, cell - 2]
-        y_p = cell_at[which, cell + 2]
-        z = cell_at[which, cell + 1 - 2 * upper]
-        turn = jnp.where(upper == 1, LANES + 1 - TE, TE - 1)
-        meets = jnp.where(upper == 1, 0, TE - 1) == depth
-        return cell, (slot, y_m, y_p, z, turn, meets)
+        beside = cell_at[which, cell + 1 - 2 * upper]
+        near = (cell_at[which, cell - 2], cell_at[which, cell + 2])
+        near += (jnp.where(upper == 1, beside, none), jnp.where(upper == 1, none, beside))
+        quarter = lane // TE
+        return cell, (slot, *near, quarter == upper, quarter == lax.rem(upper + 3, 4))
 
     bufs = ((pa, la, ua), (pb, lb, ub))
     for k in range(SWEEPS):
@@ -297,21 +309,19 @@
         lax.fori_loop(0, tiles, ghosts, 0)
 
         def relax(src, dst, size, slots, first, count, s_ref, s_size, s_first):
-            slot, y_m, y_p, z, turn, meets = slots
+            slot, y_m, y_p, z_m, z_p, first_y, last_y = slots
             row, s_row = row_of(slot, size, first), row_of(slot, s_size, s_first)
             up, down = row + TILES, row - TILES
             row_m, row_p = row_of(y_m, size, first) + (ROW - TILES), row_of(y_p, size, first) - (ROW - TILES)
-            row_z = row_of(z, size, first)
+            row_zm, row_zp = row_of(z_m, size, first), row_of(z_p, size, first)
             before, own = plane_at(src, row - ROW), plane_at(src, row)
             for step in range(0, count * ROW, ROW):
                 after = plane_at(src, row + (step + ROW))
                 total = (before + after) + plane_at(s_ref, s_row + step)
-                total = total + y_minus(src, own, down + step, row_m + step)
-                total = total + y_plus(src, own, up + step, row_p + step)
-                total = total + jnp.where(last_z, 0.0, roll(own, -1, 1))
-                total = total + jnp.where(first_z, 0.0, roll(own, 1, 1))
-                ghost = pltpu.roll(plane_at(src, row_z + step), turn, 1)
-                put_plane(dst, row + step, keep * own + gain * (total + jnp.where(meets, ghost, 0.0)))
+                along_y = y_minus(src, own, last_y, down + step, row_m + step)
+                along_y = along_y + y_plus(src, own, first_y, up + step, row_p + step)
+                along_z = z_minus(src, own, row_zm + step) + z_plus(src, own, row_zp + step)
+                put_plane(dst, row + step, keep * own + gain * (total + (along_y + along_z)))
                 before, own = own, after
 
         def sweep_tile(slot, carry):
@@ -327,22 +337,28 @@
         lax.fori_loop(0, tiles, sweep_tile, 0)
 
     field, f_l, f_u = bufs[SWEEPS % 2]
-    pot_move = pltpu.make_async_copy(field.at[ROW0 + ROW : ROW0 + (TE + 1) * ROW], pot, pot_sem.at[0])
-    pot_move.start()
+    for t in range(TILES):
+        turn = jnp.where(cell_of[0, t] % 2 == 1, LANES - TE, 0)
+
+        def turn_back(p, carry):
+            value = plane_at(field, p * ROW + row_of(t, C_SIZE, 1))
+            put_plane(pot, pl.multiple_of(p * ROW, ROW) + t, pltpu.roll(value, turn, 1))
+            return carry
+
+        lax.fori_loop(0, TE, turn_back, 0, unroll=8)
 
     def squares(ref, size, slots, local, x, first, count, x_last=None):
-        slot, _, y_p, z, turn, meets = slots
+        slot, _, y_p, _, z_p, first_y, _ = slots
         row = row_of(slot, size, first)
-        up, row_p, row_z = row + TILES, row_of(y_p, size, first) - (ROW - TILES), row_of(z, size, first)
+        up, row_p, row_z = row + TILES, row_of(y_p, size, first) - (ROW - TILES), row_of(z_p, size, first)
         target = (local * SLABX + x) * SUB
         own = plane_at(ref, row)
         for p in range(count):
             last = p == count - 1 and x_last is not None
             after = x_last if last else plane_at(ref, row + (p + 1) * ROW)
             d_x = after - own
-            d_y = y_plus(ref, own, up + p * ROW, row_p + p * ROW) - own
-            ghost = jnp.where(meets, pltpu.roll(plane_at(ref, row_z + p * ROW), turn, 1), 0.0)
-            d_z = jnp.where(last_z, ghost, roll(own, -1, 1)) - own
+            d_y = y_plus(ref, own, first_y, up + p * ROW, row_p + p * ROW) - own
+            d_z = z_plus(ref, own, row_z + p * ROW) - own
             rows = pl.ds(pl.multiple_of(target + p * SUB, SUB), SUB)
             slope[rows, :] = d_x * d_x + d_y * d_y + d_z * d_z
             own = after
@@ -366,7 +382,6 @@
         return carry
 
     lax.fori_loop(0, tiles, slope_tile, 0)
-    pot_move.wait()
 
 
 def window(which, cell, i, j, rows_gx):
@@ -489,7 +504,7 @@
         for t in range(TILES):
             for which, by in enumerate((0, -1, 1)):
                 tile = jnp.clip(i + by, 0, rows_gx - 1) * tiles + dev * TILES + t
-                cell = (pos[tile, 1] + 1) * 2 + pos[tile, 2]
+                cell = (pos[1, tile] + 1) * 2 + pos[2, tile]
                 local, inside = window(which, cell, i, j, rows_gx)
                 source, start, x, count = (
                     (sigmas.at[part], 0, HALO, TE),
@@ -518,7 +533,7 @@
             ]
             for r in range(4):
                 block = 4 * first + r + HALO + 1
-                q_ext[rows_of(block, g)] = pick([turned(cells[c], c - r) for c in range(4)])
+                q_ext[rows_of(block, g)] = pick([turned(cells[c], c - r - c % 2) for c in range(4)])
         return carry
 
     lax.fori_loop(0, HALF // 4 + 2, place_heat, 0, unroll=2)
@@ -588,8 +603,8 @@
         dev = lax.rem(to, width_gy)
         for t in range(TILES):
             tile = i * tiles + dev * TILES + t
-            col = pos[tile, 1] - 2 * j
-            cell = jnp.clip(col, 0, 1) * 2 + pos[tile, 2]
+            col = pos[1, tile] - 2 * j
+            cell = jnp.clip(col, 0, 1) * 2 + pos[2, tile]
             places.append((target, first + t, cell, (col >= 0) & (col < 2)))
 
     def pack(p, carry):
@@ -653,6 +668,7 @@
     beta_table,
 ):
     f32 = jnp.float32
+    pos = tile_pos.T
     width_gy = lax.axis_size("gy")
     chips = width_gy // 2
     tiles = width_gy * TILES
@@ -662,18 +678,16 @@
     def rows(count):
         return jax.ShapeDtypeStruct((count, LANES), f32)
 
-    phi = to_rows(phi_init)
-    phis = [shifted(phi, "gy", 2 * d, True) for d in range(1, chips)]
-    body, s, sigma, inner, outer = pl.pallas_call(
+    body, ready, sigma, inner, outer = pl.pallas_call(
         prep_kernel,
         out_shape=(
             rows(3 * TE * ROW),
-            rows(TE * ROW),
+            rows(2 * TE * ROW),
             rows(TE * ROW),
             rows(SIDE_ROWS + edge_rows),
             rows(SIDE_ROWS + edge_rows),
         ),
-        in_specs=[SMEM] + [HBM] * 5,
+        in_specs=[SMEM] * 2 + [HBM] * 5,
         out_specs=(VMEM,) * 5,
         scratch_shapes=[
             pltpu.VMEM((TE * ROW, LANES), f32),
@@ -684,10 +698,8 @@
         ],
         compiler_params=pltpu.CompilerParams(vmem_limit_bytes=62 * 1024 * 1024),
         name="prep",
-    )(sigma_table, phi, to_rows(source), to_rows(tile_mat), temp_init, slab_mat)
-    bodies = [body]
-    for there, d in zip(phis, range(1, chips)):
-        bodies += [there, shifted(s, "gy", 2 * d, True)]
+    )(sigma_table, pos, to_rows(phi_init), to_rows(source), to_rows(tile_mat), temp_init, slab_mat)
+    bodies = [body] + [shifted(ready, "gy", 2 * d, True) for d in range(1, chips)]
     bodies += [from_mate(part) for part in bodies]
     inner, outer = with_partner(inner, "gx", 0), with_partner(outer, "gx", 1)
 
@@ -701,7 +713,7 @@
     )(inner, outer)
     halos = [halo] + [shifted(halo, "gy", 2 * d, True) for d in range(1, chips)]
     sigmas = [bodies[0]] + [shifted(sigma, "gy", 2 * d, True) for d in range(1, chips)]
-    sigmas += [bodies[2 * chips - 1]] + [to_other_core(sigma, d) for d in range(1, chips)]
+    sigmas += [bodies[chips]] + [to_other_core(sigma, d) for d in range(1, chips)]
 
     native = pltpu.VMEM((width // LANES * SLABX + SUB, LANES), f32)
     t_ext, k0_ext, b_ext, edge_in, edge_out = pl.pallas_call(
@@ -712,7 +724,7 @@
         scratch_shapes=[native, native] + [pltpu.VMEM((HALO * SLABX, LANES), f32)] * 2,
         compiler_params=PARAMS,
         name="slab_prep",
-    )(tile_pos, k0_table, beta_table, temp_init, slab_mat, inner, outer)
+    )(pos, k0_table, beta_table, temp_init, slab_mat, inner, outer)
     y_in, y_out = with_partner(edge_in, "gy", 0), with_partner(edge_out, "gy", 1)
     *halos[1:], y_in = lax.optimization_barrier((*halos[1:], y_in))
     halos = halos + [from_mate(part) for part in halos]
@@ -723,19 +735,18 @@
     pot, slope = pl.pallas_call(
         functools.partial(sweep_kernel, chips),
         out_shape=(rows(TE * ROW), rows(8 * SLABX * SUB)),
-        in_specs=[SMEM] + [ANY] * (len(bodies) + width_gy),
-        out_specs=(ANY, VMEM),
+        in_specs=[SMEM] + [ANY] * (2 * width_gy),
+        out_specs=(VMEM, VMEM),
         scratch_shapes=[
             pltpu.SMEM((3, 2 * (2 * width_gy + 2)), jnp.int32),
             pltpu.SMEM((3, tiles), jnp.int32),
             fields(C_SIZE), fields(C_SIZE), fields(L_SIZE), fields(L_SIZE), fields(U_SIZE), fields(U_SIZE),
             fields(TE), fields(LOW[1]), fields(HIGH[1]),
             pltpu.SemaphoreType.DMA((6 * width_gy,)),
-            pltpu.SemaphoreType.DMA((1,)),
         ],
         compiler_params=PARAMS,
         name="sweeps",
-    )(tile_pos, *bodies, *halos)
+    )(pos, *bodies, *halos)
 
     temp, mine, bundle, *across = pl.pallas_call(
         functools.partial(slab_steps_kernel, chips),
@@ -751,7 +762,7 @@
         + [pltpu.SemaphoreType.DMA((width_gy,))],
         compiler_params=PARAMS,
         name="slab_steps",
-    )(tile_pos, k0_table, beta_table, *sigmas, *halos, slope, t_ext, k0_ext, b_ext, y_in, y_out)
+    )(pos, k0_table, beta_table, *sigmas, *halos, slope, t_ext, k0_ext, b_ext, y_in, y_out)
     got = from_mate(bundle).reshape(chips, TE * ROW, LANES)
     tile_temps = mine + got[0]
     for d in range(1, chips):

time: 67.3 us -> 67.5 us (level)
  Pallas kernels: 28.9 us -> 27.6 us
  waiting for transfers between devices: 23.6 us -> 24.6 us
    ppermute x5 -> x4, waiting for transfers between devices: 15 us -> 20.8 us  [shifted(): return lax.ppermute(value, axis, pairs)]
    ppermute x4, waiting for transfers between devices: 6.42 us -> 2.32 us  [with_partner(): lax.ppermute(value, axis, pairs + [(high, low) for low, high in pairs])]
    ppermute x6 -> x5, starting transfers between devices: 3.89 us -> 2.24 us  [from_mate(): lax.ppermute(value, 'gy', [(d, d ^ 1) for d in range(lax.axis_size('gy'))])]
    ppermute x1, starting transfers between devices: 0.01 us -> 0.9 us  [to_other_core(): lax.ppermute(value, 'gy', [(at, ((at ^ 1) + 2 * by) % count) for at in ra...]
    pallas_call x1, Pallas kernels: 14.4 us -> 13.5 us  [on_device(): pl.pallas_call(functools.partial(sweep_kernel, chips), out_shape=(rows(TE...]
    ppermute x5 -> x4, starting transfers between devices: 5.51 us -> 6.26 us  [shifted(): return lax.ppermute(value, axis, pairs)]
    ppermute x6 -> x5, waiting for transfers between devices: 2.21 us -> 1.55 us  [from_mate(): lax.ppermute(value, 'gy', [(d, d ^ 1) for d in range(lax.axis_size('gy'))])]
  transfers between devices with their start and end apart: 16 -> 14, of which waited for: 7 -> 6; matrix products, arithmetic and copies ran while one was open for 0% -> 0% of each run, Pallas kernels for 24% -> 22%
where the time goes in v10:
time: 67.5 us; the launch traced here: 66.7 us
  Pallas kernels  27.6 us (41%)
  waiting for transfers between devices  24.6 us (36%)
  starting transfers between devices  12.8 us (19%)
  between operations  0.83 us (1%)
  other arithmetic  0.77 us (1%)
    ppermute x4, waiting for transfers between devices, shifted(): return lax.ppermute(value, axis, pairs)  20.8 us
    pallas_call x1, Pallas kernels, on_device(): pl.pallas_call(functools.partial(sweep_kernel, chips), out_shape=(rows(TE...  13.5 us
    pallas_call x1, Pallas kernels, on_device(): pl.pallas_call(functools.partial(slab_steps_kernel, chips), out_shape=(ja...  8.9 us
    ppermute x4, starting transfers between devices, shifted(): return lax.ppermute(value, axis, pairs)  6.26 us
    pallas_call x1, Pallas kernels, on_device(): pl.pallas_call(prep_kernel, out_shape=(rows(3 * TE * ROW), rows(2 * TE *...  4.07 us
    ppermute x4, starting transfers between devices, with_partner(): lax.ppermute(value, axis, pairs + [(high, low) for low, high in pairs])  3.39 us
    ppermute x4, waiting for transfers between devices, with_partner(): lax.ppermute(value, axis, pairs + [(high, low) for low, high in pairs])  2.32 us
    ppermute x5, starting transfers between devices, from_mate(): lax.ppermute(value, 'gy', [(d, d ^ 1) for d in range(lax.axis_size('gy'))])  2.24 us
  transfers between devices with their start and end apart: 14, of which 6 were waited for; matrix products, arithmetic and copies ran while one was open for 0% of the time, Pallas kernels for 22%

profile of v10, /device:TPU:0, one launch (start us, length us, event | category | flops | bytes accessed | tf_op | source)
XLA Modules:
  0.0 66.7 jit_solution(6039462569451159960)
XLA Ops:
  0.7 4.1 %prep.1 = (f32[1536,128]{1,0:T(8,128)}, f32[1024,128]{1,0:T(8,128)}, f32[512,128]{1,0:T(8,128)}, f32[496,128]{1,0:T(8,128)}, f32[496,128]{1,0:T(8,128)}) custom-call(f32[4]{0:T(128)} %table.1, s32[3,64]{1,0:T(4,128)} %bitcast.26, f32[512,128]{1,0:T(8,128)} %bitcast.30, f32[512,128]{1,0:T(8,128)} %bitcast.31, s32[512,128]{1,0:T(8,128)} %bitcast.32, ...), custom_call_target="tpu_custom_call" | custom-call | tf_op jit(solution)/shard_map/prep/pallas_call | solution.py:681
  4.8 0.0 copy-start.6
  4.8 3.0 %collective-permute-start = (f32[1024,128]{1,0:T(8,128)}, f32[1024,128]{1,0:T(8,128)S(1)}, u32[]{:S(2)}, u32[]{:S(2)}) collective-permute-start(f32[1024,128]{1,0:T(8,128)} %get-tuple-element.22), channel_id=1, source_target_pairs={{0,2},{1,3},{2,0},{3,1},{4,6},{5,7},{6,4},{7,5},{8,10},{9,11},{10,... | collective-permute-start | bytes 1572872 | tf_op jit(solution)/shard_map/ppermute | solution.py:625
  7.8 0.0 collective-permute-start.1
  7.8 1.5 %collective-permute-start.3 = (f32[496,128]{1,0:T(8,128)}, f32[496,128]{1,0:T(8,128)S(1)}, u32[]{:S(2)}, u32[]{:S(2)}) collective-permute-start(f32[496,128]{1,0:T(8,128)} %get-tuple-element.23), channel_id=1, source_target_pairs={{0,4},{8,12},{16,20},{24,28},{4,0},{12,8},{20,16},{28,24},{1,5},{9... | collective-permute-start | bytes 761864 | tf_op jit(solution)/shard_map/ppermute | solution.py:631
  9.3 0.7 collective-permute-start.4
  10.0 9.7 %collective-permute-done.refs_1_ = f32[1024,128]{1,0:T(8,128)S(1)} collective-permute-done((f32[1024,128]{1,0:T(8,128)}, f32[1024,128]{1,0:T(8,128)S(1)}, u32[]{:S(2)}, u32[]{:S(2)}) %collective-permute-start) | collective-permute-done | bytes 524320 | tf_op jit(solution)/shard_map/ppermute | solution.py:625
  19.7 0.0 collective-permute-start.2
  19.7 1.4 %collective-permute-done.3.inner = f32[496,128]{1,0:T(8,128)S(1)} collective-permute-done((f32[496,128]{1,0:T(8,128)}, f32[496,128]{1,0:T(8,128)S(1)}, u32[]{:S(2)}, u32[]{:S(2)}) %collective-permute-start.3) | collective-permute-done | bytes 253984 | tf_op jit(solution)/shard_map/ppermute | solution.py:631
  21.1 0.0 collective-permute-done.4.outer
  21.2 0.6 collective-permute-start.5
  21.8 0.0 collective-permute-start.7
  21.8 1.1 %slab_prep.1 = (f32[1552,128]{1,0:T(8,128)S(1)}, f32[1552,128]{1,0:T(8,128)S(1)}, f32[1552,128]{1,0:T(8,128)S(1)}, f32[120,128]{1,0:T(8,128)S(1)}, f32[120,128]{1,0:T(8,128)S(1)}) custom-call(s32[3,64]{1,0:T(4,128)S(1)} %bitcast.27, f32[4]{0:T(128)S(1)} %copy-done.4, f32[4]{0:T(128)S(1)} %copy-done.5, f32[32,4096]{1,0:T(8,128)S(1)} %copy-done.1, ...), custom_call_target="tpu_custom_call" | custom-call | tf_op jit(solution)/shard_map/slab_prep/pallas_call | solution.py:719
  22.9 0.6 collective-permute-start.6
  23.5 0.9 %collective-permute-done.6.refs_12_ = f32[120,128]{1,0:T(8,128)S(1)} collective-permute-done((f32[120,128]{1,0:T(8,128)S(1)}, f32[120,128]{1,0:T(8,128)S(1)}, u32[]{:S(2)}, u32[]{:S(2)}) %collective-permute-start.6) | collective-permute-done | bytes 61472 | tf_op jit(solution)/shard_map/ppermute | solution.py:631
  24.4 4.1 %collective-permute-done.5.refs_5_ = f32[448,128]{1,0:T(8,128)S(1)} collective-permute-done((f32[448,128]{1,0:T(8,128)S(1)}, f32[448,128]{1,0:T(8,128)S(1)}, u32[]{:S(2)}, u32[]{:S(2)}) %collective-permute-start.5) | collective-permute-done | bytes 229408 | tf_op jit(solution)/shard_map/ppermute | solution.py:625
  28.5 0.0 collective-permute-start.8
  28.5 1.0 %collective-permute-start.9 = (f32[512,128]{1,0:T(8,128)S(1)}, f32[512,128]{1,0:T(8,128)S(1)}, u32[]{:S(2)}, u32[]{:S(2)}) collective-permute-start(f32[512,128]{1,0:T(8,128)S(1)} %copy-done.6), channel_id=1, source_target_pairs={{0,2},{1,3},{2,0},{3,1},{4,6},{5,7},{6,4},{7,5},{8,10},{9,11},{10,... | collective-permute-start | bytes 786440 | tf_op jit(solution)/shard_map/ppermute | solution.py:625
  29.4 0.0 collective-permute-done.7.refs_6_
  29.4 0.9 %collective-permute-start.10 = (f32[512,128]{1,0:T(8,128)S(1)}, f32[512,128]{1,0:T(8,128)S(1)}, u32[]{:S(2)}, u32[]{:S(2)}) collective-permute-start(f32[512,128]{1,0:T(8,128)S(1)} %copy-done.6), channel_id=1, source_target_pairs={{0,3},{1,2},{2,1},{3,0},{4,7},{5,6},{6,5},{7,4},{8,11},{9,10},{10,... | collective-permute-start | bytes 786440 | tf_op jit(solution)/shard_map/ppermute | solution.py:648
  30.3 0.0 collective-permute-done.8.refs_7_
  30.3 0.7 collective-permute-start.11
  31.0 0.0 collective-permute-done.1.refs_2_
  31.0 13.5 %sweeps.1 = (f32[512,128]{1,0:T(8,128)}, f32[2560,128]{1,0:T(8,128)S(1)}) custom-call(s32[3,64]{1,0:T(4,128)S(1)} %bitcast.28, f32[1536,128]{1,0:T(8,128)S(1)} %copy-done, f32[1024,128]{1,0:T(8,128)S(1)} %collective-permute-done.refs_1_, f32[1536,128]{1,0:T(8,128)S(1)} %collective-permute-done.1.refs_2_, f32[1024,128]{1,0:T(8,128)S(1)} %collective-permute-done.2.refs_3_, ...), custom_call_target="tpu_custom_call" | custom-call | tf_op jit(solution)/shard_map/sweeps/pallas_call | solution.py:735
  44.6 0.0 collective-permute-done.9.refs_1_
  44.6 0.0 collective-permute-done.11.refs_13_
  44.6 8.9 %slab_steps.1 = (f32[32,4096]{1,0:T(8,128)}, f32[512,128]{1,0:T(8,128)S(1)}, f32[1024,128]{1,0:T(8,128)S(1)}, f32[512,128]{1,0:T(8,128)S(1)}) custom-call(s32[3,64]{1,0:T(4,128)S(1)} %bitcast.29, f32[4]{0:T(128)S(1)} %copy-done.4, f32[4]{0:T(128)S(1)} %copy-done.5, f32[1536,128]{1,0:T(8,128)S(1)} %copy-done, f32[512,128]{1,0:T(8,128)S(1)} %collective-permute-done.9.refs_1_, ...), custom_call_target="tpu_custom_call" | custom-call | tf_op jit(solution)/shard_map/slab_steps/pallas_call | solution.py:751
  53.5 2.2 %collective-permute-start.12 = (f32[1024,128]{1,0:T(8,128)S(1)}, f32[1024,128]{1,0:T(8,128)S(1)}, u32[]{:S(2)}, u32[]{:S(2)}) collective-permute-start(f32[1024,128]{1,0:T(8,128)S(1)} %get-tuple-element.37), channel_id=1, source_target_pairs={{0,1},{1,0},{2,3},{3,2},{4,5},{5,4},{6,7},{7,6},{8,9},{9,8},{10,11... | collective-permute-start | bytes 1572872 | tf_op jit(solution)/shard_map/ppermute | solution.py:635
  55.7 1.5 %collective-permute-done.12 = f32[1024,128]{1,0:T(8,128)S(1)} collective-permute-done((f32[1024,128]{1,0:T(8,128)S(1)}, f32[1024,128]{1,0:T(8,128)S(1)}, u32[]{:S(2)}, u32[]{:S(2)}) %collective-permute-start.12) | collective-permute-done | bytes 524320 | tf_op jit(solution)/shard_map/ppermute | solution.py:635
  57.3 1.7 %collective-permute-start.13 = (f32[512,128]{1,0:T(8,128)S(1)}, f32[512,128]{1,0:T(8,128)S(1)}, u32[]{:S(2)}, u32[]{:S(2)}) collective-permute-start(f32[512,128]{1,0:T(8,128)S(1)} %slice_add_fusion), channel_id=1, source_target_pairs={{0,2},{1,3},{2,0},{3,1},{4,6},{5,7},{6,4},{7,5},{8,10},{9,11},{10,... | collective-permute-start | bytes 786440 | tf_op jit(solution)/shard_map/ppermute | solution.py:625
  59.0 7.0 %collective-permute-done.13 = f32[512,128]{1,0:T(8,128)S(1)} collective-permute-done((f32[512,128]{1,0:T(8,128)S(1)}, f32[512,128]{1,0:T(8,128)S(1)}, u32[]{:S(2)}, u32[]{:S(2)}) %collective-permute-start.13) | collective-permute-done | bytes 262176 | tf_op jit(solution)/shard_map/ppermute | solution.py:625
  66.0 0.7 %fusion = f32[512,128]{1,0:T(8,128)} fusion(f32[512,128]{1,0:T(8,128)S(1)} %collective-permute-done.13, f32[512,128]{1,0:T(8,128)S(1)} %get-tuple-element.36, f32[1024,128]{1,0:T(8,128)S(1)} %collective-permute-done.12), kind=kLoop, calls=%fused_computation.2 | loop fusion | flops 131072 | bytes 1048576 | tf_op jit(solution)/shard_map/add | solution.py:769
  (17 shorter events, 0.1 us)
Async XLA Ops:
  0.6 21.1 %copy-start.3 = (s32[64,3]{0,1:T(4,128)S(1)}, s32[64,3]{0,1:T(4,128)}, u32[]{:S(2)}) copy-start(s32[64,3]{0,1:T(4,128)} %param.13) | copy-start | bytes 2308
  0.6 21.1 %copy-start.1 = (f32[32,4096]{1,0:T(8,128)S(1)}, f32[32,4096]{1,0:T(8,128)}, u32[]{:S(2)}) copy-start(f32[32,4096]{1,0:T(8,128)} %temp.3) | copy-start | bytes 1572868
  0.7 21.1 %copy-start.2 = (s32[32,4096]{1,0:T(8,128)S(1)}, s32[32,4096]{1,0:T(8,128)}, u32[]{:S(2)}) copy-start(s32[32,4096]{1,0:T(8,128)} %mat.1) | copy-start | bytes 1572868
  0.7 21.1 %copy-start.4 = (f32[4]{0:T(128)S(1)}, f32[4]{0:T(128)}, u32[]{:S(2)}) copy-start(f32[4]{0:T(128)} %k0_table.3) | copy-start | bytes 52
  0.7 21.1 %copy-start.5 = (f32[4]{0:T(128)S(1)}, f32[4]{0:T(128)}, u32[]{:S(2)}) copy-start(f32[4]{0:T(128)} %beta_table.3) | copy-start | bytes 52
  4.8 23.7 %copy-start.6 = (f32[512,128]{1,0:T(8,128)S(1)}, f32[512,128]{1,0:T(8,128)}, u32[]{:S(2)}) copy-start(f32[512,128]{1,0:T(8,128)} %get-tuple-element.28) | copy-start | bytes 786436
  4.8 26.2 %copy-start = (f32[1536,128]{1,0:T(8,128)S(1)}, f32[1536,128]{1,0:T(8,128)}, u32[]{:S(2)}) copy-start(f32[1536,128]{1,0:T(8,128)} %get-tuple-element.21.refs_0_) | copy-start | bytes 2359300
  4.8 14.9 %collective-permute-start = (f32[1024,128]{1,0:T(8,128)}, f32[1024,128]{1,0:T(8,128)S(1)}, u32[]{:S(2)}, u32[]{:S(2)}) collective-permute-start(f32[1024,128]{1,0:T(8,128)} %get-tuple-element.22), channel_id=1, source_target_pairs={{0,2},{1,3},{2,0},{3,1},{4,6},{5,7},{6,4},{7,5},{8,10},{9,11},{10,... | collective-permute-start | bytes 1572872 | tf_op jit(solution)/shard_map/ppermute | solution.py:625
  7.8 23.2 %collective-permute-start.1 = (f32[1536,128]{1,0:T(8,128)}, f32[1536,128]{1,0:T(8,128)S(1)}, u32[]{:S(2)}, u32[]{:S(2)}) collective-permute-start(f32[1536,128]{1,0:T(8,128)} %get-tuple-element.21.refs_0_), channel_id=1, source_target_pairs={{0,1},{1,0},{2,3},{3,2},{4,5},{5,4},{6,7},{7,6},{8,9},{9,8},{10,11... | collective-permute-start | bytes 2359304 | tf_op jit(solution)/shard_map/ppermute | solution.py:635
  7.8 13.3 %collective-permute-start.3 = (f32[496,128]{1,0:T(8,128)}, f32[496,128]{1,0:T(8,128)S(1)}, u32[]{:S(2)}, u32[]{:S(2)}) collective-permute-start(f32[496,128]{1,0:T(8,128)} %get-tuple-element.23), channel_id=1, source_target_pairs={{0,4},{8,12},{16,20},{24,28},{4,0},{12,8},{20,16},{28,24},{1,5},{9... | collective-permute-start | bytes 761864 | tf_op jit(solution)/shard_map/ppermute | solution.py:631
  9.3 11.8 %collective-permute-start.4 = (f32[496,128]{1,0:T(8,128)}, f32[496,128]{1,0:T(8,128)S(1)}, u32[]{:S(2)}, u32[]{:S(2)}) collective-permute-start(f32[496,128]{1,0:T(8,128)} %get-tuple-element.24), channel_id=1, source_target_pairs={{4,8},{12,16},{20,24},{8,4},{16,12},{24,20},{5,9},{13,17},{21,25},... | collective-permute-start | bytes 761864 | tf_op jit(solution)/shard_map/ppermute | solution.py:631
  19.7 11.3 %collective-permute-start.2 = (f32[1024,128]{1,0:T(8,128)S(1)}, f32[1024,128]{1,0:T(8,128)S(1)}, u32[]{:S(2)}, u32[]{:S(2)}) collective-permute-start(f32[1024,128]{1,0:T(8,128)S(1)} %collective-permute-done.refs_1_), channel_id=1, source_target_pairs={{0,1},{1,0},{2,3},{3,2},{4,5},{5,4},{6,7},{7,6},{8,9},{9,8},{10,11... | collective-permute-start | bytes 1572872 | tf_op jit(solution)/shard_map/ppermute | solution.py:635
  21.2 7.3 %collective-permute-start.5 = (f32[448,128]{1,0:T(8,128)S(1)}, f32[448,128]{1,0:T(8,128)S(1)}, u32[]{:S(2)}, u32[]{:S(2)}) collective-permute-start(f32[448,128]{1,0:T(8,128)S(1)} %relay.1.refs_4_), channel_id=1, source_target_pairs={{0,2},{1,3},{2,0},{3,1},{4,6},{5,7},{6,4},{7,5},{8,10},{9,11},{10,... | collective-permute-start | bytes 688136 | tf_op jit(solution)/shard_map/ppermute | solution.py:625
  21.8 7.7 %collective-permute-start.7 = (f32[448,128]{1,0:T(8,128)S(1)}, f32[448,128]{1,0:T(8,128)S(1)}, u32[]{:S(2)}, u32[]{:S(2)}) collective-permute-start(f32[448,128]{1,0:T(8,128)S(1)} %relay.1.refs_4_), channel_id=1, source_target_pairs={{0,1},{1,0},{2,3},{3,2},{4,5},{5,4},{6,7},{7,6},{8,9},{9,8},{10,11... | collective-permute-start | bytes 688136 | tf_op jit(solution)/shard_map/ppermute | solution.py:635
  22.9 1.5 %collective-permute-start.6 = (f32[120,128]{1,0:T(8,128)S(1)}, f32[120,128]{1,0:T(8,128)S(1)}, u32[]{:S(2)}, u32[]{:S(2)}) collective-permute-start(f32[120,128]{1,0:T(8,128)S(1)} %get-tuple-element.25), channel_id=1, source_target_pairs={{0,1},{2,3},{1,0},{3,2},{4,5},{6,7},{5,4},{7,6},{8,9},{10,11},{9,8... | collective-permute-start | bytes 184328 | tf_op jit(solution)/shard_map/ppermute | solution.py:631
  28.5 1.9 %collective-permute-start.8 = (f32[448,128]{1,0:T(8,128)S(1)}, f32[448,128]{1,0:T(8,128)S(1)}, u32[]{:S(2)}, u32[]{:S(2)}) collective-permute-start(f32[448,128]{1,0:T(8,128)S(1)} %collective-permute-done.5.refs_5_), channel_id=1, source_target_pairs={{0,1},{1,0},{2,3},{3,2},{4,5},{5,4},{6,7},{7,6},{8,9},{9,8},{10,11... | collective-permute-start | bytes 688136 | tf_op jit(solution)/shard_map/ppermute | solution.py:635
  28.5 16.1 %collective-permute-start.9 = (f32[512,128]{1,0:T(8,128)S(1)}, f32[512,128]{1,0:T(8,128)S(1)}, u32[]{:S(2)}, u32[]{:S(2)}) collective-permute-start(f32[512,128]{1,0:T(8,128)S(1)} %copy-done.6), channel_id=1, source_target_pairs={{0,2},{1,3},{2,0},{3,1},{4,6},{5,7},{6,4},{7,5},{8,10},{9,11},{10,... | collective-permute-start | bytes 786440 | tf_op jit(solution)/shard_map/ppermute | solution.py:625
  29.4 15.2 %collective-permute-start.10 = (f32[512,128]{1,0:T(8,128)S(1)}, f32[512,128]{1,0:T(8,128)S(1)}, u32[]{:S(2)}, u32[]{:S(2)}) collective-permute-start(f32[512,128]{1,0:T(8,128)S(1)} %copy-done.6), channel_id=1, source_target_pairs={{0,3},{1,2},{2,1},{3,0},{4,7},{5,6},{6,5},{7,4},{8,11},{9,10},{10,... | collective-permute-start | bytes 786440 | tf_op jit(solution)/shard_map/ppermute | solution.py:648
  30.3 14.3 %collective-permute-start.11 = (f32[120,128]{1,0:T(8,128)S(1)}, f32[120,128]{1,0:T(8,128)S(1)}, u32[]{:S(2)}, u32[]{:S(2)}) collective-permute-start(f32[120,128]{1,0:T(8,128)S(1)} %get-tuple-element.34), channel_id=1, source_target_pairs={{1,2},{2,1},{5,6},{6,5},{9,10},{10,9},{13,14},{14,13},{17,18},{18,... | collective-permute-start | bytes 184328 | tf_op jit(solution)/shard_map/ppermute | solution.py:631
  53.5 3.8 %collective-permute-start.12 = (f32[1024,128]{1,0:T(8,128)S(1)}, f32[1024,128]{1,0:T(8,128)S(1)}, u32[]{:S(2)}, u32[]{:S(2)}) collective-permute-start(f32[1024,128]{1,0:T(8,128)S(1)} %get-tuple-element.37), channel_id=1, source_target_pairs={{0,1},{1,0},{2,3},{3,2},{4,5},{5,4},{6,7},{7,6},{8,9},{9,8},{10,11... | collective-permute-start | bytes 1572872 | tf_op jit(solution)/shard_map/ppermute | solution.py:635
  57.3 8.7 %collective-permute-start.13 = (f32[512,128]{1,0:T(8,128)S(1)}, f32[512,128]{1,0:T(8,128)S(1)}, u32[]{:S(2)}, u32[]{:S(2)}) collective-permute-start(f32[512,128]{1,0:T(8,128)S(1)} %slice_add_fusion), channel_id=1, source_target_pairs={{0,2},{1,3},{2,0},{3,1},{4,6},{5,7},{6,4},{7,5},{8,10},{9,11},{10,... | collective-permute-start | bytes 786440 | tf_op jit(solution)/shard_map/ppermute | solution.py:625

commit v11 on v10

--- a/solution.py
+++ b/solution.py
@@ -28,7 +28,7 @@
 HALO = CSWEEPS
 HALF = TE
 YBLOCKS = HALF + 2 * HALO
-C_SIZE, L_SIZE, U_SIZE = TE + 2, LOW[0] + 1, HIGH[0] + 1
+CELLS = 9
 ROW0 = ROW
 SLAB_ROWS = ROW0 + YBLOCKS * SLABX + ROW0
 
@@ -208,7 +208,7 @@
     tiles = width_gy * TILES
     none = tiles
     bodies, halos = refs[:width_gy], refs[width_gy : 2 * width_gy]
-    pot, slope, cell_at, cell_of, pa, pb, la, lb, ua, ub, s_c, s_l, s_u, sems = refs[2 * width_gy :]
+    pot, slope, cell_at, cell_of, table, pa, pb, la, lb, ua, ub, s_c, s_l, s_u, sems = refs[2 * width_gy :]
     i = lax.axis_index("gx")
     j = lax.axis_index("gy")
     rows_gx = lax.axis_size("gx")
@@ -217,12 +217,12 @@
     moves = []
     for part in range(width_gy):
         at = 0
-        pieces = [(bodies[part], 0, pa, part * C_SIZE + 1, TE), (bodies[part], TE * ROW, s_c, part * TE, TE)]
+        pieces = [(bodies[part], 0, pa, part * TE, TE), (bodies[part], TE * ROW, s_c, part * TE, TE)]
         for target, first, count in (
-            (la, part * L_SIZE, LOW[0]),
+            (la, part * LOW[0], LOW[0]),
             (s_l, part * LOW[1], LOW[1]),
             (None, 0, LOW[2]),
-            (ua, part * U_SIZE + 1, HIGH[0]),
+            (ua, part * HIGH[0], HIGH[0]),
             (s_u, part * HIGH[1], HIGH[1]),
         ):
             if target is not None:
@@ -239,8 +239,33 @@
 
     fill_maps(chips, pos, cell_at, cell_of)
 
-    def row_of(slot, size, plane):
-        return ROW0 + (lax.div(slot, TILES) * size + plane) * ROW + lax.rem(slot, TILES)
+    def row_of(slot, size):
+        pair, second = lax.shift_right_logical(slot, 1), lax.bitwise_and(slot, 1)
+        return ROW0 + pair * (size * ROW) + second
+
+    def enter(slot, carry):
+        for which, size in enumerate((TE, LOW[0], HIGH[0])):
+            cell = cell_of[which, slot]
+            upper = lax.bitwise_and(cell, 1)
+            beside = cell_at[which, cell + 1 - 2 * upper]
+            here = [cell_at[at, cell] for at in range(3)]
+            near = (slot, cell_at[which, cell - 2], cell_at[which, cell + 2])
+            near += (jnp.where(upper == 1, beside, none), jnp.where(upper == 1, none, beside))
+            rows = [row_of(at, size) for at in near]
+            if which == 0:
+                rows += [row_of(here[1], LOW[0]) + (LOW[0] - 1) * ROW, row_of(here[2], HIGH[0])]
+            else:
+                centre = row_of(here[0], TE)
+                rows += [centre + (TE - 1) * ROW, centre]
+            rows.append(upper)
+            for at, row in enumerate(rows):
+                table[(which * tiles + slot) * 8 + at] = row
+        return carry
+
+    lax.fori_loop(0, tiles, enter, 0)
+
+    def entry(which, slot):
+        return [table[(which * tiles + slot) * 8 + at] for at in range(8)]
 
     def plane_at(ref, row):
         return ref[pl.ds(row, SUB, stride=TILES), :]
@@ -248,7 +273,7 @@
     def put_plane(ref, row, value):
         ref[pl.ds(row, SUB, stride=TILES), :] = value
 
-    for ref, count in ((pa, C_SIZE), (pb, C_SIZE), (la, L_SIZE), (lb, L_SIZE), (ua, U_SIZE), (ub, U_SIZE)):
+    for ref, count in ((pa, TE), (pb, TE), (la, LOW[0]), (lb, LOW[0]), (ua, HIGH[0]), (ub, HIGH[0])):
         first = ROW0 + width_gy * count * ROW
         for row in range(first, first + count * ROW, SUB):
             ref[row : row + SUB] = zero
@@ -281,14 +306,9 @@
     def z_minus(ref, own, ghost_row):
         return roll(jnp.where(last_z, plane_at(ref, ghost_row), own), 1, 1)
 
-    def around(which, slot):
-        cell = cell_of[which, slot]
-        upper = cell % 2
-        beside = cell_at[which, cell + 1 - 2 * upper]
-        near = (cell_at[which, cell - 2], cell_at[which, cell + 2])
-        near += (jnp.where(upper == 1, beside, none), jnp.where(upper == 1, none, beside))
+    def y_ends(upper):
         quarter = lane // TE
-        return cell, (slot, *near, quarter == upper, quarter == lax.rem(upper + 3, 4))
+        return quarter == upper, quarter == lax.bitwise_and(upper + 3, 3)
 
     bufs = ((pa, la, ua), (pb, lb, ub))
     for k in range(SWEEPS):
@@ -296,101 +316,79 @@
         keep, gain = 1.0 - weight, weight / (6.0 + EPS)
         (c_src, l_src, u_src), (c_dst, l_dst, u_dst) = bufs[k % 2], bufs[(k + 1) % 2]
 
-        def ghosts(slot, carry):
-            cell = cell_of[0, slot]
-            below, above = cell_at[1, cell], cell_at[2, cell]
-            over, under = cell_at[0, cell_of[1, slot]], cell_at[0, cell_of[2, slot]]
-            put_plane(c_src, row_of(slot, C_SIZE, 0), plane_at(l_src, row_of(below, L_SIZE, LOW[0] - 1)))
-            put_plane(c_src, row_of(slot, C_SIZE, TE + 1), plane_at(u_src, row_of(above, U_SIZE, 1)))
-            put_plane(l_src, row_of(slot, L_SIZE, LOW[0]), plane_at(c_src, row_of(over, C_SIZE, 1)))
-            put_plane(u_src, row_of(slot, U_SIZE, 0), plane_at(c_src, row_of(under, C_SIZE, TE)))
-            return carry
-
-        lax.fori_loop(0, tiles, ghosts, 0)
-
-        def relax(src, dst, size, slots, first, count, s_ref, s_size, s_first):
-            slot, y_m, y_p, z_m, z_p, first_y, last_y = slots
-            row, s_row = row_of(slot, size, first), row_of(slot, s_size, s_first)
-            up, down = row + TILES, row - TILES
-            row_m, row_p = row_of(y_m, size, first) + (ROW - TILES), row_of(y_p, size, first) - (ROW - TILES)
-            row_zm, row_zp = row_of(z_m, size, first), row_of(z_p, size, first)
-            before, own = plane_at(src, row - ROW), plane_at(src, row)
-            for step in range(0, count * ROW, ROW):
-                after = plane_at(src, row + (step + ROW))
-                total = (before + after) + plane_at(s_ref, s_row + step)
-                along_y = y_minus(src, own, last_y, down + step, row_m + step)
-                along_y = along_y + y_plus(src, own, first_y, up + step, row_p + step)
+        def relax(src, dst, places, first, count, s_ref, s_row, before, beyond):
+            row, row_m, row_p, row_zm, row_zp, _, _, upper = places
+            first_y, last_y = y_ends(upper)
+            own = plane_at(src, row + first * ROW)
+            for p in range(count):
+                step = (first + p) * ROW
+                after = plane_at(src, row + (step + ROW)) if beyond is None or p < count - 1 else beyond
+                total = (before + after) + plane_at(s_ref, s_row + p * ROW)
+                along_y = y_minus(src, own, last_y, row + (step - TILES), row_m + (step + ROW - TILES))
+                along_y = along_y + y_plus(src, own, first_y, row + (step + TILES), row_p + (step + TILES - ROW))
                 along_z = z_minus(src, own, row_zm + step) + z_plus(src, own, row_zp + step)
                 put_plane(dst, row + step, keep * own + gain * (total + (along_y + along_z)))
                 before, own = own, after
 
         def sweep_tile(slot, carry):
-            _, slots = around(0, slot)
-            relax(c_src, c_dst, C_SIZE, slots, 1, TE, s_c, TE, 0)
-            _, slots = around(1, slot)
+            at = entry(0, slot)
+            relax(c_src, c_dst, at, 0, TE, s_c, at[0], plane_at(l_src, at[5]), plane_at(u_src, at[6]))
+            at = entry(1, slot)
             count = LOW[0] - 1 - k
-            relax(l_src, l_dst, L_SIZE, slots, LOW[0] - count, count, s_l, LOW[1], LOW[1] - count)
-            _, slots = around(2, slot)
-            relax(u_src, u_dst, U_SIZE, slots, 1, HIGH[0] - 1 - k, s_u, HIGH[1], 0)
+            s_row = row_of(slot, LOW[1]) + (LOW[1] - count) * ROW
+            before, beyond = plane_at(l_src, at[0] + k * ROW), plane_at(c_src, at[6])
+            relax(l_src, l_dst, at, k + 1, count, s_l, s_row, before, beyond)
+            at = entry(2, slot)
+            relax(u_src, u_dst, at, 0, HIGH[0] - 1 - k, s_u, row_of(slot, HIGH[1]), plane_at(c_src, at[5]), None)
             return carry
 
-        lax.fori_loop(0, tiles, sweep_tile, 0)
+        lax.fori_loop(0, tiles, sweep_tile, 0, unroll=2)
 
     field, f_l, f_u = bufs[SWEEPS % 2]
     for t in range(TILES):
-        turn = jnp.where(cell_of[0, t] % 2 == 1, LANES - TE, 0)
+        turn = jnp.where(table[t * 8 + 7] == 1, LANES - TE, 0)
 
         def turn_back(p, carry):
-            value = plane_at(field, p * ROW + row_of(t, C_SIZE, 1))
+            value = plane_at(field, p * ROW + (ROW0 + t))
             put_plane(pot, pl.multiple_of(p * ROW, ROW) + t, pltpu.roll(value, turn, 1))
             return carry
 
         lax.fori_loop(0, TE, turn_back, 0, unroll=8)
 
-    def squares(ref, size, slots, local, x, first, count, x_last=None):
-        slot, _, y_p, _, z_p, first_y, _ = slots
-        row = row_of(slot, size, first)
-        up, row_p, row_z = row + TILES, row_of(y_p, size, first) - (ROW - TILES), row_of(z_p, size, first)
+    def squares(ref, places, local, x, first, count, beyond):
+        row, _, row_p, _, row_z, _, _, upper = places
+        first_y, _ = y_ends(upper)
         target = (local * SLABX + x) * SUB
-        own = plane_at(ref, row)
+        own = plane_at(ref, row + first * ROW)
         for p in range(count):
-            last = p == count - 1 and x_last is not None
-            after = x_last if last else plane_at(ref, row + (p + 1) * ROW)
+            step = (first + p) * ROW
+            after = plane_at(ref, row + (step + ROW)) if beyond is None or p < count - 1 else beyond
             d_x = after - own
-            d_y = y_plus(ref, own, first_y, up + p * ROW, row_p + p * ROW) - own
-            d_z = z_plus(ref, own, row_z + p * ROW) - own
+            d_y = y_plus(ref, own, first_y, row + (step + TILES), row_p + (step + TILES - ROW)) - own
+            d_z = z_plus(ref, own, row_z + step) - own
             rows = pl.ds(pl.multiple_of(target + p * SUB, SUB), SUB)
             slope[rows, :] = d_x * d_x + d_y * d_y + d_z * d_z
             own = after
 
     def slope_tile(slot, carry):
-        for which in range(3):
-            cell, slots = around(which, slot)
-            local, inside = window(which, cell, i, j, rows_gx)
-
-            @pl.when(inside)
-            def _():
-                if which == 0:
-                    above = plane_at(f_u, row_of(cell_at[2, cell], U_SIZE, 1))
-                    squares(field, C_SIZE, slots, local, HALO, 1, TE, above)
-                elif which == 1:
-                    centre = plane_at(field, row_of(cell_at[0, cell], C_SIZE, 1))
-                    squares(f_l, L_SIZE, slots, local, HALO - 2, LOW[0] - 2, 2, centre)
-                else:
-                    squares(f_u, U_SIZE, slots, local, HALO + TE, 1, 2)
-
+        at, local = entry(0, slot), window(0, cell_of[0, slot], i, j, rows_gx)
+        squares(field, at, local, HALO, 0, TE, plane_at(f_u, at[6]))
+        at, local = entry(1, slot), window(1, cell_of[1, slot], i, j, rows_gx)
+        squares(f_l, at, local, HALO - 2, LOW[0] - 2, 2, plane_at(field, at[6]))
+        at, local = entry(2, slot), window(2, cell_of[2, slot], i, j, rows_gx)
+        squares(f_u, at, local, HALO + TE, 0, 2, None)
         return carry
 
-    lax.fori_loop(0, tiles, slope_tile, 0)
+    lax.fori_loop(0, tiles, slope_tile, 0, unroll=2)
 
 
 def window(which, cell, i, j, rows_gx):
     local = cell - 4 * j
-    inside = (local >= 0) & (local < 8)
+    inside = (local >= 0) & (local < CELLS - 1)
     if which > 0:
         row = i - 1 if which == 1 else i + 1
         inside = inside & (row >= 0) & (row < rows_gx)
-    return local, inside
+    return jnp.where(inside, local, CELLS - 1)
 
 
 def slab_steps_kernel(chips, pos, k0_table, beta_table, *refs):
@@ -505,23 +503,17 @@
             for which, by in enumerate((0, -1, 1)):
                 tile = jnp.clip(i + by, 0, rows_gx - 1) * tiles + dev * TILES + t
                 cell = (pos[1, tile] + 1) * 2 + pos[2, tile]
-                local, inside = window(which, cell, i, j, rows_gx)
+                local = window(which, cell, i, j, rows_gx)
                 source, start, x, count = (
                     (sigmas.at[part], 0, HALO, TE),
                     (halos[part], low_at, HALO - 2, 2),
                     (halos[part], high_at, HALO + TE, 2),
                 )[which]
-
-                @pl.when(inside)
-                def _():
-                    def plane(p, carry):
-                        rows = pl.ds(pl.multiple_of((local * SLABX + x + p) * SUB, SUB), SUB)
-                        at = pl.multiple_of(start + p * ROW, SUB)
-                        sigma = source[pl.ds(at + t, SUB, stride=TILES), :]
-                        heat[rows, :] = sigma * slope[rows, :]
-                        return carry
-
-                    lax.fori_loop(0, count, plane, 0, unroll=count)
+                first = pl.multiple_of((local * SLABX + x) * SUB, SUB)
+                for p in range(count):
+                    rows = pl.ds(pl.multiple_of(first + p * SUB, SUB), SUB)
+                    sigma = source[pl.ds(start + p * ROW + t, SUB, stride=TILES), :]
+                    heat[rows, :] = sigma * slope[rows, :]
 
     def place_heat(at, carry):
         first = at - 1
@@ -734,13 +726,14 @@
 
     pot, slope = pl.pallas_call(
         functools.partial(sweep_kernel, chips),
-        out_shape=(rows(TE * ROW), rows(8 * SLABX * SUB)),
+        out_shape=(rows(TE * ROW), rows(CELLS * SLABX * SUB)),
         in_specs=[SMEM] + [ANY] * (2 * width_gy),
         out_specs=(VMEM, VMEM),
         scratch_shapes=[
             pltpu.SMEM((3, 2 * (2 * width_gy + 2)), jnp.int32),
             pltpu.SMEM((3, tiles), jnp.int32),
-            fields(C_SIZE), fields(C_SIZE), fields(L_SIZE), fields(L_SIZE), fields(U_SIZE), fields(U_SIZE),
+            pltpu.SMEM((3 * tiles * 8,), jnp.int32),
+            fields(TE), fields(TE), fields(LOW[0]), fields(LOW[0]), fields(HIGH[0]), fields(HIGH[0]),
             fields(TE), fields(LOW[1]), fields(HIGH[1]),
             pltpu.SemaphoreType.DMA((6 * width_gy,)),
         ],
@@ -754,7 +747,7 @@
         + (rows(TE * ROW),) * (chips - 1),
         in_specs=[SMEM] * 3 + [ANY] * width_gy + [VMEM] * (width_gy + 6),
         out_specs=(VMEM,) * (2 + chips),
-        scratch_shapes=[pltpu.VMEM((8 * SLABX * SUB, LANES), f32)]
+        scratch_shapes=[pltpu.VMEM((CELLS * SLABX * SUB, LANES), f32)]
         + [pltpu.VMEM((SLAB_ROWS + 3 * SLABX, LANES), f32)]
         + [pltpu.VMEM((2 * SLAB_ROWS, LANES), f32)] * 2
         + [pltpu.VMEM((SLAB_ROWS, LANES), f32)] * 2

time: 67.5 us -> 65.8 us (0.975); the launches traced: 66.7 us -> 65.8 us
  Pallas kernels: 27.6 us -> 26.2 us
  waiting for transfers between devices: 24.6 us -> 25.4 us
    pallas_call x1, Pallas kernels: 13.5 us -> 11.8 us  [on_device(): pl.pallas_call(functools.partial(sweep_kernel, chips), out_shape=(rows(TE...]
    ppermute x4, starting transfers between devices: 6.26 us -> 5.14 us  [shifted(): return lax.ppermute(value, axis, pairs)]
    ppermute x5, starting transfers between devices: 2.24 us -> 3.24 us  [from_mate(): lax.ppermute(value, 'gy', [(d, d ^ 1) for d in range(lax.axis_size('gy'))])]
    ppermute x4, waiting for transfers between devices: 20.8 us -> 21.7 us  [shifted(): return lax.ppermute(value, axis, pairs)]
  transfers between devices with their start and end apart: 14 -> 14, of which waited for: 6 -> 6; matrix products, arithmetic and copies ran while one was open for 0% -> 0% of each run, Pallas kernels for 22% -> 20%
where the time goes in v11:
time: 65.8 us
  Pallas kernels  26.2 us (40%)
  waiting for transfers between devices  25.4 us (39%)
  starting transfers between devices  12.6 us (19%)
  between operations  0.82 us (1%)
  other arithmetic  0.79 us (1%)
    ppermute x4, waiting for transfers between devices, shifted(): return lax.ppermute(value, axis, pairs)  21.7 us
    pallas_call x1, Pallas kernels, on_device(): pl.pallas_call(functools.partial(sweep_kernel, chips), out_shape=(rows(TE...  11.8 us
    pallas_call x1, Pallas kernels, on_device(): pl.pallas_call(functools.partial(slab_steps_kernel, chips), out_shape=(ja...  8.79 us
    ppermute x4, starting transfers between devices, shifted(): return lax.ppermute(value, axis, pairs)  5.14 us
    pallas_call x1, Pallas kernels, on_device(): pl.pallas_call(prep_kernel, out_shape=(rows(3 * TE * ROW), rows(2 * TE *...  4.44 us
    ppermute x4, starting transfers between devices, with_partner(): lax.ppermute(value, axis, pairs + [(high, low) for low, high in pairs])  3.65 us
    ppermute x5, starting transfers between devices, from_mate(): lax.ppermute(value, 'gy', [(d, d ^ 1) for d in range(lax.axis_size('gy'))])  3.24 us
    ppermute x4, waiting for transfers between devices, with_partner(): lax.ppermute(value, axis, pairs + [(high, low) for low, high in pairs])  2.15 us
  transfers between devices with their start and end apart: 14, of which 6 were waited for; matrix products, arithmetic and copies ran while one was open for 0% of the time, Pallas kernels for 20%

profile of v11, /device:TPU:0, one launch (start us, length us, event | category | flops | bytes accessed | tf_op | source)
XLA Modules:
  0.0 65.8 jit_solution(508190577185869137)
XLA Ops:
  0.7 4.4 %prep.1 = (f32[1536,128]{1,0:T(8,128)}, f32[1024,128]{1,0:T(8,128)}, f32[512,128]{1,0:T(8,128)}, f32[496,128]{1,0:T(8,128)}, f32[496,128]{1,0:T(8,128)}) custom-call(f32[4]{0:T(128)} %table.1, s32[3,64]{1,0:T(4,128)} %bitcast.26, f32[512,128]{1,0:T(8,128)} %bitcast.30, f32[512,128]{1,0:T(8,128)} %bitcast.31, s32[512,128]{1,0:T(8,128)} %bitcast.32, ...), custom_call_target="tpu_custom_call" | custom-call | tf_op jit(solution)/shard_map/prep/pallas_call | solution.py:673
  5.1 0.0 copy-start.6
  5.2 2.3 %collective-permute-start = (f32[1024,128]{1,0:T(8,128)}, f32[1024,128]{1,0:T(8,128)S(1)}, u32[]{:S(2)}, u32[]{:S(2)}) collective-permute-start(f32[1024,128]{1,0:T(8,128)} %get-tuple-element.22), channel_id=1, source_target_pairs={{0,2},{1,3},{2,0},{3,1},{4,6},{5,7},{6,4},{7,5},{8,10},{9,11},{10,... | collective-permute-start | bytes 1572872 | tf_op jit(solution)/shard_map/ppermute | solution.py:617
  7.4 0.3 collective-permute-start.1
  7.7 2.0 %collective-permute-start.3 = (f32[496,128]{1,0:T(8,128)}, f32[496,128]{1,0:T(8,128)S(1)}, u32[]{:S(2)}, u32[]{:S(2)}) collective-permute-start(f32[496,128]{1,0:T(8,128)} %get-tuple-element.23), channel_id=1, source_target_pairs={{0,4},{8,12},{16,20},{24,28},{4,0},{12,8},{20,16},{28,24},{1,5},{9... | collective-permute-start | bytes 761864 | tf_op jit(solution)/shard_map/ppermute | solution.py:623
  9.7 0.7 %collective-permute-start.4 = (f32[496,128]{1,0:T(8,128)}, f32[496,128]{1,0:T(8,128)S(1)}, u32[]{:S(2)}, u32[]{:S(2)}) collective-permute-start(f32[496,128]{1,0:T(8,128)} %get-tuple-element.24), channel_id=1, source_target_pairs={{4,8},{12,16},{20,24},{8,4},{16,12},{24,20},{5,9},{13,17},{21,25},... | collective-permute-start | bytes 761864 | tf_op jit(solution)/shard_map/ppermute | solution.py:623
  10.4 9.9 %collective-permute-done.refs_1_ = f32[1024,128]{1,0:T(8,128)S(1)} collective-permute-done((f32[1024,128]{1,0:T(8,128)}, f32[1024,128]{1,0:T(8,128)S(1)}, u32[]{:S(2)}, u32[]{:S(2)}) %collective-permute-start) | collective-permute-done | bytes 524320 | tf_op jit(solution)/shard_map/ppermute | solution.py:617
  20.3 1.2 %collective-permute-done.3.inner = f32[496,128]{1,0:T(8,128)S(1)} collective-permute-done((f32[496,128]{1,0:T(8,128)}, f32[496,128]{1,0:T(8,128)S(1)}, u32[]{:S(2)}, u32[]{:S(2)}) %collective-permute-start.3) | collective-permute-done | bytes 253984 | tf_op jit(solution)/shard_map/ppermute | solution.py:623
  21.5 0.0 collective-permute-done.4.outer
  21.5 0.6 collective-permute-start.5
  22.2 0.2 collective-permute-start.7
  22.4 1.1 %slab_prep.1 = (f32[1552,128]{1,0:T(8,128)S(1)}, f32[1552,128]{1,0:T(8,128)S(1)}, f32[1552,128]{1,0:T(8,128)S(1)}, f32[120,128]{1,0:T(8,128)S(1)}, f32[120,128]{1,0:T(8,128)S(1)}) custom-call(s32[3,64]{1,0:T(4,128)S(1)} %bitcast.27, f32[4]{0:T(128)S(1)} %copy-done.4, f32[4]{0:T(128)S(1)} %copy-done.5, f32[32,4096]{1,0:T(8,128)S(1)} %copy-done.1, ...), custom_call_target="tpu_custom_call" | custom-call | tf_op jit(solution)/shard_map/slab_prep/pallas_call | solution.py:711
  23.5 0.4 collective-permute-start.6
  23.9 0.9 %collective-permute-done.6.refs_12_ = f32[120,128]{1,0:T(8,128)S(1)} collective-permute-done((f32[120,128]{1,0:T(8,128)S(1)}, f32[120,128]{1,0:T(8,128)S(1)}, u32[]{:S(2)}, u32[]{:S(2)}) %collective-permute-start.6) | collective-permute-done | bytes 61472 | tf_op jit(solution)/shard_map/ppermute | solution.py:623
  24.8 4.0 %collective-permute-done.5.refs_5_ = f32[448,128]{1,0:T(8,128)S(1)} collective-permute-done((f32[448,128]{1,0:T(8,128)S(1)}, f32[448,128]{1,0:T(8,128)S(1)}, u32[]{:S(2)}, u32[]{:S(2)}) %collective-permute-start.5) | collective-permute-done | bytes 229408 | tf_op jit(solution)/shard_map/ppermute | solution.py:617
  28.8 0.0 collective-permute-start.8
  28.8 1.3 %collective-permute-start.9 = (f32[512,128]{1,0:T(8,128)S(1)}, f32[512,128]{1,0:T(8,128)S(1)}, u32[]{:S(2)}, u32[]{:S(2)}) collective-permute-start(f32[512,128]{1,0:T(8,128)S(1)} %copy-done.6), channel_id=1, source_target_pairs={{0,2},{1,3},{2,0},{3,1},{4,6},{5,7},{6,4},{7,5},{8,10},{9,11},{10,... | collective-permute-start | bytes 786440 | tf_op jit(solution)/shard_map/ppermute | solution.py:617
  30.2 0.0 collective-permute-done.7.refs_6_
  30.2 0.5 collective-permute-start.10
  30.7 0.0 collective-permute-done.8.refs_7_
  30.7 0.7 collective-permute-start.11
  31.4 0.0 collective-permute-done.1.refs_2_
  31.4 0.0 collective-permute-done.2.refs_3_
  31.4 11.8 %sweeps.1 = (f32[512,128]{1,0:T(8,128)}, f32[2880,128]{1,0:T(8,128)S(1)}) custom-call(s32[3,64]{1,0:T(4,128)S(1)} %bitcast.28, f32[1536,128]{1,0:T(8,128)S(1)} %copy-done, f32[1024,128]{1,0:T(8,128)S(1)} %collective-permute-done.refs_1_, f32[1536,128]{1,0:T(8,128)S(1)} %collective-permute-done.1.refs_2_, f32[1024,128]{1,0:T(8,128)S(1)} %collective-permute-done.2.refs_3_, ...), custom_call_target="tpu_custom_call" | custom-call | tf_op jit(solution)/shard_map/sweeps/pallas_call | solution.py:727
  43.2 0.0 collective-permute-done.9.refs_1_
  43.3 0.0 collective-permute-done.11.refs_13_
  43.3 8.8 %slab_steps.1 = (f32[32,4096]{1,0:T(8,128)}, f32[512,128]{1,0:T(8,128)S(1)}, f32[1024,128]{1,0:T(8,128)S(1)}, f32[512,128]{1,0:T(8,128)S(1)}) custom-call(s32[3,64]{1,0:T(4,128)S(1)} %bitcast.29, f32[4]{0:T(128)S(1)} %copy-done.4, f32[4]{0:T(128)S(1)} %copy-done.5, f32[1536,128]{1,0:T(8,128)S(1)} %copy-done, f32[512,128]{1,0:T(8,128)S(1)} %collective-permute-done.9.refs_1_, ...), custom_call_target="tpu_custom_call" | custom-call | tf_op jit(solution)/shard_map/slab_steps/pallas_call | solution.py:744
  52.1 2.7 %collective-permute-start.12 = (f32[1024,128]{1,0:T(8,128)S(1)}, f32[1024,128]{1,0:T(8,128)S(1)}, u32[]{:S(2)}, u32[]{:S(2)}) collective-permute-start(f32[1024,128]{1,0:T(8,128)S(1)} %get-tuple-element.37), channel_id=1, source_target_pairs={{0,1},{1,0},{2,3},{3,2},{4,5},{5,4},{6,7},{7,6},{8,9},{9,8},{10,11... | collective-permute-start | bytes 1572872 | tf_op jit(solution)/shard_map/ppermute | solution.py:627
  54.8 1.5 %collective-permute-done.12 = f32[1024,128]{1,0:T(8,128)S(1)} collective-permute-done((f32[1024,128]{1,0:T(8,128)S(1)}, f32[1024,128]{1,0:T(8,128)S(1)}, u32[]{:S(2)}, u32[]{:S(2)}) %collective-permute-start.12) | collective-permute-done | bytes 524320 | tf_op jit(solution)/shard_map/ppermute | solution.py:627
  56.4 0.9 %collective-permute-start.13 = (f32[512,128]{1,0:T(8,128)S(1)}, f32[512,128]{1,0:T(8,128)S(1)}, u32[]{:S(2)}, u32[]{:S(2)}) collective-permute-start(f32[512,128]{1,0:T(8,128)S(1)} %slice_add_fusion), channel_id=1, source_target_pairs={{0,2},{1,3},{2,0},{3,1},{4,6},{5,7},{6,4},{7,5},{8,10},{9,11},{10,... | collective-permute-start | bytes 786440 | tf_op jit(solution)/shard_map/ppermute | solution.py:617
  57.3 7.7 %collective-permute-done.13 = f32[512,128]{1,0:T(8,128)S(1)} collective-permute-done((f32[512,128]{1,0:T(8,128)S(1)}, f32[512,128]{1,0:T(8,128)S(1)}, u32[]{:S(2)}, u32[]{:S(2)}) %collective-permute-start.13) | collective-permute-done | bytes 262176 | tf_op jit(solution)/shard_map/ppermute | solution.py:617
  65.0 0.8 %fusion = f32[512,128]{1,0:T(8,128)} fusion(f32[512,128]{1,0:T(8,128)S(1)} %collective-permute-done.13, f32[512,128]{1,0:T(8,128)S(1)} %get-tuple-element.36, f32[1024,128]{1,0:T(8,128)S(1)} %collective-permute-done.12), kind=kLoop, calls=%fused_computation.2 | loop fusion | flops 131072 | bytes 1048576 | tf_op jit(solution)/shard_map/add | solution.py:762
  (17 shorter events, 0.1 us)
Async XLA Ops:
  0.6 21.7 %copy-start.3 = (s32[64,3]{0,1:T(4,128)S(1)}, s32[64,3]{0,1:T(4,128)}, u32[]{:S(2)}) copy-start(s32[64,3]{0,1:T(4,128)} %param.13) | copy-start | bytes 2308
  0.6 21.7 %copy-start.1 = (f32[32,4096]{1,0:T(8,128)S(1)}, f32[32,4096]{1,0:T(8,128)}, u32[]{:S(2)}) copy-start(f32[32,4096]{1,0:T(8,128)} %temp.3) | copy-start | bytes 1572868
  0.7 21.7 %copy-start.2 = (s32[32,4096]{1,0:T(8,128)S(1)}, s32[32,4096]{1,0:T(8,128)}, u32[]{:S(2)}) copy-start(s32[32,4096]{1,0:T(8,128)} %mat.1) | copy-start | bytes 1572868
  0.7 21.7 %copy-start.4 = (f32[4]{0:T(128)S(1)}, f32[4]{0:T(128)}, u32[]{:S(2)}) copy-start(f32[4]{0:T(128)} %k0_table.3) | copy-start | bytes 52
  0.7 21.7 %copy-start.5 = (f32[4]{0:T(128)S(1)}, f32[4]{0:T(128)}, u32[]{:S(2)}) copy-start(f32[4]{0:T(128)} %beta_table.3) | copy-start | bytes 52
  5.1 23.7 %copy-start.6 = (f32[512,128]{1,0:T(8,128)S(1)}, f32[512,128]{1,0:T(8,128)}, u32[]{:S(2)}) copy-start(f32[512,128]{1,0:T(8,128)} %get-tuple-element.28) | copy-start | bytes 786436
  5.1 26.2 %copy-start = (f32[1536,128]{1,0:T(8,128)S(1)}, f32[1536,128]{1,0:T(8,128)}, u32[]{:S(2)}) copy-start(f32[1536,128]{1,0:T(8,128)} %get-tuple-element.21.refs_0_) | copy-start | bytes 2359300
  5.2 15.1 %collective-permute-start = (f32[1024,128]{1,0:T(8,128)}, f32[1024,128]{1,0:T(8,128)S(1)}, u32[]{:S(2)}, u32[]{:S(2)}) collective-permute-start(f32[1024,128]{1,0:T(8,128)} %get-tuple-element.22), channel_id=1, source_target_pairs={{0,2},{1,3},{2,0},{3,1},{4,6},{5,7},{6,4},{7,5},{8,10},{9,11},{10,... | collective-permute-start | bytes 1572872 | tf_op jit(solution)/shard_map/ppermute | solution.py:617
  7.4 23.9 %collective-permute-start.1 = (f32[1536,128]{1,0:T(8,128)}, f32[1536,128]{1,0:T(8,128)S(1)}, u32[]{:S(2)}, u32[]{:S(2)}) collective-permute-start(f32[1536,128]{1,0:T(8,128)} %get-tuple-element.21.refs_0_), channel_id=1, source_target_pairs={{0,1},{1,0},{2,3},{3,2},{4,5},{5,4},{6,7},{7,6},{8,9},{9,8},{10,11... | collective-permute-start | bytes 2359304 | tf_op jit(solution)/shard_map/ppermute | solution.py:627
  7.7 13.8 %collective-permute-start.3 = (f32[496,128]{1,0:T(8,128)}, f32[496,128]{1,0:T(8,128)S(1)}, u32[]{:S(2)}, u32[]{:S(2)}) collective-permute-start(f32[496,128]{1,0:T(8,128)} %get-tuple-element.23), channel_id=1, source_target_pairs={{0,4},{8,12},{16,20},{24,28},{4,0},{12,8},{20,16},{28,24},{1,5},{9... | collective-permute-start | bytes 761864 | tf_op jit(solution)/shard_map/ppermute | solution.py:623
  9.7 11.8 %collective-permute-start.4 = (f32[496,128]{1,0:T(8,128)}, f32[496,128]{1,0:T(8,128)S(1)}, u32[]{:S(2)}, u32[]{:S(2)}) collective-permute-start(f32[496,128]{1,0:T(8,128)} %get-tuple-element.24), channel_id=1, source_target_pairs={{4,8},{12,16},{20,24},{8,4},{16,12},{24,20},{5,9},{13,17},{21,25},... | collective-permute-start | bytes 761864 | tf_op jit(solution)/shard_map/ppermute | solution.py:623
  20.3 11.1 %collective-permute-start.2 = (f32[1024,128]{1,0:T(8,128)S(1)}, f32[1024,128]{1,0:T(8,128)S(1)}, u32[]{:S(2)}, u32[]{:S(2)}) collective-permute-start(f32[1024,128]{1,0:T(8,128)S(1)} %collective-permute-done.refs_1_), channel_id=1, source_target_pairs={{0,1},{1,0},{2,3},{3,2},{4,5},{5,4},{6,7},{7,6},{8,9},{9,8},{10,11... | collective-permute-start | bytes 1572872 | tf_op jit(solution)/shard_map/ppermute | solution.py:627
  21.5 7.3 %collective-permute-start.5 = (f32[448,128]{1,0:T(8,128)S(1)}, f32[448,128]{1,0:T(8,128)S(1)}, u32[]{:S(2)}, u32[]{:S(2)}) collective-permute-start(f32[448,128]{1,0:T(8,128)S(1)} %relay.1.refs_4_), channel_id=1, source_target_pairs={{0,2},{1,3},{2,0},{3,1},{4,6},{5,7},{6,4},{7,5},{8,10},{9,11},{10,... | collective-permute-start | bytes 688136 | tf_op jit(solution)/shard_map/ppermute | solution.py:617
  22.2 8.0 %collective-permute-start.7 = (f32[448,128]{1,0:T(8,128)S(1)}, f32[448,128]{1,0:T(8,128)S(1)}, u32[]{:S(2)}, u32[]{:S(2)}) collective-permute-start(f32[448,128]{1,0:T(8,128)S(1)} %relay.1.refs_4_), channel_id=1, source_target_pairs={{0,1},{1,0},{2,3},{3,2},{4,5},{5,4},{6,7},{7,6},{8,9},{9,8},{10,11... | collective-permute-start | bytes 688136 | tf_op jit(solution)/shard_map/ppermute | solution.py:627
  23.5 1.3 %collective-permute-start.6 = (f32[120,128]{1,0:T(8,128)S(1)}, f32[120,128]{1,0:T(8,128)S(1)}, u32[]{:S(2)}, u32[]{:S(2)}) collective-permute-start(f32[120,128]{1,0:T(8,128)S(1)} %get-tuple-element.25), channel_id=1, source_target_pairs={{0,1},{2,3},{1,0},{3,2},{4,5},{6,7},{5,4},{7,6},{8,9},{10,11},{9,8... | collective-permute-start | bytes 184328 | tf_op jit(solution)/shard_map/ppermute | solution.py:623
  28.8 1.9 %collective-permute-start.8 = (f32[448,128]{1,0:T(8,128)S(1)}, f32[448,128]{1,0:T(8,128)S(1)}, u32[]{:S(2)}, u32[]{:S(2)}) collective-permute-start(f32[448,128]{1,0:T(8,128)S(1)} %collective-permute-done.5.refs_5_), channel_id=1, source_target_pairs={{0,1},{1,0},{2,3},{3,2},{4,5},{5,4},{6,7},{7,6},{8,9},{9,8},{10,11... | collective-permute-start | bytes 688136 | tf_op jit(solution)/shard_map/ppermute | solution.py:627
  28.8 14.4 %collective-permute-start.9 = (f32[512,128]{1,0:T(8,128)S(1)}, f32[512,128]{1,0:T(8,128)S(1)}, u32[]{:S(2)}, u32[]{:S(2)}) collective-permute-start(f32[512,128]{1,0:T(8,128)S(1)} %copy-done.6), channel_id=1, source_target_pairs={{0,2},{1,3},{2,0},{3,1},{4,6},{5,7},{6,4},{7,5},{8,10},{9,11},{10,... | collective-permute-start | bytes 786440 | tf_op jit(solution)/shard_map/ppermute | solution.py:617
  30.2 13.1 %collective-permute-start.10 = (f32[512,128]{1,0:T(8,128)S(1)}, f32[512,128]{1,0:T(8,128)S(1)}, u32[]{:S(2)}, u32[]{:S(2)}) collective-permute-start(f32[512,128]{1,0:T(8,128)S(1)} %copy-done.6), channel_id=1, source_target_pairs={{0,3},{1,2},{2,1},{3,0},{4,7},{5,6},{6,5},{7,4},{8,11},{9,10},{10,... | collective-permute-start | bytes 786440 | tf_op jit(solution)/shard_map/ppermute | solution.py:640
  30.7 12.6 %collective-permute-start.11 = (f32[120,128]{1,0:T(8,128)S(1)}, f32[120,128]{1,0:T(8,128)S(1)}, u32[]{:S(2)}, u32[]{:S(2)}) collective-permute-start(f32[120,128]{1,0:T(8,128)S(1)} %get-tuple-element.34), channel_id=1, source_target_pairs={{1,2},{2,1},{5,6},{6,5},{9,10},{10,9},{13,14},{14,13},{17,18},{18,... | collective-permute-start | bytes 184328 | tf_op jit(solution)/shard_map/ppermute | solution.py:623
  52.1 4.3 %collective-permute-start.12 = (f32[1024,128]{1,0:T(8,128)S(1)}, f32[1024,128]{1,0:T(8,128)S(1)}, u32[]{:S(2)}, u32[]{:S(2)}) collective-permute-start(f32[1024,128]{1,0:T(8,128)S(1)} %get-tuple-element.37), channel_id=1, source_target_pairs={{0,1},{1,0},{2,3},{3,2},{4,5},{5,4},{6,7},{7,6},{8,9},{9,8},{10,11... | collective-permute-start | bytes 1572872 | tf_op jit(solution)/shard_map/ppermute | solution.py:627
  56.4 8.7 %collective-permute-start.13 = (f32[512,128]{1,0:T(8,128)S(1)}, f32[512,128]{1,0:T(8,128)S(1)}, u32[]{:S(2)}, u32[]{:S(2)}) collective-permute-start(f32[512,128]{1,0:T(8,128)S(1)} %slice_add_fusion), channel_id=1, source_target_pairs={{0,2},{1,3},{2,0},{3,1},{4,6},{5,7},{6,4},{7,5},{8,10},{9,11},{10,... | collective-permute-start | bytes 786440 | tf_op jit(solution)/shard_map/ppermute | solution.py:617

commit v12 on v11

--- a/solution.py
+++ b/solution.py
@@ -124,7 +124,7 @@
     return jnp.minimum(pos[0, 0], 0)
 
 
-def slab_kernel(pos, k0_table, beta_table, temp, mat, inner, outer, t_ext, k0_ext, b_ext, edge_in, edge_out, native_t, native_m, edge_low, edge_high):
+def slab_kernel(pos, k0_table, beta_table, temp, mat, inner, outer, sigma, t_ext, k0_ext, b_ext, edge_in, packet, native_t, native_m, edge_low, edge_high):
     start = loose(pos)
     even = lax.rem(lax.axis_index("gx"), 2) == 0
     blocks = temp.shape[1] // LANES
@@ -171,7 +171,8 @@
                     edge_high[first : first + SUB] = jnp.where(half, halves[0][2 + odd], halves[1][3 - odd])
     even = lax.rem(lax.axis_index("gy"), 2) == 0
     edge_in[...] = jnp.where(even, edge_high[...], edge_low[...])
-    edge_out[...] = jnp.where(even, edge_low[...], edge_high[...])
+    packet[0 : TE * ROW] = sigma[...]
+    packet[TE * ROW :] = jnp.where(even, edge_low[...], edge_high[...])
 
 
 def fill_maps(chips, pos, cell_at, cell_of):
@@ -342,7 +343,7 @@
             relax(u_src, u_dst, at, 0, HIGH[0] - 1 - k, s_u, row_of(slot, HIGH[1]), plane_at(c_src, at[5]), None)
             return carry
 
-        lax.fori_loop(0, tiles, sweep_tile, 0, unroll=2)
+        lax.fori_loop(0, tiles, sweep_tile, 0, unroll=4)
 
     field, f_l, f_u = bufs[SWEEPS % 2]
     for t in range(TILES):
@@ -395,16 +396,21 @@
     width_gy = 2 * chips
     tiles = width_gy * TILES
     halos = refs[width_gy : 2 * width_gy]
-    slope, t_in, k0_in, b_in, y_in, y_out, temp_out = refs[2 * width_gy : 2 * width_gy + 7]
-    mine, bundle = refs[2 * width_gy + 7 : 2 * width_gy + 9]
-    across = refs[2 * width_gy + 9 : 2 * width_gy + 8 + chips]
-    heat, q_ext, state_a, state_b, k0_all, b_all, blocks, sigmas, sems = refs[2 * width_gy + 8 + chips :]
+    slope, t_in, k0_in, b_in, y_in, temp_out = refs[2 * width_gy : 2 * width_gy + 6]
+    mine, bundle = refs[2 * width_gy + 6 : 2 * width_gy + 8]
+    across = refs[2 * width_gy + 8 : 2 * width_gy + 7 + chips]
+    heat, q_ext, state_a, state_b, k0_all, b_all, blocks, sigmas, y_out, sems = refs[2 * width_gy + 7 + chips :]
     moves = []
     for part in range(width_gy):
         start = 2 * TE * ROW if part % chips == 0 else 0
         source = refs[part].at[start : start + TE * ROW]
         moves.append(pltpu.make_async_copy(source, sigmas.at[part], sems.at[part]))
         moves[-1].start()
+    edges = []
+    for which, d in enumerate((1, chips - 1)):
+        source = refs[chips + d].at[TE * ROW : TE * ROW + HALO * SLABX]
+        edges.append(pltpu.make_async_copy(source, y_out.at[which], sems.at[width_gy + which]))
+        edges[-1].start()
     i = lax.axis_index("gx")
     j = lax.axis_index("gy")
     rows_gx = lax.axis_size("gx")
@@ -464,7 +470,8 @@
             temp, k0, beta = t_in[rows], k0_in[rows], b_in[rows]
             if low is not None:
                 place = slice(at * SLABX + g * SUB, at * SLABX + (g + 1) * SUB)
-                value = jnp.where(even, *((y_out[place], y_in[place])[:: 1 if low else -1]))
+                other = jnp.where(even, y_out[0, place], y_out[1, place])
+                value = jnp.where(even, *((other, y_in[place])[:: 1 if low else -1]))
                 swapped = roll(value, NZ, 1)
                 if low:
                     temp = jnp.where(half, value, temp)
@@ -479,15 +486,16 @@
             k0_all[rows], b_all[rows] = k0, beta
             store(state_a, block, g, temp, cond)
 
+    def begin_inner(block, carry):
+        begin(block, None, 0)
+        return carry
+
+    lax.fori_loop(HALO, YBLOCKS - HALO, begin_inner, 0, unroll=8)
+    for move in edges:
+        move.wait()
     for e in range(HALO):
         begin(e, True, e)
         begin(YBLOCKS - HALO + e, False, e)
-
-    def begin_inner(block, carry):
-        begin(block, None, 0)
-        return carry
-
-    lax.fori_loop(HALO, YBLOCKS - HALO, begin_inner, 0, unroll=4)
 
     def clear(at, carry):
         heat[pl.ds(pl.multiple_of(at * SUB, SUB), SUB), :] = zero
@@ -528,7 +536,7 @@
                 q_ext[rows_of(block, g)] = pick([turned(cells[c], c - r - c % 2) for c in range(4)])
         return carry
 
-    lax.fori_loop(0, HALF // 4 + 2, place_heat, 0, unroll=2)
+    lax.fori_loop(0, HALF // 4 + 2, place_heat, 0, unroll=5)
 
     for step in range(CSWEEPS):
         src, dst = (state_a, state_b)[:: 1 if step % 2 == 0 else -1]
@@ -565,7 +573,7 @@
             return ahead, flux_y
 
         first, second = load(src, 0), load(src, 1)
-        lax.fori_loop(1, YBLOCKS - 1, advance, (second, y_fluxes(0, first, second)), unroll=6)
+        lax.fori_loop(1, YBLOCKS - 1, advance, (second, y_fluxes(0, first, second)), unroll=12)
     final = state_b if CSWEEPS % 2 else state_a
 
     def give_out(yq, carry):
@@ -586,7 +594,7 @@
                 blocks[pl.ds((c * TE + g * SUB) * SUB + yq, SUB, stride=SUB), :] = value
         return carry
 
-    lax.fori_loop(0, HALF // 4, give_out, 0, unroll=2)
+    lax.fori_loop(0, HALF // 4, give_out, 0, unroll=4)
     places = []
     mate = j + 1 - 2 * lax.rem(j, 2)
     targets = [(mine, 0, j)] + [(across[d - 1], 0, j + 2 * d) for d in range(1, chips)]
@@ -608,7 +616,7 @@
             target[pl.ds(pl.multiple_of(p * ROW, ROW) + first, SUB, stride=TILES), :] = value
         return carry
 
-    lax.fori_loop(0, TE, pack, 0, unroll=4)
+    lax.fori_loop(0, TE, pack, 0, unroll=8)
 
 
 def shifted(value, axis, by, wrap=False):
@@ -704,20 +712,21 @@
         name="relay",
     )(inner, outer)
     halos = [halo] + [shifted(halo, "gy", 2 * d, True) for d in range(1, chips)]
-    sigmas = [bodies[0]] + [shifted(sigma, "gy", 2 * d, True) for d in range(1, chips)]
-    sigmas += [bodies[chips]] + [to_other_core(sigma, d) for d in range(1, chips)]
-
     native = pltpu.VMEM((width // LANES * SLABX + SUB, LANES), f32)
-    t_ext, k0_ext, b_ext, edge_in, edge_out = pl.pallas_call(
+    t_ext, k0_ext, b_ext, edge_in, packet = pl.pallas_call(
         slab_kernel,
-        out_shape=(rows(SLAB_ROWS),) * 3 + (rows(HALO * SLABX),) * 2,
-        in_specs=[SMEM] * 3 + [VMEM] * 4,
+        out_shape=(rows(SLAB_ROWS),) * 3 + (rows(HALO * SLABX), rows(TE * ROW + HALO * SLABX)),
+        in_specs=[SMEM] * 3 + [VMEM] * 5,
         out_specs=(VMEM,) * 5,
         scratch_shapes=[native, native] + [pltpu.VMEM((HALO * SLABX, LANES), f32)] * 2,
         compiler_params=PARAMS,
         name="slab_prep",
-    )(pos, k0_table, beta_table, temp_init, slab_mat, inner, outer)
-    y_in, y_out = with_partner(edge_in, "gy", 0), with_partner(edge_out, "gy", 1)
+    )(pos, k0_table, beta_table, temp_init, slab_mat, inner, outer, sigma)
+    y_in = with_partner(edge_in, "gy", 0)
+    sigmas = [bodies[0]] + [shifted(sigma, "gy", 2 * d, True) for d in range(1, chips)]
+    sigmas += [bodies[chips]] + [
+        to_other_core(packet if d in (1, chips - 1) else sigma, d) for d in range(1, chips)
+    ]
     *halos[1:], y_in = lax.optimization_barrier((*halos[1:], y_in))
     halos = halos + [from_mate(part) for part in halos]
 
@@ -745,17 +754,17 @@
         functools.partial(slab_steps_kernel, chips),
         out_shape=(jax.ShapeDtypeStruct((size_x, width), f32), rows(TE * ROW), rows(chips * TE * ROW))
         + (rows(TE * ROW),) * (chips - 1),
-        in_specs=[SMEM] * 3 + [ANY] * width_gy + [VMEM] * (width_gy + 6),
+        in_specs=[SMEM] * 3 + [ANY] * width_gy + [VMEM] * (width_gy + 5),
         out_specs=(VMEM,) * (2 + chips),
         scratch_shapes=[pltpu.VMEM((CELLS * SLABX * SUB, LANES), f32)]
         + [pltpu.VMEM((SLAB_ROWS + 3 * SLABX, LANES), f32)]
         + [pltpu.VMEM((2 * SLAB_ROWS, LANES), f32)] * 2
         + [pltpu.VMEM((SLAB_ROWS, LANES), f32)] * 2
         + [pltpu.VMEM((4 * TE * SUB, LANES), f32), pltpu.VMEM((width_gy, TE * ROW, LANES), f32)]
-        + [pltpu.SemaphoreType.DMA((width_gy,))],
+        + [pltpu.VMEM((2, HALO * SLABX, LANES), f32), pltpu.SemaphoreType.DMA((width_gy + 2,))],
         compiler_params=PARAMS,
         name="slab_steps",
-    )(pos, k0_table, beta_table, *sigmas, *halos, slope, t_ext, k0_ext, b_ext, y_in, y_out)
+    )(pos, k0_table, beta_table, *sigmas, *halos, slope, t_ext, k0_ext, b_ext, y_in)
     got = from_mate(bundle).reshape(chips, TE * ROW, LANES)
     tile_temps = mine + got[0]
     for d in range(1, chips):

time: 65.8 us -> 67.5 us (1.026)
  Pallas kernels: 26.2 us -> 30.1 us
  starting transfers between devices: 12.6 us -> 10.4 us
    pallas_call x1, Pallas kernels: 8.79 us -> 13.2 us  [on_device(): pl.pallas_call(functools.partial(slab_steps_kernel, chips), out_shape=(ja...]
    ppermute x5, starting transfers between devices: 3.24 us -> 0.42 us  [from_mate(): lax.ppermute(value, 'gy', [(d, d ^ 1) for d in range(lax.axis_size('gy'))])]
    ppermute x4, waiting for transfers between devices: 21.7 us -> 19.4 us  [shifted(): return lax.ppermute(value, axis, pairs)]
    ppermute x5, waiting for transfers between devices: 1.55 us -> 3.27 us  [from_mate(): lax.ppermute(value, 'gy', [(d, d ^ 1) for d in range(lax.axis_size('gy'))])]
    ppermute x1, starting transfers between devices: 0.54 us -> 1.74 us  [to_other_core(): lax.ppermute(value, 'gy', [(at, ((at ^ 1) + 2 * by) % count) for at in ra...]
    ppermute x4 -> x3, starting transfers between devices: 3.65 us -> 2.55 us  [with_partner(): lax.ppermute(value, axis, pairs + [(high, low) for low, high in pairs])]
    ppermute x4 -> x3, waiting for transfers between devices: 2.15 us -> 2.52 us  [with_partner(): lax.ppermute(value, axis, pairs + [(high, low) for low, high in pairs])]
  transfers between devices with their start and end apart: 14 -> 13, of which waited for: 6 -> 7; matrix products, arithmetic and copies ran while one was open for 0% -> 0% of each run, Pallas kernels for 20% -> 19%
where the time goes in v12:
time: 67.5 us; the launch traced here: 67.3 us
  Pallas kernels  30.1 us (45%)
  waiting for transfers between devices  25.1 us (37%)
  starting transfers between devices  10.4 us (15%)
  other arithmetic  0.79 us (1%)
  between operations  0.77 us (1%)
    ppermute x4, waiting for transfers between devices, shifted(): return lax.ppermute(value, axis, pairs)  19.4 us
    pallas_call x1, Pallas kernels, on_device(): pl.pallas_call(functools.partial(slab_steps_kernel, chips), out_shape=(ja...  13.2 us
    pallas_call x1, Pallas kernels, on_device(): pl.pallas_call(functools.partial(sweep_kernel, chips), out_shape=(rows(TE...  11.3 us
    ppermute x4, starting transfers between devices, shifted(): return lax.ppermute(value, axis, pairs)  5.73 us
    pallas_call x1, Pallas kernels, on_device(): pl.pallas_call(prep_kernel, out_shape=(rows(3 * TE * ROW), rows(2 * TE *...  4.09 us
    ppermute x5, waiting for transfers between devices, from_mate(): lax.ppermute(value, 'gy', [(d, d ^ 1) for d in range(lax.axis_size('gy'))])  3.27 us
    ppermute x3, starting transfers between devices, with_partner(): lax.ppermute(value, axis, pairs + [(high, low) for low, high in pairs])  2.55 us
    ppermute x3, waiting for transfers between devices, with_partner(): lax.ppermute(value, axis, pairs + [(high, low) for low, high in pairs])  2.52 us
  transfers between devices with their start and end apart: 13, of which 7 were waited for; matrix products, arithmetic and copies ran while one was open for 0% of the time, Pallas kernels for 19%

profile of v12, /device:TPU:0, one launch (start us, length us, event | category | flops | bytes accessed | tf_op | source)
XLA Modules:
  0.0 67.3 jit_solution(9621907979379213035)
XLA Ops:
  0.7 4.1 %prep.1 = (f32[1536,128]{1,0:T(8,128)}, f32[1024,128]{1,0:T(8,128)}, f32[512,128]{1,0:T(8,128)}, f32[496,128]{1,0:T(8,128)}, f32[496,128]{1,0:T(8,128)}) custom-call(f32[4]{0:T(128)} %table.1, s32[3,64]{1,0:T(4,128)} %bitcast.26, f32[512,128]{1,0:T(8,128)} %bitcast.30, f32[512,128]{1,0:T(8,128)} %bitcast.31, s32[512,128]{1,0:T(8,128)} %bitcast.32, ...), custom_call_target="tpu_custom_call" | custom-call | tf_op jit(solution)/shard_map/prep/pallas_call | solution.py:681
  4.8 3.4 %collective-permute-start = (f32[1024,128]{1,0:T(8,128)}, f32[1024,128]{1,0:T(8,128)S(1)}, u32[]{:S(2)}, u32[]{:S(2)}) collective-permute-start(f32[1024,128]{1,0:T(8,128)} %get-tuple-element.22), channel_id=1, source_target_pairs={{0,2},{1,3},{2,0},{3,1},{4,6},{5,7},{6,4},{7,5},{8,10},{9,11},{10,... | collective-permute-start | bytes 1572872 | tf_op jit(solution)/shard_map/ppermute | solution.py:625
  8.2 0.0 collective-permute-start.1
  8.2 1.5 %collective-permute-start.3 = (f32[496,128]{1,0:T(8,128)}, f32[496,128]{1,0:T(8,128)S(1)}, u32[]{:S(2)}, u32[]{:S(2)}) collective-permute-start(f32[496,128]{1,0:T(8,128)} %get-tuple-element.23), channel_id=1, source_target_pairs={{0,4},{8,12},{16,20},{24,28},{4,0},{12,8},{20,16},{28,24},{1,5},{9... | collective-permute-start | bytes 761864 | tf_op jit(solution)/shard_map/ppermute | solution.py:631
  9.7 0.7 collective-permute-start.4
  10.4 9.6 %collective-permute-done.refs_1_ = f32[1024,128]{1,0:T(8,128)S(1)} collective-permute-done((f32[1024,128]{1,0:T(8,128)}, f32[1024,128]{1,0:T(8,128)S(1)}, u32[]{:S(2)}, u32[]{:S(2)}) %collective-permute-start) | collective-permute-done | bytes 524320 | tf_op jit(solution)/shard_map/ppermute | solution.py:625
  19.9 0.0 collective-permute-start.2
  19.9 1.6 %collective-permute-done.3.inner = f32[496,128]{1,0:T(8,128)S(1)} collective-permute-done((f32[496,128]{1,0:T(8,128)}, f32[496,128]{1,0:T(8,128)S(1)}, u32[]{:S(2)}, u32[]{:S(2)}) %collective-permute-start.3) | collective-permute-done | bytes 253984 | tf_op jit(solution)/shard_map/ppermute | solution.py:631
  21.5 0.0 collective-permute-done.4.outer
  21.5 0.3 collective-permute-start.5
  21.8 0.2 collective-permute-start.7
  22.0 0.0 copy-done.1
  22.0 1.5 %slab_prep.1 = (f32[1552,128]{1,0:T(8,128)S(1)}, f32[1552,128]{1,0:T(8,128)S(1)}, f32[1552,128]{1,0:T(8,128)S(1)}, f32[120,128]{1,0:T(8,128)S(1)}, f32[632,128]{1,0:T(8,128)S(1)}) custom-call(s32[3,64]{1,0:T(4,128)S(1)} %bitcast.27, f32[4]{0:T(128)S(1)} %copy-done.4, f32[4]{0:T(128)S(1)} %copy-done.5, f32[32,4096]{1,0:T(8,128)S(1)} %copy-done.1, ...), custom_call_target="tpu_custom_call" | custom-call | tf_op jit(solution)/shard_map/slab_prep/pallas_call | solution.py:716
  23.5 0.4 collective-permute-start.6
  23.9 0.9 %collective-permute-done.6.refs_12_ = f32[120,128]{1,0:T(8,128)S(1)} collective-permute-done((f32[120,128]{1,0:T(8,128)S(1)}, f32[120,128]{1,0:T(8,128)S(1)}, u32[]{:S(2)}, u32[]{:S(2)}) %collective-permute-start.6) | collective-permute-done | bytes 61472 | tf_op jit(solution)/shard_map/ppermute | solution.py:631
  24.8 1.7 %collective-permute-start.10 = (f32[632,128]{1,0:T(8,128)S(1)}, f32[632,128]{1,0:T(8,128)S(1)}, u32[]{:S(2)}, u32[]{:S(2)}) collective-permute-start(f32[632,128]{1,0:T(8,128)S(1)} %get-tuple-element.29), channel_id=1, source_target_pairs={{0,3},{1,2},{2,1},{3,0},{4,7},{5,6},{6,5},{7,4},{8,11},{9,10},{10,... | collective-permute-start | bytes 970760 | tf_op jit(solution)/shard_map/ppermute | solution.py:648
  26.6 3.2 %collective-permute-done.5.refs_5_ = f32[448,128]{1,0:T(8,128)S(1)} collective-permute-done((f32[448,128]{1,0:T(8,128)S(1)}, f32[448,128]{1,0:T(8,128)S(1)}, u32[]{:S(2)}, u32[]{:S(2)}) %collective-permute-start.5) | collective-permute-done | bytes 229408 | tf_op jit(solution)/shard_map/ppermute | solution.py:625
  29.8 0.1 collective-permute-start.9
  29.9 0.0 collective-permute-done.7.refs_6_
  29.9 0.0 collective-permute-start.8
  29.9 1.5 %collective-permute-done.8.refs_7_ = f32[448,128]{1,0:T(8,128)S(1)} collective-permute-done((f32[448,128]{1,0:T(8,128)S(1)}, f32[448,128]{1,0:T(8,128)S(1)}, u32[]{:S(2)}, u32[]{:S(2)}) %collective-permute-start.8) | collective-permute-done | bytes 229408 | tf_op jit(solution)/shard_map/ppermute | solution.py:635
  31.4 0.0 collective-permute-done.1.refs_2_
  31.4 0.0 collective-permute-done.2.refs_3_
  31.4 11.3 %sweeps.1 = (f32[512,128]{1,0:T(8,128)}, f32[2880,128]{1,0:T(8,128)S(1)}) custom-call(s32[3,64]{1,0:T(4,128)S(1)} %bitcast.28, f32[1536,128]{1,0:T(8,128)S(1)} %copy-done, f32[1024,128]{1,0:T(8,128)S(1)} %collective-permute-done.refs_1_, f32[1536,128]{1,0:T(8,128)S(1)} %collective-permute-done.1.refs_2_, f32[1024,128]{1,0:T(8,128)S(1)} %collective-permute-done.2.refs_3_, ...), custom_call_target="tpu_custom_call" | custom-call | tf_op jit(solution)/shard_map/sweeps/pallas_call | solution.py:736
  42.7 0.0 collective-permute-done.9.refs_1_
  42.7 0.0 collective-permute-done.10.refs_3_
  42.7 13.2 %slab_steps.1 = (f32[32,4096]{1,0:T(8,128)}, f32[512,128]{1,0:T(8,128)S(1)}, f32[1024,128]{1,0:T(8,128)S(1)}, f32[512,128]{1,0:T(8,128)S(1)}) custom-call(s32[3,64]{1,0:T(4,128)S(1)} %bitcast.29, f32[4]{0:T(128)S(1)} %copy-done.4, f32[4]{0:T(128)S(1)} %copy-done.5, f32[1536,128]{1,0:T(8,128)S(1)} %copy-done, f32[512,128]{1,0:T(8,128)S(1)} %collective-permute-done.9.refs_1_, ...), custom_call_target="tpu_custom_call" | custom-call | tf_op jit(solution)/shard_map/slab_steps/pallas_call | solution.py:753
  55.9 0.2 collective-permute-start.11
  56.1 1.8 %collective-permute-done.11 = f32[1024,128]{1,0:T(8,128)S(1)} collective-permute-done((f32[1024,128]{1,0:T(8,128)S(1)}, f32[1024,128]{1,0:T(8,128)S(1)}, u32[]{:S(2)}, u32[]{:S(2)}) %collective-permute-start.11) | collective-permute-done | bytes 524320 | tf_op jit(solution)/shard_map/ppermute | solution.py:635
  57.9 2.0 %collective-permute-start.12 = (f32[512,128]{1,0:T(8,128)S(1)}, f32[512,128]{1,0:T(8,128)S(1)}, u32[]{:S(2)}, u32[]{:S(2)}) collective-permute-start(f32[512,128]{1,0:T(8,128)S(1)} %slice_add_fusion), channel_id=1, source_target_pairs={{0,2},{1,3},{2,0},{3,1},{4,6},{5,7},{6,4},{7,5},{8,10},{9,11},{10,... | collective-permute-start | bytes 786440 | tf_op jit(solution)/shard_map/ppermute | solution.py:625
  59.9 6.6 %collective-permute-done.12 = f32[512,128]{1,0:T(8,128)S(1)} collective-permute-done((f32[512,128]{1,0:T(8,128)S(1)}, f32[512,128]{1,0:T(8,128)S(1)}, u32[]{:S(2)}, u32[]{:S(2)}) %collective-permute-start.12) | collective-permute-done | bytes 262176 | tf_op jit(solution)/shard_map/ppermute | solution.py:625
  66.5 0.8 %fusion = f32[512,128]{1,0:T(8,128)} fusion(f32[512,128]{1,0:T(8,128)S(1)} %collective-permute-done.12, f32[512,128]{1,0:T(8,128)S(1)} %get-tuple-element.36, f32[1024,128]{1,0:T(8,128)S(1)} %collective-permute-done.11), kind=kLoop, calls=%fused_computation.2 | loop fusion | flops 131072 | bytes 1048576 | tf_op jit(solution)/shard_map/add | solution.py:771
  (13 shorter events, 0.1 us)
Async XLA Ops:
  0.6 21.4 %copy-start.3 = (s32[64,3]{0,1:T(4,128)S(1)}, s32[64,3]{0,1:T(4,128)}, u32[]{:S(2)}) copy-start(s32[64,3]{0,1:T(4,128)} %param.13) | copy-start | bytes 2308
  0.6 21.4 %copy-start.1 = (f32[32,4096]{1,0:T(8,128)S(1)}, f32[32,4096]{1,0:T(8,128)}, u32[]{:S(2)}) copy-start(f32[32,4096]{1,0:T(8,128)} %temp.3) | copy-start | bytes 1572868
  0.7 21.4 %copy-start.2 = (s32[32,4096]{1,0:T(8,128)S(1)}, s32[32,4096]{1,0:T(8,128)}, u32[]{:S(2)}) copy-start(s32[32,4096]{1,0:T(8,128)} %mat.1) | copy-start | bytes 1572868
  0.7 21.3 %copy-start.4 = (f32[4]{0:T(128)S(1)}, f32[4]{0:T(128)}, u32[]{:S(2)}) copy-start(f32[4]{0:T(128)} %k0_table.3) | copy-start | bytes 52
  0.7 21.3 %copy-start.5 = (f32[4]{0:T(128)S(1)}, f32[4]{0:T(128)}, u32[]{:S(2)}) copy-start(f32[4]{0:T(128)} %beta_table.3) | copy-start | bytes 52
  4.8 26.6 %copy-start = (f32[1536,128]{1,0:T(8,128)S(1)}, f32[1536,128]{1,0:T(8,128)}, u32[]{:S(2)}) copy-start(f32[1536,128]{1,0:T(8,128)} %get-tuple-element.21.refs_0_) | copy-start | bytes 2359300
  4.8 15.1 %collective-permute-start = (f32[1024,128]{1,0:T(8,128)}, f32[1024,128]{1,0:T(8,128)S(1)}, u32[]{:S(2)}, u32[]{:S(2)}) collective-permute-start(f32[1024,128]{1,0:T(8,128)} %get-tuple-element.22), channel_id=1, source_target_pairs={{0,2},{1,3},{2,0},{3,1},{4,6},{5,7},{6,4},{7,5},{8,10},{9,11},{10,... | collective-permute-start | bytes 1572872 | tf_op jit(solution)/shard_map/ppermute | solution.py:625
  8.2 23.2 %collective-permute-start.1 = (f32[1536,128]{1,0:T(8,128)}, f32[1536,128]{1,0:T(8,128)S(1)}, u32[]{:S(2)}, u32[]{:S(2)}) collective-permute-start(f32[1536,128]{1,0:T(8,128)} %get-tuple-element.21.refs_0_), channel_id=1, source_target_pairs={{0,1},{1,0},{2,3},{3,2},{4,5},{5,4},{6,7},{7,6},{8,9},{9,8},{10,11... | collective-permute-start | bytes 2359304 | tf_op jit(solution)/shard_map/ppermute | solution.py:635
  8.2 13.3 %collective-permute-start.3 = (f32[496,128]{1,0:T(8,128)}, f32[496,128]{1,0:T(8,128)S(1)}, u32[]{:S(2)}, u32[]{:S(2)}) collective-permute-start(f32[496,128]{1,0:T(8,128)} %get-tuple-element.23), channel_id=1, source_target_pairs={{0,4},{8,12},{16,20},{24,28},{4,0},{12,8},{20,16},{28,24},{1,5},{9... | collective-permute-start | bytes 761864 | tf_op jit(solution)/shard_map/ppermute | solution.py:631
  9.7 11.8 %collective-permute-start.4 = (f32[496,128]{1,0:T(8,128)}, f32[496,128]{1,0:T(8,128)S(1)}, u32[]{:S(2)}, u32[]{:S(2)}) collective-permute-start(f32[496,128]{1,0:T(8,128)} %get-tuple-element.24), channel_id=1, source_target_pairs={{4,8},{12,16},{20,24},{8,4},{16,12},{24,20},{5,9},{13,17},{21,25},... | collective-permute-start | bytes 761864 | tf_op jit(solution)/shard_map/ppermute | solution.py:631
  19.9 11.5 %collective-permute-start.2 = (f32[1024,128]{1,0:T(8,128)S(1)}, f32[1024,128]{1,0:T(8,128)S(1)}, u32[]{:S(2)}, u32[]{:S(2)}) collective-permute-start(f32[1024,128]{1,0:T(8,128)S(1)} %collective-permute-done.refs_1_), channel_id=1, source_target_pairs={{0,1},{1,0},{2,3},{3,2},{4,5},{5,4},{6,7},{7,6},{8,9},{9,8},{10,11... | collective-permute-start | bytes 1572872 | tf_op jit(solution)/shard_map/ppermute | solution.py:635
  21.5 8.2 %collective-permute-start.5 = (f32[448,128]{1,0:T(8,128)S(1)}, f32[448,128]{1,0:T(8,128)S(1)}, u32[]{:S(2)}, u32[]{:S(2)}) collective-permute-start(f32[448,128]{1,0:T(8,128)S(1)} %relay.1.refs_4_), channel_id=1, source_target_pairs={{0,2},{1,3},{2,0},{3,1},{4,6},{5,7},{6,4},{7,5},{8,10},{9,11},{10,... | collective-permute-start | bytes 688136 | tf_op jit(solution)/shard_map/ppermute | solution.py:625
  21.8 8.1 %collective-permute-start.7 = (f32[448,128]{1,0:T(8,128)S(1)}, f32[448,128]{1,0:T(8,128)S(1)}, u32[]{:S(2)}, u32[]{:S(2)}) collective-permute-start(f32[448,128]{1,0:T(8,128)S(1)} %relay.1.refs_4_), channel_id=1, source_target_pairs={{0,1},{1,0},{2,3},{3,2},{4,5},{5,4},{6,7},{7,6},{8,9},{9,8},{10,11... | collective-permute-start | bytes 688136 | tf_op jit(solution)/shard_map/ppermute | solution.py:635
  23.5 1.3 %collective-permute-start.6 = (f32[120,128]{1,0:T(8,128)S(1)}, f32[120,128]{1,0:T(8,128)S(1)}, u32[]{:S(2)}, u32[]{:S(2)}) collective-permute-start(f32[120,128]{1,0:T(8,128)S(1)} %get-tuple-element.26), channel_id=1, source_target_pairs={{0,1},{2,3},{1,0},{3,2},{4,5},{6,7},{5,4},{7,6},{8,9},{10,11},{9,8... | collective-permute-start | bytes 184328 | tf_op jit(solution)/shard_map/ppermute | solution.py:631
  24.8 17.8 %collective-permute-start.10 = (f32[632,128]{1,0:T(8,128)S(1)}, f32[632,128]{1,0:T(8,128)S(1)}, u32[]{:S(2)}, u32[]{:S(2)}) collective-permute-start(f32[632,128]{1,0:T(8,128)S(1)} %get-tuple-element.29), channel_id=1, source_target_pairs={{0,3},{1,2},{2,1},{3,0},{4,7},{5,6},{6,5},{7,4},{8,11},{9,10},{10,... | collective-permute-start | bytes 970760 | tf_op jit(solution)/shard_map/ppermute | solution.py:648
  29.8 12.9 %collective-permute-start.9 = (f32[512,128]{1,0:T(8,128)}, f32[512,128]{1,0:T(8,128)S(1)}, u32[]{:S(2)}, u32[]{:S(2)}) collective-permute-start(f32[512,128]{1,0:T(8,128)} %get-tuple-element.25.sigma), channel_id=1, source_target_pairs={{0,2},{1,3},{2,0},{3,1},{4,6},{5,7},{6,4},{7,5},{8,10},{9,11},{10,... | collective-permute-start | bytes 786440 | tf_op jit(solution)/shard_map/ppermute | solution.py:625
  29.9 1.5 %collective-permute-start.8 = (f32[448,128]{1,0:T(8,128)S(1)}, f32[448,128]{1,0:T(8,128)S(1)}, u32[]{:S(2)}, u32[]{:S(2)}) collective-permute-start(f32[448,128]{1,0:T(8,128)S(1)} %collective-permute-done.5.refs_5_), channel_id=1, source_target_pairs={{0,1},{1,0},{2,3},{3,2},{4,5},{5,4},{6,7},{7,6},{8,9},{9,8},{10,11... | collective-permute-start | bytes 688136 | tf_op jit(solution)/shard_map/ppermute | solution.py:635
  55.9 2.0 %collective-permute-start.11 = (f32[1024,128]{1,0:T(8,128)S(1)}, f32[1024,128]{1,0:T(8,128)S(1)}, u32[]{:S(2)}, u32[]{:S(2)}) collective-permute-start(f32[1024,128]{1,0:T(8,128)S(1)} %get-tuple-element.37), channel_id=1, source_target_pairs={{0,1},{1,0},{2,3},{3,2},{4,5},{5,4},{6,7},{7,6},{8,9},{9,8},{10,11... | collective-permute-start | bytes 1572872 | tf_op jit(solution)/shard_map/ppermute | solution.py:635
  57.9 8.6 %collective-permute-start.12 = (f32[512,128]{1,0:T(8,128)S(1)}, f32[512,128]{1,0:T(8,128)S(1)}, u32[]{:S(2)}, u32[]{:S(2)}) collective-permute-start(f32[512,128]{1,0:T(8,128)S(1)} %slice_add_fusion), channel_id=1, source_target_pairs={{0,2},{1,3},{2,0},{3,1},{4,6},{5,7},{6,4},{7,5},{8,10},{9,11},{10,... | collective-permute-start | bytes 786440 | tf_op jit(solution)/shard_map/ppermute | solution.py:625

commit v13 on v12

--- a/solution.py
+++ b/solution.py
@@ -200,8 +200,12 @@
 
 def part_device(part, chips, j):
     mate = j + 1 - 2 * lax.rem(j, 2)
-    base = j if part < chips else mate
-    return lax.rem(base - 2 * (part % chips) + 2 * chips, 2 * chips)
+    if isinstance(part, int):
+        base, back = (j, part) if part < chips else (mate, part - chips)
+    else:
+        base = jnp.where(part < chips, j, mate)
+        back = lax.rem(part, chips)
+    return lax.rem(base - 2 * back + 2 * chips, 2 * chips)
 
 
 def sweep_kernel(chips, pos, *refs):
@@ -209,7 +213,8 @@
     tiles = width_gy * TILES
     none = tiles
     bodies, halos = refs[:width_gy], refs[width_gy : 2 * width_gy]
-    pot, slope, cell_at, cell_of, table, pa, pb, la, lb, ua, ub, s_c, s_l, s_u, sems = refs[2 * width_gy :]
+    pot, slope, cell_at, cell_of, table, c_buf, l_buf, u_buf, s_c, s_l, s_u, sems = refs[2 * width_gy :]
+    c_turn, l_turn, u_turn = (ref.shape[0] // 2 for ref in (c_buf, l_buf, u_buf))
     i = lax.axis_index("gx")
     j = lax.axis_index("gy")
     rows_gx = lax.axis_size("gx")
@@ -218,12 +223,12 @@
     moves = []
     for part in range(width_gy):
         at = 0
-        pieces = [(bodies[part], 0, pa, part * TE, TE), (bodies[part], TE * ROW, s_c, part * TE, TE)]
+        pieces = [(bodies[part], 0, c_buf, part * TE, TE), (bodies[part], TE * ROW, s_c, part * TE, TE)]
         for target, first, count in (
-            (la, part * LOW[0], LOW[0]),
+            (l_buf, part * LOW[0], LOW[0]),
             (s_l, part * LOW[1], LOW[1]),
             (None, 0, LOW[2]),
-            (ua, part * HIGH[0], HIGH[0]),
+            (u_buf, part * HIGH[0], HIGH[0]),
             (s_u, part * HIGH[1], HIGH[1]),
         ):
             if target is not None:
@@ -274,10 +279,11 @@
     def put_plane(ref, row, value):
         ref[pl.ds(row, SUB, stride=TILES), :] = value
 
-    for ref, count in ((pa, TE), (pb, TE), (la, LOW[0]), (lb, LOW[0]), (ua, HIGH[0]), (ub, HIGH[0])):
-        first = ROW0 + width_gy * count * ROW
-        for row in range(first, first + count * ROW, SUB):
-            ref[row : row + SUB] = zero
+    for ref, count in ((c_buf, TE), (l_buf, LOW[0]), (u_buf, HIGH[0])):
+        for first in (0, ref.shape[0] // 2):
+            first = first + ROW0 + width_gy * count * ROW
+            for row in range(first, first + count * ROW, SUB):
+                ref[row : row + SUB] = zero
 
     def clear(at, carry):
         slope[pl.ds(pl.multiple_of(at * SUB, SUB), SUB), :] = zero
@@ -311,41 +317,55 @@
         quarter = lane // TE
         return quarter == upper, quarter == lax.bitwise_and(upper + 3, 3)
 
-    bufs = ((pa, la, ua), (pb, lb, ub))
-    for k in range(SWEEPS):
-        weight = cheb_weight(k, SWEEPS)
-        keep, gain = 1.0 - weight, weight / (6.0 + EPS)
-        (c_src, l_src, u_src), (c_dst, l_dst, u_dst) = bufs[k % 2], bufs[(k + 1) % 2]
-
-        def relax(src, dst, places, first, count, s_ref, s_row, before, beyond):
-            row, row_m, row_p, row_zm, row_zp, _, _, upper = places
-            first_y, last_y = y_ends(upper)
-            own = plane_at(src, row + first * ROW)
-            for p in range(count):
-                step = (first + p) * ROW
-                after = plane_at(src, row + (step + ROW)) if beyond is None or p < count - 1 else beyond
-                total = (before + after) + plane_at(s_ref, s_row + p * ROW)
-                along_y = y_minus(src, own, last_y, row + (step - TILES), row_m + (step + ROW - TILES))
-                along_y = along_y + y_plus(src, own, first_y, row + (step + TILES), row_p + (step + TILES - ROW))
-                along_z = z_minus(src, own, row_zm + step) + z_plus(src, own, row_zp + step)
-                put_plane(dst, row + step, keep * own + gain * (total + (along_y + along_z)))
-                before, own = own, after
+    def relax(ref, places, now, after_turn, first, count, s_ref, s_row, before, beyond, keep, gain):
+        row, row_m, row_p, row_zm, row_zp, _, _, upper = places
+        target = row + after_turn
+        row, row_m, row_p, row_zm, row_zp = (at + now for at in (row, row_m, row_p, row_zm, row_zp))
+        first_y, last_y = y_ends(upper)
+        own = plane_at(ref, row + first * ROW)
+        results = []
+        for p in range(count):
+            step = (first + p) * ROW
+            after = plane_at(ref, row + (step + ROW)) if p < count - 1 else beyond
+            total = (before + after) + plane_at(s_ref, s_row + p * ROW)
+            along_y = y_minus(ref, own, last_y, row + (step - TILES), row_m + (step + ROW - TILES))
+            along_y = along_y + y_plus(ref, own, first_y, row + (step + TILES), row_p + (step + TILES - ROW))
+            along_z = z_minus(ref, own, row_zm + step) + z_plus(ref, own, row_zp + step)
+            results.append(keep * own + gain * (total + (along_y + along_z)))
+            before, own = own, after
+            if len(results) == 8 or p == count - 1:
+                for at, value in enumerate(results, p + 1 - len(results)):
+                    put_plane(ref, target + (first + at) * ROW, value)
+                results = []
+
+    def sweep(k, carry):
+        parity = lax.bitwise_and(k, 1)
+        c_now, l_now, u_now = parity * c_turn, parity * l_turn, parity * u_turn
+        weights = [cheb_weight(at, SWEEPS) for at in range(SWEEPS)]
+        keep, gain = jnp.float32(1.0 - weights[0]), jnp.float32(weights[0] / (6.0 + EPS))
+        for at in range(1, SWEEPS):
+            keep = jnp.where(k == at, jnp.float32(1.0 - weights[at]), keep)
+            gain = jnp.where(k == at, jnp.float32(weights[at] / (6.0 + EPS)), gain)
 
         def sweep_tile(slot, carry):
             at = entry(0, slot)
-            relax(c_src, c_dst, at, 0, TE, s_c, at[0], plane_at(l_src, at[5]), plane_at(u_src, at[6]))
+            ends = plane_at(l_buf, at[5] + l_now), plane_at(u_buf, at[6] + u_now)
+            relax(c_buf, at, c_now, c_turn - c_now, 0, TE, s_c, at[0], *ends, keep, gain)
             at = entry(1, slot)
-            count = LOW[0] - 1 - k
-            s_row = row_of(slot, LOW[1]) + (LOW[1] - count) * ROW
-            before, beyond = plane_at(l_src, at[0] + k * ROW), plane_at(c_src, at[6])
-            relax(l_src, l_dst, at, k + 1, count, s_l, s_row, before, beyond)
+            ends = plane_at(l_buf, at[0] + l_now), plane_at(c_buf, at[6] + c_now)
+            relax(l_buf, at, l_now, l_turn - l_now, 1, LOW[0] - 1, s_l, row_of(slot, LOW[1]), *ends, keep, gain)
             at = entry(2, slot)
-            relax(u_src, u_dst, at, 0, HIGH[0] - 1 - k, s_u, row_of(slot, HIGH[1]), plane_at(c_src, at[5]), None)
+            ends = plane_at(c_buf, at[5] + c_now), plane_at(u_buf, at[0] + u_now + (HIGH[0] - 1) * ROW)
+            relax(u_buf, at, u_now, u_turn - u_now, 0, HIGH[0] - 1, s_u, row_of(slot, HIGH[1]), *ends, keep, gain)
             return carry
 
-        lax.fori_loop(0, tiles, sweep_tile, 0, unroll=4)
-
-    field, f_l, f_u = bufs[SWEEPS % 2]
+        lax.fori_loop(0, tiles, sweep_tile, 0, unroll=2)
+        return carry
+
+    lax.fori_loop(0, SWEEPS, sweep, 0)
+
+    assert SWEEPS % 2 == 0
+    field, f_l, f_u = c_buf, l_buf, u_buf
     for t in range(TILES):
         turn = jnp.where(table[t * 8 + 7] == 1, LANES - TE, 0)
 
@@ -380,7 +400,7 @@
         squares(f_u, at, local, HALO + TE, 0, 2, None)
         return carry
 
-    lax.fori_loop(0, tiles, slope_tile, 0, unroll=2)
+    lax.fori_loop(0, tiles, slope_tile, 0)
 
 
 def window(which, cell, i, j, rows_gx):
@@ -399,12 +419,13 @@
     slope, t_in, k0_in, b_in, y_in, temp_out = refs[2 * width_gy : 2 * width_gy + 6]
     mine, bundle = refs[2 * width_gy + 6 : 2 * width_gy + 8]
     across = refs[2 * width_gy + 8 : 2 * width_gy + 7 + chips]
-    heat, q_ext, state_a, state_b, k0_all, b_all, blocks, sigmas, y_out, sems = refs[2 * width_gy + 7 + chips :]
+    heat, q_ext, state, k0_all, b_all, blocks, sigmas, y_out, sems = refs[2 * width_gy + 7 + chips :]
     moves = []
     for part in range(width_gy):
         start = 2 * TE * ROW if part % chips == 0 else 0
         source = refs[part].at[start : start + TE * ROW]
-        moves.append(pltpu.make_async_copy(source, sigmas.at[part], sems.at[part]))
+        target = sigmas.at[part * TE * ROW : (part + 1) * TE * ROW]
+        moves.append(pltpu.make_async_copy(source, target, sems.at[part]))
         moves[-1].start()
     edges = []
     for which, d in enumerate((1, chips - 1)):
@@ -447,19 +468,20 @@
         near = near * (2.0 - value * near)
         return near * (2.0 - value * near)
 
-    def both_of(block, g, by=0):
-        first = 2 * (ROW0 + block * SLABX + g * SUB + by)
+    def both_of(base, g, by=0):
+        first = base + 2 * (g * SUB + by)
         return pl.ds(first, SUB, stride=2), pl.ds(first + 1, SUB, stride=2)
 
-    def load(ref, block, by=0):
-        places = [both_of(block, g, by) for g in range(groups)]
-        return [ref[at, :] for at, _ in places], [ref[at, :] for _, at in places]
-
-    def store(ref, block, g, temp, cond=None):
-        first, second = both_of(block, g)
-        ref[first, :] = temp
-        if cond is not None:
-            ref[second, :] = cond
+    def base_of(block):
+        return 2 * ROW0 + block * (2 * SLABX)
+
+    def load(base, by=0):
+        places = [both_of(base, g, by) for g in range(groups)]
+        return [state[at, :] for at, _ in places], [state[at, :] for _, at in places]
+
+    def store(base, g, temp, cond):
+        first, second = both_of(base, g)
+        state[first, :], state[second, :] = temp, cond
 
     even = lax.rem(j, 2) == 0
 
@@ -484,13 +506,13 @@
             values.append((rows, temp, k0, beta, k0 * inverse(1.0 + beta * temp * temp)))
         for g, (rows, temp, k0, beta, cond) in enumerate(values):
             k0_all[rows], b_all[rows] = k0, beta
-            store(state_a, block, g, temp, cond)
+            store(base_of(block), g, temp, cond)
 
     def begin_inner(block, carry):
         begin(block, None, 0)
         return carry
 
-    lax.fori_loop(HALO, YBLOCKS - HALO, begin_inner, 0, unroll=8)
+    lax.fori_loop(HALO, YBLOCKS - HALO, begin_inner, 0, unroll=4)
     for move in edges:
         move.wait()
     for e in range(HALO):
@@ -505,23 +527,28 @@
     for move in moves:
         move.wait()
     low_at, high_at = (LOW[0] + LOW[1]) * ROW, LOW_ROWS + (HIGH[0] + HIGH[1]) * ROW
+    def put_heat(which, by, dev, t, x, count, sigma_of):
+        tile = jnp.clip(i + by, 0, rows_gx - 1) * tiles + dev * TILES + t
+        cell = (pos[1, tile] + 1) * 2 + pos[2, tile]
+        first = pl.multiple_of((window(which, cell, i, j, rows_gx) * SLABX + x) * SUB, SUB)
+        for p in range(count):
+            rows = pl.ds(pl.multiple_of(first + p * SUB, SUB), SUB)
+            heat[rows, :] = sigma_of(p) * slope[rows, :]
+
+    def own_heat(slot, carry):
+        part, t = lax.div(slot, TILES), lax.rem(slot, TILES)
+        row = part * (TE * ROW) + t
+        dev = part_device(part, chips, j)
+        put_heat(0, 0, dev, t, HALO, TE, lambda p: sigmas[pl.ds(row + p * ROW, SUB, stride=TILES), :])
+        return carry
+
+    lax.fori_loop(0, tiles, own_heat, 0)
     for part in range(width_gy):
         dev = part_device(part, chips, j)
         for t in range(TILES):
-            for which, by in enumerate((0, -1, 1)):
-                tile = jnp.clip(i + by, 0, rows_gx - 1) * tiles + dev * TILES + t
-                cell = (pos[1, tile] + 1) * 2 + pos[2, tile]
-                local = window(which, cell, i, j, rows_gx)
-                source, start, x, count = (
-                    (sigmas.at[part], 0, HALO, TE),
-                    (halos[part], low_at, HALO - 2, 2),
-                    (halos[part], high_at, HALO + TE, 2),
-                )[which]
-                first = pl.multiple_of((local * SLABX + x) * SUB, SUB)
-                for p in range(count):
-                    rows = pl.ds(pl.multiple_of(first + p * SUB, SUB), SUB)
-                    sigma = source[pl.ds(start + p * ROW + t, SUB, stride=TILES), :]
-                    heat[rows, :] = sigma * slope[rows, :]
+            for which, by, x, at in ((1, -1, HALO - 2, low_at), (2, 1, HALO + TE, high_at)):
+                rows = lambda p: pl.ds(at + p * ROW + t, SUB, stride=TILES)
+                put_heat(which, by, dev, t, x, 2, lambda p: halos[part][rows(p), :])
 
     def place_heat(at, carry):
         first = at - 1
@@ -536,24 +563,28 @@
                 q_ext[rows_of(block, g)] = pick([turned(cells[c], c - r - c % 2) for c in range(4)])
         return carry
 
-    lax.fori_loop(0, HALF // 4 + 2, place_heat, 0, unroll=5)
-
-    for step in range(CSWEEPS):
-        src, dst = (state_a, state_b)[:: 1 if step % 2 == 0 else -1]
-
-        def y_fluxes(block, now, ahead):
-            closed = (low_y & (block == HALO - 1)) | (high_y & (block == HALO + HALF - 1))
-            return [flux(now, ahead, g, closed) for g in range(groups)]
-
-        def flux(now, other, g, closed=None):
-            value = (now[1][g] + other[1][g]) * (other[0][g] - now[0][g])
-            return value if closed is None else jnp.where(closed, 0.0, value)
+    lax.fori_loop(0, HALF // 4 + 2, place_heat, 0, unroll=2)
+
+    turn = state.shape[0] // 2
+
+    def flux(now, other, g, closed=None):
+        value = (now[1][g] + other[1][g]) * (other[0][g] - now[0][g])
+        return value if closed is None else jnp.where(closed, 0.0, value)
+
+    def y_fluxes(block, now, ahead):
+        closed = (low_y & (block == HALO - 1)) | (high_y & (block == HALO + HALF - 1))
+        return [flux(now, ahead, g, closed) for g in range(groups)]
+
+    def conduct(step, carry):
+        source = lax.bitwise_and(step, 1) * turn
+        target = turn - source
 
         def advance(block, carry):
             now, before = carry
-            ahead = load(src, block + 1)
+            base = source + base_of(block)
+            ahead = load(base + 2 * SLABX)
             flux_y = y_fluxes(block, now, ahead)
-            x_p, x_m = load(src, block, 1), load(src, block, -1)
+            x_p, x_m = load(base, 1), load(base, -1)
             results = []
             for g in range(groups):
                 temp, cond = now[0][g], now[1][g]
@@ -563,25 +594,25 @@
                 flux_z = jnp.where(no_z, 0.0, flux_z)
                 div = (flux_y[g] - before[g]) + (up + down) + (flux_z - roll(flux_z, 1, 1))
                 new = temp + DT * (0.5 * div + q_ext[rows_of(block + 1, g)])
-                if step < CSWEEPS - 1:
-                    rows = rows_of(block, g)
-                    results.append((new, k0_all[rows] * inverse(1.0 + b_all[rows] * new * new)))
-                else:
-                    results.append((new,))
+                rows = rows_of(block, g)
+                results.append((new, k0_all[rows] * inverse(1.0 + b_all[rows] * new * new)))
             for g in range(groups):
-                store(dst, block, g, *results[g])
+                store(target + base_of(block), g, *results[g])
             return ahead, flux_y
 
-        first, second = load(src, 0), load(src, 1)
-        lax.fori_loop(1, YBLOCKS - 1, advance, (second, y_fluxes(0, first, second)), unroll=12)
-    final = state_b if CSWEEPS % 2 else state_a
+        first, second = load(source + base_of(0)), load(source + base_of(1))
+        lax.fori_loop(1, YBLOCKS - 1, advance, (second, y_fluxes(0, first, second)), unroll=6)
+        return carry
+
+    lax.fori_loop(0, CSWEEPS, conduct, 0)
+    final = (CSWEEPS % 2) * turn
 
     def give_out(yq, carry):
         for g in range(TE // SUB):
             x = slice(g * SUB, (g + 1) * SUB)
             turns = []
             for r in range(4):
-                value = final[both_of(HALO + 4 * yq + r, g, HALO)[0], :]
+                value = state[both_of(final + base_of(HALO + 4 * yq + r), g, HALO)[0], :]
                 turns.append([turned(value, by) for by in range(4)])
             for pair in range(2):
                 even, odd = turns[2 * pair], turns[2 * pair + 1]
@@ -594,7 +625,7 @@
                 blocks[pl.ds((c * TE + g * SUB) * SUB + yq, SUB, stride=SUB), :] = value
         return carry
 
-    lax.fori_loop(0, HALF // 4, give_out, 0, unroll=4)
+    lax.fori_loop(0, HALF // 4, give_out, 0, unroll=2)
     places = []
     mate = j + 1 - 2 * lax.rem(j, 2)
     targets = [(mine, 0, j)] + [(across[d - 1], 0, j + 2 * d) for d in range(1, chips)]
@@ -616,7 +647,7 @@
             target[pl.ds(pl.multiple_of(p * ROW, ROW) + first, SUB, stride=TILES), :] = value
         return carry
 
-    lax.fori_loop(0, TE, pack, 0, unroll=8)
+    lax.fori_loop(0, TE, pack, 0, unroll=4)
 
 
 def shifted(value, axis, by, wrap=False):
@@ -730,8 +761,8 @@
     *halos[1:], y_in = lax.optimization_barrier((*halos[1:], y_in))
     halos = halos + [from_mate(part) for part in halos]
 
-    def fields(count):
-        return pltpu.VMEM((2 * ROW0 + (width_gy + 1) * count * ROW, LANES), f32)
+    def fields(count, buffers=1):
+        return pltpu.VMEM((buffers * (2 * ROW0 + (width_gy + 1) * count * ROW), LANES), f32)
 
     pot, slope = pl.pallas_call(
         functools.partial(sweep_kernel, chips),
@@ -742,7 +773,7 @@
             pltpu.SMEM((3, 2 * (2 * width_gy + 2)), jnp.int32),
             pltpu.SMEM((3, tiles), jnp.int32),
             pltpu.SMEM((3 * tiles * 8,), jnp.int32),
-            fields(TE), fields(TE), fields(LOW[0]), fields(LOW[0]), fields(HIGH[0]), fields(HIGH[0]),
+            fields(TE, 2), fields(LOW[0], 2), fields(HIGH[0], 2),
             fields(TE), fields(LOW[1]), fields(HIGH[1]),
             pltpu.SemaphoreType.DMA((6 * width_gy,)),
         ],
@@ -758,9 +789,9 @@
         out_specs=(VMEM,) * (2 + chips),
         scratch_shapes=[pltpu.VMEM((CELLS * SLABX * SUB, LANES), f32)]
         + [pltpu.VMEM((SLAB_ROWS + 3 * SLABX, LANES), f32)]
-        + [pltpu.VMEM((2 * SLAB_ROWS, LANES), f32)] * 2
+        + [pltpu.VMEM((4 * SLAB_ROWS, LANES), f32)]
         + [pltpu.VMEM((SLAB_ROWS, LANES), f32)] * 2
-        + [pltpu.VMEM((4 * TE * SUB, LANES), f32), pltpu.VMEM((width_gy, TE * ROW, LANES), f32)]
+        + [pltpu.VMEM((4 * TE * SUB, LANES), f32), pltpu.VMEM((width_gy * TE * ROW, LANES), f32)]
         + [pltpu.VMEM((2, HALO * SLABX, LANES), f32), pltpu.SemaphoreType.DMA((width_gy + 2,))],
         compiler_params=PARAMS,
         name="slab_steps",

time: 67.5 us -> 77.4 us (1.15)
  Pallas kernels: 30.1 us -> 40.2 us
    pallas_call x1, Pallas kernels: 11.3 us -> 19.7 us  [on_device(): pl.pallas_call(functools.partial(sweep_kernel, chips), out_shape=(rows(TE...]
    pallas_call x1, Pallas kernels: 13.2 us -> 14.8 us  [on_device(): pl.pallas_call(functools.partial(slab_steps_kernel, chips), out_shape=(ja...]
    ppermute x4, waiting for transfers between devices: 19.4 us -> 20.5 us  [shifted(): return lax.ppermute(value, axis, pairs)]
    ppermute x4, starting transfers between devices: 5.73 us -> 6.78 us  [shifted(): return lax.ppermute(value, axis, pairs)]
    ppermute x1, starting transfers between devices: 1.74 us -> 0.72 us  [to_other_core(): lax.ppermute(value, 'gy', [(at, ((at ^ 1) + 2 * by) % count) for at in ra...]
  transfers between devices with their start and end apart: 13 -> 13, of which waited for: 7 -> 7; matrix products, arithmetic and copies ran while one was open for 0% -> 0% of each run, Pallas kernels for 19% -> 28%
where the time goes in v13:
time: 77.4 us; the launch traced here: 77.2 us
  Pallas kernels  40.2 us (52%)
  waiting for transfers between devices  25.7 us (33%)
  starting transfers between devices  9.72 us (13%)
  other arithmetic  0.79 us (1%)
  between operations  0.79 us (1%)
    ppermute x4, waiting for transfers between devices, shifted(): return lax.ppermute(value, axis, pairs)  20.5 us
    pallas_call x1, Pallas kernels, on_device(): pl.pallas_call(functools.partial(sweep_kernel, chips), out_shape=(rows(TE...  19.7 us
    pallas_call x1, Pallas kernels, on_device(): pl.pallas_call(functools.partial(slab_steps_kernel, chips), out_shape=(ja...  14.8 us
    ppermute x4, starting transfers between devices, shifted(): return lax.ppermute(value, axis, pairs)  6.78 us
    pallas_call x1, Pallas kernels, on_device(): pl.pallas_call(prep_kernel, out_shape=(rows(3 * TE * ROW), rows(2 * TE *...  4.09 us
    ppermute x5, waiting for transfers between devices, from_mate(): lax.ppermute(value, 'gy', [(d, d ^ 1) for d in range(lax.axis_size('gy'))])  3.27 us
    ppermute x3, starting transfers between devices, with_partner(): lax.ppermute(value, axis, pairs + [(high, low) for low, high in pairs])  2.01 us
    ppermute x3, waiting for transfers between devices, with_partner(): lax.ppermute(value, axis, pairs + [(high, low) for low, high in pairs])  1.95 us
  transfers between devices with their start and end apart: 13, of which 7 were waited for; matrix products, arithmetic and copies ran while one was open for 0% of the time, Pallas kernels for 28%

profile of v13, /device:TPU:0, one launch (start us, length us, event | category | flops | bytes accessed | tf_op | source)
XLA Modules:
  0.0 77.2 jit_solution(12796443963288646580)
XLA Ops:
  0.7 4.1 %prep.1 = (f32[1536,128]{1,0:T(8,128)}, f32[1024,128]{1,0:T(8,128)}, f32[512,128]{1,0:T(8,128)}, f32[496,128]{1,0:T(8,128)}, f32[496,128]{1,0:T(8,128)}) custom-call(f32[4]{0:T(128)} %table.1, s32[3,64]{1,0:T(4,128)} %bitcast.26, f32[512,128]{1,0:T(8,128)} %bitcast.30, f32[512,128]{1,0:T(8,128)} %bitcast.31, s32[512,128]{1,0:T(8,128)} %bitcast.32, ...), custom_call_target="tpu_custom_call" | custom-call | tf_op jit(solution)/shard_map/prep/pallas_call | solution.py:712
  4.8 3.4 %collective-permute-start = (f32[1024,128]{1,0:T(8,128)}, f32[1024,128]{1,0:T(8,128)S(1)}, u32[]{:S(2)}, u32[]{:S(2)}) collective-permute-start(f32[1024,128]{1,0:T(8,128)} %get-tuple-element.22), channel_id=1, source_target_pairs={{0,2},{1,3},{2,0},{3,1},{4,6},{5,7},{6,4},{7,5},{8,10},{9,11},{10,... | collective-permute-start | bytes 1572872 | tf_op jit(solution)/shard_map/ppermute | solution.py:656
  8.2 0.0 collective-permute-start.1
  8.2 0.8 %collective-permute-start.3 = (f32[496,128]{1,0:T(8,128)}, f32[496,128]{1,0:T(8,128)S(1)}, u32[]{:S(2)}, u32[]{:S(2)}) collective-permute-start(f32[496,128]{1,0:T(8,128)} %get-tuple-element.23), channel_id=1, source_target_pairs={{0,4},{8,12},{16,20},{24,28},{4,0},{12,8},{20,16},{28,24},{1,5},{9... | collective-permute-start | bytes 761864 | tf_op jit(solution)/shard_map/ppermute | solution.py:662
  8.9 0.7 collective-permute-start.4
  9.6 10.1 %collective-permute-done.refs_1_ = f32[1024,128]{1,0:T(8,128)S(1)} collective-permute-done((f32[1024,128]{1,0:T(8,128)}, f32[1024,128]{1,0:T(8,128)S(1)}, u32[]{:S(2)}, u32[]{:S(2)}) %collective-permute-start) | collective-permute-done | bytes 524320 | tf_op jit(solution)/shard_map/ppermute | solution.py:656
  19.7 0.0 collective-permute-start.2
  19.7 1.1 %collective-permute-done.3.inner = f32[496,128]{1,0:T(8,128)S(1)} collective-permute-done((f32[496,128]{1,0:T(8,128)}, f32[496,128]{1,0:T(8,128)S(1)}, u32[]{:S(2)}, u32[]{:S(2)}) %collective-permute-start.3) | collective-permute-done | bytes 253984 | tf_op jit(solution)/shard_map/ppermute | solution.py:662
  20.8 0.0 collective-permute-done.4.outer
  20.8 1.3 %collective-permute-start.5 = (f32[448,128]{1,0:T(8,128)S(1)}, f32[448,128]{1,0:T(8,128)S(1)}, u32[]{:S(2)}, u32[]{:S(2)}) collective-permute-start(f32[448,128]{1,0:T(8,128)S(1)} %relay.1.refs_4_), channel_id=1, source_target_pairs={{0,2},{1,3},{2,0},{3,1},{4,6},{5,7},{6,4},{7,5},{8,10},{9,11},{10,... | collective-permute-start | bytes 688136 | tf_op jit(solution)/shard_map/ppermute | solution.py:656
  22.1 0.0 collective-permute-start.7
  22.1 0.0 copy-done.1
  22.2 1.5 %slab_prep.1 = (f32[1552,128]{1,0:T(8,128)S(1)}, f32[1552,128]{1,0:T(8,128)S(1)}, f32[1552,128]{1,0:T(8,128)S(1)}, f32[120,128]{1,0:T(8,128)S(1)}, f32[632,128]{1,0:T(8,128)S(1)}) custom-call(s32[3,64]{1,0:T(4,128)S(1)} %bitcast.27, f32[4]{0:T(128)S(1)} %copy-done.4, f32[4]{0:T(128)S(1)} %copy-done.5, f32[32,4096]{1,0:T(8,128)S(1)} %copy-done.1, ...), custom_call_target="tpu_custom_call" | custom-call | tf_op jit(solution)/shard_map/slab_prep/pallas_call | solution.py:747
  23.7 0.6 collective-permute-start.6
  24.2 0.9 %collective-permute-done.6.refs_12_ = f32[120,128]{1,0:T(8,128)S(1)} collective-permute-done((f32[120,128]{1,0:T(8,128)S(1)}, f32[120,128]{1,0:T(8,128)S(1)}, u32[]{:S(2)}, u32[]{:S(2)}) %collective-permute-start.6) | collective-permute-done | bytes 61472 | tf_op jit(solution)/shard_map/ppermute | solution.py:662
  25.1 0.7 collective-permute-start.10
  25.9 2.2 %collective-permute-done.5.refs_5_ = f32[448,128]{1,0:T(8,128)S(1)} collective-permute-done((f32[448,128]{1,0:T(8,128)S(1)}, f32[448,128]{1,0:T(8,128)S(1)}, u32[]{:S(2)}, u32[]{:S(2)}) %collective-permute-start.5) | collective-permute-done | bytes 229408 | tf_op jit(solution)/shard_map/ppermute | solution.py:656
  28.1 1.8 %collective-permute-start.9 = (f32[512,128]{1,0:T(8,128)}, f32[512,128]{1,0:T(8,128)S(1)}, u32[]{:S(2)}, u32[]{:S(2)}) collective-permute-start(f32[512,128]{1,0:T(8,128)} %get-tuple-element.25.sigma), channel_id=1, source_target_pairs={{0,2},{1,3},{2,0},{3,1},{4,6},{5,7},{6,4},{7,5},{8,10},{9,11},{10,... | collective-permute-start | bytes 786440 | tf_op jit(solution)/shard_map/ppermute | solution.py:656
  29.9 0.0 collective-permute-done.7.refs_6_
  29.9 0.0 collective-permute-start.8
  29.9 1.5 %collective-permute-done.8.refs_7_ = f32[448,128]{1,0:T(8,128)S(1)} collective-permute-done((f32[448,128]{1,0:T(8,128)S(1)}, f32[448,128]{1,0:T(8,128)S(1)}, u32[]{:S(2)}, u32[]{:S(2)}) %collective-permute-start.8) | collective-permute-done | bytes 229408 | tf_op jit(solution)/shard_map/ppermute | solution.py:666
  31.4 0.0 collective-permute-done.1.refs_2_
  31.4 0.0 collective-permute-done.2.refs_3_
  31.4 19.7 %sweeps.1 = (f32[512,128]{1,0:T(8,128)}, f32[2880,128]{1,0:T(8,128)S(1)}) custom-call(s32[3,64]{1,0:T(4,128)S(1)} %bitcast.28, f32[1536,128]{1,0:T(8,128)S(1)} %copy-done, f32[1024,128]{1,0:T(8,128)S(1)} %collective-permute-done.refs_1_, f32[1536,128]{1,0:T(8,128)S(1)} %collective-permute-done.1.refs_2_, f32[1024,128]{1,0:T(8,128)S(1)} %collective-permute-done.2.refs_3_, ...), custom_call_target="tpu_custom_call" | custom-call | tf_op jit(solution)/shard_map/sweeps/pallas_call | solution.py:767
  51.1 0.0 collective-permute-done.9.refs_1_
  51.1 0.0 collective-permute-done.10.refs_3_
  51.1 14.8 %slab_steps.1 = (f32[32,4096]{1,0:T(8,128)}, f32[512,128]{1,0:T(8,128)S(1)}, f32[1024,128]{1,0:T(8,128)S(1)}, f32[512,128]{1,0:T(8,128)S(1)}) custom-call(s32[3,64]{1,0:T(4,128)S(1)} %bitcast.29, f32[4]{0:T(128)S(1)} %copy-done.4, f32[4]{0:T(128)S(1)} %copy-done.5, f32[1536,128]{1,0:T(8,128)S(1)} %copy-done, f32[512,128]{1,0:T(8,128)S(1)} %collective-permute-done.9.refs_1_, ...), custom_call_target="tpu_custom_call" | custom-call | tf_op jit(solution)/shard_map/slab_steps/pallas_call | solution.py:784
  66.0 0.2 collective-permute-start.11
  66.2 1.8 %collective-permute-done.11 = f32[1024,128]{1,0:T(8,128)S(1)} collective-permute-done((f32[1024,128]{1,0:T(8,128)S(1)}, f32[1024,128]{1,0:T(8,128)S(1)}, u32[]{:S(2)}, u32[]{:S(2)}) %collective-permute-start.11) | collective-permute-done | bytes 524320 | tf_op jit(solution)/shard_map/ppermute | solution.py:666
  68.0 0.3 collective-permute-start.12
  68.3 8.1 %collective-permute-done.12 = f32[512,128]{1,0:T(8,128)S(1)} collective-permute-done((f32[512,128]{1,0:T(8,128)S(1)}, f32[512,128]{1,0:T(8,128)S(1)}, u32[]{:S(2)}, u32[]{:S(2)}) %collective-permute-start.12) | collective-permute-done | bytes 262176 | tf_op jit(solution)/shard_map/ppermute | solution.py:656
  76.4 0.8 fusion
  (13 shorter events, 0.1 us)
Async XLA Ops:
  0.6 21.5 %copy-start.3 = (s32[64,3]{0,1:T(4,128)S(1)}, s32[64,3]{0,1:T(4,128)}, u32[]{:S(2)}) copy-start(s32[64,3]{0,1:T(4,128)} %param.13) | copy-start | bytes 2308
  0.6 21.5 %copy-start.1 = (f32[32,4096]{1,0:T(8,128)S(1)}, f32[32,4096]{1,0:T(8,128)}, u32[]{:S(2)}) copy-start(f32[32,4096]{1,0:T(8,128)} %temp.3) | copy-start | bytes 1572868
  0.7 21.5 %copy-start.2 = (s32[32,4096]{1,0:T(8,128)S(1)}, s32[32,4096]{1,0:T(8,128)}, u32[]{:S(2)}) copy-start(s32[32,4096]{1,0:T(8,128)} %mat.1) | copy-start | bytes 1572868
  0.7 21.5 %copy-start.4 = (f32[4]{0:T(128)S(1)}, f32[4]{0:T(128)}, u32[]{:S(2)}) copy-start(f32[4]{0:T(128)} %k0_table.3) | copy-start | bytes 52
  0.7 21.5 %copy-start.5 = (f32[4]{0:T(128)S(1)}, f32[4]{0:T(128)}, u32[]{:S(2)}) copy-start(f32[4]{0:T(128)} %beta_table.3) | copy-start | bytes 52
  4.8 26.6 %copy-start = (f32[1536,128]{1,0:T(8,128)S(1)}, f32[1536,128]{1,0:T(8,128)}, u32[]{:S(2)}) copy-start(f32[1536,128]{1,0:T(8,128)} %get-tuple-element.21.refs_0_) | copy-start | bytes 2359300
  4.8 14.9 %collective-permute-start = (f32[1024,128]{1,0:T(8,128)}, f32[1024,128]{1,0:T(8,128)S(1)}, u32[]{:S(2)}, u32[]{:S(2)}) collective-permute-start(f32[1024,128]{1,0:T(8,128)} %get-tuple-element.22), channel_id=1, source_target_pairs={{0,2},{1,3},{2,0},{3,1},{4,6},{5,7},{6,4},{7,5},{8,10},{9,11},{10,... | collective-permute-start | bytes 1572872 | tf_op jit(solution)/shard_map/ppermute | solution.py:656
  8.2 23.2 %collective-permute-start.1 = (f32[1536,128]{1,0:T(8,128)}, f32[1536,128]{1,0:T(8,128)S(1)}, u32[]{:S(2)}, u32[]{:S(2)}) collective-permute-start(f32[1536,128]{1,0:T(8,128)} %get-tuple-element.21.refs_0_), channel_id=1, source_target_pairs={{0,1},{1,0},{2,3},{3,2},{4,5},{5,4},{6,7},{7,6},{8,9},{9,8},{10,11... | collective-permute-start | bytes 2359304 | tf_op jit(solution)/shard_map/ppermute | solution.py:666
  8.2 12.6 %collective-permute-start.3 = (f32[496,128]{1,0:T(8,128)}, f32[496,128]{1,0:T(8,128)S(1)}, u32[]{:S(2)}, u32[]{:S(2)}) collective-permute-start(f32[496,128]{1,0:T(8,128)} %get-tuple-element.23), channel_id=1, source_target_pairs={{0,4},{8,12},{16,20},{24,28},{4,0},{12,8},{20,16},{28,24},{1,5},{9... | collective-permute-start | bytes 761864 | tf_op jit(solution)/shard_map/ppermute | solution.py:662
  8.9 11.8 %collective-permute-start.4 = (f32[496,128]{1,0:T(8,128)}, f32[496,128]{1,0:T(8,128)S(1)}, u32[]{:S(2)}, u32[]{:S(2)}) collective-permute-start(f32[496,128]{1,0:T(8,128)} %get-tuple-element.24), channel_id=1, source_target_pairs={{4,8},{12,16},{20,24},{8,4},{16,12},{24,20},{5,9},{13,17},{21,25},... | collective-permute-start | bytes 761864 | tf_op jit(solution)/shard_map/ppermute | solution.py:662
  19.7 11.7 %collective-permute-start.2 = (f32[1024,128]{1,0:T(8,128)S(1)}, f32[1024,128]{1,0:T(8,128)S(1)}, u32[]{:S(2)}, u32[]{:S(2)}) collective-permute-start(f32[1024,128]{1,0:T(8,128)S(1)} %collective-permute-done.refs_1_), channel_id=1, source_target_pairs={{0,1},{1,0},{2,3},{3,2},{4,5},{5,4},{6,7},{7,6},{8,9},{9,8},{10,11... | collective-permute-start | bytes 1572872 | tf_op jit(solution)/shard_map/ppermute | solution.py:666
  20.8 7.3 %collective-permute-start.5 = (f32[448,128]{1,0:T(8,128)S(1)}, f32[448,128]{1,0:T(8,128)S(1)}, u32[]{:S(2)}, u32[]{:S(2)}) collective-permute-start(f32[448,128]{1,0:T(8,128)S(1)} %relay.1.refs_4_), channel_id=1, source_target_pairs={{0,2},{1,3},{2,0},{3,1},{4,6},{5,7},{6,4},{7,5},{8,10},{9,11},{10,... | collective-permute-start | bytes 688136 | tf_op jit(solution)/shard_map/ppermute | solution.py:656
  22.1 7.8 %collective-permute-start.7 = (f32[448,128]{1,0:T(8,128)S(1)}, f32[448,128]{1,0:T(8,128)S(1)}, u32[]{:S(2)}, u32[]{:S(2)}) collective-permute-start(f32[448,128]{1,0:T(8,128)S(1)} %relay.1.refs_4_), channel_id=1, source_target_pairs={{0,1},{1,0},{2,3},{3,2},{4,5},{5,4},{6,7},{7,6},{8,9},{9,8},{10,11... | collective-permute-start | bytes 688136 | tf_op jit(solution)/shard_map/ppermute | solution.py:666
  23.7 1.5 %collective-permute-start.6 = (f32[120,128]{1,0:T(8,128)S(1)}, f32[120,128]{1,0:T(8,128)S(1)}, u32[]{:S(2)}, u32[]{:S(2)}) collective-permute-start(f32[120,128]{1,0:T(8,128)S(1)} %get-tuple-element.26), channel_id=1, source_target_pairs={{0,1},{2,3},{1,0},{3,2},{4,5},{6,7},{5,4},{7,6},{8,9},{10,11},{9,8... | collective-permute-start | bytes 184328 | tf_op jit(solution)/shard_map/ppermute | solution.py:662
  25.1 26.0 %collective-permute-start.10 = (f32[632,128]{1,0:T(8,128)S(1)}, f32[632,128]{1,0:T(8,128)S(1)}, u32[]{:S(2)}, u32[]{:S(2)}) collective-permute-start(f32[632,128]{1,0:T(8,128)S(1)} %get-tuple-element.29), channel_id=1, source_target_pairs={{0,3},{1,2},{2,1},{3,0},{4,7},{5,6},{6,5},{7,4},{8,11},{9,10},{10,... | collective-permute-start | bytes 970760 | tf_op jit(solution)/shard_map/ppermute | solution.py:679
  28.1 23.0 %collective-permute-start.9 = (f32[512,128]{1,0:T(8,128)}, f32[512,128]{1,0:T(8,128)S(1)}, u32[]{:S(2)}, u32[]{:S(2)}) collective-permute-start(f32[512,128]{1,0:T(8,128)} %get-tuple-element.25.sigma), channel_id=1, source_target_pairs={{0,2},{1,3},{2,0},{3,1},{4,6},{5,7},{6,4},{7,5},{8,10},{9,11},{10,... | collective-permute-start | bytes 786440 | tf_op jit(solution)/shard_map/ppermute | solution.py:656
  29.9 1.5 %collective-permute-start.8 = (f32[448,128]{1,0:T(8,128)S(1)}, f32[448,128]{1,0:T(8,128)S(1)}, u32[]{:S(2)}, u32[]{:S(2)}) collective-permute-start(f32[448,128]{1,0:T(8,128)S(1)} %collective-permute-done.5.refs_5_), channel_id=1, source_target_pairs={{0,1},{1,0},{2,3},{3,2},{4,5},{5,4},{6,7},{7,6},{8,9},{9,8},{10,11... | collective-permute-start | bytes 688136 | tf_op jit(solution)/shard_map/ppermute | solution.py:666
  66.0 2.0 %collective-permute-start.11 = (f32[1024,128]{1,0:T(8,128)S(1)}, f32[1024,128]{1,0:T(8,128)S(1)}, u32[]{:S(2)}, u32[]{:S(2)}) collective-permute-start(f32[1024,128]{1,0:T(8,128)S(1)} %get-tuple-element.37), channel_id=1, source_target_pairs={{0,1},{1,0},{2,3},{3,2},{4,5},{5,4},{6,7},{7,6},{8,9},{9,8},{10,11... | collective-permute-start | bytes 1572872 | tf_op jit(solution)/shard_map/ppermute | solution.py:666
  68.0 8.4 %collective-permute-start.12 = (f32[512,128]{1,0:T(8,128)S(1)}, f32[512,128]{1,0:T(8,128)S(1)}, u32[]{:S(2)}, u32[]{:S(2)}) collective-permute-start(f32[512,128]{1,0:T(8,128)S(1)} %slice_add_fusion), channel_id=1, source_target_pairs={{0,2},{1,3},{2,0},{3,1},{4,6},{5,7},{6,4},{7,5},{8,10},{9,11},{10,... | collective-permute-start | bytes 786440 | tf_op jit(solution)/shard_map/ppermute | solution.py:656

commit v14 on v11

--- a/solution.py
+++ b/solution.py
@@ -199,8 +199,12 @@
 
 def part_device(part, chips, j):
     mate = j + 1 - 2 * lax.rem(j, 2)
-    base = j if part < chips else mate
-    return lax.rem(base - 2 * (part % chips) + 2 * chips, 2 * chips)
+    if isinstance(part, int):
+        base, back = (j, part) if part < chips else (mate, part - chips)
+    else:
+        base = jnp.where(part < chips, j, mate)
+        back = lax.rem(part, chips)
+    return lax.rem(base - 2 * back + 2 * chips, 2 * chips)
 
 
 def sweep_kernel(chips, pos, *refs):
@@ -311,39 +315,50 @@
         return quarter == upper, quarter == lax.bitwise_and(upper + 3, 3)
 
     bufs = ((pa, la, ua), (pb, lb, ub))
-    for k in range(SWEEPS):
-        weight = cheb_weight(k, SWEEPS)
-        keep, gain = 1.0 - weight, weight / (6.0 + EPS)
-        (c_src, l_src, u_src), (c_dst, l_dst, u_dst) = bufs[k % 2], bufs[(k + 1) % 2]
-
-        def relax(src, dst, places, first, count, s_ref, s_row, before, beyond):
-            row, row_m, row_p, row_zm, row_zp, _, _, upper = places
-            first_y, last_y = y_ends(upper)
-            own = plane_at(src, row + first * ROW)
-            for p in range(count):
-                step = (first + p) * ROW
-                after = plane_at(src, row + (step + ROW)) if beyond is None or p < count - 1 else beyond
-                total = (before + after) + plane_at(s_ref, s_row + p * ROW)
-                along_y = y_minus(src, own, last_y, row + (step - TILES), row_m + (step + ROW - TILES))
-                along_y = along_y + y_plus(src, own, first_y, row + (step + TILES), row_p + (step + TILES - ROW))
-                along_z = z_minus(src, own, row_zm + step) + z_plus(src, own, row_zp + step)
-                put_plane(dst, row + step, keep * own + gain * (total + (along_y + along_z)))
-                before, own = own, after
+    weights = [cheb_weight(k, SWEEPS) for k in range(SWEEPS)]
+
+    def relax(src, dst, places, first, count, s_ref, s_row, before, beyond, keep, gain):
+        row, row_m, row_p, row_zm, row_zp, _, _, upper = places
+        first_y, last_y = y_ends(upper)
+        own = plane_at(src, row + first * ROW)
+        for p in range(count):
+            step = (first + p) * ROW
+            after = plane_at(src, row + (step + ROW)) if p < count - 1 else beyond
+            total = (before + after) + plane_at(s_ref, s_row + p * ROW)
+            along_y = y_minus(src, own, last_y, row + (step - TILES), row_m + (step + ROW - TILES))
+            along_y = along_y + y_plus(src, own, first_y, row + (step + TILES), row_p + (step + TILES - ROW))
+            along_z = z_minus(src, own, row_zm + step) + z_plus(src, own, row_zp + step)
+            put_plane(dst, row + step, keep * own + gain * (total + (along_y + along_z)))
+            before, own = own, after
+
+    def sweep(src, dst, keep, gain):
+        (c_src, l_src, u_src), (c_dst, l_dst, u_dst) = src, dst
 
         def sweep_tile(slot, carry):
             at = entry(0, slot)
-            relax(c_src, c_dst, at, 0, TE, s_c, at[0], plane_at(l_src, at[5]), plane_at(u_src, at[6]))
+            ends = plane_at(l_src, at[5]), plane_at(u_src, at[6])
+            relax(c_src, c_dst, at, 0, TE, s_c, at[0], *ends, keep, gain)
             at = entry(1, slot)
-            count = LOW[0] - 1 - k
-            s_row = row_of(slot, LOW[1]) + (LOW[1] - count) * ROW
-            before, beyond = plane_at(l_src, at[0] + k * ROW), plane_at(c_src, at[6])
-            relax(l_src, l_dst, at, k + 1, count, s_l, s_row, before, beyond)
+            ends = plane_at(l_src, at[0]), plane_at(c_src, at[6])
+            relax(l_src, l_dst, at, 1, LOW[0] - 1, s_l, row_of(slot, LOW[1]), *ends, keep, gain)
             at = entry(2, slot)
-            relax(u_src, u_dst, at, 0, HIGH[0] - 1 - k, s_u, row_of(slot, HIGH[1]), plane_at(c_src, at[5]), None)
+            ends = plane_at(c_src, at[5]), plane_at(u_src, at[0] + (HIGH[0] - 1) * ROW)
+            relax(u_src, u_dst, at, 0, HIGH[0] - 1, s_u, row_of(slot, HIGH[1]), *ends, keep, gain)
             return carry
 
         lax.fori_loop(0, tiles, sweep_tile, 0, unroll=2)
 
+    def two_sweeps(pair, carry):
+        for half, (src, dst) in enumerate((bufs, bufs[::-1])):
+            keep, gain = jnp.float32(0.0), jnp.float32(0.0)
+            for at in range(SWEEPS // 2):
+                weight = weights[2 * at + half]
+                keep = jnp.where(pair == at, jnp.float32(1.0 - weight), keep)
+                gain = jnp.where(pair == at, jnp.float32(weight / (6.0 + EPS)), gain)
+            sweep(src, dst, keep, gain)
+        return carry
+
+    lax.fori_loop(0, SWEEPS // 2, two_sweeps, 0)
     field, f_l, f_u = bufs[SWEEPS % 2]
     for t in range(TILES):
         turn = jnp.where(table[t * 8 + 7] == 1, LANES - TE, 0)
@@ -403,7 +418,8 @@
     for part in range(width_gy):
         start = 2 * TE * ROW if part % chips == 0 else 0
         source = refs[part].at[start : start + TE * ROW]
-        moves.append(pltpu.make_async_copy(source, sigmas.at[part], sems.at[part]))
+        target = sigmas.at[part * TE * ROW : (part + 1) * TE * ROW]
+        moves.append(pltpu.make_async_copy(source, target, sems.at[part]))
         moves[-1].start()
     i = lax.axis_index("gx")
     j = lax.axis_index("gy")
@@ -497,23 +513,28 @@
     for move in moves:
         move.wait()
     low_at, high_at = (LOW[0] + LOW[1]) * ROW, LOW_ROWS + (HIGH[0] + HIGH[1]) * ROW
+    def put_heat(which, by, dev, t, x, count, sigma_of):
+        tile = jnp.clip(i + by, 0, rows_gx - 1) * tiles + dev * TILES + t
+        cell = (pos[1, tile] + 1) * 2 + pos[2, tile]
+        first = pl.multiple_of((window(which, cell, i, j, rows_gx) * SLABX + x) * SUB, SUB)
+        for p in range(count):
+            rows = pl.ds(pl.multiple_of(first + p * SUB, SUB), SUB)
+            heat[rows, :] = sigma_of(p) * slope[rows, :]
+
+    def own_heat(slot, carry):
+        part, t = lax.div(slot, TILES), lax.rem(slot, TILES)
+        row = part * (TE * ROW) + t
+        dev = part_device(part, chips, j)
+        put_heat(0, 0, dev, t, HALO, TE, lambda p: sigmas[pl.ds(row + p * ROW, SUB, stride=TILES), :])
+        return carry
+
+    lax.fori_loop(0, tiles, own_heat, 0)
     for part in range(width_gy):
         dev = part_device(part, chips, j)
         for t in range(TILES):
-            for which, by in enumerate((0, -1, 1)):
-                tile = jnp.clip(i + by, 0, rows_gx - 1) * tiles + dev * TILES + t
-                cell = (pos[1, tile] + 1) * 2 + pos[2, tile]
-                local = window(which, cell, i, j, rows_gx)
-                source, start, x, count = (
-                    (sigmas.at[part], 0, HALO, TE),
-                    (halos[part], low_at, HALO - 2, 2),
-                    (halos[part], high_at, HALO + TE, 2),
-                )[which]
-                first = pl.multiple_of((local * SLABX + x) * SUB, SUB)
-                for p in range(count):
-                    rows = pl.ds(pl.multiple_of(first + p * SUB, SUB), SUB)
-                    sigma = source[pl.ds(start + p * ROW + t, SUB, stride=TILES), :]
-                    heat[rows, :] = sigma * slope[rows, :]
+            for which, by, x, at in ((1, -1, HALO - 2, low_at), (2, 1, HALO + TE, high_at)):
+                rows = lambda p: pl.ds(at + p * ROW + t, SUB, stride=TILES)
+                put_heat(which, by, dev, t, x, 2, lambda p: halos[part][rows(p), :])
 
     def place_heat(at, carry):
         first = at - 1
@@ -565,7 +586,7 @@
             return ahead, flux_y
 
         first, second = load(src, 0), load(src, 1)
-        lax.fori_loop(1, YBLOCKS - 1, advance, (second, y_fluxes(0, first, second)), unroll=6)
+        lax.fori_loop(1, YBLOCKS - 1, advance, (second, y_fluxes(0, first, second)), unroll=3)
     final = state_b if CSWEEPS % 2 else state_a
 
     def give_out(yq, carry):
@@ -692,7 +713,6 @@
         name="prep",
     )(sigma_table, pos, to_rows(phi_init), to_rows(source), to_rows(tile_mat), temp_init, slab_mat)
     bodies = [body] + [shifted(ready, "gy", 2 * d, True) for d in range(1, chips)]
-    bodies += [from_mate(part) for part in bodies]
     inner, outer = with_partner(inner, "gx", 0), with_partner(outer, "gx", 1)
 
     halo = pl.pallas_call(
@@ -704,9 +724,7 @@
         name="relay",
     )(inner, outer)
     halos = [halo] + [shifted(halo, "gy", 2 * d, True) for d in range(1, chips)]
-    sigmas = [bodies[0]] + [shifted(sigma, "gy", 2 * d, True) for d in range(1, chips)]
-    sigmas += [bodies[chips]] + [to_other_core(sigma, d) for d in range(1, chips)]
-
+    inner, halos[0] = lax.optimization_barrier((inner, halos[0]))
     native = pltpu.VMEM((width // LANES * SLABX + SUB, LANES), f32)
     t_ext, k0_ext, b_ext, edge_in, edge_out = pl.pallas_call(
         slab_kernel,
@@ -718,6 +736,10 @@
         name="slab_prep",
     )(pos, k0_table, beta_table, temp_init, slab_mat, inner, outer)
     y_in, y_out = with_partner(edge_in, "gy", 0), with_partner(edge_out, "gy", 1)
+    *bodies[1:], y_in = lax.optimization_barrier((*bodies[1:], y_in))
+    bodies += [from_mate(part) for part in bodies]
+    sigmas = [bodies[0]] + [shifted(sigma, "gy", 2 * d, True) for d in range(1, chips)]
+    sigmas += [bodies[chips]] + [to_other_core(sigma, d) for d in range(1, chips)]
     *halos[1:], y_in = lax.optimization_barrier((*halos[1:], y_in))
     halos = halos + [from_mate(part) for part in halos]
 
@@ -751,7 +773,7 @@
         + [pltpu.VMEM((SLAB_ROWS + 3 * SLABX, LANES), f32)]
         + [pltpu.VMEM((2 * SLAB_ROWS, LANES), f32)] * 2
         + [pltpu.VMEM((SLAB_ROWS, LANES), f32)] * 2
-        + [pltpu.VMEM((4 * TE * SUB, LANES), f32), pltpu.VMEM((width_gy, TE * ROW, LANES), f32)]
+        + [pltpu.VMEM((4 * TE * SUB, LANES), f32), pltpu.VMEM((width_gy * TE * ROW, LANES), f32)]
         + [pltpu.SemaphoreType.DMA((width_gy,))],
         compiler_params=PARAMS,
         name="slab_steps",

time: 65.8 us -> 70.4 us (1.070)
  Pallas kernels: 26.2 us -> 29.1 us
  waiting for transfers between devices: 25.4 us -> 26.7 us
    ppermute x4, waiting for transfers between devices: 2.15 us -> 11 us  [with_partner(): lax.ppermute(value, axis, pairs + [(high, low) for low, high in pairs])]
    ppermute x4, waiting for transfers between devices: 21.7 us -> 14.2 us  [shifted(): return lax.ppermute(value, axis, pairs)]
    pallas_call x1, Pallas kernels: 8.79 us -> 11.6 us  [on_device(): pl.pallas_call(functools.partial(slab_steps_kernel, chips), out_shape=(ja...]
    ppermute x5, starting transfers between devices: 3.24 us -> 2.26 us  [from_mate(): lax.ppermute(value, 'gy', [(d, d ^ 1) for d in range(lax.axis_size('gy'))])]
    ppermute x1, starting transfers between devices: 0.54 us -> 1.32 us  [to_other_core(): lax.ppermute(value, 'gy', [(at, ((at ^ 1) + 2 * by) % count) for at in ra...]
  transfers between devices with their start and end apart: 14 -> 14, of which waited for: 6 -> 5; matrix products, arithmetic and copies ran while one was open for 0% -> 0% of each run, Pallas kernels for 20% -> 19%
where the time goes in v14:
time: 70.4 us; the launch traced here: 70.2 us
  Pallas kernels  29.1 us (41%)
  waiting for transfers between devices  26.7 us (38%)
  starting transfers between devices  12.6 us (18%)
  between operations  0.86 us (1%)
  other arithmetic  0.78 us (1%)
    ppermute x4, waiting for transfers between devices, shifted(): return lax.ppermute(value, axis, pairs)  14.2 us
    pallas_call x1, Pallas kernels, on_device(): pl.pallas_call(functools.partial(sweep_kernel, chips), out_shape=(rows(TE...  12.3 us
    pallas_call x1, Pallas kernels, on_device(): pl.pallas_call(functools.partial(slab_steps_kernel, chips), out_shape=(ja...  11.6 us
    ppermute x4, waiting for transfers between devices, with_partner(): lax.ppermute(value, axis, pairs + [(high, low) for low, high in pairs])  11 us
    ppermute x4, starting transfers between devices, shifted(): return lax.ppermute(value, axis, pairs)  5.78 us
    pallas_call x1, Pallas kernels, on_device(): pl.pallas_call(prep_kernel, out_shape=(rows(3 * TE * ROW), rows(2 * TE *...  4.08 us
    ppermute x4, starting transfers between devices, with_partner(): lax.ppermute(value, axis, pairs + [(high, low) for low, high in pairs])  3.27 us
    ppermute x5, starting transfers between devices, from_mate(): lax.ppermute(value, 'gy', [(d, d ^ 1) for d in range(lax.axis_size('gy'))])  2.26 us
  transfers between devices with their start and end apart: 14, of which 5 were waited for; matrix products, arithmetic and copies ran while one was open for 0% of the time, Pallas kernels for 19%

profile of v14, /device:TPU:0, one launch (start us, length us, event | category | flops | bytes accessed | tf_op | source)
XLA Modules:
  0.0 70.2 jit_solution(1782192133692589323)
XLA Ops:
  0.7 4.1 %prep.1 = (f32[1536,128]{1,0:T(8,128)}, f32[1024,128]{1,0:T(8,128)}, f32[512,128]{1,0:T(8,128)}, f32[496,128]{1,0:T(8,128)}, f32[496,128]{1,0:T(8,128)}) custom-call(f32[4]{0:T(128)} %table.1, s32[3,64]{1,0:T(4,128)} %bitcast.26, f32[512,128]{1,0:T(8,128)} %bitcast.30, f32[512,128]{1,0:T(8,128)} %bitcast.31, s32[512,128]{1,0:T(8,128)} %bitcast.32, ...), custom_call_target="tpu_custom_call" | custom-call | tf_op jit(solution)/shard_map/prep/pallas_call | solution.py:694
  4.8 0.0 copy-start.6
  4.8 3.0 %collective-permute-start = (f32[1024,128]{1,0:T(8,128)}, f32[1024,128]{1,0:T(8,128)S(1)}, u32[]{:S(2)}, u32[]{:S(2)}) collective-permute-start(f32[1024,128]{1,0:T(8,128)} %get-tuple-element.26), channel_id=1, source_target_pairs={{0,2},{1,3},{2,0},{3,1},{4,6},{5,7},{6,4},{7,5},{8,10},{9,11},{10,... | collective-permute-start | bytes 1572872 | tf_op jit(solution)/shard_map/ppermute | solution.py:638
  7.8 1.9 %collective-permute-start.1 = (f32[496,128]{1,0:T(8,128)}, f32[496,128]{1,0:T(8,128)S(1)}, u32[]{:S(2)}, u32[]{:S(2)}) collective-permute-start(f32[496,128]{1,0:T(8,128)} %get-tuple-element.27), channel_id=1, source_target_pairs={{0,4},{8,12},{16,20},{24,28},{4,0},{12,8},{20,16},{28,24},{1,5},{9... | collective-permute-start | bytes 761864 | tf_op jit(solution)/shard_map/ppermute | solution.py:644
  9.7 0.7 collective-permute-start.2
  10.3 0.1 collective-permute-start.4
  10.4 9.7 %collective-permute-done.1.inner = f32[496,128]{1,0:T(8,128)S(1)} collective-permute-done((f32[496,128]{1,0:T(8,128)}, f32[496,128]{1,0:T(8,128)S(1)}, u32[]{:S(2)}, u32[]{:S(2)}) %collective-permute-start.1) | collective-permute-done | bytes 253984 | tf_op jit(solution)/shard_map/ppermute | solution.py:644
  20.2 0.0 collective-permute-done.2.outer
  20.3 1.1 %slab_prep.1 = (f32[1552,128]{1,0:T(8,128)S(1)}, f32[1552,128]{1,0:T(8,128)S(1)}, f32[1552,128]{1,0:T(8,128)S(1)}, f32[120,128]{1,0:T(8,128)S(1)}, f32[120,128]{1,0:T(8,128)S(1)}) custom-call(s32[3,64]{1,0:T(4,128)S(1)} %bitcast.27, f32[4]{0:T(128)S(1)} %copy-done.4, f32[4]{0:T(128)S(1)} %copy-done.5, f32[32,4096]{1,0:T(8,128)S(1)} %copy-done.1, ...), custom_call_target="tpu_custom_call" | custom-call | tf_op jit(solution)/shard_map/slab_prep/pallas_call | solution.py:729
  21.4 0.1 collective-permute-start.3
  21.4 1.2 %collective-permute-done.3.refs_12_ = f32[120,128]{1,0:T(8,128)S(1)} collective-permute-done((f32[120,128]{1,0:T(8,128)S(1)}, f32[120,128]{1,0:T(8,128)S(1)}, u32[]{:S(2)}, u32[]{:S(2)}) %collective-permute-start.3) | collective-permute-done | bytes 61472 | tf_op jit(solution)/shard_map/ppermute | solution.py:644
  22.7 0.0 collective-permute-done.refs_1_
  22.7 0.2 collective-permute-start.5
  22.8 0.5 collective-permute-start.6
  23.4 0.1 collective-permute-start.7
  23.5 7.3 %collective-permute-done.6.refs_5_ = f32[448,128]{1,0:T(8,128)S(1)} collective-permute-done((f32[448,128]{1,0:T(8,128)S(1)}, f32[448,128]{1,0:T(8,128)S(1)}, u32[]{:S(2)}, u32[]{:S(2)}) %collective-permute-start.6) | collective-permute-done | bytes 229408 | tf_op jit(solution)/shard_map/ppermute | solution.py:638
  30.7 0.0 collective-permute-start.8
  30.7 0.5 collective-permute-start.9
  31.2 0.0 collective-permute-done.7.refs_6_
  31.3 1.3 %collective-permute-start.10 = (f32[512,128]{1,0:T(8,128)S(1)}, f32[512,128]{1,0:T(8,128)S(1)}, u32[]{:S(2)}, u32[]{:S(2)}) collective-permute-start(f32[512,128]{1,0:T(8,128)S(1)} %copy-done.6), channel_id=1, source_target_pairs={{0,3},{1,2},{2,1},{3,0},{4,7},{5,6},{6,5},{7,4},{8,11},{9,10},{10,... | collective-permute-start | bytes 786440 | tf_op jit(solution)/shard_map/ppermute | solution.py:661
  32.6 0.0 collective-permute-done.8.refs_7_
  32.6 0.7 collective-permute-start.11
  33.2 0.0 collective-permute-done.4.refs_2_
  33.3 12.3 %sweeps.1 = (f32[512,128]{1,0:T(8,128)}, f32[2880,128]{1,0:T(8,128)S(1)}) custom-call(s32[3,64]{1,0:T(4,128)S(1)} %bitcast.28, f32[1536,128]{1,0:T(8,128)S(1)} %copy-done, f32[1024,128]{1,0:T(8,128)S(1)} %collective-permute-done.refs_1_, f32[1536,128]{1,0:T(8,128)S(1)} %collective-permute-done.4.refs_2_, f32[1024,128]{1,0:T(8,128)S(1)} %collective-permute-done.5.refs_3_, ...), custom_call_target="tpu_custom_call" | custom-call | tf_op jit(solution)/shard_map/sweeps/pallas_call | solution.py:749
  45.6 0.0 collective-permute-done.10.refs_3_
  45.6 0.0 collective-permute-done.11.refs_13_
  45.6 11.6 %slab_steps.1 = (f32[32,4096]{1,0:T(8,128)}, f32[512,128]{1,0:T(8,128)S(1)}, f32[1024,128]{1,0:T(8,128)S(1)}, f32[512,128]{1,0:T(8,128)S(1)}) custom-call(s32[3,64]{1,0:T(4,128)S(1)} %bitcast.29, f32[4]{0:T(128)S(1)} %copy-done.4, f32[4]{0:T(128)S(1)} %copy-done.5, f32[1536,128]{1,0:T(8,128)S(1)} %copy-done, f32[512,128]{1,0:T(8,128)S(1)} %collective-permute-done.9.refs_1_, ...), custom_call_target="tpu_custom_call" | custom-call | tf_op jit(solution)/shard_map/slab_steps/pallas_call | solution.py:766
  57.2 2.0 %collective-permute-start.12 = (f32[1024,128]{1,0:T(8,128)S(1)}, f32[1024,128]{1,0:T(8,128)S(1)}, u32[]{:S(2)}, u32[]{:S(2)}) collective-permute-start(f32[1024,128]{1,0:T(8,128)S(1)} %get-tuple-element.45), channel_id=1, source_target_pairs={{0,1},{1,0},{2,3},{3,2},{4,5},{5,4},{6,7},{7,6},{8,9},{9,8},{10,11... | collective-permute-start | bytes 1572872 | tf_op jit(solution)/shard_map/ppermute | solution.py:648
  59.2 1.5 %collective-permute-done.12 = f32[1024,128]{1,0:T(8,128)S(1)} collective-permute-done((f32[1024,128]{1,0:T(8,128)S(1)}, f32[1024,128]{1,0:T(8,128)S(1)}, u32[]{:S(2)}, u32[]{:S(2)}) %collective-permute-start.12) | collective-permute-done | bytes 524320 | tf_op jit(solution)/shard_map/ppermute | solution.py:648
  60.8 1.7 %collective-permute-start.13 = (f32[512,128]{1,0:T(8,128)S(1)}, f32[512,128]{1,0:T(8,128)S(1)}, u32[]{:S(2)}, u32[]{:S(2)}) collective-permute-start(f32[512,128]{1,0:T(8,128)S(1)} %slice_add_fusion), channel_id=1, source_target_pairs={{0,2},{1,3},{2,0},{3,1},{4,6},{5,7},{6,4},{7,5},{8,10},{9,11},{10,... | collective-permute-start | bytes 786440 | tf_op jit(solution)/shard_map/ppermute | solution.py:638
  62.5 6.9 %collective-permute-done.13 = f32[512,128]{1,0:T(8,128)S(1)} collective-permute-done((f32[512,128]{1,0:T(8,128)S(1)}, f32[512,128]{1,0:T(8,128)S(1)}, u32[]{:S(2)}, u32[]{:S(2)}) %collective-permute-start.13) | collective-permute-done | bytes 262176 | tf_op jit(solution)/shard_map/ppermute | solution.py:638
  69.4 0.7 %fusion = f32[512,128]{1,0:T(8,128)} fusion(f32[512,128]{1,0:T(8,128)S(1)} %collective-permute-done.13, f32[512,128]{1,0:T(8,128)S(1)} %get-tuple-element.44, f32[1024,128]{1,0:T(8,128)S(1)} %collective-permute-done.12), kind=kLoop, calls=%fused_computation.2 | loop fusion | flops 131072 | bytes 1048576 | tf_op jit(solution)/shard_map/add | solution.py:784
  (17 shorter events, 0.1 us)
Async XLA Ops:
  0.6 19.6 %copy-start.3 = (s32[64,3]{0,1:T(4,128)S(1)}, s32[64,3]{0,1:T(4,128)}, u32[]{:S(2)}) copy-start(s32[64,3]{0,1:T(4,128)} %param.13) | copy-start | bytes 2308
  0.6 19.6 %copy-start.1 = (f32[32,4096]{1,0:T(8,128)S(1)}, f32[32,4096]{1,0:T(8,128)}, u32[]{:S(2)}) copy-start(f32[32,4096]{1,0:T(8,128)} %temp.3) | copy-start | bytes 1572868
  0.7 19.6 %copy-start.2 = (s32[32,4096]{1,0:T(8,128)S(1)}, s32[32,4096]{1,0:T(8,128)}, u32[]{:S(2)}) copy-start(s32[32,4096]{1,0:T(8,128)} %mat.1) | copy-start | bytes 1572868
  0.7 19.6 %copy-start.4 = (f32[4]{0:T(128)S(1)}, f32[4]{0:T(128)}, u32[]{:S(2)}) copy-start(f32[4]{0:T(128)} %k0_table.3) | copy-start | bytes 52
  0.7 19.6 %copy-start.5 = (f32[4]{0:T(128)S(1)}, f32[4]{0:T(128)}, u32[]{:S(2)}) copy-start(f32[4]{0:T(128)} %beta_table.3) | copy-start | bytes 52
  4.8 25.9 %copy-start.6 = (f32[512,128]{1,0:T(8,128)S(1)}, f32[512,128]{1,0:T(8,128)}, u32[]{:S(2)}) copy-start(f32[512,128]{1,0:T(8,128)} %get-tuple-element.36) | copy-start | bytes 786436
  4.8 28.5 %copy-start = (f32[1536,128]{1,0:T(8,128)S(1)}, f32[1536,128]{1,0:T(8,128)}, u32[]{:S(2)}) copy-start(f32[1536,128]{1,0:T(8,128)} %get-tuple-element.25.refs_0_) | copy-start | bytes 2359300
  4.8 17.9 %collective-permute-start = (f32[1024,128]{1,0:T(8,128)}, f32[1024,128]{1,0:T(8,128)S(1)}, u32[]{:S(2)}, u32[]{:S(2)}) collective-permute-start(f32[1024,128]{1,0:T(8,128)} %get-tuple-element.26), channel_id=1, source_target_pairs={{0,2},{1,3},{2,0},{3,1},{4,6},{5,7},{6,4},{7,5},{8,10},{9,11},{10,... | collective-permute-start | bytes 1572872 | tf_op jit(solution)/shard_map/ppermute | solution.py:638
  7.8 12.4 %collective-permute-start.1 = (f32[496,128]{1,0:T(8,128)}, f32[496,128]{1,0:T(8,128)S(1)}, u32[]{:S(2)}, u32[]{:S(2)}) collective-permute-start(f32[496,128]{1,0:T(8,128)} %get-tuple-element.27), channel_id=1, source_target_pairs={{0,4},{8,12},{16,20},{24,28},{4,0},{12,8},{20,16},{28,24},{1,5},{9... | collective-permute-start | bytes 761864 | tf_op jit(solution)/shard_map/ppermute | solution.py:644
  9.7 10.5 %collective-permute-start.2 = (f32[496,128]{1,0:T(8,128)}, f32[496,128]{1,0:T(8,128)S(1)}, u32[]{:S(2)}, u32[]{:S(2)}) collective-permute-start(f32[496,128]{1,0:T(8,128)} %get-tuple-element.28), channel_id=1, source_target_pairs={{4,8},{12,16},{20,24},{8,4},{16,12},{24,20},{5,9},{13,17},{21,25},... | collective-permute-start | bytes 761864 | tf_op jit(solution)/shard_map/ppermute | solution.py:644
  10.3 22.9 %collective-permute-start.4 = (f32[1536,128]{1,0:T(8,128)}, f32[1536,128]{1,0:T(8,128)S(1)}, u32[]{:S(2)}, u32[]{:S(2)}) collective-permute-start(f32[1536,128]{1,0:T(8,128)} %get-tuple-element.25.refs_0_), channel_id=1, source_target_pairs={{0,1},{1,0},{2,3},{3,2},{4,5},{5,4},{6,7},{7,6},{8,9},{9,8},{10,11... | collective-permute-start | bytes 2359304 | tf_op jit(solution)/shard_map/ppermute | solution.py:648
  21.4 1.3 %collective-permute-start.3 = (f32[120,128]{1,0:T(8,128)S(1)}, f32[120,128]{1,0:T(8,128)S(1)}, u32[]{:S(2)}, u32[]{:S(2)}) collective-permute-start(f32[120,128]{1,0:T(8,128)S(1)} %get-tuple-element.30), channel_id=1, source_target_pairs={{0,1},{2,3},{1,0},{3,2},{4,5},{6,7},{5,4},{7,6},{8,9},{10,11},{9,8... | collective-permute-start | bytes 184328 | tf_op jit(solution)/shard_map/ppermute | solution.py:644
  22.7 10.6 %collective-permute-start.5 = (f32[1024,128]{1,0:T(8,128)S(1)}, f32[1024,128]{1,0:T(8,128)S(1)}, u32[]{:S(2)}, u32[]{:S(2)}) collective-permute-start(f32[1024,128]{1,0:T(8,128)S(1)} %collective-permute-done.refs_1_), channel_id=1, source_target_pairs={{0,1},{1,0},{2,3},{3,2},{4,5},{5,4},{6,7},{7,6},{8,9},{9,8},{10,11... | collective-permute-start | bytes 1572872 | tf_op jit(solution)/shard_map/ppermute | solution.py:648
  22.8 7.9 %collective-permute-start.6 = (f32[448,128]{1,0:T(8,128)S(1)}, f32[448,128]{1,0:T(8,128)S(1)}, u32[]{:S(2)}, u32[]{:S(2)}) collective-permute-start(f32[448,128]{1,0:T(8,128)S(1)} %relay.1.refs_4_), channel_id=1, source_target_pairs={{0,2},{1,3},{2,0},{3,1},{4,6},{5,7},{6,4},{7,5},{8,10},{9,11},{10,... | collective-permute-start | bytes 688136 | tf_op jit(solution)/shard_map/ppermute | solution.py:638
  23.4 7.9 %collective-permute-start.7 = (f32[448,128]{1,0:T(8,128)S(1)}, f32[448,128]{1,0:T(8,128)S(1)}, u32[]{:S(2)}, u32[]{:S(2)}) collective-permute-start(f32[448,128]{1,0:T(8,128)S(1)} %relay.1.refs_4_), channel_id=1, source_target_pairs={{0,1},{1,0},{2,3},{3,2},{4,5},{5,4},{6,7},{7,6},{8,9},{9,8},{10,11... | collective-permute-start | bytes 688136 | tf_op jit(solution)/shard_map/ppermute | solution.py:648
  30.7 1.9 %collective-permute-start.8 = (f32[448,128]{1,0:T(8,128)S(1)}, f32[448,128]{1,0:T(8,128)S(1)}, u32[]{:S(2)}, u32[]{:S(2)}) collective-permute-start(f32[448,128]{1,0:T(8,128)S(1)} %collective-permute-done.6.refs_5_), channel_id=1, source_target_pairs={{0,1},{1,0},{2,3},{3,2},{4,5},{5,4},{6,7},{7,6},{8,9},{9,8},{10,11... | collective-permute-start | bytes 688136 | tf_op jit(solution)/shard_map/ppermute | solution.py:648
  30.7 14.8 %collective-permute-start.9 = (f32[512,128]{1,0:T(8,128)S(1)}, f32[512,128]{1,0:T(8,128)S(1)}, u32[]{:S(2)}, u32[]{:S(2)}) collective-permute-start(f32[512,128]{1,0:T(8,128)S(1)} %copy-done.6), channel_id=1, source_target_pairs={{0,2},{1,3},{2,0},{3,1},{4,6},{5,7},{6,4},{7,5},{8,10},{9,11},{10,... | collective-permute-start | bytes 786440 | tf_op jit(solution)/shard_map/ppermute | solution.py:638
  31.3 14.3 %collective-permute-start.10 = (f32[512,128]{1,0:T(8,128)S(1)}, f32[512,128]{1,0:T(8,128)S(1)}, u32[]{:S(2)}, u32[]{:S(2)}) collective-permute-start(f32[512,128]{1,0:T(8,128)S(1)} %copy-done.6), channel_id=1, source_target_pairs={{0,3},{1,2},{2,1},{3,0},{4,7},{5,6},{6,5},{7,4},{8,11},{9,10},{10,... | collective-permute-start | bytes 786440 | tf_op jit(solution)/shard_map/ppermute | solution.py:661
  32.6 13.0 %collective-permute-start.11 = (f32[120,128]{1,0:T(8,128)S(1)}, f32[120,128]{1,0:T(8,128)S(1)}, u32[]{:S(2)}, u32[]{:S(2)}) collective-permute-start(f32[120,128]{1,0:T(8,128)S(1)} %get-tuple-element.42), channel_id=1, source_target_pairs={{1,2},{2,1},{5,6},{6,5},{9,10},{10,9},{13,14},{14,13},{17,18},{18,... | collective-permute-start | bytes 184328 | tf_op jit(solution)/shard_map/ppermute | solution.py:644
  57.2 3.5 %collective-permute-start.12 = (f32[1024,128]{1,0:T(8,128)S(1)}, f32[1024,128]{1,0:T(8,128)S(1)}, u32[]{:S(2)}, u32[]{:S(2)}) collective-permute-start(f32[1024,128]{1,0:T(8,128)S(1)} %get-tuple-element.45), channel_id=1, source_target_pairs={{0,1},{1,0},{2,3},{3,2},{4,5},{5,4},{6,7},{7,6},{8,9},{9,8},{10,11... | collective-permute-start | bytes 1572872 | tf_op jit(solution)/shard_map/ppermute | solution.py:648
  60.8 8.7 %collective-permute-start.13 = (f32[512,128]{1,0:T(8,128)S(1)}, f32[512,128]{1,0:T(8,128)S(1)}, u32[]{:S(2)}, u32[]{:S(2)}) collective-permute-start(f32[512,128]{1,0:T(8,128)S(1)} %slice_add_fusion), channel_id=1, source_target_pairs={{0,2},{1,3},{2,0},{3,1},{4,6},{5,7},{6,4},{7,5},{8,10},{9,11},{10,... | collective-permute-start | bytes 786440 | tf_op jit(solution)/shard_map/ppermute | solution.py:638

commit v15 on v11

--- a/solution.py
+++ b/solution.py
@@ -48,10 +48,10 @@
     return pltpu.roll(value, by % value.shape[axis], axis)
 
 
-def prep_kernel(table, pos, phi, src, mat, temp, slab, body, ready, sigma, inner, outer, src_v, mat_v, ends_t, ends_m, sems):
+def prep_kernel(table, pos, phi, src, mat, temp, slab, ready, sigma, inner, outer, phi_v, src_v, mat_v, ends_t, ends_m, sems):
     rows = TE * ROW
     size_x, width = temp.shape
-    moves = [(phi, body.at[0:rows]), (src, src_v), (mat, mat_v)]
+    moves = [(phi, phi_v), (src, src_v), (mat, mat_v)]
     for which, first in enumerate((0, size_x - SUB)):
         moves.append((temp.at[first : first + SUB], ends_t.at[which]))
         moves.append((slab.at[first : first + SUB], ends_m.at[which]))
@@ -60,32 +60,33 @@
         move.start()
     for move in moves:
         move.wait()
-    sigma[...] = lookup(table, mat_v[...])
-    body[rows : 2 * rows] = src_v[...] / sigma[...]
     first = (lax.axis_index("gx") * lax.axis_size("gy") + lax.axis_index("gy")) * TILES
-    for t in range(TILES):
-
-        @pl.when(pos[2, first + t] == 1)
-        def _():
-            def plane(p, carry):
-                for ref, start in ((body, 0), (body, rows), (sigma, 0)):
-                    at = pl.ds(pl.multiple_of(p * ROW, ROW) + (start + t), SUB, stride=TILES)
-                    ref[at, :] = roll(ref[at, :], TE, 1)
-                return carry
-
-            lax.fori_loop(0, TE, plane, 0, unroll=8)
-
-    ready[...] = body[0 : 2 * rows]
-    body[2 * rows : 3 * rows] = sigma[...]
+    upper = [pos[2, first + t] == 1 for t in range(TILES)]
+
+    def plane(p, carry):
+        values = []
+        for t in range(TILES):
+            row = pl.multiple_of(p * ROW, ROW) + t
+            at = pl.ds(row, SUB, stride=TILES)
+            conduct = lookup(table, mat_v[at, :])
+            three = (phi_v[at, :], src_v[at, :] / conduct, conduct)
+            values.append((row, [jnp.where(upper[t], roll(v, TE, 1), v) for v in three]))
+        for row, (potential, s, conduct) in values:
+            ready[pl.ds(row, SUB, stride=TILES), :] = potential
+            ready[pl.ds(row + rows, SUB, stride=TILES), :] = s
+            sigma[pl.ds(row, SUB, stride=TILES), :] = conduct
+        return carry
+
+    lax.fori_loop(0, TE, plane, 0, unroll=8)
     even = lax.rem(lax.axis_index("gx"), 2) == 0
 
     @pl.when(even)
     def _():
-        fill_sides(body, sigma, ends_t, ends_m, inner, outer)
+        fill_sides(ready, sigma, ends_t, ends_m, inner, outer)
 
     @pl.when(jnp.logical_not(even))
     def _():
-        fill_sides(body, sigma, ends_t, ends_m, outer, inner)
+        fill_sides(ready, sigma, ends_t, ends_m, outer, inner)
 
 
 def fill_sides(body, sigma, ends_t, ends_m, up, down):
@@ -342,7 +343,7 @@
             relax(u_src, u_dst, at, 0, HIGH[0] - 1 - k, s_u, row_of(slot, HIGH[1]), plane_at(c_src, at[5]), None)
             return carry
 
-        lax.fori_loop(0, tiles, sweep_tile, 0, unroll=2)
+        lax.fori_loop(0, tiles, sweep_tile, 0, unroll=4)
 
     field, f_l, f_u = bufs[SWEEPS % 2]
     for t in range(TILES):
@@ -401,9 +402,7 @@
     heat, q_ext, state_a, state_b, k0_all, b_all, blocks, sigmas, sems = refs[2 * width_gy + 8 + chips :]
     moves = []
     for part in range(width_gy):
-        start = 2 * TE * ROW if part % chips == 0 else 0
-        source = refs[part].at[start : start + TE * ROW]
-        moves.append(pltpu.make_async_copy(source, sigmas.at[part], sems.at[part]))
+        moves.append(pltpu.make_async_copy(refs[part], sigmas.at[part], sems.at[part]))
         moves[-1].start()
     i = lax.axis_index("gx")
     j = lax.axis_index("gy")
@@ -565,7 +564,7 @@
             return ahead, flux_y
 
         first, second = load(src, 0), load(src, 1)
-        lax.fori_loop(1, YBLOCKS - 1, advance, (second, y_fluxes(0, first, second)), unroll=6)
+        lax.fori_loop(1, YBLOCKS - 1, advance, (second, y_fluxes(0, first, second)), unroll=9)
     final = state_b if CSWEEPS % 2 else state_a
 
     def give_out(yq, carry):
@@ -670,18 +669,18 @@
     def rows(count):
         return jax.ShapeDtypeStruct((count, LANES), f32)
 
-    body, ready, sigma, inner, outer = pl.pallas_call(
+    ready, sigma, inner, outer = pl.pallas_call(
         prep_kernel,
         out_shape=(
-            rows(3 * TE * ROW),
             rows(2 * TE * ROW),
             rows(TE * ROW),
             rows(SIDE_ROWS + edge_rows),
             rows(SIDE_ROWS + edge_rows),
         ),
         in_specs=[SMEM] * 2 + [HBM] * 5,
-        out_specs=(VMEM,) * 5,
+        out_specs=(VMEM,) * 4,
         scratch_shapes=[
+            pltpu.VMEM((TE * ROW, LANES), f32),
             pltpu.VMEM((TE * ROW, LANES), f32),
             pltpu.VMEM((TE * ROW, LANES), jnp.int32),
             pltpu.VMEM((2, SUB, width), f32),
@@ -691,7 +690,7 @@
         compiler_params=pltpu.CompilerParams(vmem_limit_bytes=62 * 1024 * 1024),
         name="prep",
     )(sigma_table, pos, to_rows(phi_init), to_rows(source), to_rows(tile_mat), temp_init, slab_mat)
-    bodies = [body] + [shifted(ready, "gy", 2 * d, True) for d in range(1, chips)]
+    bodies = [ready] + [shifted(ready, "gy", 2 * d, True) for d in range(1, chips)]
     bodies += [from_mate(part) for part in bodies]
     inner, outer = with_partner(inner, "gx", 0), with_partner(outer, "gx", 1)
 
@@ -704,8 +703,8 @@
         name="relay",
     )(inner, outer)
     halos = [halo] + [shifted(halo, "gy", 2 * d, True) for d in range(1, chips)]
-    sigmas = [bodies[0]] + [shifted(sigma, "gy", 2 * d, True) for d in range(1, chips)]
-    sigmas += [bodies[chips]] + [to_other_core(sigma, d) for d in range(1, chips)]
+    sigmas = [sigma] + [shifted(sigma, "gy", 2 * d, True) for d in range(1, chips)]
+    sigmas += [from_mate(sigma)] + [to_other_core(sigma, d) for d in range(1, chips)]
 
     native = pltpu.VMEM((width // LANES * SLABX + SUB, LANES), f32)
     t_ext, k0_ext, b_ext, edge_in, edge_out = pl.pallas_call(

time: 65.8 us -> 64.8 us (0.985)
  Pallas kernels: 26.2 us -> 24.7 us
    pallas_call x1, Pallas kernels: 4.44 us -> 3.73 us  [on_device(): pl.pallas_call(prep_kernel, out_shape=(rows(2 * TE * ROW), rows(TE * ROW)...]
    ppermute x4, starting transfers between devices: 5.14 us -> 5.81 us  [shifted(): return lax.ppermute(value, axis, pairs)]
    ppermute x5 -> x6, starting transfers between devices: 3.24 us -> 3.19 us  [from_mate(): lax.ppermute(value, 'gy', [(d, d ^ 1) for d in range(lax.axis_size('gy'))])]
    ppermute x5 -> x6, waiting for transfers between devices: 1.55 us -> 1.55 us  [from_mate(): lax.ppermute(value, 'gy', [(d, d ^ 1) for d in range(lax.axis_size('gy'))])]
  transfers between devices with their start and end apart: 14 -> 15, of which waited for: 6 -> 6; matrix products, arithmetic and copies ran while one was open for 0% -> 0% of each run, Pallas kernels for 20% -> 19%
where the time goes in v15:
time: 64.8 us; the launch traced here: 64.6 us
  waiting for transfers between devices  25.5 us (39%)
  Pallas kernels  24.7 us (38%)
  starting transfers between devices  12.8 us (20%)
  between operations  0.82 us (1%)
  other arithmetic  0.79 us (1%)
    ppermute x4, waiting for transfers between devices, shifted(): return lax.ppermute(value, axis, pairs)  21.7 us
    pallas_call x1, Pallas kernels, on_device(): pl.pallas_call(functools.partial(sweep_kernel, chips), out_shape=(rows(TE...  11.3 us
    pallas_call x1, Pallas kernels, on_device(): pl.pallas_call(functools.partial(slab_steps_kernel, chips), out_shape=(ja...  8.61 us
    ppermute x4, starting transfers between devices, shifted(): return lax.ppermute(value, axis, pairs)  5.81 us
    pallas_call x1, Pallas kernels, on_device(): pl.pallas_call(prep_kernel, out_shape=(rows(2 * TE * ROW), rows(TE * ROW)...  3.73 us
    ppermute x4, starting transfers between devices, with_partner(): lax.ppermute(value, axis, pairs + [(high, low) for low, high in pairs])  3.2 us
    ppermute x6, starting transfers between devices, from_mate(): lax.ppermute(value, 'gy', [(d, d ^ 1) for d in range(lax.axis_size('gy'))])  3.19 us
    ppermute x4, waiting for transfers between devices, with_partner(): lax.ppermute(value, axis, pairs + [(high, low) for low, high in pairs])  2.16 us
  transfers between devices with their start and end apart: 15, of which 6 were waited for; matrix products, arithmetic and copies ran while one was open for 0% of the time, Pallas kernels for 19%

profile of v15, /device:TPU:0, one launch (start us, length us, event | category | flops | bytes accessed | tf_op | source)
XLA Modules:
  0.0 64.6 jit_solution(1428677223061290416)
XLA Ops:
  0.7 3.7 %prep.1 = (f32[1024,128]{1,0:T(8,128)}, f32[512,128]{1,0:T(8,128)}, f32[496,128]{1,0:T(8,128)}, f32[496,128]{1,0:T(8,128)}) custom-call(f32[4]{0:T(128)} %table.1, s32[3,64]{1,0:T(4,128)} %bitcast.26, f32[512,128]{1,0:T(8,128)} %bitcast.30, f32[512,128]{1,0:T(8,128)} %bitcast.31, s32[512,128]{1,0:T(8,128)} %bitcast.32, f32[32,4096]{1,0:T(8,128)} %temp.3, ...), custom_call_target="tpu_custom_call" | custom-call | tf_op jit(solution)/shard_map/prep/pallas_call | solution.py:672
  4.4 0.0 copy-start.3
  4.4 0.0 copy-start.2
  4.5 3.0 %collective-permute-start = (f32[1024,128]{1,0:T(8,128)}, f32[1024,128]{1,0:T(8,128)S(1)}, u32[]{:S(2)}, u32[]{:S(2)}) collective-permute-start(f32[1024,128]{1,0:T(8,128)} %get-tuple-element.20.refs_0_), channel_id=1, source_target_pairs={{0,2},{1,3},{2,0},{3,1},{4,6},{5,7},{6,4},{7,5},{8,10},{9,11},{10,... | collective-permute-start | bytes 1572872 | tf_op jit(solution)/shard_map/ppermute | solution.py:616
  7.5 0.0 collective-permute-start.1
  7.5 1.5 %collective-permute-start.3 = (f32[496,128]{1,0:T(8,128)}, f32[496,128]{1,0:T(8,128)S(1)}, u32[]{:S(2)}, u32[]{:S(2)}) collective-permute-start(f32[496,128]{1,0:T(8,128)} %get-tuple-element.21), channel_id=1, source_target_pairs={{0,4},{8,12},{16,20},{24,28},{4,0},{12,8},{20,16},{28,24},{1,5},{9... | collective-permute-start | bytes 761864 | tf_op jit(solution)/shard_map/ppermute | solution.py:622
  9.0 0.7 %collective-permute-start.4 = (f32[496,128]{1,0:T(8,128)}, f32[496,128]{1,0:T(8,128)S(1)}, u32[]{:S(2)}, u32[]{:S(2)}) collective-permute-start(f32[496,128]{1,0:T(8,128)} %get-tuple-element.22), channel_id=1, source_target_pairs={{4,8},{12,16},{20,24},{8,4},{16,12},{24,20},{5,9},{13,17},{21,25},... | collective-permute-start | bytes 761864 | tf_op jit(solution)/shard_map/ppermute | solution.py:622
  9.6 9.9 %collective-permute-done.refs_1_ = f32[1024,128]{1,0:T(8,128)S(1)} collective-permute-done((f32[1024,128]{1,0:T(8,128)}, f32[1024,128]{1,0:T(8,128)S(1)}, u32[]{:S(2)}, u32[]{:S(2)}) %collective-permute-start) | collective-permute-done | bytes 524320 | tf_op jit(solution)/shard_map/ppermute | solution.py:616
  19.6 0.0 collective-permute-start.2
  19.6 1.2 %collective-permute-done.3.inner = f32[496,128]{1,0:T(8,128)S(1)} collective-permute-done((f32[496,128]{1,0:T(8,128)}, f32[496,128]{1,0:T(8,128)S(1)}, u32[]{:S(2)}, u32[]{:S(2)}) %collective-permute-start.3) | collective-permute-done | bytes 253984 | tf_op jit(solution)/shard_map/ppermute | solution.py:622
  20.8 0.0 collective-permute-done.4.outer
  20.8 0.6 collective-permute-start.5
  21.4 0.2 collective-permute-start.7
  21.7 1.1 %slab_prep.1 = (f32[1552,128]{1,0:T(8,128)S(1)}, f32[1552,128]{1,0:T(8,128)S(1)}, f32[1552,128]{1,0:T(8,128)S(1)}, f32[120,128]{1,0:T(8,128)S(1)}, f32[120,128]{1,0:T(8,128)S(1)}) custom-call(s32[3,64]{1,0:T(4,128)S(1)} %bitcast.27, f32[4]{0:T(128)S(1)} %copy-done.5, f32[4]{0:T(128)S(1)} %copy-done.6, f32[32,4096]{1,0:T(8,128)S(1)} %copy-done, ...), custom_call_target="tpu_custom_call" | custom-call | tf_op jit(solution)/shard_map/slab_prep/pallas_call | solution.py:710
  22.8 0.4 collective-permute-start.6
  23.2 0.9 %collective-permute-done.6.refs_12_ = f32[120,128]{1,0:T(8,128)S(1)} collective-permute-done((f32[120,128]{1,0:T(8,128)S(1)}, f32[120,128]{1,0:T(8,128)S(1)}, u32[]{:S(2)}, u32[]{:S(2)}) %collective-permute-start.6) | collective-permute-done | bytes 61472 | tf_op jit(solution)/shard_map/ppermute | solution.py:622
  24.1 4.0 %collective-permute-done.5.refs_5_ = f32[448,128]{1,0:T(8,128)S(1)} collective-permute-done((f32[448,128]{1,0:T(8,128)S(1)}, f32[448,128]{1,0:T(8,128)S(1)}, u32[]{:S(2)}, u32[]{:S(2)}) %collective-permute-start.5) | collective-permute-done | bytes 229408 | tf_op jit(solution)/shard_map/ppermute | solution.py:616
  28.1 0.0 collective-permute-start.8
  28.1 1.3 %collective-permute-start.9 = (f32[512,128]{1,0:T(8,128)S(1)}, f32[512,128]{1,0:T(8,128)S(1)}, u32[]{:S(2)}, u32[]{:S(2)}) collective-permute-start(f32[512,128]{1,0:T(8,128)S(1)} %copy-done.3), channel_id=1, source_target_pairs={{0,2},{1,3},{2,0},{3,1},{4,6},{5,7},{6,4},{7,5},{8,10},{9,11},{10,... | collective-permute-start | bytes 786440 | tf_op jit(solution)/shard_map/ppermute | solution.py:616
  29.5 0.2 collective-permute-start.10
  29.7 0.0 collective-permute-done.1.refs_2_
  29.7 0.6 collective-permute-start.11
  30.3 0.7 %collective-permute-start.12 = (f32[120,128]{1,0:T(8,128)S(1)}, f32[120,128]{1,0:T(8,128)S(1)}, u32[]{:S(2)}, u32[]{:S(2)}) collective-permute-start(f32[120,128]{1,0:T(8,128)S(1)} %get-tuple-element.32), channel_id=1, source_target_pairs={{1,2},{2,1},{5,6},{6,5},{9,10},{10,9},{13,14},{14,13},{17,18},{18,... | collective-permute-start | bytes 184328 | tf_op jit(solution)/shard_map/ppermute | solution.py:622
  31.0 11.3 %sweeps.1 = (f32[512,128]{1,0:T(8,128)}, f32[2880,128]{1,0:T(8,128)S(1)}) custom-call(s32[3,64]{1,0:T(4,128)S(1)} %bitcast.28, f32[1024,128]{1,0:T(8,128)S(1)} %copy-done.2, f32[1024,128]{1,0:T(8,128)S(1)} %collective-permute-done.refs_1_, f32[1024,128]{1,0:T(8,128)S(1)} %collective-permute-done.1.refs_2_, f32[1024,128]{1,0:T(8,128)S(1)} %collective-permute-done.2.refs_3_, ...), custom_call_target="tpu_custom_call" | custom-call | tf_op jit(solution)/shard_map/sweeps/pallas_call | solution.py:726
  42.2 0.0 collective-permute-done.10.refs_2_
  42.3 0.0 collective-permute-done.11.refs_3_
  42.3 8.6 %slab_steps.1 = (f32[32,4096]{1,0:T(8,128)}, f32[512,128]{1,0:T(8,128)S(1)}, f32[1024,128]{1,0:T(8,128)S(1)}, f32[512,128]{1,0:T(8,128)S(1)}) custom-call(s32[3,64]{1,0:T(4,128)S(1)} %bitcast.29, f32[4]{0:T(128)S(1)} %copy-done.5, f32[4]{0:T(128)S(1)} %copy-done.6, f32[512,128]{1,0:T(8,128)S(1)} %copy-done.3, f32[512,128]{1,0:T(8,128)S(1)} %collective-permute-done.9.refs_1_, ...), custom_call_target="tpu_custom_call" | custom-call | tf_op jit(solution)/shard_map/slab_steps/pallas_call | solution.py:743
  50.9 2.7 %collective-permute-start.13 = (f32[1024,128]{1,0:T(8,128)S(1)}, f32[1024,128]{1,0:T(8,128)S(1)}, u32[]{:S(2)}, u32[]{:S(2)}) collective-permute-start(f32[1024,128]{1,0:T(8,128)S(1)} %get-tuple-element.35), channel_id=1, source_target_pairs={{0,1},{1,0},{2,3},{3,2},{4,5},{5,4},{6,7},{7,6},{8,9},{9,8},{10,11... | collective-permute-start | bytes 1572872 | tf_op jit(solution)/shard_map/ppermute | solution.py:626
  53.6 1.5 %collective-permute-done.13 = f32[1024,128]{1,0:T(8,128)S(1)} collective-permute-done((f32[1024,128]{1,0:T(8,128)S(1)}, f32[1024,128]{1,0:T(8,128)S(1)}, u32[]{:S(2)}, u32[]{:S(2)}) %collective-permute-start.13) | collective-permute-done | bytes 524320 | tf_op jit(solution)/shard_map/ppermute | solution.py:626
  55.2 0.9 %collective-permute-start.14 = (f32[512,128]{1,0:T(8,128)S(1)}, f32[512,128]{1,0:T(8,128)S(1)}, u32[]{:S(2)}, u32[]{:S(2)}) collective-permute-start(f32[512,128]{1,0:T(8,128)S(1)} %slice_add_fusion), channel_id=1, source_target_pairs={{0,2},{1,3},{2,0},{3,1},{4,6},{5,7},{6,4},{7,5},{8,10},{9,11},{10,... | collective-permute-start | bytes 786440 | tf_op jit(solution)/shard_map/ppermute | solution.py:616
  56.1 7.8 %collective-permute-done.14 = f32[512,128]{1,0:T(8,128)S(1)} collective-permute-done((f32[512,128]{1,0:T(8,128)S(1)}, f32[512,128]{1,0:T(8,128)S(1)}, u32[]{:S(2)}, u32[]{:S(2)}) %collective-permute-start.14) | collective-permute-done | bytes 262176 | tf_op jit(solution)/shard_map/ppermute | solution.py:616
  63.9 0.8 %fusion = f32[512,128]{1,0:T(8,128)} fusion(f32[512,128]{1,0:T(8,128)S(1)} %collective-permute-done.14, f32[512,128]{1,0:T(8,128)S(1)} %get-tuple-element.34, f32[1024,128]{1,0:T(8,128)S(1)} %collective-permute-done.13), kind=kLoop, calls=%fused_computation.2 | loop fusion | flops 131072 | bytes 1048576 | tf_op jit(solution)/shard_map/add | solution.py:761
  (19 shorter events, 0.1 us)
Async XLA Ops:
  0.6 21.0 %copy-start.4 = (s32[64,3]{0,1:T(4,128)S(1)}, s32[64,3]{0,1:T(4,128)}, u32[]{:S(2)}) copy-start(s32[64,3]{0,1:T(4,128)} %param.13) | copy-start | bytes 2308
  0.6 21.0 %copy-start = (f32[32,4096]{1,0:T(8,128)S(1)}, f32[32,4096]{1,0:T(8,128)}, u32[]{:S(2)}) copy-start(f32[32,4096]{1,0:T(8,128)} %temp.3) | copy-start | bytes 1572868
  0.7 21.0 %copy-start.1 = (s32[32,4096]{1,0:T(8,128)S(1)}, s32[32,4096]{1,0:T(8,128)}, u32[]{:S(2)}) copy-start(s32[32,4096]{1,0:T(8,128)} %mat.1) | copy-start | bytes 1572868
  0.7 21.0 %copy-start.5 = (f32[4]{0:T(128)S(1)}, f32[4]{0:T(128)}, u32[]{:S(2)}) copy-start(f32[4]{0:T(128)} %k0_table.3) | copy-start | bytes 52
  0.7 21.0 %copy-start.6 = (f32[4]{0:T(128)S(1)}, f32[4]{0:T(128)}, u32[]{:S(2)}) copy-start(f32[4]{0:T(128)} %beta_table.3) | copy-start | bytes 52
  4.4 23.7 %copy-start.3 = (f32[512,128]{1,0:T(8,128)S(1)}, f32[512,128]{1,0:T(8,128)}, u32[]{:S(2)}) copy-start(f32[512,128]{1,0:T(8,128)} %get-tuple-element.26.refs_0_) | copy-start | bytes 786436
  4.4 26.5 %copy-start.2 = (f32[1024,128]{1,0:T(8,128)S(1)}, f32[1024,128]{1,0:T(8,128)}, u32[]{:S(2)}) copy-start(f32[1024,128]{1,0:T(8,128)} %get-tuple-element.20.refs_0_) | copy-start | bytes 1572868
  4.5 15.1 %collective-permute-start = (f32[1024,128]{1,0:T(8,128)}, f32[1024,128]{1,0:T(8,128)S(1)}, u32[]{:S(2)}, u32[]{:S(2)}) collective-permute-start(f32[1024,128]{1,0:T(8,128)} %get-tuple-element.20.refs_0_), channel_id=1, source_target_pairs={{0,2},{1,3},{2,0},{3,1},{4,6},{5,7},{6,4},{7,5},{8,10},{9,11},{10,... | collective-permute-start | bytes 1572872 | tf_op jit(solution)/shard_map/ppermute | solution.py:616
  7.5 22.2 %collective-permute-start.1 = (f32[1024,128]{1,0:T(8,128)}, f32[1024,128]{1,0:T(8,128)S(1)}, u32[]{:S(2)}, u32[]{:S(2)}) collective-permute-start(f32[1024,128]{1,0:T(8,128)} %get-tuple-element.20.refs_0_), channel_id=1, source_target_pairs={{0,1},{1,0},{2,3},{3,2},{4,5},{5,4},{6,7},{7,6},{8,9},{9,8},{10,11... | collective-permute-start | bytes 1572872 | tf_op jit(solution)/shard_map/ppermute | solution.py:626
  7.5 13.3 %collective-permute-start.3 = (f32[496,128]{1,0:T(8,128)}, f32[496,128]{1,0:T(8,128)S(1)}, u32[]{:S(2)}, u32[]{:S(2)}) collective-permute-start(f32[496,128]{1,0:T(8,128)} %get-tuple-element.21), channel_id=1, source_target_pairs={{0,4},{8,12},{16,20},{24,28},{4,0},{12,8},{20,16},{28,24},{1,5},{9... | collective-permute-start | bytes 761864 | tf_op jit(solution)/shard_map/ppermute | solution.py:622
  9.0 11.8 %collective-permute-start.4 = (f32[496,128]{1,0:T(8,128)}, f32[496,128]{1,0:T(8,128)S(1)}, u32[]{:S(2)}, u32[]{:S(2)}) collective-permute-start(f32[496,128]{1,0:T(8,128)} %get-tuple-element.22), channel_id=1, source_target_pairs={{4,8},{12,16},{20,24},{8,4},{16,12},{24,20},{5,9},{13,17},{21,25},... | collective-permute-start | bytes 761864 | tf_op jit(solution)/shard_map/ppermute | solution.py:622
  19.6 11.4 %collective-permute-start.2 = (f32[1024,128]{1,0:T(8,128)S(1)}, f32[1024,128]{1,0:T(8,128)S(1)}, u32[]{:S(2)}, u32[]{:S(2)}) collective-permute-start(f32[1024,128]{1,0:T(8,128)S(1)} %collective-permute-done.refs_1_), channel_id=1, source_target_pairs={{0,1},{1,0},{2,3},{3,2},{4,5},{5,4},{6,7},{7,6},{8,9},{9,8},{10,11... | collective-permute-start | bytes 1572872 | tf_op jit(solution)/shard_map/ppermute | solution.py:626
  20.8 7.3 %collective-permute-start.5 = (f32[448,128]{1,0:T(8,128)S(1)}, f32[448,128]{1,0:T(8,128)S(1)}, u32[]{:S(2)}, u32[]{:S(2)}) collective-permute-start(f32[448,128]{1,0:T(8,128)S(1)} %relay.1.refs_4_), channel_id=1, source_target_pairs={{0,2},{1,3},{2,0},{3,1},{4,6},{5,7},{6,4},{7,5},{8,10},{9,11},{10,... | collective-permute-start | bytes 688136 | tf_op jit(solution)/shard_map/ppermute | solution.py:616
  21.4 8.0 %collective-permute-start.7 = (f32[448,128]{1,0:T(8,128)S(1)}, f32[448,128]{1,0:T(8,128)S(1)}, u32[]{:S(2)}, u32[]{:S(2)}) collective-permute-start(f32[448,128]{1,0:T(8,128)S(1)} %relay.1.refs_4_), channel_id=1, source_target_pairs={{0,1},{1,0},{2,3},{3,2},{4,5},{5,4},{6,7},{7,6},{8,9},{9,8},{10,11... | collective-permute-start | bytes 688136 | tf_op jit(solution)/shard_map/ppermute | solution.py:626
  22.8 1.3 %collective-permute-start.6 = (f32[120,128]{1,0:T(8,128)S(1)}, f32[120,128]{1,0:T(8,128)S(1)}, u32[]{:S(2)}, u32[]{:S(2)}) collective-permute-start(f32[120,128]{1,0:T(8,128)S(1)} %get-tuple-element.23), channel_id=1, source_target_pairs={{0,1},{2,3},{1,0},{3,2},{4,5},{6,7},{5,4},{7,6},{8,9},{10,11},{9,8... | collective-permute-start | bytes 184328 | tf_op jit(solution)/shard_map/ppermute | solution.py:622
  28.1 2.2 %collective-permute-start.8 = (f32[448,128]{1,0:T(8,128)S(1)}, f32[448,128]{1,0:T(8,128)S(1)}, u32[]{:S(2)}, u32[]{:S(2)}) collective-permute-start(f32[448,128]{1,0:T(8,128)S(1)} %collective-permute-done.5.refs_5_), channel_id=1, source_target_pairs={{0,1},{1,0},{2,3},{3,2},{4,5},{5,4},{6,7},{7,6},{8,9},{9,8},{10,11... | collective-permute-start | bytes 688136 | tf_op jit(solution)/shard_map/ppermute | solution.py:626
  28.1 14.1 %collective-permute-start.9 = (f32[512,128]{1,0:T(8,128)S(1)}, f32[512,128]{1,0:T(8,128)S(1)}, u32[]{:S(2)}, u32[]{:S(2)}) collective-permute-start(f32[512,128]{1,0:T(8,128)S(1)} %copy-done.3), channel_id=1, source_target_pairs={{0,2},{1,3},{2,0},{3,1},{4,6},{5,7},{6,4},{7,5},{8,10},{9,11},{10,... | collective-permute-start | bytes 786440 | tf_op jit(solution)/shard_map/ppermute | solution.py:616
  29.5 12.8 %collective-permute-start.10 = (f32[512,128]{1,0:T(8,128)S(1)}, f32[512,128]{1,0:T(8,128)S(1)}, u32[]{:S(2)}, u32[]{:S(2)}) collective-permute-start(f32[512,128]{1,0:T(8,128)S(1)} %copy-done.3), channel_id=1, source_target_pairs={{0,1},{1,0},{2,3},{3,2},{4,5},{5,4},{6,7},{7,6},{8,9},{9,8},{10,11... | collective-permute-start | bytes 786440 | tf_op jit(solution)/shard_map/ppermute | solution.py:626
  29.7 12.6 %collective-permute-start.11 = (f32[512,128]{1,0:T(8,128)S(1)}, f32[512,128]{1,0:T(8,128)S(1)}, u32[]{:S(2)}, u32[]{:S(2)}) collective-permute-start(f32[512,128]{1,0:T(8,128)S(1)} %copy-done.3), channel_id=1, source_target_pairs={{0,3},{1,2},{2,1},{3,0},{4,7},{5,6},{6,5},{7,4},{8,11},{9,10},{10,... | collective-permute-start | bytes 786440 | tf_op jit(solution)/shard_map/ppermute | solution.py:639
  30.3 12.0 %collective-permute-start.12 = (f32[120,128]{1,0:T(8,128)S(1)}, f32[120,128]{1,0:T(8,128)S(1)}, u32[]{:S(2)}, u32[]{:S(2)}) collective-permute-start(f32[120,128]{1,0:T(8,128)S(1)} %get-tuple-element.32), channel_id=1, source_target_pairs={{1,2},{2,1},{5,6},{6,5},{9,10},{10,9},{13,14},{14,13},{17,18},{18,... | collective-permute-start | bytes 184328 | tf_op jit(solution)/shard_map/ppermute | solution.py:622
  50.9 4.3 %collective-permute-start.13 = (f32[1024,128]{1,0:T(8,128)S(1)}, f32[1024,128]{1,0:T(8,128)S(1)}, u32[]{:S(2)}, u32[]{:S(2)}) collective-permute-start(f32[1024,128]{1,0:T(8,128)S(1)} %get-tuple-element.35), channel_id=1, source_target_pairs={{0,1},{1,0},{2,3},{3,2},{4,5},{5,4},{6,7},{7,6},{8,9},{9,8},{10,11... | collective-permute-start | bytes 1572872 | tf_op jit(solution)/shard_map/ppermute | solution.py:626
  55.2 8.7 %collective-permute-start.14 = (f32[512,128]{1,0:T(8,128)S(1)}, f32[512,128]{1,0:T(8,128)S(1)}, u32[]{:S(2)}, u32[]{:S(2)}) collective-permute-start(f32[512,128]{1,0:T(8,128)S(1)} %slice_add_fusion), channel_id=1, source_target_pairs={{0,2},{1,3},{2,0},{3,1},{4,6},{5,7},{6,4},{7,5},{8,10},{9,11},{10,... | collective-permute-start | bytes 786440 | tf_op jit(solution)/shard_map/ppermute | solution.py:616

commit v16 on v15

--- a/solution.py
+++ b/solution.py
@@ -125,7 +125,7 @@
     return jnp.minimum(pos[0, 0], 0)
 
 
-def slab_kernel(pos, k0_table, beta_table, temp, mat, inner, outer, t_ext, k0_ext, b_ext, edge_in, edge_out, native_t, native_m, edge_low, edge_high):
+def slab_kernel(pos, k0_table, beta_table, temp, mat, inner, outer, sigma, t_ext, k0_ext, b_ext, edge_in, packet, native_t, native_m, edge_low, edge_high):
     start = loose(pos)
     even = lax.rem(lax.axis_index("gx"), 2) == 0
     blocks = temp.shape[1] // LANES
@@ -172,7 +172,8 @@
                     edge_high[first : first + SUB] = jnp.where(half, halves[0][2 + odd], halves[1][3 - odd])
     even = lax.rem(lax.axis_index("gy"), 2) == 0
     edge_in[...] = jnp.where(even, edge_high[...], edge_low[...])
-    edge_out[...] = jnp.where(even, edge_low[...], edge_high[...])
+    packet[0 : TE * ROW] = sigma[...]
+    packet[TE * ROW :] = jnp.where(even, edge_low[...], edge_high[...])
 
 
 def fill_maps(chips, pos, cell_at, cell_of):
@@ -396,14 +397,19 @@
     width_gy = 2 * chips
     tiles = width_gy * TILES
     halos = refs[width_gy : 2 * width_gy]
-    slope, t_in, k0_in, b_in, y_in, y_out, temp_out = refs[2 * width_gy : 2 * width_gy + 7]
-    mine, bundle = refs[2 * width_gy + 7 : 2 * width_gy + 9]
-    across = refs[2 * width_gy + 9 : 2 * width_gy + 8 + chips]
-    heat, q_ext, state_a, state_b, k0_all, b_all, blocks, sigmas, sems = refs[2 * width_gy + 8 + chips :]
+    slope, t_in, k0_in, b_in, y_in, temp_out = refs[2 * width_gy : 2 * width_gy + 6]
+    mine, bundle = refs[2 * width_gy + 6 : 2 * width_gy + 8]
+    across = refs[2 * width_gy + 8 : 2 * width_gy + 7 + chips]
+    heat, q_ext, state_a, state_b, k0_all, b_all, blocks, sigmas, y_out, sems = refs[2 * width_gy + 7 + chips :]
     moves = []
     for part in range(width_gy):
-        moves.append(pltpu.make_async_copy(refs[part], sigmas.at[part], sems.at[part]))
+        moves.append(pltpu.make_async_copy(refs[part].at[0 : TE * ROW], sigmas.at[part], sems.at[part]))
         moves[-1].start()
+    edges = []
+    for which, d in enumerate((1, chips - 1)):
+        source = refs[chips + d].at[TE * ROW : TE * ROW + HALO * SLABX]
+        edges.append(pltpu.make_async_copy(source, y_out.at[which], sems.at[width_gy + which]))
+        edges[-1].start()
     i = lax.axis_index("gx")
     j = lax.axis_index("gy")
     rows_gx = lax.axis_size("gx")
@@ -463,7 +469,8 @@
             temp, k0, beta = t_in[rows], k0_in[rows], b_in[rows]
             if low is not None:
                 place = slice(at * SLABX + g * SUB, at * SLABX + (g + 1) * SUB)
-                value = jnp.where(even, *((y_out[place], y_in[place])[:: 1 if low else -1]))
+                other = jnp.where(even, y_out[0, place], y_out[1, place])
+                value = jnp.where(even, *((other, y_in[place])[:: 1 if low else -1]))
                 swapped = roll(value, NZ, 1)
                 if low:
                     temp = jnp.where(half, value, temp)
@@ -478,15 +485,16 @@
             k0_all[rows], b_all[rows] = k0, beta
             store(state_a, block, g, temp, cond)
 
+    def begin_inner(block, carry):
+        begin(block, None, 0)
+        return carry
+
+    lax.fori_loop(HALO, YBLOCKS - HALO, begin_inner, 0, unroll=4)
+    for move in edges:
+        move.wait()
     for e in range(HALO):
         begin(e, True, e)
         begin(YBLOCKS - HALO + e, False, e)
-
-    def begin_inner(block, carry):
-        begin(block, None, 0)
-        return carry
-
-    lax.fori_loop(HALO, YBLOCKS - HALO, begin_inner, 0, unroll=4)
 
     def clear(at, carry):
         heat[pl.ds(pl.multiple_of(at * SUB, SUB), SUB), :] = zero
@@ -703,20 +711,21 @@
         name="relay",
     )(inner, outer)
     halos = [halo] + [shifted(halo, "gy", 2 * d, True) for d in range(1, chips)]
-    sigmas = [sigma] + [shifted(sigma, "gy", 2 * d, True) for d in range(1, chips)]
-    sigmas += [from_mate(sigma)] + [to_other_core(sigma, d) for d in range(1, chips)]
-
     native = pltpu.VMEM((width // LANES * SLABX + SUB, LANES), f32)
-    t_ext, k0_ext, b_ext, edge_in, edge_out = pl.pallas_call(
+    t_ext, k0_ext, b_ext, edge_in, packet = pl.pallas_call(
         slab_kernel,
-        out_shape=(rows(SLAB_ROWS),) * 3 + (rows(HALO * SLABX),) * 2,
-        in_specs=[SMEM] * 3 + [VMEM] * 4,
+        out_shape=(rows(SLAB_ROWS),) * 3 + (rows(HALO * SLABX), rows(TE * ROW + HALO * SLABX)),
+        in_specs=[SMEM] * 3 + [VMEM] * 5,
         out_specs=(VMEM,) * 5,
         scratch_shapes=[native, native] + [pltpu.VMEM((HALO * SLABX, LANES), f32)] * 2,
         compiler_params=PARAMS,
         name="slab_prep",
-    )(pos, k0_table, beta_table, temp_init, slab_mat, inner, outer)
-    y_in, y_out = with_partner(edge_in, "gy", 0), with_partner(edge_out, "gy", 1)
+    )(pos, k0_table, beta_table, temp_init, slab_mat, inner, outer, sigma)
+    y_in = with_partner(edge_in, "gy", 0)
+    sigmas = [sigma] + [shifted(sigma, "gy", 2 * d, True) for d in range(1, chips)]
+    sigmas += [from_mate(sigma)] + [
+        to_other_core(packet if d in (1, chips - 1) else sigma, d) for d in range(1, chips)
+    ]
     *halos[1:], y_in = lax.optimization_barrier((*halos[1:], y_in))
     halos = halos + [from_mate(part) for part in halos]
 
@@ -744,17 +753,17 @@
         functools.partial(slab_steps_kernel, chips),
         out_shape=(jax.ShapeDtypeStruct((size_x, width), f32), rows(TE * ROW), rows(chips * TE * ROW))
         + (rows(TE * ROW),) * (chips - 1),
-        in_specs=[SMEM] * 3 + [ANY] * width_gy + [VMEM] * (width_gy + 6),
+        in_specs=[SMEM] * 3 + [ANY] * width_gy + [VMEM] * (width_gy + 5),
         out_specs=(VMEM,) * (2 + chips),
         scratch_shapes=[pltpu.VMEM((CELLS * SLABX * SUB, LANES), f32)]
         + [pltpu.VMEM((SLAB_ROWS + 3 * SLABX, LANES), f32)]
         + [pltpu.VMEM((2 * SLAB_ROWS, LANES), f32)] * 2
         + [pltpu.VMEM((SLAB_ROWS, LANES), f32)] * 2
         + [pltpu.VMEM((4 * TE * SUB, LANES), f32), pltpu.VMEM((width_gy, TE * ROW, LANES), f32)]
-        + [pltpu.SemaphoreType.DMA((width_gy,))],
+        + [pltpu.VMEM((2, HALO * SLABX, LANES), f32), pltpu.SemaphoreType.DMA((width_gy + 2,))],
         compiler_params=PARAMS,
         name="slab_steps",
-    )(pos, k0_table, beta_table, *sigmas, *halos, slope, t_ext, k0_ext, b_ext, y_in, y_out)
+    )(pos, k0_table, beta_table, *sigmas, *halos, slope, t_ext, k0_ext, b_ext, y_in)
     got = from_mate(bundle).reshape(chips, TE * ROW, LANES)
     tile_temps = mine + got[0]
     for d in range(1, chips):

time: 64.8 us -> 62.9 us (0.971)
  starting transfers between devices: 12.8 us -> 10.4 us
    ppermute x6, starting transfers between devices: 3.19 us -> 0.73 us  [from_mate(): lax.ppermute(value, 'gy', [(d, d ^ 1) for d in range(lax.axis_size('gy'))])]
    ppermute x4, waiting for transfers between devices: 21.7 us -> 20.3 us  [shifted(): return lax.ppermute(value, axis, pairs)]
    ppermute x6, waiting for transfers between devices: 1.55 us -> 2.96 us  [from_mate(): lax.ppermute(value, 'gy', [(d, d ^ 1) for d in range(lax.axis_size('gy'))])]
    ppermute x1, starting transfers between devices: 0.59 us -> 1.37 us  [to_other_core(): lax.ppermute(value, 'gy', [(at, ((at ^ 1) + 2 * by) % count) for at in ra...]
    ppermute x4 -> x3, starting transfers between devices: 3.2 us -> 2.55 us  [with_partner(): lax.ppermute(value, axis, pairs + [(high, low) for low, high in pairs])]
    ppermute x4 -> x3, waiting for transfers between devices: 2.16 us -> 2.15 us  [with_partner(): lax.ppermute(value, axis, pairs + [(high, low) for low, high in pairs])]
  transfers between devices with their start and end apart: 15 -> 14, of which waited for: 6 -> 7; matrix products, arithmetic and copies ran while one was open for 0% -> 0% of each run, Pallas kernels for 19% -> 20%
where the time goes in v16:
time: 62.9 us; the launch traced here: 62.7 us
  waiting for transfers between devices  25.4 us (40%)
  Pallas kernels  25.3 us (40%)
  starting transfers between devices  10.4 us (17%)
  other arithmetic  0.78 us (1%)
  between operations  0.78 us (1%)
    ppermute x4, waiting for transfers between devices, shifted(): return lax.ppermute(value, axis, pairs)  20.3 us
    pallas_call x1, Pallas kernels, on_device(): pl.pallas_call(functools.partial(sweep_kernel, chips), out_shape=(rows(TE...  11.2 us
    pallas_call x1, Pallas kernels, on_device(): pl.pallas_call(functools.partial(slab_steps_kernel, chips), out_shape=(ja...  8.78 us
    ppermute x4, starting transfers between devices, shifted(): return lax.ppermute(value, axis, pairs)  5.73 us
    pallas_call x1, Pallas kernels, on_device(): pl.pallas_call(prep_kernel, out_shape=(rows(2 * TE * ROW), rows(TE * ROW)...  3.73 us
    ppermute x6, waiting for transfers between devices, from_mate(): lax.ppermute(value, 'gy', [(d, d ^ 1) for d in range(lax.axis_size('gy'))])  2.96 us
    ppermute x3, starting transfers between devices, with_partner(): lax.ppermute(value, axis, pairs + [(high, low) for low, high in pairs])  2.55 us
    ppermute x3, waiting for transfers between devices, with_partner(): lax.ppermute(value, axis, pairs + [(high, low) for low, high in pairs])  2.15 us
  transfers between devices with their start and end apart: 14, of which 7 were waited for; matrix products, arithmetic and copies ran while one was open for 0% of the time, Pallas kernels for 20%

profile of v16, /device:TPU:0, one launch (start us, length us, event | category | flops | bytes accessed | tf_op | source)
XLA Modules:
  0.0 62.7 jit_solution(16042326332753429106)
XLA Ops:
  0.7 3.7 %prep.1 = (f32[1024,128]{1,0:T(8,128)}, f32[512,128]{1,0:T(8,128)}, f32[496,128]{1,0:T(8,128)}, f32[496,128]{1,0:T(8,128)}) custom-call(f32[4]{0:T(128)} %table.1, s32[3,64]{1,0:T(4,128)} %bitcast.26, f32[512,128]{1,0:T(8,128)} %bitcast.30, f32[512,128]{1,0:T(8,128)} %bitcast.31, s32[512,128]{1,0:T(8,128)} %bitcast.32, f32[32,4096]{1,0:T(8,128)} %temp.3, ...), custom_call_target="tpu_custom_call" | custom-call | tf_op jit(solution)/shard_map/prep/pallas_call | solution.py:680
  4.4 0.0 copy-start.2
  4.4 3.0 %collective-permute-start = (f32[1024,128]{1,0:T(8,128)}, f32[1024,128]{1,0:T(8,128)S(1)}, u32[]{:S(2)}, u32[]{:S(2)}) collective-permute-start(f32[1024,128]{1,0:T(8,128)} %get-tuple-element.20.refs_0_), channel_id=1, source_target_pairs={{0,2},{1,3},{2,0},{3,1},{4,6},{5,7},{6,4},{7,5},{8,10},{9,11},{10,... | collective-permute-start | bytes 1572872 | tf_op jit(solution)/shard_map/ppermute | solution.py:624
  7.4 0.0 collective-permute-start.1
  7.4 1.5 %collective-permute-start.3 = (f32[496,128]{1,0:T(8,128)}, f32[496,128]{1,0:T(8,128)S(1)}, u32[]{:S(2)}, u32[]{:S(2)}) collective-permute-start(f32[496,128]{1,0:T(8,128)} %get-tuple-element.21), channel_id=1, source_target_pairs={{0,4},{8,12},{16,20},{24,28},{4,0},{12,8},{20,16},{28,24},{1,5},{9... | collective-permute-start | bytes 761864 | tf_op jit(solution)/shard_map/ppermute | solution.py:630
  9.0 0.7 %collective-permute-start.4 = (f32[496,128]{1,0:T(8,128)}, f32[496,128]{1,0:T(8,128)S(1)}, u32[]{:S(2)}, u32[]{:S(2)}) collective-permute-start(f32[496,128]{1,0:T(8,128)} %get-tuple-element.22), channel_id=1, source_target_pairs={{4,8},{12,16},{20,24},{8,4},{16,12},{24,20},{5,9},{13,17},{21,25},... | collective-permute-start | bytes 761864 | tf_op jit(solution)/shard_map/ppermute | solution.py:630
  9.6 9.9 %collective-permute-done.refs_1_ = f32[1024,128]{1,0:T(8,128)S(1)} collective-permute-done((f32[1024,128]{1,0:T(8,128)}, f32[1024,128]{1,0:T(8,128)S(1)}, u32[]{:S(2)}, u32[]{:S(2)}) %collective-permute-start) | collective-permute-done | bytes 524320 | tf_op jit(solution)/shard_map/ppermute | solution.py:624
  19.6 0.0 collective-permute-start.2
  19.6 1.2 %collective-permute-done.3.inner = f32[496,128]{1,0:T(8,128)S(1)} collective-permute-done((f32[496,128]{1,0:T(8,128)}, f32[496,128]{1,0:T(8,128)S(1)}, u32[]{:S(2)}, u32[]{:S(2)}) %collective-permute-start.3) | collective-permute-done | bytes 253984 | tf_op jit(solution)/shard_map/ppermute | solution.py:630
  20.8 0.0 collective-permute-done.4.outer
  20.8 0.6 collective-permute-start.5
  21.4 0.2 collective-permute-start.7
  21.7 1.5 %slab_prep.1 = (f32[1552,128]{1,0:T(8,128)S(1)}, f32[1552,128]{1,0:T(8,128)S(1)}, f32[1552,128]{1,0:T(8,128)S(1)}, f32[120,128]{1,0:T(8,128)S(1)}, f32[632,128]{1,0:T(8,128)S(1)}) custom-call(s32[3,64]{1,0:T(4,128)S(1)} %bitcast.27, f32[4]{0:T(128)S(1)} %copy-done.4, f32[4]{0:T(128)S(1)} %copy-done.5, f32[32,4096]{1,0:T(8,128)S(1)} %copy-done, ...), custom_call_target="tpu_custom_call" | custom-call | tf_op jit(solution)/shard_map/slab_prep/pallas_call | solution.py:715
  23.2 0.4 collective-permute-start.6
  23.5 0.9 %collective-permute-done.6.refs_12_ = f32[120,128]{1,0:T(8,128)S(1)} collective-permute-done((f32[120,128]{1,0:T(8,128)S(1)}, f32[120,128]{1,0:T(8,128)S(1)}, u32[]{:S(2)}, u32[]{:S(2)}) %collective-permute-start.6) | collective-permute-done | bytes 61472 | tf_op jit(solution)/shard_map/ppermute | solution.py:630
  24.5 1.4 %collective-permute-start.11 = (f32[632,128]{1,0:T(8,128)S(1)}, f32[632,128]{1,0:T(8,128)S(1)}, u32[]{:S(2)}, u32[]{:S(2)}) collective-permute-start(f32[632,128]{1,0:T(8,128)S(1)} %get-tuple-element.27), channel_id=1, source_target_pairs={{0,3},{1,2},{2,1},{3,0},{4,7},{5,6},{6,5},{7,4},{8,11},{9,10},{10,... | collective-permute-start | bytes 970760 | tf_op jit(solution)/shard_map/ppermute | solution.py:647
  25.9 2.8 %collective-permute-done.5.refs_5_ = f32[448,128]{1,0:T(8,128)S(1)} collective-permute-done((f32[448,128]{1,0:T(8,128)S(1)}, f32[448,128]{1,0:T(8,128)S(1)}, u32[]{:S(2)}, u32[]{:S(2)}) %collective-permute-start.5) | collective-permute-done | bytes 229408 | tf_op jit(solution)/shard_map/ppermute | solution.py:624
  28.7 0.0 collective-permute-start.10
  28.7 0.0 collective-permute-done.7.refs_6_
  28.7 1.2 %collective-permute-start.9 = (f32[512,128]{1,0:T(8,128)}, f32[512,128]{1,0:T(8,128)S(1)}, u32[]{:S(2)}, u32[]{:S(2)}) collective-permute-start(f32[512,128]{1,0:T(8,128)} %get-tuple-element.23.sigma.refs_0_), channel_id=1, source_target_pairs={{0,2},{1,3},{2,0},{3,1},{4,6},{5,7},{6,4},{7,5},{8,10},{9,11},{10,... | collective-permute-start | bytes 786440 | tf_op jit(solution)/shard_map/ppermute | solution.py:624
  29.8 0.0 collective-permute-done.1.refs_2_
  29.8 0.2 collective-permute-start.8
  30.1 1.3 %collective-permute-done.8.refs_7_ = f32[448,128]{1,0:T(8,128)S(1)} collective-permute-done((f32[448,128]{1,0:T(8,128)S(1)}, f32[448,128]{1,0:T(8,128)S(1)}, u32[]{:S(2)}, u32[]{:S(2)}) %collective-permute-start.8) | collective-permute-done | bytes 229408 | tf_op jit(solution)/shard_map/ppermute | solution.py:634
  31.3 0.0 collective-permute-done.2.refs_3_
  31.3 11.2 %sweeps.1 = (f32[512,128]{1,0:T(8,128)}, f32[2880,128]{1,0:T(8,128)S(1)}) custom-call(s32[3,64]{1,0:T(4,128)S(1)} %bitcast.28, f32[1024,128]{1,0:T(8,128)S(1)} %copy-done.2, f32[1024,128]{1,0:T(8,128)S(1)} %collective-permute-done.refs_1_, f32[1024,128]{1,0:T(8,128)S(1)} %collective-permute-done.1.refs_2_, f32[1024,128]{1,0:T(8,128)S(1)} %collective-permute-done.2.refs_3_, ...), custom_call_target="tpu_custom_call" | custom-call | tf_op jit(solution)/shard_map/sweeps/pallas_call | solution.py:735
  42.6 0.0 collective-permute-done.10.refs_2_
  42.6 8.8 %slab_steps.1 = (f32[32,4096]{1,0:T(8,128)}, f32[512,128]{1,0:T(8,128)S(1)}, f32[1024,128]{1,0:T(8,128)S(1)}, f32[512,128]{1,0:T(8,128)S(1)}) custom-call(s32[3,64]{1,0:T(4,128)S(1)} %bitcast.29, f32[4]{0:T(128)S(1)} %copy-done.4, f32[4]{0:T(128)S(1)} %copy-done.5, f32[512,128]{1,0:T(8,128)} %get-tuple-element.23.sigma.refs_0_, ...), custom_call_target="tpu_custom_call" | custom-call | tf_op jit(solution)/shard_map/slab_steps/pallas_call | solution.py:752
  51.4 0.3 collective-permute-start.12
  51.7 1.7 %collective-permute-done.12 = f32[1024,128]{1,0:T(8,128)S(1)} collective-permute-done((f32[1024,128]{1,0:T(8,128)S(1)}, f32[1024,128]{1,0:T(8,128)S(1)}, u32[]{:S(2)}, u32[]{:S(2)}) %collective-permute-start.12) | collective-permute-done | bytes 524320 | tf_op jit(solution)/shard_map/ppermute | solution.py:634
  53.4 0.9 %collective-permute-start.13 = (f32[512,128]{1,0:T(8,128)S(1)}, f32[512,128]{1,0:T(8,128)S(1)}, u32[]{:S(2)}, u32[]{:S(2)}) collective-permute-start(f32[512,128]{1,0:T(8,128)S(1)} %slice_add_fusion), channel_id=1, source_target_pairs={{0,2},{1,3},{2,0},{3,1},{4,6},{5,7},{6,4},{7,5},{8,10},{9,11},{10,... | collective-permute-start | bytes 786440 | tf_op jit(solution)/shard_map/ppermute | solution.py:624
  54.3 7.6 %collective-permute-done.13 = f32[512,128]{1,0:T(8,128)S(1)} collective-permute-done((f32[512,128]{1,0:T(8,128)S(1)}, f32[512,128]{1,0:T(8,128)S(1)}, u32[]{:S(2)}, u32[]{:S(2)}) %collective-permute-start.13) | collective-permute-done | bytes 262176 | tf_op jit(solution)/shard_map/ppermute | solution.py:624
  61.9 0.7 %fusion = f32[512,128]{1,0:T(8,128)} fusion(f32[512,128]{1,0:T(8,128)S(1)} %collective-permute-done.13, f32[512,128]{1,0:T(8,128)S(1)} %get-tuple-element.34, f32[1024,128]{1,0:T(8,128)S(1)} %collective-permute-done.12), kind=kLoop, calls=%fused_computation.2 | loop fusion | flops 131072 | bytes 1048576 | tf_op jit(solution)/shard_map/add | solution.py:770
  (15 shorter events, 0.1 us)
Async XLA Ops:
  0.6 21.0 %copy-start.3 = (s32[64,3]{0,1:T(4,128)S(1)}, s32[64,3]{0,1:T(4,128)}, u32[]{:S(2)}) copy-start(s32[64,3]{0,1:T(4,128)} %param.13) | copy-start | bytes 2308
  0.6 21.0 %copy-start = (f32[32,4096]{1,0:T(8,128)S(1)}, f32[32,4096]{1,0:T(8,128)}, u32[]{:S(2)}) copy-start(f32[32,4096]{1,0:T(8,128)} %temp.3) | copy-start | bytes 1572868
  0.7 21.0 %copy-start.1 = (s32[32,4096]{1,0:T(8,128)S(1)}, s32[32,4096]{1,0:T(8,128)}, u32[]{:S(2)}) copy-start(s32[32,4096]{1,0:T(8,128)} %mat.1) | copy-start | bytes 1572868
  0.7 21.0 %copy-start.4 = (f32[4]{0:T(128)S(1)}, f32[4]{0:T(128)}, u32[]{:S(2)}) copy-start(f32[4]{0:T(128)} %k0_table.3) | copy-start | bytes 52
  0.7 21.0 %copy-start.5 = (f32[4]{0:T(128)S(1)}, f32[4]{0:T(128)}, u32[]{:S(2)}) copy-start(f32[4]{0:T(128)} %beta_table.3) | copy-start | bytes 52
  4.4 26.9 %copy-start.2 = (f32[1024,128]{1,0:T(8,128)S(1)}, f32[1024,128]{1,0:T(8,128)}, u32[]{:S(2)}) copy-start(f32[1024,128]{1,0:T(8,128)} %get-tuple-element.20.refs_0_) | copy-start | bytes 1572868
  4.4 15.1 %collective-permute-start = (f32[1024,128]{1,0:T(8,128)}, f32[1024,128]{1,0:T(8,128)S(1)}, u32[]{:S(2)}, u32[]{:S(2)}) collective-permute-start(f32[1024,128]{1,0:T(8,128)} %get-tuple-element.20.refs_0_), channel_id=1, source_target_pairs={{0,2},{1,3},{2,0},{3,1},{4,6},{5,7},{6,4},{7,5},{8,10},{9,11},{10,... | collective-permute-start | bytes 1572872 | tf_op jit(solution)/shard_map/ppermute | solution.py:624
  7.4 22.4 %collective-permute-start.1 = (f32[1024,128]{1,0:T(8,128)}, f32[1024,128]{1,0:T(8,128)S(1)}, u32[]{:S(2)}, u32[]{:S(2)}) collective-permute-start(f32[1024,128]{1,0:T(8,128)} %get-tuple-element.20.refs_0_), channel_id=1, source_target_pairs={{0,1},{1,0},{2,3},{3,2},{4,5},{5,4},{6,7},{7,6},{8,9},{9,8},{10,11... | collective-permute-start | bytes 1572872 | tf_op jit(solution)/shard_map/ppermute | solution.py:634
  7.4 13.3 %collective-permute-start.3 = (f32[496,128]{1,0:T(8,128)}, f32[496,128]{1,0:T(8,128)S(1)}, u32[]{:S(2)}, u32[]{:S(2)}) collective-permute-start(f32[496,128]{1,0:T(8,128)} %get-tuple-element.21), channel_id=1, source_target_pairs={{0,4},{8,12},{16,20},{24,28},{4,0},{12,8},{20,16},{28,24},{1,5},{9... | collective-permute-start | bytes 761864 | tf_op jit(solution)/shard_map/ppermute | solution.py:630
  9.0 11.8 %collective-permute-start.4 = (f32[496,128]{1,0:T(8,128)}, f32[496,128]{1,0:T(8,128)S(1)}, u32[]{:S(2)}, u32[]{:S(2)}) collective-permute-start(f32[496,128]{1,0:T(8,128)} %get-tuple-element.22), channel_id=1, source_target_pairs={{4,8},{12,16},{20,24},{8,4},{16,12},{24,20},{5,9},{13,17},{21,25},... | collective-permute-start | bytes 761864 | tf_op jit(solution)/shard_map/ppermute | solution.py:630
  19.6 11.8 %collective-permute-start.2 = (f32[1024,128]{1,0:T(8,128)S(1)}, f32[1024,128]{1,0:T(8,128)S(1)}, u32[]{:S(2)}, u32[]{:S(2)}) collective-permute-start(f32[1024,128]{1,0:T(8,128)S(1)} %collective-permute-done.refs_1_), channel_id=1, source_target_pairs={{0,1},{1,0},{2,3},{3,2},{4,5},{5,4},{6,7},{7,6},{8,9},{9,8},{10,11... | collective-permute-start | bytes 1572872 | tf_op jit(solution)/shard_map/ppermute | solution.py:634
  20.8 7.9 %collective-permute-start.5 = (f32[448,128]{1,0:T(8,128)S(1)}, f32[448,128]{1,0:T(8,128)S(1)}, u32[]{:S(2)}, u32[]{:S(2)}) collective-permute-start(f32[448,128]{1,0:T(8,128)S(1)} %relay.1.refs_4_), channel_id=1, source_target_pairs={{0,2},{1,3},{2,0},{3,1},{4,6},{5,7},{6,4},{7,5},{8,10},{9,11},{10,... | collective-permute-start | bytes 688136 | tf_op jit(solution)/shard_map/ppermute | solution.py:624
  21.4 7.2 %collective-permute-start.7 = (f32[448,128]{1,0:T(8,128)S(1)}, f32[448,128]{1,0:T(8,128)S(1)}, u32[]{:S(2)}, u32[]{:S(2)}) collective-permute-start(f32[448,128]{1,0:T(8,128)S(1)} %relay.1.refs_4_), channel_id=1, source_target_pairs={{0,1},{1,0},{2,3},{3,2},{4,5},{5,4},{6,7},{7,6},{8,9},{9,8},{10,11... | collective-permute-start | bytes 688136 | tf_op jit(solution)/shard_map/ppermute | solution.py:634
  23.2 1.3 %collective-permute-start.6 = (f32[120,128]{1,0:T(8,128)S(1)}, f32[120,128]{1,0:T(8,128)S(1)}, u32[]{:S(2)}, u32[]{:S(2)}) collective-permute-start(f32[120,128]{1,0:T(8,128)S(1)} %get-tuple-element.24), channel_id=1, source_target_pairs={{0,1},{2,3},{1,0},{3,2},{4,5},{6,7},{5,4},{7,6},{8,9},{10,11},{9,8... | collective-permute-start | bytes 184328 | tf_op jit(solution)/shard_map/ppermute | solution.py:630
  24.5 18.1 %collective-permute-start.11 = (f32[632,128]{1,0:T(8,128)S(1)}, f32[632,128]{1,0:T(8,128)S(1)}, u32[]{:S(2)}, u32[]{:S(2)}) collective-permute-start(f32[632,128]{1,0:T(8,128)S(1)} %get-tuple-element.27), channel_id=1, source_target_pairs={{0,3},{1,2},{2,1},{3,0},{4,7},{5,6},{6,5},{7,4},{8,11},{9,10},{10,... | collective-permute-start | bytes 970760 | tf_op jit(solution)/shard_map/ppermute | solution.py:647
  28.7 13.9 %collective-permute-start.10 = (f32[512,128]{1,0:T(8,128)}, f32[512,128]{1,0:T(8,128)S(1)}, u32[]{:S(2)}, u32[]{:S(2)}) collective-permute-start(f32[512,128]{1,0:T(8,128)} %get-tuple-element.23.sigma.refs_0_), channel_id=1, source_target_pairs={{0,1},{1,0},{2,3},{3,2},{4,5},{5,4},{6,7},{7,6},{8,9},{9,8},{10,11... | collective-permute-start | bytes 786440 | tf_op jit(solution)/shard_map/ppermute | solution.py:634
  28.7 13.9 %collective-permute-start.9 = (f32[512,128]{1,0:T(8,128)}, f32[512,128]{1,0:T(8,128)S(1)}, u32[]{:S(2)}, u32[]{:S(2)}) collective-permute-start(f32[512,128]{1,0:T(8,128)} %get-tuple-element.23.sigma.refs_0_), channel_id=1, source_target_pairs={{0,2},{1,3},{2,0},{3,1},{4,6},{5,7},{6,4},{7,5},{8,10},{9,11},{10,... | collective-permute-start | bytes 786440 | tf_op jit(solution)/shard_map/ppermute | solution.py:624
  29.8 1.5 %collective-permute-start.8 = (f32[448,128]{1,0:T(8,128)S(1)}, f32[448,128]{1,0:T(8,128)S(1)}, u32[]{:S(2)}, u32[]{:S(2)}) collective-permute-start(f32[448,128]{1,0:T(8,128)S(1)} %collective-permute-done.5.refs_5_), channel_id=1, source_target_pairs={{0,1},{1,0},{2,3},{3,2},{4,5},{5,4},{6,7},{7,6},{8,9},{9,8},{10,11... | collective-permute-start | bytes 688136 | tf_op jit(solution)/shard_map/ppermute | solution.py:634
  51.4 2.0 %collective-permute-start.12 = (f32[1024,128]{1,0:T(8,128)S(1)}, f32[1024,128]{1,0:T(8,128)S(1)}, u32[]{:S(2)}, u32[]{:S(2)}) collective-permute-start(f32[1024,128]{1,0:T(8,128)S(1)} %get-tuple-element.35), channel_id=1, source_target_pairs={{0,1},{1,0},{2,3},{3,2},{4,5},{5,4},{6,7},{7,6},{8,9},{9,8},{10,11... | collective-permute-start | bytes 1572872 | tf_op jit(solution)/shard_map/ppermute | solution.py:634
  53.4 8.5 %collective-permute-start.13 = (f32[512,128]{1,0:T(8,128)S(1)}, f32[512,128]{1,0:T(8,128)S(1)}, u32[]{:S(2)}, u32[]{:S(2)}) collective-permute-start(f32[512,128]{1,0:T(8,128)S(1)} %slice_add_fusion), channel_id=1, source_target_pairs={{0,2},{1,3},{2,0},{3,1},{4,6},{5,7},{6,4},{7,5},{8,10},{9,11},{10,... | collective-permute-start | bytes 786440 | tf_op jit(solution)/shard_map/ppermute | solution.py:624

commit v17 on v16

--- a/solution.py
+++ b/solution.py
@@ -125,7 +125,7 @@
     return jnp.minimum(pos[0, 0], 0)
 
 
-def slab_kernel(pos, k0_table, beta_table, temp, mat, inner, outer, sigma, t_ext, k0_ext, b_ext, edge_in, packet, native_t, native_m, edge_low, edge_high):
+def slab_kernel(pos, k0_table, beta_table, temp, mat, inner, outer, sigma, t_ext, k0_ext, b_ext, packet_in, packet, native_t, native_m, edge_low, edge_high):
     start = loose(pos)
     even = lax.rem(lax.axis_index("gx"), 2) == 0
     blocks = temp.shape[1] // LANES
@@ -171,7 +171,8 @@
                     first = (y - HALF + HALO) * SLABX + g * SUB
                     edge_high[first : first + SUB] = jnp.where(half, halves[0][2 + odd], halves[1][3 - odd])
     even = lax.rem(lax.axis_index("gy"), 2) == 0
-    edge_in[...] = jnp.where(even, edge_high[...], edge_low[...])
+    packet_in[0 : TE * ROW] = sigma[...]
+    packet_in[TE * ROW :] = jnp.where(even, edge_high[...], edge_low[...])
     packet[0 : TE * ROW] = sigma[...]
     packet[TE * ROW :] = jnp.where(even, edge_low[...], edge_high[...])
 
@@ -397,18 +398,18 @@
     width_gy = 2 * chips
     tiles = width_gy * TILES
     halos = refs[width_gy : 2 * width_gy]
-    slope, t_in, k0_in, b_in, y_in, temp_out = refs[2 * width_gy : 2 * width_gy + 6]
-    mine, bundle = refs[2 * width_gy + 6 : 2 * width_gy + 8]
-    across = refs[2 * width_gy + 8 : 2 * width_gy + 7 + chips]
-    heat, q_ext, state_a, state_b, k0_all, b_all, blocks, sigmas, y_out, sems = refs[2 * width_gy + 7 + chips :]
+    slope, t_in, k0_in, b_in, temp_out = refs[2 * width_gy : 2 * width_gy + 5]
+    mine, bundle = refs[2 * width_gy + 5 : 2 * width_gy + 7]
+    across = refs[2 * width_gy + 7 : 2 * width_gy + 6 + chips]
+    heat, q_ext, state_a, state_b, k0_all, b_all, blocks, sigmas, y_edges, sems = refs[2 * width_gy + 6 + chips :]
     moves = []
     for part in range(width_gy):
         moves.append(pltpu.make_async_copy(refs[part].at[0 : TE * ROW], sigmas.at[part], sems.at[part]))
         moves[-1].start()
     edges = []
-    for which, d in enumerate((1, chips - 1)):
+    for which, d in enumerate((1, chips - 1, 0)):
         source = refs[chips + d].at[TE * ROW : TE * ROW + HALO * SLABX]
-        edges.append(pltpu.make_async_copy(source, y_out.at[which], sems.at[width_gy + which]))
+        edges.append(pltpu.make_async_copy(source, y_edges.at[which], sems.at[width_gy + which]))
         edges[-1].start()
     i = lax.axis_index("gx")
     j = lax.axis_index("gy")
@@ -469,8 +470,8 @@
             temp, k0, beta = t_in[rows], k0_in[rows], b_in[rows]
             if low is not None:
                 place = slice(at * SLABX + g * SUB, at * SLABX + (g + 1) * SUB)
-                other = jnp.where(even, y_out[0, place], y_out[1, place])
-                value = jnp.where(even, *((other, y_in[place])[:: 1 if low else -1]))
+                other = jnp.where(even, y_edges[0, place], y_edges[1, place])
+                value = jnp.where(even, *((other, y_edges[2, place])[:: 1 if low else -1]))
                 swapped = roll(value, NZ, 1)
                 if low:
                     temp = jnp.where(half, value, temp)
@@ -712,21 +713,21 @@
     )(inner, outer)
     halos = [halo] + [shifted(halo, "gy", 2 * d, True) for d in range(1, chips)]
     native = pltpu.VMEM((width // LANES * SLABX + SUB, LANES), f32)
-    t_ext, k0_ext, b_ext, edge_in, packet = pl.pallas_call(
+    t_ext, k0_ext, b_ext, packet_in, packet = pl.pallas_call(
         slab_kernel,
-        out_shape=(rows(SLAB_ROWS),) * 3 + (rows(HALO * SLABX), rows(TE * ROW + HALO * SLABX)),
+        out_shape=(rows(SLAB_ROWS),) * 3 + (rows(TE * ROW + HALO * SLABX),) * 2,
         in_specs=[SMEM] * 3 + [VMEM] * 5,
         out_specs=(VMEM,) * 5,
         scratch_shapes=[native, native] + [pltpu.VMEM((HALO * SLABX, LANES), f32)] * 2,
         compiler_params=PARAMS,
         name="slab_prep",
     )(pos, k0_table, beta_table, temp_init, slab_mat, inner, outer, sigma)
-    y_in = with_partner(edge_in, "gy", 0)
+    y_in = from_mate(packet_in)
+    *halos[1:], y_in = lax.optimization_barrier((*halos[1:], y_in))
     sigmas = [sigma] + [shifted(sigma, "gy", 2 * d, True) for d in range(1, chips)]
-    sigmas += [from_mate(sigma)] + [
+    sigmas += [y_in] + [
         to_other_core(packet if d in (1, chips - 1) else sigma, d) for d in range(1, chips)
     ]
-    *halos[1:], y_in = lax.optimization_barrier((*halos[1:], y_in))
     halos = halos + [from_mate(part) for part in halos]
 
     def fields(count):
@@ -753,17 +754,17 @@
         functools.partial(slab_steps_kernel, chips),
         out_shape=(jax.ShapeDtypeStruct((size_x, width), f32), rows(TE * ROW), rows(chips * TE * ROW))
         + (rows(TE * ROW),) * (chips - 1),
-        in_specs=[SMEM] * 3 + [ANY] * width_gy + [VMEM] * (width_gy + 5),
+        in_specs=[SMEM] * 3 + [ANY] * width_gy + [VMEM] * (width_gy + 4),
         out_specs=(VMEM,) * (2 + chips),
         scratch_shapes=[pltpu.VMEM((CELLS * SLABX * SUB, LANES), f32)]
         + [pltpu.VMEM((SLAB_ROWS + 3 * SLABX, LANES), f32)]
         + [pltpu.VMEM((2 * SLAB_ROWS, LANES), f32)] * 2
         + [pltpu.VMEM((SLAB_ROWS, LANES), f32)] * 2
         + [pltpu.VMEM((4 * TE * SUB, LANES), f32), pltpu.VMEM((width_gy, TE * ROW, LANES), f32)]
-        + [pltpu.VMEM((2, HALO * SLABX, LANES), f32), pltpu.SemaphoreType.DMA((width_gy + 2,))],
+        + [pltpu.VMEM((3, HALO * SLABX, LANES), f32), pltpu.SemaphoreType.DMA((width_gy + 3,))],
         compiler_params=PARAMS,
         name="slab_steps",
-    )(pos, k0_table, beta_table, *sigmas, *halos, slope, t_ext, k0_ext, b_ext, y_in)
+    )(pos, k0_table, beta_table, *sigmas, *halos, slope, t_ext, k0_ext, b_ext)
     got = from_mate(bundle).reshape(chips, TE * ROW, LANES)
     tile_temps = mine + got[0]
     for d in range(1, chips):

time: 62.9 us -> 65.7 us (1.045)
  waiting for transfers between devices: 25.4 us -> 28.4 us
  local copies, waits for them, and re-layouts: 0.03 us -> 0.97 us
  starting transfers between devices: 10.4 us -> 9.47 us
    ppermute x3 -> x2, waiting for transfers between devices: 2.15 us -> 10.2 us  [with_partner(): lax.ppermute(value, axis, pairs + [(high, low) for low, high in pairs])]
    ppermute x4, waiting for transfers between devices: 20.3 us -> 15.3 us  [shifted(): return lax.ppermute(value, axis, pairs)]
    ppermute x1, starting transfers between devices: 1.37 us -> 0.01 us  [to_other_core(): lax.ppermute(value, 'gy', [(at, ((at ^ 1) + 2 * by) % count) for at in ra...]
    unnamed x12 -> x16, local copies, waits for them, and re-layouts: 0.03 us -> 0.97 us
    ppermute x6, starting transfers between devices: 0.73 us -> 1.5 us  [from_mate(): lax.ppermute(value, 'gy', [(d, d ^ 1) for d in range(lax.axis_size('gy'))])]
    ppermute x3 -> x2, starting transfers between devices: 2.55 us -> 2.18 us  [with_partner(): lax.ppermute(value, axis, pairs + [(high, low) for low, high in pairs])]
  transfers between devices with their start and end apart: 14 -> 13, of which waited for: 7 -> 6; matrix products, arithmetic and copies ran while one was open for 0% -> 0% of each run, Pallas kernels for 20% -> 19%
where the time goes in v17:
time: 65.7 us; the launch traced here: 65.5 us
  waiting for transfers between devices  28.4 us (43%)
  Pallas kernels  25 us (38%)
  starting transfers between devices  9.47 us (14%)
  local copies, waits for them, and re-layouts  0.97 us (1%)
  other arithmetic  0.78 us (1%)
  between operations  0.78 us (1%)
    ppermute x4, waiting for transfers between devices, shifted(): return lax.ppermute(value, axis, pairs)  15.3 us
    pallas_call x1, Pallas kernels, on_device(): pl.pallas_call(functools.partial(sweep_kernel, chips), out_shape=(rows(TE...  11.2 us
    ppermute x2, waiting for transfers between devices, with_partner(): lax.ppermute(value, axis, pairs + [(high, low) for low, high in pairs])  10.2 us
    pallas_call x1, Pallas kernels, on_device(): pl.pallas_call(functools.partial(slab_steps_kernel, chips), out_shape=(ja...  8.88 us
    ppermute x4, starting transfers between devices, shifted(): return lax.ppermute(value, axis, pairs)  5.78 us
    pallas_call x1, Pallas kernels, on_device(): pl.pallas_call(prep_kernel, out_shape=(rows(2 * TE * ROW), rows(TE * ROW)...  3.73 us
    ppermute x6, waiting for transfers between devices, from_mate(): lax.ppermute(value, 'gy', [(d, d ^ 1) for d in range(lax.axis_size('gy'))])  2.92 us
    ppermute x2, starting transfers between devices, with_partner(): lax.ppermute(value, axis, pairs + [(high, low) for low, high in pairs])  2.18 us
  transfers between devices with their start and end apart: 13, of which 6 were waited for; matrix products, arithmetic and copies ran while one was open for 0% of the time, Pallas kernels for 19%

profile of v17, /device:TPU:0, one launch (start us, length us, event | category | flops | bytes accessed | tf_op | source)
XLA Modules:
  0.0 65.5 jit_solution(17592355071130986682)
XLA Ops:
  0.7 3.7 %prep.1 = (f32[1024,128]{1,0:T(8,128)}, f32[512,128]{1,0:T(8,128)}, f32[496,128]{1,0:T(8,128)}, f32[496,128]{1,0:T(8,128)}) custom-call(f32[4]{0:T(128)} %table.1, s32[3,64]{1,0:T(4,128)} %bitcast.26, f32[512,128]{1,0:T(8,128)} %bitcast.30, f32[512,128]{1,0:T(8,128)} %bitcast.31, s32[512,128]{1,0:T(8,128)} %bitcast.32, f32[32,4096]{1,0:T(8,128)} %temp.3, ...), custom_call_target="tpu_custom_call" | custom-call | tf_op jit(solution)/shard_map/prep/pallas_call | solution.py:681
  4.4 3.0 %collective-permute-start = (f32[1024,128]{1,0:T(8,128)}, f32[1024,128]{1,0:T(8,128)S(1)}, u32[]{:S(2)}, u32[]{:S(2)}) collective-permute-start(f32[1024,128]{1,0:T(8,128)} %get-tuple-element.20.refs_0_), channel_id=1, source_target_pairs={{0,2},{1,3},{2,0},{3,1},{4,6},{5,7},{6,4},{7,5},{8,10},{9,11},{10,... | collective-permute-start | bytes 1572872 | tf_op jit(solution)/shard_map/ppermute | solution.py:625
  7.4 1.5 %collective-permute-start.3 = (f32[496,128]{1,0:T(8,128)}, f32[496,128]{1,0:T(8,128)S(1)}, u32[]{:S(2)}, u32[]{:S(2)}) collective-permute-start(f32[496,128]{1,0:T(8,128)} %get-tuple-element.21), channel_id=1, source_target_pairs={{0,4},{8,12},{16,20},{24,28},{4,0},{12,8},{20,16},{28,24},{1,5},{9... | collective-permute-start | bytes 761864 | tf_op jit(solution)/shard_map/ppermute | solution.py:631
  8.9 0.7 %collective-permute-start.4 = (f32[496,128]{1,0:T(8,128)}, f32[496,128]{1,0:T(8,128)S(1)}, u32[]{:S(2)}, u32[]{:S(2)}) collective-permute-start(f32[496,128]{1,0:T(8,128)} %get-tuple-element.22), channel_id=1, source_target_pairs={{4,8},{12,16},{20,24},{8,4},{16,12},{24,20},{5,9},{13,17},{21,25},... | collective-permute-start | bytes 761864 | tf_op jit(solution)/shard_map/ppermute | solution.py:631
  9.6 10.2 %collective-permute-done.3.inner = f32[496,128]{1,0:T(8,128)S(1)} collective-permute-done((f32[496,128]{1,0:T(8,128)}, f32[496,128]{1,0:T(8,128)S(1)}, u32[]{:S(2)}, u32[]{:S(2)}) %collective-permute-start.3) | collective-permute-done | bytes 253984 | tf_op jit(solution)/shard_map/ppermute | solution.py:631
  19.8 0.0 collective-permute-done.4.outer
  19.8 0.0 copy-start.2
  19.9 0.9 %copy-done.2 = f32[512,128]{1,0:T(8,128)S(1)} copy-done((f32[512,128]{1,0:T(8,128)S(1)}, f32[512,128]{1,0:T(8,128)}, u32[]{:S(2)}) %copy-start.2) | copy-done | bytes 262168
  20.8 1.1 %slab_prep.1 = (f32[1552,128]{1,0:T(8,128)S(1)}, f32[1552,128]{1,0:T(8,128)S(1)}, f32[1552,128]{1,0:T(8,128)S(1)}, f32[632,128]{1,0:T(8,128)S(1)}, f32[632,128]{1,0:T(8,128)S(1)}) custom-call(s32[3,64]{1,0:T(4,128)S(1)} %bitcast.27, f32[4]{0:T(128)S(1)} %copy-done.6, f32[4]{0:T(128)S(1)} %copy-done.7, f32[32,4096]{1,0:T(8,128)S(1)} %copy-done, ...), custom_call_target="tpu_custom_call" | custom-call | tf_op jit(solution)/shard_map/slab_prep/pallas_call | solution.py:716
  21.9 0.1 collective-permute-start.6
  22.1 0.6 collective-permute-start.5
  22.7 0.2 collective-permute-start.1
  22.9 0.0 collective-permute-done.refs_1_
  22.9 0.3 collective-permute-start.2
  23.2 0.2 collective-permute-start.7
  23.4 6.7 %collective-permute-done.5.refs_5_ = f32[448,128]{1,0:T(8,128)S(1)} collective-permute-done((f32[448,128]{1,0:T(8,128)S(1)}, f32[448,128]{1,0:T(8,128)S(1)}, u32[]{:S(2)}, u32[]{:S(2)}) %collective-permute-start.5) | collective-permute-done | bytes 229408 | tf_op jit(solution)/shard_map/ppermute | solution.py:625
  30.1 0.0 collective-permute-start.10
  30.1 0.0 collective-permute-done.6.refs_2_
  30.1 1.3 %collective-permute-start.9 = (f32[512,128]{1,0:T(8,128)S(1)}, f32[512,128]{1,0:T(8,128)S(1)}, u32[]{:S(2)}, u32[]{:S(2)}) collective-permute-start(f32[512,128]{1,0:T(8,128)S(1)} %copy-done.3), channel_id=1, source_target_pairs={{0,2},{1,3},{2,0},{3,1},{4,6},{5,7},{6,4},{7,5},{8,10},{9,11},{10,... | collective-permute-start | bytes 786440 | tf_op jit(solution)/shard_map/ppermute | solution.py:625
  31.4 0.0 collective-permute-done.7.refs_6_
  31.4 0.5 collective-permute-start.8
  32.0 0.0 collective-permute-done.1.refs_2_
  32.0 1.1 %collective-permute-done.8.refs_7_ = f32[448,128]{1,0:T(8,128)S(1)} collective-permute-done((f32[448,128]{1,0:T(8,128)S(1)}, f32[448,128]{1,0:T(8,128)S(1)}, u32[]{:S(2)}, u32[]{:S(2)}) %collective-permute-start.8) | collective-permute-done | bytes 229408 | tf_op jit(solution)/shard_map/ppermute | solution.py:635
  33.1 0.0 collective-permute-done.2.refs_3_
  33.1 11.2 %sweeps.1 = (f32[512,128]{1,0:T(8,128)}, f32[2880,128]{1,0:T(8,128)S(1)}) custom-call(s32[3,64]{1,0:T(4,128)S(1)} %bitcast.28, f32[1024,128]{1,0:T(8,128)S(1)} %copy-done.4, f32[1024,128]{1,0:T(8,128)S(1)} %collective-permute-done.refs_1_, f32[1024,128]{1,0:T(8,128)S(1)} %collective-permute-done.1.refs_2_, f32[1024,128]{1,0:T(8,128)S(1)} %collective-permute-done.2.refs_3_, ...), custom_call_target="tpu_custom_call" | custom-call | tf_op jit(solution)/shard_map/sweeps/pallas_call | solution.py:736
  44.4 1.0 %collective-permute-done.9.refs_1_ = f32[512,128]{1,0:T(8,128)S(1)} collective-permute-done((f32[512,128]{1,0:T(8,128)S(1)}, f32[512,128]{1,0:T(8,128)S(1)}, u32[]{:S(2)}, u32[]{:S(2)}) %collective-permute-start.9) | collective-permute-done | bytes 262176 | tf_op jit(solution)/shard_map/ppermute | solution.py:625
  45.4 8.9 %slab_steps.1 = (f32[32,4096]{1,0:T(8,128)}, f32[512,128]{1,0:T(8,128)S(1)}, f32[1024,128]{1,0:T(8,128)S(1)}, f32[512,128]{1,0:T(8,128)S(1)}) custom-call(s32[3,64]{1,0:T(4,128)S(1)} %bitcast.29, f32[4]{0:T(128)S(1)} %copy-done.6, f32[4]{0:T(128)S(1)} %copy-done.7, f32[512,128]{1,0:T(8,128)S(1)} %copy-done.3, f32[512,128]{1,0:T(8,128)S(1)} %collective-permute-done.9.refs_1_, ...), custom_call_target="tpu_custom_call" | custom-call | tf_op jit(solution)/shard_map/slab_steps/pallas_call | solution.py:753
  54.3 0.2 collective-permute-start.11
  54.5 1.8 %collective-permute-done.11 = f32[1024,128]{1,0:T(8,128)S(1)} collective-permute-done((f32[1024,128]{1,0:T(8,128)S(1)}, f32[1024,128]{1,0:T(8,128)S(1)}, u32[]{:S(2)}, u32[]{:S(2)}) %collective-permute-start.11) | collective-permute-done | bytes 524320 | tf_op jit(solution)/shard_map/ppermute | solution.py:635
  56.3 0.9 %collective-permute-start.12 = (f32[512,128]{1,0:T(8,128)S(1)}, f32[512,128]{1,0:T(8,128)S(1)}, u32[]{:S(2)}, u32[]{:S(2)}) collective-permute-start(f32[512,128]{1,0:T(8,128)S(1)} %slice_add_fusion), channel_id=1, source_target_pairs={{0,2},{1,3},{2,0},{3,1},{4,6},{5,7},{6,4},{7,5},{8,10},{9,11},{10,... | collective-permute-start | bytes 786440 | tf_op jit(solution)/shard_map/ppermute | solution.py:625
  57.1 7.6 %collective-permute-done.12 = f32[512,128]{1,0:T(8,128)S(1)} collective-permute-done((f32[512,128]{1,0:T(8,128)S(1)}, f32[512,128]{1,0:T(8,128)S(1)}, u32[]{:S(2)}, u32[]{:S(2)}) %collective-permute-start.12) | collective-permute-done | bytes 262176 | tf_op jit(solution)/shard_map/ppermute | solution.py:625
  64.7 0.8 %fusion = f32[512,128]{1,0:T(8,128)} fusion(f32[512,128]{1,0:T(8,128)S(1)} %collective-permute-done.12, f32[512,128]{1,0:T(8,128)S(1)} %get-tuple-element.34, f32[1024,128]{1,0:T(8,128)S(1)} %collective-permute-done.11), kind=kLoop, calls=%fused_computation.2 | loop fusion | flops 131072 | bytes 1048576 | tf_op jit(solution)/shard_map/add | solution.py:771
  (17 shorter events, 0.1 us)
Async XLA Ops:
  0.6 19.2 %copy-start.5 = (s32[64,3]{0,1:T(4,128)S(1)}, s32[64,3]{0,1:T(4,128)}, u32[]{:S(2)}) copy-start(s32[64,3]{0,1:T(4,128)} %param.13) | copy-start | bytes 2308
  0.6 19.2 %copy-start = (f32[32,4096]{1,0:T(8,128)S(1)}, f32[32,4096]{1,0:T(8,128)}, u32[]{:S(2)}) copy-start(f32[32,4096]{1,0:T(8,128)} %temp.3) | copy-start | bytes 1572868
  0.7 19.2 %copy-start.1 = (s32[32,4096]{1,0:T(8,128)S(1)}, s32[32,4096]{1,0:T(8,128)}, u32[]{:S(2)}) copy-start(s32[32,4096]{1,0:T(8,128)} %mat.1) | copy-start | bytes 1572868
  0.7 19.2 %copy-start.6 = (f32[4]{0:T(128)S(1)}, f32[4]{0:T(128)}, u32[]{:S(2)}) copy-start(f32[4]{0:T(128)} %k0_table.3) | copy-start | bytes 52
  0.7 19.2 %copy-start.7 = (f32[4]{0:T(128)S(1)}, f32[4]{0:T(128)}, u32[]{:S(2)}) copy-start(f32[4]{0:T(128)} %beta_table.3) | copy-start | bytes 52
  4.4 18.4 %collective-permute-start = (f32[1024,128]{1,0:T(8,128)}, f32[1024,128]{1,0:T(8,128)S(1)}, u32[]{:S(2)}, u32[]{:S(2)}) collective-permute-start(f32[1024,128]{1,0:T(8,128)} %get-tuple-element.20.refs_0_), channel_id=1, source_target_pairs={{0,2},{1,3},{2,0},{3,1},{4,6},{5,7},{6,4},{7,5},{8,10},{9,11},{10,... | collective-permute-start | bytes 1572872 | tf_op jit(solution)/shard_map/ppermute | solution.py:625
  7.4 12.4 %collective-permute-start.3 = (f32[496,128]{1,0:T(8,128)}, f32[496,128]{1,0:T(8,128)S(1)}, u32[]{:S(2)}, u32[]{:S(2)}) collective-permute-start(f32[496,128]{1,0:T(8,128)} %get-tuple-element.21), channel_id=1, source_target_pairs={{0,4},{8,12},{16,20},{24,28},{4,0},{12,8},{20,16},{28,24},{1,5},{9... | collective-permute-start | bytes 761864 | tf_op jit(solution)/shard_map/ppermute | solution.py:631
  8.9 10.9 %collective-permute-start.4 = (f32[496,128]{1,0:T(8,128)}, f32[496,128]{1,0:T(8,128)S(1)}, u32[]{:S(2)}, u32[]{:S(2)}) collective-permute-start(f32[496,128]{1,0:T(8,128)} %get-tuple-element.22), channel_id=1, source_target_pairs={{4,8},{12,16},{20,24},{8,4},{16,12},{24,20},{5,9},{13,17},{21,25},... | collective-permute-start | bytes 761864 | tf_op jit(solution)/shard_map/ppermute | solution.py:631
  19.8 1.0 %copy-start.2 = (f32[512,128]{1,0:T(8,128)S(1)}, f32[512,128]{1,0:T(8,128)}, u32[]{:S(2)}) copy-start(f32[512,128]{1,0:T(8,128)} %get-tuple-element.23.sigma.refs_0_) | copy-start | bytes 786436
  20.8 1.9 %copy-start.4 = (f32[1024,128]{1,0:T(8,128)S(1)}, f32[1024,128]{1,0:T(8,128)}, u32[]{:S(2)}) copy-start(f32[1024,128]{1,0:T(8,128)} %get-tuple-element.20.refs_0_) | copy-start | bytes 1572868
  20.8 9.3 %copy-start.3 = (f32[512,128]{1,0:T(8,128)S(1)}, f32[512,128]{1,0:T(8,128)}, u32[]{:S(2)}) copy-start(f32[512,128]{1,0:T(8,128)} %get-tuple-element.23.sigma.refs_0_) | copy-start | bytes 786436
  21.9 8.2 %collective-permute-start.6 = (f32[632,128]{1,0:T(8,128)S(1)}, f32[632,128]{1,0:T(8,128)S(1)}, u32[]{:S(2)}, u32[]{:S(2)}) collective-permute-start(f32[632,128]{1,0:T(8,128)S(1)} %get-tuple-element.24), channel_id=1, source_target_pairs={{0,1},{1,0},{2,3},{3,2},{4,5},{5,4},{6,7},{7,6},{8,9},{9,8},{10,11... | collective-permute-start | bytes 970760 | tf_op jit(solution)/shard_map/ppermute | solution.py:635
  22.1 8.1 %collective-permute-start.5 = (f32[448,128]{1,0:T(8,128)S(1)}, f32[448,128]{1,0:T(8,128)S(1)}, u32[]{:S(2)}, u32[]{:S(2)}) collective-permute-start(f32[448,128]{1,0:T(8,128)S(1)} %relay.1.refs_4_), channel_id=1, source_target_pairs={{0,2},{1,3},{2,0},{3,1},{4,6},{5,7},{6,4},{7,5},{8,10},{9,11},{10,... | collective-permute-start | bytes 688136 | tf_op jit(solution)/shard_map/ppermute | solution.py:625
  22.7 9.3 %collective-permute-start.1 = (f32[1024,128]{1,0:T(8,128)S(1)}, f32[1024,128]{1,0:T(8,128)S(1)}, u32[]{:S(2)}, u32[]{:S(2)}) collective-permute-start(f32[1024,128]{1,0:T(8,128)S(1)} %copy-done.4), channel_id=1, source_target_pairs={{0,1},{1,0},{2,3},{3,2},{4,5},{5,4},{6,7},{7,6},{8,9},{9,8},{10,11... | collective-permute-start | bytes 1572872 | tf_op jit(solution)/shard_map/ppermute | solution.py:635
  22.9 10.2 %collective-permute-start.2 = (f32[1024,128]{1,0:T(8,128)S(1)}, f32[1024,128]{1,0:T(8,128)S(1)}, u32[]{:S(2)}, u32[]{:S(2)}) collective-permute-start(f32[1024,128]{1,0:T(8,128)S(1)} %collective-permute-done.refs_1_), channel_id=1, source_target_pairs={{0,1},{1,0},{2,3},{3,2},{4,5},{5,4},{6,7},{7,6},{8,9},{9,8},{10,11... | collective-permute-start | bytes 1572872 | tf_op jit(solution)/shard_map/ppermute | solution.py:635
  23.2 8.3 %collective-permute-start.7 = (f32[448,128]{1,0:T(8,128)S(1)}, f32[448,128]{1,0:T(8,128)S(1)}, u32[]{:S(2)}, u32[]{:S(2)}) collective-permute-start(f32[448,128]{1,0:T(8,128)S(1)} %relay.1.refs_4_), channel_id=1, source_target_pairs={{0,1},{1,0},{2,3},{3,2},{4,5},{5,4},{6,7},{7,6},{8,9},{9,8},{10,11... | collective-permute-start | bytes 688136 | tf_op jit(solution)/shard_map/ppermute | solution.py:635
  30.1 15.3 %collective-permute-start.10 = (f32[632,128]{1,0:T(8,128)S(1)}, f32[632,128]{1,0:T(8,128)S(1)}, u32[]{:S(2)}, u32[]{:S(2)}) collective-permute-start(f32[632,128]{1,0:T(8,128)S(1)} %get-tuple-element.28), channel_id=1, source_target_pairs={{0,3},{1,2},{2,1},{3,0},{4,7},{5,6},{6,5},{7,4},{8,11},{9,10},{10,... | collective-permute-start | bytes 970760 | tf_op jit(solution)/shard_map/ppermute | solution.py:648
  30.1 15.3 %collective-permute-start.9 = (f32[512,128]{1,0:T(8,128)S(1)}, f32[512,128]{1,0:T(8,128)S(1)}, u32[]{:S(2)}, u32[]{:S(2)}) collective-permute-start(f32[512,128]{1,0:T(8,128)S(1)} %copy-done.3), channel_id=1, source_target_pairs={{0,2},{1,3},{2,0},{3,1},{4,6},{5,7},{6,4},{7,5},{8,10},{9,11},{10,... | collective-permute-start | bytes 786440 | tf_op jit(solution)/shard_map/ppermute | solution.py:625
  31.4 1.7 %collective-permute-start.8 = (f32[448,128]{1,0:T(8,128)S(1)}, f32[448,128]{1,0:T(8,128)S(1)}, u32[]{:S(2)}, u32[]{:S(2)}) collective-permute-start(f32[448,128]{1,0:T(8,128)S(1)} %collective-permute-done.5.refs_5_), channel_id=1, source_target_pairs={{0,1},{1,0},{2,3},{3,2},{4,5},{5,4},{6,7},{7,6},{8,9},{9,8},{10,11... | collective-permute-start | bytes 688136 | tf_op jit(solution)/shard_map/ppermute | solution.py:635
  54.3 2.0 %collective-permute-start.11 = (f32[1024,128]{1,0:T(8,128)S(1)}, f32[1024,128]{1,0:T(8,128)S(1)}, u32[]{:S(2)}, u32[]{:S(2)}) collective-permute-start(f32[1024,128]{1,0:T(8,128)S(1)} %get-tuple-element.35), channel_id=1, source_target_pairs={{0,1},{1,0},{2,3},{3,2},{4,5},{5,4},{6,7},{7,6},{8,9},{9,8},{10,11... | collective-permute-start | bytes 1572872 | tf_op jit(solution)/shard_map/ppermute | solution.py:635
  56.3 8.4 %collective-permute-start.12 = (f32[512,128]{1,0:T(8,128)S(1)}, f32[512,128]{1,0:T(8,128)S(1)}, u32[]{:S(2)}, u32[]{:S(2)}) collective-permute-start(f32[512,128]{1,0:T(8,128)S(1)} %slice_add_fusion), channel_id=1, source_target_pairs={{0,2},{1,3},{2,0},{3,1},{4,6},{5,7},{6,4},{7,5},{8,10},{9,11},{10,... | collective-permute-start | bytes 786440 | tf_op jit(solution)/shard_map/ppermute | solution.py:625

commit v18 on v16

--- a/solution.py
+++ b/solution.py
@@ -355,7 +355,7 @@
             put_plane(pot, pl.multiple_of(p * ROW, ROW) + t, pltpu.roll(value, turn, 1))
             return carry
 
-        lax.fori_loop(0, TE, turn_back, 0, unroll=8)
+        lax.fori_loop(0, TE, turn_back, 0, unroll=16)
 
     def squares(ref, places, local, x, first, count, beyond):
         row, _, row_p, _, row_z, _, _, upper = places
@@ -381,7 +381,7 @@
         squares(f_u, at, local, HALO + TE, 0, 2, None)
         return carry
 
-    lax.fori_loop(0, tiles, slope_tile, 0, unroll=2)
+    lax.fori_loop(0, tiles, slope_tile, 0, unroll=4)
 
 
 def window(which, cell, i, j, rows_gx):

time: 62.9 us -> 62.5 us (level)
  no operation moved by 1% of the time
where the time goes in v18:
time: 62.5 us; the launch traced here: 62.3 us
  waiting for transfers between devices  25.4 us (41%)
  Pallas kernels  24.9 us (40%)
  starting transfers between devices  10.4 us (17%)
  other arithmetic  0.78 us (1%)
  between operations  0.78 us (1%)
    ppermute x4, waiting for transfers between devices, shifted(): return lax.ppermute(value, axis, pairs)  20.3 us
    pallas_call x1, Pallas kernels, on_device(): pl.pallas_call(functools.partial(sweep_kernel, chips), out_shape=(rows(TE...  10.8 us
    pallas_call x1, Pallas kernels, on_device(): pl.pallas_call(functools.partial(slab_steps_kernel, chips), out_shape=(ja...  8.78 us
    ppermute x4, starting transfers between devices, shifted(): return lax.ppermute(value, axis, pairs)  5.73 us
    pallas_call x1, Pallas kernels, on_device(): pl.pallas_call(prep_kernel, out_shape=(rows(2 * TE * ROW), rows(TE * ROW)...  3.73 us
    ppermute x6, waiting for transfers between devices, from_mate(): lax.ppermute(value, 'gy', [(d, d ^ 1) for d in range(lax.axis_size('gy'))])  2.96 us
    ppermute x3, starting transfers between devices, with_partner(): lax.ppermute(value, axis, pairs + [(high, low) for low, high in pairs])  2.55 us
    ppermute x3, waiting for transfers between devices, with_partner(): lax.ppermute(value, axis, pairs + [(high, low) for low, high in pairs])  2.15 us
  transfers between devices with their start and end apart: 14, of which 7 were waited for; matrix products, arithmetic and copies ran while one was open for 0% of the time, Pallas kernels for 20%

profile of v18, /device:TPU:0, one launch (start us, length us, event | category | flops | bytes accessed | tf_op | source)
XLA Modules:
  0.0 62.3 jit_solution(14486355296131430074)
XLA Ops:
  0.7 3.7 %prep.1 = (f32[1024,128]{1,0:T(8,128)}, f32[512,128]{1,0:T(8,128)}, f32[496,128]{1,0:T(8,128)}, f32[496,128]{1,0:T(8,128)}) custom-call(f32[4]{0:T(128)} %table.1, s32[3,64]{1,0:T(4,128)} %bitcast.26, f32[512,128]{1,0:T(8,128)} %bitcast.30, f32[512,128]{1,0:T(8,128)} %bitcast.31, s32[512,128]{1,0:T(8,128)} %bitcast.32, f32[32,4096]{1,0:T(8,128)} %temp.3, ...), custom_call_target="tpu_custom_call" | custom-call | tf_op jit(solution)/shard_map/prep/pallas_call | solution.py:680
  4.4 0.0 copy-start.2
  4.4 3.0 %collective-permute-start = (f32[1024,128]{1,0:T(8,128)}, f32[1024,128]{1,0:T(8,128)S(1)}, u32[]{:S(2)}, u32[]{:S(2)}) collective-permute-start(f32[1024,128]{1,0:T(8,128)} %get-tuple-element.20.refs_0_), channel_id=1, source_target_pairs={{0,2},{1,3},{2,0},{3,1},{4,6},{5,7},{6,4},{7,5},{8,10},{9,11},{10,... | collective-permute-start | bytes 1572872 | tf_op jit(solution)/shard_map/ppermute | solution.py:624
  7.4 0.0 collective-permute-start.1
  7.4 1.5 %collective-permute-start.3 = (f32[496,128]{1,0:T(8,128)}, f32[496,128]{1,0:T(8,128)S(1)}, u32[]{:S(2)}, u32[]{:S(2)}) collective-permute-start(f32[496,128]{1,0:T(8,128)} %get-tuple-element.21), channel_id=1, source_target_pairs={{0,4},{8,12},{16,20},{24,28},{4,0},{12,8},{20,16},{28,24},{1,5},{9... | collective-permute-start | bytes 761864 | tf_op jit(solution)/shard_map/ppermute | solution.py:630
  9.0 0.7 %collective-permute-start.4 = (f32[496,128]{1,0:T(8,128)}, f32[496,128]{1,0:T(8,128)S(1)}, u32[]{:S(2)}, u32[]{:S(2)}) collective-permute-start(f32[496,128]{1,0:T(8,128)} %get-tuple-element.22), channel_id=1, source_target_pairs={{4,8},{12,16},{20,24},{8,4},{16,12},{24,20},{5,9},{13,17},{21,25},... | collective-permute-start | bytes 761864 | tf_op jit(solution)/shard_map/ppermute | solution.py:630
  9.6 9.9 %collective-permute-done.refs_1_ = f32[1024,128]{1,0:T(8,128)S(1)} collective-permute-done((f32[1024,128]{1,0:T(8,128)}, f32[1024,128]{1,0:T(8,128)S(1)}, u32[]{:S(2)}, u32[]{:S(2)}) %collective-permute-start) | collective-permute-done | bytes 524320 | tf_op jit(solution)/shard_map/ppermute | solution.py:624
  19.6 0.0 collective-permute-start.2
  19.6 1.2 %collective-permute-done.3.inner = f32[496,128]{1,0:T(8,128)S(1)} collective-permute-done((f32[496,128]{1,0:T(8,128)}, f32[496,128]{1,0:T(8,128)S(1)}, u32[]{:S(2)}, u32[]{:S(2)}) %collective-permute-start.3) | collective-permute-done | bytes 253984 | tf_op jit(solution)/shard_map/ppermute | solution.py:630
  20.8 0.0 collective-permute-done.4.outer
  20.8 0.6 %collective-permute-start.5 = (f32[448,128]{1,0:T(8,128)S(1)}, f32[448,128]{1,0:T(8,128)S(1)}, u32[]{:S(2)}, u32[]{:S(2)}) collective-permute-start(f32[448,128]{1,0:T(8,128)S(1)} %relay.1.refs_4_), channel_id=1, source_target_pairs={{0,2},{1,3},{2,0},{3,1},{4,6},{5,7},{6,4},{7,5},{8,10},{9,11},{10,... | collective-permute-start | bytes 688136 | tf_op jit(solution)/shard_map/ppermute | solution.py:624
  21.4 0.2 collective-permute-start.7
  21.7 1.5 %slab_prep.1 = (f32[1552,128]{1,0:T(8,128)S(1)}, f32[1552,128]{1,0:T(8,128)S(1)}, f32[1552,128]{1,0:T(8,128)S(1)}, f32[120,128]{1,0:T(8,128)S(1)}, f32[632,128]{1,0:T(8,128)S(1)}) custom-call(s32[3,64]{1,0:T(4,128)S(1)} %bitcast.27, f32[4]{0:T(128)S(1)} %copy-done.4, f32[4]{0:T(128)S(1)} %copy-done.5, f32[32,4096]{1,0:T(8,128)S(1)} %copy-done, ...), custom_call_target="tpu_custom_call" | custom-call | tf_op jit(solution)/shard_map/slab_prep/pallas_call | solution.py:715
  23.2 0.4 collective-permute-start.6
  23.5 0.9 %collective-permute-done.6.refs_12_ = f32[120,128]{1,0:T(8,128)S(1)} collective-permute-done((f32[120,128]{1,0:T(8,128)S(1)}, f32[120,128]{1,0:T(8,128)S(1)}, u32[]{:S(2)}, u32[]{:S(2)}) %collective-permute-start.6) | collective-permute-done | bytes 61472 | tf_op jit(solution)/shard_map/ppermute | solution.py:630
  24.5 1.4 %collective-permute-start.11 = (f32[632,128]{1,0:T(8,128)S(1)}, f32[632,128]{1,0:T(8,128)S(1)}, u32[]{:S(2)}, u32[]{:S(2)}) collective-permute-start(f32[632,128]{1,0:T(8,128)S(1)} %get-tuple-element.27), channel_id=1, source_target_pairs={{0,3},{1,2},{2,1},{3,0},{4,7},{5,6},{6,5},{7,4},{8,11},{9,10},{10,... | collective-permute-start | bytes 970760 | tf_op jit(solution)/shard_map/ppermute | solution.py:647
  25.9 2.8 %collective-permute-done.5.refs_5_ = f32[448,128]{1,0:T(8,128)S(1)} collective-permute-done((f32[448,128]{1,0:T(8,128)S(1)}, f32[448,128]{1,0:T(8,128)S(1)}, u32[]{:S(2)}, u32[]{:S(2)}) %collective-permute-start.5) | collective-permute-done | bytes 229408 | tf_op jit(solution)/shard_map/ppermute | solution.py:624
  28.7 0.0 collective-permute-start.10
  28.7 0.0 collective-permute-done.7.refs_6_
  28.7 1.2 %collective-permute-start.9 = (f32[512,128]{1,0:T(8,128)}, f32[512,128]{1,0:T(8,128)S(1)}, u32[]{:S(2)}, u32[]{:S(2)}) collective-permute-start(f32[512,128]{1,0:T(8,128)} %get-tuple-element.23.sigma.refs_0_), channel_id=1, source_target_pairs={{0,2},{1,3},{2,0},{3,1},{4,6},{5,7},{6,4},{7,5},{8,10},{9,11},{10,... | collective-permute-start | bytes 786440 | tf_op jit(solution)/shard_map/ppermute | solution.py:624
  29.8 0.0 collective-permute-done.1.refs_2_
  29.8 0.2 collective-permute-start.8
  30.1 1.3 %collective-permute-done.8.refs_7_ = f32[448,128]{1,0:T(8,128)S(1)} collective-permute-done((f32[448,128]{1,0:T(8,128)S(1)}, f32[448,128]{1,0:T(8,128)S(1)}, u32[]{:S(2)}, u32[]{:S(2)}) %collective-permute-start.8) | collective-permute-done | bytes 229408 | tf_op jit(solution)/shard_map/ppermute | solution.py:634
  31.3 10.8 %sweeps.1 = (f32[512,128]{1,0:T(8,128)}, f32[2880,128]{1,0:T(8,128)S(1)}) custom-call(s32[3,64]{1,0:T(4,128)S(1)} %bitcast.28, f32[1024,128]{1,0:T(8,128)S(1)} %copy-done.2, f32[1024,128]{1,0:T(8,128)S(1)} %collective-permute-done.refs_1_, f32[1024,128]{1,0:T(8,128)S(1)} %collective-permute-done.1.refs_2_, f32[1024,128]{1,0:T(8,128)S(1)} %collective-permute-done.2.refs_3_, ...), custom_call_target="tpu_custom_call" | custom-call | tf_op jit(solution)/shard_map/sweeps/pallas_call | solution.py:735
  42.2 0.0 collective-permute-done.10.refs_2_
  42.2 0.0 collective-permute-done.11.refs_3_
  42.2 8.8 %slab_steps.1 = (f32[32,4096]{1,0:T(8,128)}, f32[512,128]{1,0:T(8,128)S(1)}, f32[1024,128]{1,0:T(8,128)S(1)}, f32[512,128]{1,0:T(8,128)S(1)}) custom-call(s32[3,64]{1,0:T(4,128)S(1)} %bitcast.29, f32[4]{0:T(128)S(1)} %copy-done.4, f32[4]{0:T(128)S(1)} %copy-done.5, f32[512,128]{1,0:T(8,128)} %get-tuple-element.23.sigma.refs_0_, ...), custom_call_target="tpu_custom_call" | custom-call | tf_op jit(solution)/shard_map/slab_steps/pallas_call | solution.py:752
  51.0 0.3 collective-permute-start.12
  51.3 1.7 %collective-permute-done.12 = f32[1024,128]{1,0:T(8,128)S(1)} collective-permute-done((f32[1024,128]{1,0:T(8,128)S(1)}, f32[1024,128]{1,0:T(8,128)S(1)}, u32[]{:S(2)}, u32[]{:S(2)}) %collective-permute-start.12) | collective-permute-done | bytes 524320 | tf_op jit(solution)/shard_map/ppermute | solution.py:634
  53.0 0.9 %collective-permute-start.13 = (f32[512,128]{1,0:T(8,128)S(1)}, f32[512,128]{1,0:T(8,128)S(1)}, u32[]{:S(2)}, u32[]{:S(2)}) collective-permute-start(f32[512,128]{1,0:T(8,128)S(1)} %slice_add_fusion), channel_id=1, source_target_pairs={{0,2},{1,3},{2,0},{3,1},{4,6},{5,7},{6,4},{7,5},{8,10},{9,11},{10,... | collective-permute-start | bytes 786440 | tf_op jit(solution)/shard_map/ppermute | solution.py:624
  53.9 7.6 %collective-permute-done.13 = f32[512,128]{1,0:T(8,128)S(1)} collective-permute-done((f32[512,128]{1,0:T(8,128)S(1)}, f32[512,128]{1,0:T(8,128)S(1)}, u32[]{:S(2)}, u32[]{:S(2)}) %collective-permute-start.13) | collective-permute-done | bytes 262176 | tf_op jit(solution)/shard_map/ppermute | solution.py:624
  61.5 0.7 %fusion = f32[512,128]{1,0:T(8,128)} fusion(f32[512,128]{1,0:T(8,128)S(1)} %collective-permute-done.13, f32[512,128]{1,0:T(8,128)S(1)} %get-tuple-element.34, f32[1024,128]{1,0:T(8,128)S(1)} %collective-permute-done.12), kind=kLoop, calls=%fused_computation.2 | loop fusion | flops 131072 | bytes 1048576 | tf_op jit(solution)/shard_map/add | solution.py:770
  (15 shorter events, 0.1 us)
Async XLA Ops:
  0.6 21.0 %copy-start.3 = (s32[64,3]{0,1:T(4,128)S(1)}, s32[64,3]{0,1:T(4,128)}, u32[]{:S(2)}) copy-start(s32[64,3]{0,1:T(4,128)} %param.13) | copy-start | bytes 2308
  0.6 21.0 %copy-start = (f32[32,4096]{1,0:T(8,128)S(1)}, f32[32,4096]{1,0:T(8,128)}, u32[]{:S(2)}) copy-start(f32[32,4096]{1,0:T(8,128)} %temp.3) | copy-start | bytes 1572868
  0.7 21.0 %copy-start.1 = (s32[32,4096]{1,0:T(8,128)S(1)}, s32[32,4096]{1,0:T(8,128)}, u32[]{:S(2)}) copy-start(s32[32,4096]{1,0:T(8,128)} %mat.1) | copy-start | bytes 1572868
  0.7 21.0 %copy-start.4 = (f32[4]{0:T(128)S(1)}, f32[4]{0:T(128)}, u32[]{:S(2)}) copy-start(f32[4]{0:T(128)} %k0_table.3) | copy-start | bytes 52
  0.7 21.0 %copy-start.5 = (f32[4]{0:T(128)S(1)}, f32[4]{0:T(128)}, u32[]{:S(2)}) copy-start(f32[4]{0:T(128)} %beta_table.3) | copy-start | bytes 52
  4.4 26.9 %copy-start.2 = (f32[1024,128]{1,0:T(8,128)S(1)}, f32[1024,128]{1,0:T(8,128)}, u32[]{:S(2)}) copy-start(f32[1024,128]{1,0:T(8,128)} %get-tuple-element.20.refs_0_) | copy-start | bytes 1572868
  4.4 15.1 %collective-permute-start = (f32[1024,128]{1,0:T(8,128)}, f32[1024,128]{1,0:T(8,128)S(1)}, u32[]{:S(2)}, u32[]{:S(2)}) collective-permute-start(f32[1024,128]{1,0:T(8,128)} %get-tuple-element.20.refs_0_), channel_id=1, source_target_pairs={{0,2},{1,3},{2,0},{3,1},{4,6},{5,7},{6,4},{7,5},{8,10},{9,11},{10,... | collective-permute-start | bytes 1572872 | tf_op jit(solution)/shard_map/ppermute | solution.py:624
  7.4 22.4 %collective-permute-start.1 = (f32[1024,128]{1,0:T(8,128)}, f32[1024,128]{1,0:T(8,128)S(1)}, u32[]{:S(2)}, u32[]{:S(2)}) collective-permute-start(f32[1024,128]{1,0:T(8,128)} %get-tuple-element.20.refs_0_), channel_id=1, source_target_pairs={{0,1},{1,0},{2,3},{3,2},{4,5},{5,4},{6,7},{7,6},{8,9},{9,8},{10,11... | collective-permute-start | bytes 1572872 | tf_op jit(solution)/shard_map/ppermute | solution.py:634
  7.4 13.3 %collective-permute-start.3 = (f32[496,128]{1,0:T(8,128)}, f32[496,128]{1,0:T(8,128)S(1)}, u32[]{:S(2)}, u32[]{:S(2)}) collective-permute-start(f32[496,128]{1,0:T(8,128)} %get-tuple-element.21), channel_id=1, source_target_pairs={{0,4},{8,12},{16,20},{24,28},{4,0},{12,8},{20,16},{28,24},{1,5},{9... | collective-permute-start | bytes 761864 | tf_op jit(solution)/shard_map/ppermute | solution.py:630
  9.0 11.8 %collective-permute-start.4 = (f32[496,128]{1,0:T(8,128)}, f32[496,128]{1,0:T(8,128)S(1)}, u32[]{:S(2)}, u32[]{:S(2)}) collective-permute-start(f32[496,128]{1,0:T(8,128)} %get-tuple-element.22), channel_id=1, source_target_pairs={{4,8},{12,16},{20,24},{8,4},{16,12},{24,20},{5,9},{13,17},{21,25},... | collective-permute-start | bytes 761864 | tf_op jit(solution)/shard_map/ppermute | solution.py:630
  19.6 11.8 %collective-permute-start.2 = (f32[1024,128]{1,0:T(8,128)S(1)}, f32[1024,128]{1,0:T(8,128)S(1)}, u32[]{:S(2)}, u32[]{:S(2)}) collective-permute-start(f32[1024,128]{1,0:T(8,128)S(1)} %collective-permute-done.refs_1_), channel_id=1, source_target_pairs={{0,1},{1,0},{2,3},{3,2},{4,5},{5,4},{6,7},{7,6},{8,9},{9,8},{10,11... | collective-permute-start | bytes 1572872 | tf_op jit(solution)/shard_map/ppermute | solution.py:634
  20.8 7.9 %collective-permute-start.5 = (f32[448,128]{1,0:T(8,128)S(1)}, f32[448,128]{1,0:T(8,128)S(1)}, u32[]{:S(2)}, u32[]{:S(2)}) collective-permute-start(f32[448,128]{1,0:T(8,128)S(1)} %relay.1.refs_4_), channel_id=1, source_target_pairs={{0,2},{1,3},{2,0},{3,1},{4,6},{5,7},{6,4},{7,5},{8,10},{9,11},{10,... | collective-permute-start | bytes 688136 | tf_op jit(solution)/shard_map/ppermute | solution.py:624
  21.4 7.2 %collective-permute-start.7 = (f32[448,128]{1,0:T(8,128)S(1)}, f32[448,128]{1,0:T(8,128)S(1)}, u32[]{:S(2)}, u32[]{:S(2)}) collective-permute-start(f32[448,128]{1,0:T(8,128)S(1)} %relay.1.refs_4_), channel_id=1, source_target_pairs={{0,1},{1,0},{2,3},{3,2},{4,5},{5,4},{6,7},{7,6},{8,9},{9,8},{10,11... | collective-permute-start | bytes 688136 | tf_op jit(solution)/shard_map/ppermute | solution.py:634
  23.2 1.3 %collective-permute-start.6 = (f32[120,128]{1,0:T(8,128)S(1)}, f32[120,128]{1,0:T(8,128)S(1)}, u32[]{:S(2)}, u32[]{:S(2)}) collective-permute-start(f32[120,128]{1,0:T(8,128)S(1)} %get-tuple-element.24), channel_id=1, source_target_pairs={{0,1},{2,3},{1,0},{3,2},{4,5},{6,7},{5,4},{7,6},{8,9},{10,11},{9,8... | collective-permute-start | bytes 184328 | tf_op jit(solution)/shard_map/ppermute | solution.py:630
  24.5 17.7 %collective-permute-start.11 = (f32[632,128]{1,0:T(8,128)S(1)}, f32[632,128]{1,0:T(8,128)S(1)}, u32[]{:S(2)}, u32[]{:S(2)}) collective-permute-start(f32[632,128]{1,0:T(8,128)S(1)} %get-tuple-element.27), channel_id=1, source_target_pairs={{0,3},{1,2},{2,1},{3,0},{4,7},{5,6},{6,5},{7,4},{8,11},{9,10},{10,... | collective-permute-start | bytes 970760 | tf_op jit(solution)/shard_map/ppermute | solution.py:647
  28.7 13.5 %collective-permute-start.10 = (f32[512,128]{1,0:T(8,128)}, f32[512,128]{1,0:T(8,128)S(1)}, u32[]{:S(2)}, u32[]{:S(2)}) collective-permute-start(f32[512,128]{1,0:T(8,128)} %get-tuple-element.23.sigma.refs_0_), channel_id=1, source_target_pairs={{0,1},{1,0},{2,3},{3,2},{4,5},{5,4},{6,7},{7,6},{8,9},{9,8},{10,11... | collective-permute-start | bytes 786440 | tf_op jit(solution)/shard_map/ppermute | solution.py:634
  28.7 13.5 %collective-permute-start.9 = (f32[512,128]{1,0:T(8,128)}, f32[512,128]{1,0:T(8,128)S(1)}, u32[]{:S(2)}, u32[]{:S(2)}) collective-permute-start(f32[512,128]{1,0:T(8,128)} %get-tuple-element.23.sigma.refs_0_), channel_id=1, source_target_pairs={{0,2},{1,3},{2,0},{3,1},{4,6},{5,7},{6,4},{7,5},{8,10},{9,11},{10,... | collective-permute-start | bytes 786440 | tf_op jit(solution)/shard_map/ppermute | solution.py:624
  29.8 1.5 %collective-permute-start.8 = (f32[448,128]{1,0:T(8,128)S(1)}, f32[448,128]{1,0:T(8,128)S(1)}, u32[]{:S(2)}, u32[]{:S(2)}) collective-permute-start(f32[448,128]{1,0:T(8,128)S(1)} %collective-permute-done.5.refs_5_), channel_id=1, source_target_pairs={{0,1},{1,0},{2,3},{3,2},{4,5},{5,4},{6,7},{7,6},{8,9},{9,8},{10,11... | collective-permute-start | bytes 688136 | tf_op jit(solution)/shard_map/ppermute | solution.py:634
  51.0 2.0 %collective-permute-start.12 = (f32[1024,128]{1,0:T(8,128)S(1)}, f32[1024,128]{1,0:T(8,128)S(1)}, u32[]{:S(2)}, u32[]{:S(2)}) collective-permute-start(f32[1024,128]{1,0:T(8,128)S(1)} %get-tuple-element.35), channel_id=1, source_target_pairs={{0,1},{1,0},{2,3},{3,2},{4,5},{5,4},{6,7},{7,6},{8,9},{9,8},{10,11... | collective-permute-start | bytes 1572872 | tf_op jit(solution)/shard_map/ppermute | solution.py:634
  53.0 8.5 %collective-permute-start.13 = (f32[512,128]{1,0:T(8,128)S(1)}, f32[512,128]{1,0:T(8,128)S(1)}, u32[]{:S(2)}, u32[]{:S(2)}) collective-permute-start(f32[512,128]{1,0:T(8,128)S(1)} %slice_add_fusion), channel_id=1, source_target_pairs={{0,2},{1,3},{2,0},{3,1},{4,6},{5,7},{6,4},{7,5},{8,10},{9,11},{10,... | collective-permute-start | bytes 786440 | tf_op jit(solution)/shard_map/ppermute | solution.py:624
